TPU v7x, 32 devices: a whole 2x2x4 slice. The times are simulated.
32 devices in a mesh: groups: 2 (over y), tm: 4 (over z), segment: 2 (over x), chan: 2 (over core).
Axes of the slice: x: 2, y: 2, z: 4, core: 2. Of those that a mesh axis runs over, the one named last changes fastest.
Arguments:
- records: bfloat16 [8, 1024, 256], P('groups', 'tm', 'chan'), parts along dimension 0, may hold values from -6 to 6
- conv_weight: bfloat16 [8, 512, 2, 256], P('segment', None, None, 'chan'), may hold values from -0.25 to 0.25
- conv_bias: bfloat16 [8, 2, 256], P('segment', None, 'chan'), may hold values from -3 to 3
- res_weight: bfloat16 [8, 256, 256], P('segment'), may hold values from -0.375 to 0.375
- skip_weight: bfloat16 [8, 256, 256], P('segment', None, 'chan'), may hold values from -0.375 to 0.375
Outputs:
- skip_out: bfloat16 [8, 1024, 256], P(('groups', 'segment'), 'tm', 'chan'), parts along dimension 0
There are 2 independent parts, one for each index of `groups`. A program takes and returns all parts, laid end to end along the dimension named above; an argument that names none is the same for every part. Nothing has to cross between parts.
All inputs are finite; a program needn't handle non-finite values.
Results may differ from a plain program's by a relative error of at most 0.011.
Values may be sent and summed in bfloat16 or wider, within the bound.
No kernel may reach another device: no remote copies, remote signals or barrier semaphores. Data moves between devices by JAX's collectives and lax.ppermute only.
A program may use at most 64 MiB of HBM per device.

v0:
```python
import jax
import jax.numpy as jnp
from jax import lax
from jax.sharding import PartitionSpec as P


def from_behind(block, axis, distance):
    devices = range(lax.axis_size(axis))
    route = [(i - distance, i) for i in devices if i - distance in devices]
    return lax.ppermute(block, axis, route)


def lagged(stream, lag_size):
    seg_rows = stream.shape[1]
    if lag_size < seg_rows:
        tail_rows = stream[:, seg_rows - lag_size :, :]
        received = from_behind(tail_rows, "tm", 1)
        return jnp.concatenate([received, stream[:, : seg_rows - lag_size, :]], axis=1)
    return from_behind(stream, "tm", lag_size // seg_rows)


def layer_stack(stream, conv_weight, conv_bias, res_weight, skip_weight, shard_rows):
    seg_rows = stream.shape[1]
    tm_count = lax.axis_size("tm")
    lag_sizes = [
        shard_rows // 8,
        shard_rows,
        shard_rows * max(1, tm_count // 8),
        shard_rows * max(1, tm_count // 2),
    ]
    own_width = skip_weight.shape[2]
    skip_total = jnp.zeros((stream.shape[0], seg_rows, own_width), jnp.float32)
    for depth in range(conv_weight.shape[0]):
        past_rows = lagged(stream, lag_sizes[depth % 4])
        now_full, past_full = (stream, past_rows)
        full_width = now_full.shape[2]
        pre_act = jnp.einsum(
            "bsk,kgc->bsgc",
            past_full,
            conv_weight[depth, :full_width],
            preferred_element_type=jnp.float32,
        )
        pre_act = pre_act + jnp.einsum(
            "bsk,kgc->bsgc",
            now_full,
            conv_weight[depth, full_width:],
            preferred_element_type=jnp.float32,
        )
        pre_act = pre_act + conv_bias[depth].astype(jnp.float32)
        gate_out = (jnp.tanh(pre_act[:, :, 0, :]) * jax.nn.sigmoid(pre_act[:, :, 1, :])).astype(
            jnp.bfloat16
        )
        full_units = lax.all_gather(gate_out, "chan", axis=2, tiled=True)
        skip_total = skip_total + jnp.einsum(
            "bsk,kc->bsc", full_units, skip_weight[depth], preferred_element_type=jnp.float32
        )
        res_columns = res_weight[depth]
        update = jnp.einsum(
            "bsk,kc->bsc", full_units, res_columns, preferred_element_type=jnp.float32
        )
        stream = (stream.astype(jnp.float32) + update).astype(jnp.bfloat16)
    return (stream, skip_total)


def shards(records, conv_weight, conv_bias, res_weight, skip_weight):
    shard_rows = records.shape[1]
    stream_in = lax.all_gather(records, "chan", axis=2, tiled=True)
    segment_id = lax.axis_index("segment")
    sections = lax.axis_size("segment")
    record_count = records.shape[0]
    seg_rows = stream_in.shape[1]
    own_width = skip_weight.shape[2]
    held_stream = jnp.zeros_like(stream_in[0:1])
    skip_acc = jnp.zeros((record_count, seg_rows, own_width), jnp.float32)

    def step_tick(moment, state_pair):
        held_stream, skip_acc = state_pair
        fresh_input = lax.dynamic_slice_in_dim(
            stream_in, jnp.minimum(moment, record_count - 1), 1, 0
        )
        current = jnp.where(segment_id == 0, fresh_input, held_stream)
        out_stream, skip_part = layer_stack(
            current, conv_weight, conv_bias, res_weight, skip_weight, shard_rows
        )
        record_slot = moment - segment_id
        is_valid = jnp.logical_and(record_slot >= 0, record_slot < record_count)
        clipped = jnp.clip(record_slot, 0, record_count - 1)
        prior_sum = lax.dynamic_slice_in_dim(skip_acc, clipped, 1, 0)
        skip_acc = lax.dynamic_update_slice_in_dim(
            skip_acc, prior_sum + jnp.where(is_valid, skip_part, 0.0), clipped, 0
        )
        held_stream = from_behind(out_stream, "segment", 1)
        return (held_stream, skip_acc)

    held_stream, skip_acc = lax.fori_loop(
        0, record_count + sections - 1, step_tick, (held_stream, skip_acc)
    )
    result = lax.psum_scatter(
        skip_acc.astype(jnp.bfloat16), "segment", scatter_dimension=0, tiled=True
    )
    return result


def solution(mesh):
    return jax.shard_map(
        shards,
        mesh=mesh,
        in_specs=(
            P("groups", "tm", "chan"),
            P("segment", None, None, "chan"),
            P("segment", None, "chan"),
            P("segment", None, None),
            P("segment", None, "chan"),
        ),
        out_specs=P(("groups", "segment"), "tm", "chan"),
        check_vma=False,
    )
```

profile of v0, /device:TPU:0, one launch (start us, length us, event | category | flops | bytes accessed | tf_op | source)
XLA Modules:
  0.0 273.3 jit_solution(13598324782009054806)
XLA Ops:
  6.5 2.5 all_gather.35
  11.5 236.7 %while.16 = (s32[]{:T(128)}, bf16[1,256,256]{2,1,0:T(8,128)(2,1)S(1)}, f32[4,256,128]{2,1,0:T(8,128)S(1)}, pred[]{:T(512)}, bf16[4,256,256]{2,1,0:T(8,128)(2,1)S...) while((s32[]{:T(128)}, ...), condition=%wide.region_1.2_spmd, body=%wide.region_0.1_spmd.sunk | while | flops 472220672 | bytes 14100926 | solution.py:95
  11.5 4.9 %collective-permute-start = (bf16[1,32,256]{2,1,0:T(8,128)(2,1)S(1)}, bf16[1,32,256]{2,1,0:T(8,128)(2,1)S(1)}, u32[]{:S(2)}, u32[]{:S(2)}) collective-permute-start(bf16[1,32,256]{2,1,0:T(8,128)(2,1)S(1)} %slice.435), channel_id=1, source_target_pairs={{0,4},{4,8},{8,12},{1,5},{5,9},{9,13},{2,6},{6,10},{10,14},{3,7},{... | collective-permute-start | bytes 49160 | tf_op jit(solution)/shard_map/while/body/eval_jaxpr/ppermute | solution.py:10
  18.0 1.9 all-gather.8
  20.1 4.2 %collective-permute-start.1 = (bf16[1,256,256]{2,1,0:T(8,128)(2,1)S(1)}, bf16[1,256,256]{2,1,0:T(8,128)(2,1)S(1)}, u32[]{:S(2)}, u32[]{:S(2)}) collective-permute-start(bf16[1,256,256]{2,1,0:T(8,128)(2,1)S(1)} %fusion.178), channel_id=1, source_target_pairs={{0,4},{4,8},{8,12},{1,5},{5,9},{9,13},{2,6},{6,10},{10,14},{3,7},{... | collective-permute-start | bytes 393224 | tf_op jit(solution)/shard_map/while/body/eval_jaxpr/ppermute | solution.py:10
  24.7 2.7 collective-permute-done.1
  27.7 1.9 all-gather.9
  29.8 4.4 %collective-permute-start.2 = (bf16[1,256,256]{2,1,0:T(8,128)(2,1)S(1)}, bf16[1,256,256]{2,1,0:T(8,128)(2,1)S(1)}, u32[]{:S(2)}, u32[]{:S(2)}) collective-permute-start(bf16[1,256,256]{2,1,0:T(8,128)(2,1)S(1)} %fusion.182), channel_id=1, source_target_pairs={{0,4},{4,8},{8,12},{1,5},{5,9},{9,13},{2,6},{6,10},{10,14},{3,7},{... | collective-permute-start | bytes 393224 | tf_op jit(solution)/shard_map/while/body/eval_jaxpr/ppermute | solution.py:10
  34.5 2.7 collective-permute-done.2
  37.5 1.9 all-gather.10
  39.6 5.4 %collective-permute-start.3 = (bf16[1,256,256]{2,1,0:T(8,128)(2,1)S(1)}, bf16[1,256,256]{2,1,0:T(8,128)(2,1)S(1)}, u32[]{:S(2)}, u32[]{:S(2)}) collective-permute-start(bf16[1,256,256]{2,1,0:T(8,128)(2,1)S(1)} %fusion.186), channel_id=1, source_target_pairs={{0,8},{4,12},{1,9},{5,13},{2,10},{6,14},{3,11},{7,15},{16,24},{20,... | collective-permute-start | bytes 393224 | tf_op jit(solution)/shard_map/while/body/eval_jaxpr/ppermute | solution.py:10
  45.4 2.7 collective-permute-done.3
  48.4 1.9 all-gather.11
  50.5 3.4 %collective-permute-start.4 = (bf16[1,256,256]{2,1,0:T(8,128)(2,1)S(1)}, bf16[1,256,256]{2,1,0:T(8,128)(2,1)S(1)}, u32[]{:S(2)}, u32[]{:S(2)}) collective-permute-start(bf16[1,256,256]{2,1,0:T(8,128)(2,1)S(1)} %fusion.190), channel_id=1, source_target_pairs={{0,2},{1,3},{4,6},{5,7},{8,10},{9,11},{12,14},{13,15},{16,18},{17,... | collective-permute-start | bytes 393224 | tf_op jit(solution)/shard_map/while/body/eval_jaxpr/ppermute | solution.py:10
  54.1 2.9 %collective-permute-done.4 = bf16[1,256,256]{2,1,0:T(8,128)(2,1)S(1)} collective-permute-done((bf16[1,256,256]{2,1,0:T(8,128)(2,1)S(1)}, bf16[1,256,256]{2,1,0:T(8,128)(2,1)S(1)}, u32[]{:S(2)}, u32[]{:S(2)}) %collective-permute-start.4) | collective-permute-done | bytes 131104 | tf_op jit(solution)/shard_map/while/body/eval_jaxpr/ppermute | solution.py:10
  57.0 6.1 %collective-permute-start = (bf16[1,32,256]{2,1,0:T(8,128)(2,1)S(1)}, bf16[1,32,256]{2,1,0:T(8,128)(2,1)S(1)}, u32[]{:S(2)}, u32[]{:S(2)}) collective-permute-start(bf16[1,32,256]{2,1,0:T(8,128)(2,1)S(1)} %slice.435), channel_id=1, source_target_pairs={{0,4},{4,8},{8,12},{1,5},{5,9},{9,13},{2,6},{6,10},{10,14},{3,7},{... | collective-permute-start | bytes 49160 | tf_op jit(solution)/shard_map/while/body/eval_jaxpr/ppermute | solution.py:10
  64.8 1.9 all-gather.8
  66.9 4.2 %collective-permute-start.1 = (bf16[1,256,256]{2,1,0:T(8,128)(2,1)S(1)}, bf16[1,256,256]{2,1,0:T(8,128)(2,1)S(1)}, u32[]{:S(2)}, u32[]{:S(2)}) collective-permute-start(bf16[1,256,256]{2,1,0:T(8,128)(2,1)S(1)} %fusion.178), channel_id=1, source_target_pairs={{0,4},{4,8},{8,12},{1,5},{5,9},{9,13},{2,6},{6,10},{10,14},{3,7},{... | collective-permute-start | bytes 393224 | tf_op jit(solution)/shard_map/while/body/eval_jaxpr/ppermute | solution.py:10
  71.5 2.7 collective-permute-done.1
  74.4 1.9 all-gather.9
  76.5 4.4 %collective-permute-start.2 = (bf16[1,256,256]{2,1,0:T(8,128)(2,1)S(1)}, bf16[1,256,256]{2,1,0:T(8,128)(2,1)S(1)}, u32[]{:S(2)}, u32[]{:S(2)}) collective-permute-start(bf16[1,256,256]{2,1,0:T(8,128)(2,1)S(1)} %fusion.182), channel_id=1, source_target_pairs={{0,4},{4,8},{8,12},{1,5},{5,9},{9,13},{2,6},{6,10},{10,14},{3,7},{... | collective-permute-start | bytes 393224 | tf_op jit(solution)/shard_map/while/body/eval_jaxpr/ppermute | solution.py:10
  81.3 2.7 collective-permute-done.2
  84.2 1.9 all-gather.10
  86.3 5.5 %collective-permute-start.3 = (bf16[1,256,256]{2,1,0:T(8,128)(2,1)S(1)}, bf16[1,256,256]{2,1,0:T(8,128)(2,1)S(1)}, u32[]{:S(2)}, u32[]{:S(2)}) collective-permute-start(bf16[1,256,256]{2,1,0:T(8,128)(2,1)S(1)} %fusion.186), channel_id=1, source_target_pairs={{0,8},{4,12},{1,9},{5,13},{2,10},{6,14},{3,11},{7,15},{16,24},{20,... | collective-permute-start | bytes 393224 | tf_op jit(solution)/shard_map/while/body/eval_jaxpr/ppermute | solution.py:10
  92.2 2.7 collective-permute-done.3
  95.2 1.9 all-gather.11
  97.3 4.4 %collective-permute-start.4 = (bf16[1,256,256]{2,1,0:T(8,128)(2,1)S(1)}, bf16[1,256,256]{2,1,0:T(8,128)(2,1)S(1)}, u32[]{:S(2)}, u32[]{:S(2)}) collective-permute-start(bf16[1,256,256]{2,1,0:T(8,128)(2,1)S(1)} %fusion.190), channel_id=1, source_target_pairs={{0,2},{1,3},{4,6},{5,7},{8,10},{9,11},{12,14},{13,15},{16,18},{17,... | collective-permute-start | bytes 393224 | tf_op jit(solution)/shard_map/while/body/eval_jaxpr/ppermute | solution.py:10
  101.9 2.9 %collective-permute-done.4 = bf16[1,256,256]{2,1,0:T(8,128)(2,1)S(1)} collective-permute-done((bf16[1,256,256]{2,1,0:T(8,128)(2,1)S(1)}, bf16[1,256,256]{2,1,0:T(8,128)(2,1)S(1)}, u32[]{:S(2)}, u32[]{:S(2)}) %collective-permute-start.4) | collective-permute-done | bytes 131104 | tf_op jit(solution)/shard_map/while/body/eval_jaxpr/ppermute | solution.py:10
  104.8 6.1 %collective-permute-start = (bf16[1,32,256]{2,1,0:T(8,128)(2,1)S(1)}, bf16[1,32,256]{2,1,0:T(8,128)(2,1)S(1)}, u32[]{:S(2)}, u32[]{:S(2)}) collective-permute-start(bf16[1,32,256]{2,1,0:T(8,128)(2,1)S(1)} %slice.435), channel_id=1, source_target_pairs={{0,4},{4,8},{8,12},{1,5},{5,9},{9,13},{2,6},{6,10},{10,14},{3,7},{... | collective-permute-start | bytes 49160 | tf_op jit(solution)/shard_map/while/body/eval_jaxpr/ppermute | solution.py:10
  112.6 1.9 all-gather.8
  114.7 4.2 %collective-permute-start.1 = (bf16[1,256,256]{2,1,0:T(8,128)(2,1)S(1)}, bf16[1,256,256]{2,1,0:T(8,128)(2,1)S(1)}, u32[]{:S(2)}, u32[]{:S(2)}) collective-permute-start(bf16[1,256,256]{2,1,0:T(8,128)(2,1)S(1)} %fusion.178), channel_id=1, source_target_pairs={{0,4},{4,8},{8,12},{1,5},{5,9},{9,13},{2,6},{6,10},{10,14},{3,7},{... | collective-permute-start | bytes 393224 | tf_op jit(solution)/shard_map/while/body/eval_jaxpr/ppermute | solution.py:10
  119.3 2.7 collective-permute-done.1
  122.2 1.9 all-gather.9
  124.3 4.4 %collective-permute-start.2 = (bf16[1,256,256]{2,1,0:T(8,128)(2,1)S(1)}, bf16[1,256,256]{2,1,0:T(8,128)(2,1)S(1)}, u32[]{:S(2)}, u32[]{:S(2)}) collective-permute-start(bf16[1,256,256]{2,1,0:T(8,128)(2,1)S(1)} %fusion.182), channel_id=1, source_target_pairs={{0,4},{4,8},{8,12},{1,5},{5,9},{9,13},{2,6},{6,10},{10,14},{3,7},{... | collective-permute-start | bytes 393224 | tf_op jit(solution)/shard_map/while/body/eval_jaxpr/ppermute | solution.py:10
  129.1 2.7 collective-permute-done.2
  132.0 1.9 all-gather.10
  134.1 5.5 %collective-permute-start.3 = (bf16[1,256,256]{2,1,0:T(8,128)(2,1)S(1)}, bf16[1,256,256]{2,1,0:T(8,128)(2,1)S(1)}, u32[]{:S(2)}, u32[]{:S(2)}) collective-permute-start(bf16[1,256,256]{2,1,0:T(8,128)(2,1)S(1)} %fusion.186), channel_id=1, source_target_pairs={{0,8},{4,12},{1,9},{5,13},{2,10},{6,14},{3,11},{7,15},{16,24},{20,... | collective-permute-start | bytes 393224 | tf_op jit(solution)/shard_map/while/body/eval_jaxpr/ppermute | solution.py:10
  140.0 2.7 collective-permute-done.3
  143.0 1.9 all-gather.11
  145.1 4.4 %collective-permute-start.4 = (bf16[1,256,256]{2,1,0:T(8,128)(2,1)S(1)}, bf16[1,256,256]{2,1,0:T(8,128)(2,1)S(1)}, u32[]{:S(2)}, u32[]{:S(2)}) collective-permute-start(bf16[1,256,256]{2,1,0:T(8,128)(2,1)S(1)} %fusion.190), channel_id=1, source_target_pairs={{0,2},{1,3},{4,6},{5,7},{8,10},{9,11},{12,14},{13,15},{16,18},{17,... | collective-permute-start | bytes 393224 | tf_op jit(solution)/shard_map/while/body/eval_jaxpr/ppermute | solution.py:10
  149.7 2.9 %collective-permute-done.4 = bf16[1,256,256]{2,1,0:T(8,128)(2,1)S(1)} collective-permute-done((bf16[1,256,256]{2,1,0:T(8,128)(2,1)S(1)}, bf16[1,256,256]{2,1,0:T(8,128)(2,1)S(1)}, u32[]{:S(2)}, u32[]{:S(2)}) %collective-permute-start.4) | collective-permute-done | bytes 131104 | tf_op jit(solution)/shard_map/while/body/eval_jaxpr/ppermute | solution.py:10
  152.6 6.1 %collective-permute-start = (bf16[1,32,256]{2,1,0:T(8,128)(2,1)S(1)}, bf16[1,32,256]{2,1,0:T(8,128)(2,1)S(1)}, u32[]{:S(2)}, u32[]{:S(2)}) collective-permute-start(bf16[1,32,256]{2,1,0:T(8,128)(2,1)S(1)} %slice.435), channel_id=1, source_target_pairs={{0,4},{4,8},{8,12},{1,5},{5,9},{9,13},{2,6},{6,10},{10,14},{3,7},{... | collective-permute-start | bytes 49160 | tf_op jit(solution)/shard_map/while/body/eval_jaxpr/ppermute | solution.py:10
  160.4 1.9 all-gather.8
  162.5 4.2 %collective-permute-start.1 = (bf16[1,256,256]{2,1,0:T(8,128)(2,1)S(1)}, bf16[1,256,256]{2,1,0:T(8,128)(2,1)S(1)}, u32[]{:S(2)}, u32[]{:S(2)}) collective-permute-start(bf16[1,256,256]{2,1,0:T(8,128)(2,1)S(1)} %fusion.178), channel_id=1, source_target_pairs={{0,4},{4,8},{8,12},{1,5},{5,9},{9,13},{2,6},{6,10},{10,14},{3,7},{... | collective-permute-start | bytes 393224 | tf_op jit(solution)/shard_map/while/body/eval_jaxpr/ppermute | solution.py:10
  167.1 2.7 collective-permute-done.1
  170.0 1.9 all-gather.9
  172.1 4.4 %collective-permute-start.2 = (bf16[1,256,256]{2,1,0:T(8,128)(2,1)S(1)}, bf16[1,256,256]{2,1,0:T(8,128)(2,1)S(1)}, u32[]{:S(2)}, u32[]{:S(2)}) collective-permute-start(bf16[1,256,256]{2,1,0:T(8,128)(2,1)S(1)} %fusion.182), channel_id=1, source_target_pairs={{0,4},{4,8},{8,12},{1,5},{5,9},{9,13},{2,6},{6,10},{10,14},{3,7},{... | collective-permute-start | bytes 393224 | tf_op jit(solution)/shard_map/while/body/eval_jaxpr/ppermute | solution.py:10
  176.9 2.7 collective-permute-done.2
  179.9 1.9 all-gather.10
  182.0 5.5 %collective-permute-start.3 = (bf16[1,256,256]{2,1,0:T(8,128)(2,1)S(1)}, bf16[1,256,256]{2,1,0:T(8,128)(2,1)S(1)}, u32[]{:S(2)}, u32[]{:S(2)}) collective-permute-start(bf16[1,256,256]{2,1,0:T(8,128)(2,1)S(1)} %fusion.186), channel_id=1, source_target_pairs={{0,8},{4,12},{1,9},{5,13},{2,10},{6,14},{3,11},{7,15},{16,24},{20,... | collective-permute-start | bytes 393224 | tf_op jit(solution)/shard_map/while/body/eval_jaxpr/ppermute | solution.py:10
  187.8 2.7 collective-permute-done.3
  190.8 1.9 all-gather.11
  192.9 4.4 %collective-permute-start.4 = (bf16[1,256,256]{2,1,0:T(8,128)(2,1)S(1)}, bf16[1,256,256]{2,1,0:T(8,128)(2,1)S(1)}, u32[]{:S(2)}, u32[]{:S(2)}) collective-permute-start(bf16[1,256,256]{2,1,0:T(8,128)(2,1)S(1)} %fusion.190), channel_id=1, source_target_pairs={{0,2},{1,3},{4,6},{5,7},{8,10},{9,11},{12,14},{13,15},{16,18},{17,... | collective-permute-start | bytes 393224 | tf_op jit(solution)/shard_map/while/body/eval_jaxpr/ppermute | solution.py:10
  197.5 2.9 %collective-permute-done.4 = bf16[1,256,256]{2,1,0:T(8,128)(2,1)S(1)} collective-permute-done((bf16[1,256,256]{2,1,0:T(8,128)(2,1)S(1)}, bf16[1,256,256]{2,1,0:T(8,128)(2,1)S(1)}, u32[]{:S(2)}, u32[]{:S(2)}) %collective-permute-start.4) | collective-permute-done | bytes 131104 | tf_op jit(solution)/shard_map/while/body/eval_jaxpr/ppermute | solution.py:10
  200.4 6.1 %collective-permute-start = (bf16[1,32,256]{2,1,0:T(8,128)(2,1)S(1)}, bf16[1,32,256]{2,1,0:T(8,128)(2,1)S(1)}, u32[]{:S(2)}, u32[]{:S(2)}) collective-permute-start(bf16[1,32,256]{2,1,0:T(8,128)(2,1)S(1)} %slice.435), channel_id=1, source_target_pairs={{0,4},{4,8},{8,12},{1,5},{5,9},{9,13},{2,6},{6,10},{10,14},{3,7},{... | collective-permute-start | bytes 49160 | tf_op jit(solution)/shard_map/while/body/eval_jaxpr/ppermute | solution.py:10
  210.3 4.2 %collective-permute-start.1 = (bf16[1,256,256]{2,1,0:T(8,128)(2,1)S(1)}, bf16[1,256,256]{2,1,0:T(8,128)(2,1)S(1)}, u32[]{:S(2)}, u32[]{:S(2)}) collective-permute-start(bf16[1,256,256]{2,1,0:T(8,128)(2,1)S(1)} %fusion.178), channel_id=1, source_target_pairs={{0,4},{4,8},{8,12},{1,5},{5,9},{9,13},{2,6},{6,10},{10,14},{3,7},{... | collective-permute-start | bytes 393224 | tf_op jit(solution)/shard_map/while/body/eval_jaxpr/ppermute | solution.py:10
  214.9 2.7 collective-permute-done.1
  220.0 4.4 %collective-permute-start.2 = (bf16[1,256,256]{2,1,0:T(8,128)(2,1)S(1)}, bf16[1,256,256]{2,1,0:T(8,128)(2,1)S(1)}, u32[]{:S(2)}, u32[]{:S(2)}) collective-permute-start(bf16[1,256,256]{2,1,0:T(8,128)(2,1)S(1)} %fusion.182), channel_id=1, source_target_pairs={{0,4},{4,8},{8,12},{1,5},{5,9},{9,13},{2,6},{6,10},{10,14},{3,7},{... | collective-permute-start | bytes 393224 | tf_op jit(solution)/shard_map/while/body/eval_jaxpr/ppermute | solution.py:10
  224.7 2.7 collective-permute-done.2
  229.8 5.5 %collective-permute-start.3 = (bf16[1,256,256]{2,1,0:T(8,128)(2,1)S(1)}, bf16[1,256,256]{2,1,0:T(8,128)(2,1)S(1)}, u32[]{:S(2)}, u32[]{:S(2)}) collective-permute-start(bf16[1,256,256]{2,1,0:T(8,128)(2,1)S(1)} %fusion.186), channel_id=1, source_target_pairs={{0,8},{4,12},{1,9},{5,13},{2,10},{6,14},{3,11},{7,15},{16,24},{20,... | collective-permute-start | bytes 393224 | tf_op jit(solution)/shard_map/while/body/eval_jaxpr/ppermute | solution.py:10
  235.6 2.7 collective-permute-done.3
  240.7 4.4 %collective-permute-start.4 = (bf16[1,256,256]{2,1,0:T(8,128)(2,1)S(1)}, bf16[1,256,256]{2,1,0:T(8,128)(2,1)S(1)}, u32[]{:S(2)}, u32[]{:S(2)}) collective-permute-start(bf16[1,256,256]{2,1,0:T(8,128)(2,1)S(1)} %fusion.190), channel_id=1, source_target_pairs={{0,2},{1,3},{4,6},{5,7},{8,10},{9,11},{12,14},{13,15},{16,18},{17,... | collective-permute-start | bytes 393224 | tf_op jit(solution)/shard_map/while/body/eval_jaxpr/ppermute | solution.py:10
  245.3 2.9 %collective-permute-done.4 = bf16[1,256,256]{2,1,0:T(8,128)(2,1)S(1)} collective-permute-done((bf16[1,256,256]{2,1,0:T(8,128)(2,1)S(1)}, bf16[1,256,256]{2,1,0:T(8,128)(2,1)S(1)}, u32[]{:S(2)}, u32[]{:S(2)}) %collective-permute-start.4) | collective-permute-done | bytes 131104 | tf_op jit(solution)/shard_map/while/body/eval_jaxpr/ppermute | solution.py:10
  248.9 17.5 %reduce-scatter.2.cloned.1.call-done = bf16[2,256,128]{2,1,0:T(8,128)(2,1)} async-done(((bf16[4,256,128]{2,1,0:T(8,128)(2,1)}), bf16[2,256,128]{2,1,0:T(8,128)(2,1)}) %reduce-scatter.2.cloned.1.call-update) | async-done | bytes 131088 | tf_op jit(solution)/shard_map/reduce_scatter | solution.py:98
  (141 shorter events, 32.7 us)
Async XLA Ops:
  6.5 259.9 %reduce-scatter.2.cloned.1.call-start = ((), (), s32[]{:S(2)}) async-start(), calls=%async_computation.1 | async-start | bytes 393216 | tf_op jit(solution)/shard_map/reduce_scatter | solution.py:98
  9.0 1.5 copy-start.1
  10.4 1.0 copy-start
  10.4 1.0 copy-start.2
  11.5 6.3 %collective-permute-start = (bf16[1,32,256]{2,1,0:T(8,128)(2,1)S(1)}, bf16[1,32,256]{2,1,0:T(8,128)(2,1)S(1)}, u32[]{:S(2)}, u32[]{:S(2)}) collective-permute-start(bf16[1,32,256]{2,1,0:T(8,128)(2,1)S(1)} %slice.435), channel_id=1, source_target_pairs={{0,4},{4,8},{8,12},{1,5},{5,9},{9,13},{2,6},{6,10},{10,14},{3,7},{... | collective-permute-start | bytes 49160 | tf_op jit(solution)/shard_map/while/body/eval_jaxpr/ppermute | solution.py:10
  20.1 7.3 %collective-permute-start.1 = (bf16[1,256,256]{2,1,0:T(8,128)(2,1)S(1)}, bf16[1,256,256]{2,1,0:T(8,128)(2,1)S(1)}, u32[]{:S(2)}, u32[]{:S(2)}) collective-permute-start(bf16[1,256,256]{2,1,0:T(8,128)(2,1)S(1)} %fusion.178), channel_id=1, source_target_pairs={{0,4},{4,8},{8,12},{1,5},{5,9},{9,13},{2,6},{6,10},{10,14},{3,7},{... | collective-permute-start | bytes 393224 | tf_op jit(solution)/shard_map/while/body/eval_jaxpr/ppermute | solution.py:10
  29.8 7.5 %collective-permute-start.2 = (bf16[1,256,256]{2,1,0:T(8,128)(2,1)S(1)}, bf16[1,256,256]{2,1,0:T(8,128)(2,1)S(1)}, u32[]{:S(2)}, u32[]{:S(2)}) collective-permute-start(bf16[1,256,256]{2,1,0:T(8,128)(2,1)S(1)} %fusion.182), channel_id=1, source_target_pairs={{0,4},{4,8},{8,12},{1,5},{5,9},{9,13},{2,6},{6,10},{10,14},{3,7},{... | collective-permute-start | bytes 393224 | tf_op jit(solution)/shard_map/while/body/eval_jaxpr/ppermute | solution.py:10
  39.6 8.5 %collective-permute-start.3 = (bf16[1,256,256]{2,1,0:T(8,128)(2,1)S(1)}, bf16[1,256,256]{2,1,0:T(8,128)(2,1)S(1)}, u32[]{:S(2)}, u32[]{:S(2)}) collective-permute-start(bf16[1,256,256]{2,1,0:T(8,128)(2,1)S(1)} %fusion.186), channel_id=1, source_target_pairs={{0,8},{4,12},{1,9},{5,13},{2,10},{6,14},{3,11},{7,15},{16,24},{20,... | collective-permute-start | bytes 393224 | tf_op jit(solution)/shard_map/while/body/eval_jaxpr/ppermute | solution.py:10
  50.5 6.5 %collective-permute-start.4 = (bf16[1,256,256]{2,1,0:T(8,128)(2,1)S(1)}, bf16[1,256,256]{2,1,0:T(8,128)(2,1)S(1)}, u32[]{:S(2)}, u32[]{:S(2)}) collective-permute-start(bf16[1,256,256]{2,1,0:T(8,128)(2,1)S(1)} %fusion.190), channel_id=1, source_target_pairs={{0,2},{1,3},{4,6},{5,7},{8,10},{9,11},{12,14},{13,15},{16,18},{17,... | collective-permute-start | bytes 393224 | tf_op jit(solution)/shard_map/while/body/eval_jaxpr/ppermute | solution.py:10
  57.0 7.6 %collective-permute-start = (bf16[1,32,256]{2,1,0:T(8,128)(2,1)S(1)}, bf16[1,32,256]{2,1,0:T(8,128)(2,1)S(1)}, u32[]{:S(2)}, u32[]{:S(2)}) collective-permute-start(bf16[1,32,256]{2,1,0:T(8,128)(2,1)S(1)} %slice.435), channel_id=1, source_target_pairs={{0,4},{4,8},{8,12},{1,5},{5,9},{9,13},{2,6},{6,10},{10,14},{3,7},{... | collective-permute-start | bytes 49160 | tf_op jit(solution)/shard_map/while/body/eval_jaxpr/ppermute | solution.py:10
  66.9 7.3 %collective-permute-start.1 = (bf16[1,256,256]{2,1,0:T(8,128)(2,1)S(1)}, bf16[1,256,256]{2,1,0:T(8,128)(2,1)S(1)}, u32[]{:S(2)}, u32[]{:S(2)}) collective-permute-start(bf16[1,256,256]{2,1,0:T(8,128)(2,1)S(1)} %fusion.178), channel_id=1, source_target_pairs={{0,4},{4,8},{8,12},{1,5},{5,9},{9,13},{2,6},{6,10},{10,14},{3,7},{... | collective-permute-start | bytes 393224 | tf_op jit(solution)/shard_map/while/body/eval_jaxpr/ppermute | solution.py:10
  76.5 7.5 %collective-permute-start.2 = (bf16[1,256,256]{2,1,0:T(8,128)(2,1)S(1)}, bf16[1,256,256]{2,1,0:T(8,128)(2,1)S(1)}, u32[]{:S(2)}, u32[]{:S(2)}) collective-permute-start(bf16[1,256,256]{2,1,0:T(8,128)(2,1)S(1)} %fusion.182), channel_id=1, source_target_pairs={{0,4},{4,8},{8,12},{1,5},{5,9},{9,13},{2,6},{6,10},{10,14},{3,7},{... | collective-permute-start | bytes 393224 | tf_op jit(solution)/shard_map/while/body/eval_jaxpr/ppermute | solution.py:10
  86.3 8.6 %collective-permute-start.3 = (bf16[1,256,256]{2,1,0:T(8,128)(2,1)S(1)}, bf16[1,256,256]{2,1,0:T(8,128)(2,1)S(1)}, u32[]{:S(2)}, u32[]{:S(2)}) collective-permute-start(bf16[1,256,256]{2,1,0:T(8,128)(2,1)S(1)} %fusion.186), channel_id=1, source_target_pairs={{0,8},{4,12},{1,9},{5,13},{2,10},{6,14},{3,11},{7,15},{16,24},{20,... | collective-permute-start | bytes 393224 | tf_op jit(solution)/shard_map/while/body/eval_jaxpr/ppermute | solution.py:10
  97.3 7.5 %collective-permute-start.4 = (bf16[1,256,256]{2,1,0:T(8,128)(2,1)S(1)}, bf16[1,256,256]{2,1,0:T(8,128)(2,1)S(1)}, u32[]{:S(2)}, u32[]{:S(2)}) collective-permute-start(bf16[1,256,256]{2,1,0:T(8,128)(2,1)S(1)} %fusion.190), channel_id=1, source_target_pairs={{0,2},{1,3},{4,6},{5,7},{8,10},{9,11},{12,14},{13,15},{16,18},{17,... | collective-permute-start | bytes 393224 | tf_op jit(solution)/shard_map/while/body/eval_jaxpr/ppermute | solution.py:10
  104.8 7.6 %collective-permute-start = (bf16[1,32,256]{2,1,0:T(8,128)(2,1)S(1)}, bf16[1,32,256]{2,1,0:T(8,128)(2,1)S(1)}, u32[]{:S(2)}, u32[]{:S(2)}) collective-permute-start(bf16[1,32,256]{2,1,0:T(8,128)(2,1)S(1)} %slice.435), channel_id=1, source_target_pairs={{0,4},{4,8},{8,12},{1,5},{5,9},{9,13},{2,6},{6,10},{10,14},{3,7},{... | collective-permute-start | bytes 49160 | tf_op jit(solution)/shard_map/while/body/eval_jaxpr/ppermute | solution.py:10
  114.7 7.3 %collective-permute-start.1 = (bf16[1,256,256]{2,1,0:T(8,128)(2,1)S(1)}, bf16[1,256,256]{2,1,0:T(8,128)(2,1)S(1)}, u32[]{:S(2)}, u32[]{:S(2)}) collective-permute-start(bf16[1,256,256]{2,1,0:T(8,128)(2,1)S(1)} %fusion.178), channel_id=1, source_target_pairs={{0,4},{4,8},{8,12},{1,5},{5,9},{9,13},{2,6},{6,10},{10,14},{3,7},{... | collective-permute-start | bytes 393224 | tf_op jit(solution)/shard_map/while/body/eval_jaxpr/ppermute | solution.py:10
  124.3 7.5 %collective-permute-start.2 = (bf16[1,256,256]{2,1,0:T(8,128)(2,1)S(1)}, bf16[1,256,256]{2,1,0:T(8,128)(2,1)S(1)}, u32[]{:S(2)}, u32[]{:S(2)}) collective-permute-start(bf16[1,256,256]{2,1,0:T(8,128)(2,1)S(1)} %fusion.182), channel_id=1, source_target_pairs={{0,4},{4,8},{8,12},{1,5},{5,9},{9,13},{2,6},{6,10},{10,14},{3,7},{... | collective-permute-start | bytes 393224 | tf_op jit(solution)/shard_map/while/body/eval_jaxpr/ppermute | solution.py:10
  134.1 8.6 %collective-permute-start.3 = (bf16[1,256,256]{2,1,0:T(8,128)(2,1)S(1)}, bf16[1,256,256]{2,1,0:T(8,128)(2,1)S(1)}, u32[]{:S(2)}, u32[]{:S(2)}) collective-permute-start(bf16[1,256,256]{2,1,0:T(8,128)(2,1)S(1)} %fusion.186), channel_id=1, source_target_pairs={{0,8},{4,12},{1,9},{5,13},{2,10},{6,14},{3,11},{7,15},{16,24},{20,... | collective-permute-start | bytes 393224 | tf_op jit(solution)/shard_map/while/body/eval_jaxpr/ppermute | solution.py:10
  145.1 7.5 %collective-permute-start.4 = (bf16[1,256,256]{2,1,0:T(8,128)(2,1)S(1)}, bf16[1,256,256]{2,1,0:T(8,128)(2,1)S(1)}, u32[]{:S(2)}, u32[]{:S(2)}) collective-permute-start(bf16[1,256,256]{2,1,0:T(8,128)(2,1)S(1)} %fusion.190), channel_id=1, source_target_pairs={{0,2},{1,3},{4,6},{5,7},{8,10},{9,11},{12,14},{13,15},{16,18},{17,... | collective-permute-start | bytes 393224 | tf_op jit(solution)/shard_map/while/body/eval_jaxpr/ppermute | solution.py:10
  152.6 7.6 %collective-permute-start = (bf16[1,32,256]{2,1,0:T(8,128)(2,1)S(1)}, bf16[1,32,256]{2,1,0:T(8,128)(2,1)S(1)}, u32[]{:S(2)}, u32[]{:S(2)}) collective-permute-start(bf16[1,32,256]{2,1,0:T(8,128)(2,1)S(1)} %slice.435), channel_id=1, source_target_pairs={{0,4},{4,8},{8,12},{1,5},{5,9},{9,13},{2,6},{6,10},{10,14},{3,7},{... | collective-permute-start | bytes 49160 | tf_op jit(solution)/shard_map/while/body/eval_jaxpr/ppermute | solution.py:10
  162.5 7.3 %collective-permute-start.1 = (bf16[1,256,256]{2,1,0:T(8,128)(2,1)S(1)}, bf16[1,256,256]{2,1,0:T(8,128)(2,1)S(1)}, u32[]{:S(2)}, u32[]{:S(2)}) collective-permute-start(bf16[1,256,256]{2,1,0:T(8,128)(2,1)S(1)} %fusion.178), channel_id=1, source_target_pairs={{0,4},{4,8},{8,12},{1,5},{5,9},{9,13},{2,6},{6,10},{10,14},{3,7},{... | collective-permute-start | bytes 393224 | tf_op jit(solution)/shard_map/while/body/eval_jaxpr/ppermute | solution.py:10
  172.1 7.5 %collective-permute-start.2 = (bf16[1,256,256]{2,1,0:T(8,128)(2,1)S(1)}, bf16[1,256,256]{2,1,0:T(8,128)(2,1)S(1)}, u32[]{:S(2)}, u32[]{:S(2)}) collective-permute-start(bf16[1,256,256]{2,1,0:T(8,128)(2,1)S(1)} %fusion.182), channel_id=1, source_target_pairs={{0,4},{4,8},{8,12},{1,5},{5,9},{9,13},{2,6},{6,10},{10,14},{3,7},{... | collective-permute-start | bytes 393224 | tf_op jit(solution)/shard_map/while/body/eval_jaxpr/ppermute | solution.py:10
  182.0 8.6 %collective-permute-start.3 = (bf16[1,256,256]{2,1,0:T(8,128)(2,1)S(1)}, bf16[1,256,256]{2,1,0:T(8,128)(2,1)S(1)}, u32[]{:S(2)}, u32[]{:S(2)}) collective-permute-start(bf16[1,256,256]{2,1,0:T(8,128)(2,1)S(1)} %fusion.186), channel_id=1, source_target_pairs={{0,8},{4,12},{1,9},{5,13},{2,10},{6,14},{3,11},{7,15},{16,24},{20,... | collective-permute-start | bytes 393224 | tf_op jit(solution)/shard_map/while/body/eval_jaxpr/ppermute | solution.py:10
  192.9 7.5 %collective-permute-start.4 = (bf16[1,256,256]{2,1,0:T(8,128)(2,1)S(1)}, bf16[1,256,256]{2,1,0:T(8,128)(2,1)S(1)}, u32[]{:S(2)}, u32[]{:S(2)}) collective-permute-start(bf16[1,256,256]{2,1,0:T(8,128)(2,1)S(1)} %fusion.190), channel_id=1, source_target_pairs={{0,2},{1,3},{4,6},{5,7},{8,10},{9,11},{12,14},{13,15},{16,18},{17,... | collective-permute-start | bytes 393224 | tf_op jit(solution)/shard_map/while/body/eval_jaxpr/ppermute | solution.py:10
  200.4 7.6 %collective-permute-start = (bf16[1,32,256]{2,1,0:T(8,128)(2,1)S(1)}, bf16[1,32,256]{2,1,0:T(8,128)(2,1)S(1)}, u32[]{:S(2)}, u32[]{:S(2)}) collective-permute-start(bf16[1,32,256]{2,1,0:T(8,128)(2,1)S(1)} %slice.435), channel_id=1, source_target_pairs={{0,4},{4,8},{8,12},{1,5},{5,9},{9,13},{2,6},{6,10},{10,14},{3,7},{... | collective-permute-start | bytes 49160 | tf_op jit(solution)/shard_map/while/body/eval_jaxpr/ppermute | solution.py:10
  210.3 7.3 %collective-permute-start.1 = (bf16[1,256,256]{2,1,0:T(8,128)(2,1)S(1)}, bf16[1,256,256]{2,1,0:T(8,128)(2,1)S(1)}, u32[]{:S(2)}, u32[]{:S(2)}) collective-permute-start(bf16[1,256,256]{2,1,0:T(8,128)(2,1)S(1)} %fusion.178), channel_id=1, source_target_pairs={{0,4},{4,8},{8,12},{1,5},{5,9},{9,13},{2,6},{6,10},{10,14},{3,7},{... | collective-permute-start | bytes 393224 | tf_op jit(solution)/shard_map/while/body/eval_jaxpr/ppermute | solution.py:10
  220.0 7.5 %collective-permute-start.2 = (bf16[1,256,256]{2,1,0:T(8,128)(2,1)S(1)}, bf16[1,256,256]{2,1,0:T(8,128)(2,1)S(1)}, u32[]{:S(2)}, u32[]{:S(2)}) collective-permute-start(bf16[1,256,256]{2,1,0:T(8,128)(2,1)S(1)} %fusion.182), channel_id=1, source_target_pairs={{0,4},{4,8},{8,12},{1,5},{5,9},{9,13},{2,6},{6,10},{10,14},{3,7},{... | collective-permute-start | bytes 393224 | tf_op jit(solution)/shard_map/while/body/eval_jaxpr/ppermute | solution.py:10
  229.8 8.6 %collective-permute-start.3 = (bf16[1,256,256]{2,1,0:T(8,128)(2,1)S(1)}, bf16[1,256,256]{2,1,0:T(8,128)(2,1)S(1)}, u32[]{:S(2)}, u32[]{:S(2)}) collective-permute-start(bf16[1,256,256]{2,1,0:T(8,128)(2,1)S(1)} %fusion.186), channel_id=1, source_target_pairs={{0,8},{4,12},{1,9},{5,13},{2,10},{6,14},{3,11},{7,15},{16,24},{20,... | collective-permute-start | bytes 393224 | tf_op jit(solution)/shard_map/while/body/eval_jaxpr/ppermute | solution.py:10
  240.7 7.5 %collective-permute-start.4 = (bf16[1,256,256]{2,1,0:T(8,128)(2,1)S(1)}, bf16[1,256,256]{2,1,0:T(8,128)(2,1)S(1)}, u32[]{:S(2)}, u32[]{:S(2)}) collective-permute-start(bf16[1,256,256]{2,1,0:T(8,128)(2,1)S(1)} %fusion.190), channel_id=1, source_target_pairs={{0,2},{1,3},{4,6},{5,7},{8,10},{9,11},{12,14},{13,15},{16,18},{17,... | collective-permute-start | bytes 393224 | tf_op jit(solution)/shard_map/while/body/eval_jaxpr/ppermute | solution.py:10
Sparse Core Ops, SparseCore 0:
  249.0 17.3 reduce-scatter.1
where the time goes:
time: 274 us; the launch traced here: 273 us
  starting transfers between devices  121 us (44%)
  waiting for transfers between devices  78.2 us (29%)
  blocking collectives  40.5 us (15%)
  matrix products  14.6 us (5%)
  between operations  13.4 us (5%)
    ppermute x25, starting transfers between devices, from_behind(): return lax.ppermute(block, axis, route)  121 us
    ppermute x25, waiting for transfers between devices, from_behind(): return lax.ppermute(block, axis, route)  60.7 us
    all_gather x20, blocking collectives, layer_stack(): full_units = lax.all_gather(gate_out, 'chan', axis=2, tiled=True)  38 us
    reduce_scatter x1, waiting for transfers between devices, shards(): lax.psum_scatter(skip_acc.astype(jnp.bfloat16), 'segment', scatter_dimens...  17.5 us
  transfers between devices with their start and end apart: 26, of which 26 were waited for; matrix products, arithmetic and copies ran while one was open for 3% of the time, Pallas kernels for 0%

commit v1 on v0

v1 whole, which is shorter than its diff:
```python
import functools

import jax
import jax.numpy as jnp
from jax import lax
from jax.experimental import pallas as pl
from jax.experimental.pallas import tpu as pltpu
from jax.sharding import PartitionSpec as P

VMEM = pl.BlockSpec(memory_space=pltpu.VMEM)
ROW_TILE = 256


def swap_cores(block):
    cores = lax.axis_size("chan")
    return lax.ppermute(block, "chan", [(i, cores - 1 - i) for i in range(cores)])


def section_body(own_pack, other_pack, res_ref, skip_ref, streams, units, lags, core):
    layers, depth = res_ref.shape[0], res_ref.shape[1]
    half = depth // 2
    head = max(lags)
    total = streams.shape[1] - head
    own_rows = pl.ds(pl.multiple_of(core * half, half), half)
    other_rows = pl.ds(pl.multiple_of((1 - core) * half, half), half)
    for layer in range(layers):
        now_buf, next_buf = streams.at[layer % 2], streams.at[(layer + 1) % 2]
        lag = lags[layer % 4]
        res = jnp.concatenate([res_ref[layer, own_rows, :], res_ref[layer, other_rows, :]], 0)

        def tile(row, lag=lag, layer=layer, now_buf=now_buf, next_buf=next_buf, res=res):
            past = now_buf[pl.ds(head - lag + row, ROW_TILE), :]
            now = now_buf[pl.ds(head + row, ROW_TILE), :]
            parts = []
            for pack in (own_pack, other_pack):
                pre = jnp.dot(past, pack[layer, :depth], preferred_element_type=jnp.float32)
                pre += jnp.dot(now, pack[layer, depth : 2 * depth], preferred_element_type=jnp.float32)
                pre += pack[layer, 2 * depth : 2 * depth + 1].astype(jnp.float32)
                gate = 0.5 * jnp.tanh(0.5 * pre[:, half:]) + 0.5
                parts.append((jnp.tanh(pre[:, :half]) * gate).astype(jnp.bfloat16))
            unit = jnp.concatenate(parts, 1)
            units[layer, pl.ds(row, ROW_TILE), :] = unit
            update = jnp.dot(unit, res, preferred_element_type=jnp.float32)
            next_buf[pl.ds(head + row, ROW_TILE), :] = (now.astype(jnp.float32) + update).astype(jnp.bfloat16)

        if total // ROW_TILE <= 4:
            for step in range(total // ROW_TILE):
                tile(step * ROW_TILE)
        else:
            pl.loop(0, total // ROW_TILE)(lambda step: tile(pl.multiple_of(step * ROW_TILE, ROW_TILE)))


def emit(skip_ref, streams, units, lags, core, first, skip_outs, stream_out, layers):
    half = skip_ref.shape[2]
    head = max(lags)
    total = streams.shape[1] - head
    own_rows = pl.ds(pl.multiple_of(core * half, half), half)
    other_rows = pl.ds(pl.multiple_of((1 - core) * half, half), half)
    rows = skip_outs[0].shape[0]
    blocks = total // rows
    for turn, out in enumerate(skip_outs):
        at = pl.multiple_of(lax.rem(first + turn, blocks) * rows, rows)
        acc = jnp.zeros((rows, half), jnp.float32)
        for layer in range(layers):
            unit = units[layer, pl.ds(at, rows), :]
            acc += jnp.dot(unit[:, :half], skip_ref[layer, own_rows, :], preferred_element_type=jnp.float32)
            acc += jnp.dot(unit[:, half:], skip_ref[layer, other_rows, :], preferred_element_type=jnp.float32)
        out[...] = acc.astype(out.dtype)
    if stream_out is not None:
        part = total // 2
        start = pl.multiple_of(head + core * part, 16)
        stream_out[...] = streams[layers % 2, pl.ds(start, part), :]


def section_kernel(stage, shift, lags, n_in, n_skip, has_stream, *refs):
    own_pack, other_pack, res_ref, skip_ref = refs[:4]
    inputs = refs[4 : 4 + n_in]
    skip_outs = refs[4 + n_in : 4 + n_in + n_skip]
    stream_out = refs[4 + n_in + n_skip] if has_stream else None
    streams, units = refs[-2:]
    core, place = lax.axis_index("chan"), lax.axis_index("tm")
    count = lax.axis_size("tm")
    head = max(lags)
    layers = res_ref.shape[0]
    half = skip_ref.shape[2]

    @pl.when(lax.axis_index("segment") == stage)
    def _():
        streams[:, :head, :] = jnp.zeros((2, head, streams.shape[2]), streams.dtype)
        if stage == 0:
            rows = inputs[0].shape[0]
            for side, blocks in ((core, inputs[: n_in // 2]), (1 - core, inputs[n_in // 2 :])):
                lanes = pl.ds(pl.multiple_of(side * half, half), half)
                for turn, block in enumerate(blocks):
                    at = lax.rem(place - turn + count, count) * rows + head
                    streams[0, pl.ds(pl.multiple_of(at, 16), rows), lanes] = block[...]
        else:
            part = inputs[0].shape[0]
            for side, block in ((core, inputs[0]), (1 - core, inputs[1])):
                streams[0, pl.ds(pl.multiple_of(head + side * part, 16), part), :] = block[...]
        section_body(own_pack, other_pack, res_ref, skip_ref, streams, units, lags, core)
        emit(skip_ref, streams, units, lags, core, place + shift, skip_outs, stream_out, layers)


def run_section(stage, last, shift, lags, packs, res_weight, skip_weight, inputs, rows, n_skip):
    layers, depth = res_weight.shape[:2]
    total = rows * lax.axis_size("tm")
    half = skip_weight.shape[2]
    outs = [jax.ShapeDtypeStruct((rows, half), jnp.bfloat16)] * n_skip
    if not last:
        outs.append(jax.ShapeDtypeStruct((total // 2, depth), jnp.bfloat16))
    scratch = [
        pltpu.VMEM((2, max(lags) + total, depth), jnp.bfloat16),
        pltpu.VMEM((layers, total, depth), jnp.bfloat16),
    ]
    held = 2 * (2 * (max(lags) + total) * depth + layers * total * depth + 2 * total * depth)
    return pl.pallas_call(
        functools.partial(section_kernel, stage, shift, lags, len(inputs), n_skip, not last),
        out_shape=outs,
        in_specs=[VMEM] * (4 + len(inputs)),
        out_specs=[VMEM] * len(outs),
        scratch_shapes=scratch,
        compiler_params=pltpu.CompilerParams(vmem_limit_bytes=held + (14 << 20)),
    )(*packs, res_weight, skip_weight, *inputs)


def shards(records, conv_weight, conv_bias, res_weight, skip_weight):
    record_count, rows, half = records.shape
    layers, taps = conv_weight.shape[:2]
    count, sections = lax.axis_size("tm"), lax.axis_size("segment")
    place, segment = lax.axis_index("tm"), lax.axis_index("segment")
    lags = [rows // 8, rows, rows * max(1, count // 8), rows * max(1, count // 2)]
    share = record_count // sections

    own_blocks = []
    for turn in range(count):
        slot = lax.rem(lax.rem(place + turn, count), record_count)
        block = lax.dynamic_index_in_dim(records, slot, 0, keepdims=False)
        if turn:
            block = lax.ppermute(block, "tm", [(i, (i + turn) % count) for i in range(count)])
        own_blocks.append(block)
    other_blocks = [swap_cores(block) for block in own_blocks]

    bias_rows = jnp.pad(conv_bias.reshape(layers, 1, 2 * half), ((0, 0), (0, 15), (0, 0)))
    own_pack = jnp.concatenate([conv_weight.reshape(layers, taps, 2 * half), bias_rows], 1)
    packs = (own_pack, swap_cores(own_pack))

    inputs = own_blocks + other_blocks
    skip_parts = None
    for stage in range(sections):
        last = stage == sections - 1
        outs = run_section(stage, last, stage * share, lags, packs, res_weight, skip_weight, inputs, rows, record_count)
        blocks = outs[:record_count]
        if skip_parts is None:
            skip_parts = blocks
        else:
            skip_parts = [jnp.where(segment == stage, new, old) for new, old in zip(blocks, skip_parts)]
        if not last:
            moved = lax.ppermute(outs[-1], "segment", [(i, (i + 1) % sections) for i in range(sections)])
            inputs = [moved, swap_cores(moved)]

    result = jnp.zeros((share, rows, half), jnp.float32)
    first = segment * share
    for turn in range(record_count):
        pairs = []
        for z in range(count):
            for s in range(sections):
                to = (z + turn + s * share) % count
                pairs.append((z * sections + s, to * sections + (z % record_count) // share))
        got = lax.ppermute(skip_parts[turn], ("tm", "segment"), pairs)
        for s in range(sections):
            source = lax.rem(lax.rem(place - turn - s * share + 2 * count, count), record_count)
            inside = jnp.logical_and(source >= first, source < first + share)
            for j in range(share):
                mine = jnp.logical_and(inside, source - first == j)
                result = result.at[j].add(jnp.where(mine, got.astype(jnp.float32), 0.0))
    return result.astype(jnp.bfloat16)


def solution(mesh):
    return jax.shard_map(
        shards,
        mesh=mesh,
        in_specs=(
            P("groups", "tm", "chan"),
            P("segment", None, None, "chan"),
            P("segment", None, "chan"),
            P("segment", None, None),
            P("segment", None, "chan"),
        ),
        out_specs=P(("groups", "segment"), "tm", "chan"),
        check_vma=False,
    )
```

time: 274 us -> 50.4 us (0.18)
  the two profiles are of different devices: /device:TPU:0 before, /device:TPU:6 now
where the time goes in v1:
time: 50.4 us; the launch traced here: 50.2 us
  starting transfers between devices  20.3 us (40%)
  waiting for transfers between devices  18.9 us (38%)
  Pallas kernels  5.06 us (10%)
  local copies, waits for them, and re-layouts  4.37 us (9%)
  other arithmetic  1.25 us (2%)
    ppermute x4, starting transfers between devices, shards(): got = lax.ppermute(skip_parts[turn], ('tm', 'segment'), pairs)  8.38 us
    ppermute x1, waiting for transfers between devices, shards(): lax.ppermute(outs[-1], 'segment', [(i, (i + 1) % sections) for i in range...  6.82 us
    ppermute x4, waiting for transfers between devices, shards(): got = lax.ppermute(skip_parts[turn], ('tm', 'segment'), pairs)  6.22 us
    ppermute x1, starting transfers between devices, shards(): lax.ppermute(outs[-1], 'segment', [(i, (i + 1) % sections) for i in range...  5.73 us
    ppermute x3, starting transfers between devices, shards(): lax.ppermute(block, 'tm', [(i, (i + turn) % count) for i in range(count)])  5.57 us
    pallas_call x2, Pallas kernels, run_section(): pl.pallas_call(functools.partial(section_kernel, stage, shift, lags, len(...  5.06 us
    ppermute x3, waiting for transfers between devices, shards(): lax.ppermute(block, 'tm', [(i, (i + turn) % count) for i in range(count)])  3.41 us
    unnamed x20, local copies, waits for them, and re-layouts  2.59 us
  transfers between devices with their start and end apart: 14, of which 8 were waited for; matrix products, arithmetic and copies ran while one was open for 1% of the time, Pallas kernels for 0%

profile of v1, /device:TPU:6, one launch (start us, length us, event | category | flops | bytes accessed | tf_op | source)
XLA Modules:
  0.0 50.2 jit_solution(11565756761772818501)
XLA Ops:
  0.0 0.0 copy-start.9
  0.0 1.7 %reshape.472 = bf16[4,512,256]{2,1,0:T(8,128)(2,1)S(1)} reshape(bf16[4,512,2,128]{3,2,1,0:T(2,128)(2,1)} %param.38) | data formatting | bytes 2097152 | tf_op jit(solution)/shard_map/reshape | solution.py:145
  1.8 0.0 copy-done.9
  1.8 0.0 copy-start.8
  1.8 0.0 copy-start
  1.8 0.0 copy-start.1
  1.8 0.1 fusion.1.refs_0_
  1.9 0.1 collective-permute-start
  2.0 0.7 %copy-done.8 = bf16[4,256,128]{2,1,0:T(8,128)(2,1)S(1)} copy-done((bf16[4,256,128]{2,1,0:T(8,128)(2,1)S(1)}, bf16[4,256,128]{2,1,0:T(8,128)(2,1)}, u32[]{:S(2)}) %copy-start.8) | copy-done | bytes 262168
  2.8 1.6 %collective-permute-start.1 = (bf16[256,128]{1,0:T(8,128)(2,1)S(1)}, bf16[256,128]{1,0:T(8,128)(2,1)S(1)}, u32[]{:S(2)}, u32[]{:S(2)}) collective-permute-start(bf16[256,128]{1,0:T(8,128)(2,1)S(1)} %get-tuple-element.216), channel_id=1, source_target_pairs={{0,4},{4,8},{8,12},{12,0},{1,5},{5,9},{9,13},{13,1},{2,6},{6,10},{... | collective-permute-start | bytes 196616 | tf_op jit(solution)/shard_map/ppermute | solution.py:140
  4.4 2.6 %collective-permute-start.2 = (bf16[256,128]{1,0:T(8,128)(2,1)S(1)}, bf16[256,128]{1,0:T(8,128)(2,1)S(1)}, u32[]{:S(2)}, u32[]{:S(2)}) collective-permute-start(bf16[256,128]{1,0:T(8,128)(2,1)S(1)} %get-tuple-element.218), channel_id=1, source_target_pairs={{0,8},{4,12},{8,0},{12,4},{1,9},{5,13},{9,1},{13,5},{2,10},{6,14},... | collective-permute-start | bytes 196616 | tf_op jit(solution)/shard_map/ppermute | solution.py:140
  7.0 1.3 %collective-permute-start.3 = (bf16[256,128]{1,0:T(8,128)(2,1)S(1)}, bf16[256,128]{1,0:T(8,128)(2,1)S(1)}, u32[]{:S(2)}, u32[]{:S(2)}) collective-permute-start(bf16[256,128]{1,0:T(8,128)(2,1)S(1)} %get-tuple-element.215), channel_id=1, source_target_pairs={{0,12},{4,0},{8,4},{12,8},{1,13},{5,1},{9,5},{13,9},{2,14},{6,2},{... | collective-permute-start | bytes 196616 | tf_op jit(solution)/shard_map/ppermute | solution.py:140
  8.3 0.0 collective-permute-start.4
  8.3 1.0 %collective-permute-done.1.refs_5_ = bf16[256,128]{1,0:T(8,128)(2,1)S(1)} collective-permute-done((bf16[256,128]{1,0:T(8,128)(2,1)S(1)}, bf16[256,128]{1,0:T(8,128)(2,1)S(1)}, u32[]{:S(2)}, u32[]{:S(2)}) %collective-permute-start.1) | collective-permute-done | bytes 65568 | tf_op jit(solution)/shard_map/ppermute | solution.py:140
  9.3 0.0 collective-permute-start.5
  9.3 2.4 %collective-permute-done.2.refs_6_ = bf16[256,128]{1,0:T(8,128)(2,1)S(1)} collective-permute-done((bf16[256,128]{1,0:T(8,128)(2,1)S(1)}, bf16[256,128]{1,0:T(8,128)(2,1)S(1)}, u32[]{:S(2)}, u32[]{:S(2)}) %collective-permute-start.2) | collective-permute-done | bytes 65568 | tf_op jit(solution)/shard_map/ppermute | solution.py:140
  11.7 0.0 collective-permute-start.6
  11.7 0.0 collective-permute-done.3.refs_7_
  11.7 0.5 %collective-permute-start.7 = (bf16[256,128]{1,0:T(8,128)(2,1)S(1)}, bf16[256,128]{1,0:T(8,128)(2,1)S(1)}, u32[]{:S(2)}, u32[]{:S(2)}) collective-permute-start(bf16[256,128]{1,0:T(8,128)(2,1)S(1)} %collective-permute-done.3.refs_7_), channel_id=1, source_target_pairs={{0,1},{1,0},{2,3},{3,2},{4,5},{5,4},{6,7},{7,6},{8,9},{9,8},{10,11... | collective-permute-start | bytes 196616 | tf_op jit(solution)/shard_map/ppermute | solution.py:16
  12.2 0.0 collective-permute-done.4.refs_8_
  12.3 0.0 collective-permute-done.5.refs_9_
  12.3 0.7 %collective-permute-done.6.refs_10_ = bf16[256,128]{1,0:T(8,128)(2,1)S(1)} collective-permute-done((bf16[256,128]{1,0:T(8,128)(2,1)S(1)}, bf16[256,128]{1,0:T(8,128)(2,1)S(1)}, u32[]{:S(2)}, u32[]{:S(2)}) %collective-permute-start.6) | collective-permute-done | bytes 65568 | tf_op jit(solution)/shard_map/ppermute | solution.py:16
  13.0 0.2 collective-permute-done.7.refs_11_
  13.2 0.0 collective-permute-done.refs_1_
  13.2 0.0 copy-done
  13.2 0.0 copy-done.1
  13.2 0.0 copy-start.2
  13.2 0.6 %copy-done.2 = bf16[256,128]{1,0:T(8,128)(2,1)} copy-done((bf16[256,128]{1,0:T(8,128)(2,1)}, bf16[256,128]{1,0:T(8,128)(2,1)S(1)}, u32[]{:S(2)}) %copy-start.2) | copy-done | bytes 65560
  13.8 0.0 copy-start.4
  13.8 0.6 %copy-done.4 = bf16[256,128]{1,0:T(8,128)(2,1)} copy-done((bf16[256,128]{1,0:T(8,128)(2,1)}, bf16[256,128]{1,0:T(8,128)(2,1)S(1)}, u32[]{:S(2)}) %copy-start.4) | copy-done | bytes 65560
  14.4 0.0 copy-start.6
  14.4 0.6 %copy-done.6 = bf16[256,128]{1,0:T(8,128)(2,1)} copy-done((bf16[256,128]{1,0:T(8,128)(2,1)}, bf16[256,128]{1,0:T(8,128)(2,1)S(1)}, u32[]{:S(2)}) %copy-start.6) | copy-done | bytes 65560
  15.1 5.7 %collective-permute-start.8 = (bf16[512,256]{1,0:T(8,128)(2,1)S(1)}, bf16[512,256]{1,0:T(8,128)(2,1)S(1)}, u32[]{:S(2)}, u32[]{:S(2)}) collective-permute-start(bf16[512,256]{1,0:T(8,128)(2,1)S(1)} %get-tuple-element.206), channel_id=1, source_target_pairs={{0,2},{2,0},{1,3},{3,1},{4,6},{6,4},{5,7},{7,5},{8,10},{10,8},{9,1... | collective-permute-start | bytes 786440 | tf_op jit(solution)/shard_map/ppermute | solution.py:159
  20.8 6.8 %collective-permute-done.8.refs_4_ = bf16[512,256]{1,0:T(8,128)(2,1)S(1)} collective-permute-done((bf16[512,256]{1,0:T(8,128)(2,1)S(1)}, bf16[512,256]{1,0:T(8,128)(2,1)S(1)}, u32[]{:S(2)}, u32[]{:S(2)}) %collective-permute-start.8) | collective-permute-done | bytes 262176 | tf_op jit(solution)/shard_map/ppermute | solution.py:159
  27.6 0.0 collective-permute-start.9
  27.6 0.0 copy-start.7
  27.6 0.0 copy-start.5
  27.6 0.0 copy-start.3
  27.6 1.5 %collective-permute-done.9.refs_5_ = bf16[512,256]{1,0:T(8,128)(2,1)S(1)} collective-permute-done((bf16[512,256]{1,0:T(8,128)(2,1)S(1)}, bf16[512,256]{1,0:T(8,128)(2,1)S(1)}, u32[]{:S(2)}, u32[]{:S(2)}) %collective-permute-start.9) | collective-permute-done | bytes 262176 | tf_op jit(solution)/shard_map/ppermute | solution.py:16
  29.1 5.0 %shard_map.56 = (bf16[256,128]{1,0:T(8,128)(2,1)S(1)}, bf16[256,128]{1,0:T(8,128)(2,1)S(1)}, bf16[256,128]{1,0:T(8,128)(2,1)S(1)}, bf16[256,128]{1,0:T(8,128)(2,1)S(1)}) custom-call(bf16[4,528,256]{2,1,0:T(8,128)(2,1)S(1)} %fusion.1.refs_0_, bf16[4,528,256]{2,1,0:T(8,128)(2,1)S(1)} %collective-permute-done.refs_1_, bf16[4,256,256]{2,1,0:T(8,128)(2,1)S(1)} %copy-done, ...), custom_call_target="tpu_custom_call" | custom-call | tf_op jit(solution)/shard_map/pallas_call | solution.py:117
  34.2 0.0 copy-done.7
  34.2 0.1 collective-permute-start.13
  34.3 0.0 copy-done.5
  34.3 1.9 %collective-permute-start.12 = (bf16[256,128]{1,0:T(8,128)(2,1)S(1)}, bf16[256,128]{1,0:T(8,128)(2,1)S(1)}, u32[]{:S(2)}, u32[]{:S(2)}) collective-permute-start(bf16[256,128]{1,0:T(8,128)(2,1)S(1)} %broadcast_select_fusion.1), channel_id=1, source_target_pairs={{0,8},{2,0},{4,12},{6,4},{8,2},{10,10},{12,6},{14,14},{1,9},{3,1},... | collective-permute-start | bytes 196616 | tf_op jit(solution)/shard_map/ppermute | solution.py:170
  36.2 0.0 copy-done.3
  36.3 5.7 %collective-permute-start.10 = (bf16[256,128]{1,0:T(8,128)(2,1)S(1)}, bf16[256,128]{1,0:T(8,128)(2,1)S(1)}, u32[]{:S(2)}, u32[]{:S(2)}) collective-permute-start(bf16[256,128]{1,0:T(8,128)(2,1)S(1)} %broadcast_select_fusion.3), channel_id=1, source_target_pairs={{0,0},{2,8},{4,4},{6,12},{8,10},{10,2},{12,14},{14,6},{1,1},{3,9},... | collective-permute-start | bytes 196616 | tf_op jit(solution)/shard_map/ppermute | solution.py:170
  42.0 0.7 %collective-permute-start.11 = (bf16[256,128]{1,0:T(8,128)(2,1)S(1)}, bf16[256,128]{1,0:T(8,128)(2,1)S(1)}, u32[]{:S(2)}, u32[]{:S(2)}) collective-permute-start(bf16[256,128]{1,0:T(8,128)(2,1)S(1)} %broadcast_select_fusion.2), channel_id=1, source_target_pairs={{0,4},{2,12},{4,8},{6,0},{8,14},{10,6},{12,2},{14,10},{1,5},{3,13}... | collective-permute-start | bytes 196616 | tf_op jit(solution)/shard_map/ppermute | solution.py:170
  42.7 2.0 %collective-permute-done.10 = bf16[256,128]{1,0:T(8,128)(2,1)S(1)} collective-permute-done((bf16[256,128]{1,0:T(8,128)(2,1)S(1)}, bf16[256,128]{1,0:T(8,128)(2,1)S(1)}, u32[]{:S(2)}, u32[]{:S(2)}) %collective-permute-start.10) | collective-permute-done | bytes 65568 | tf_op jit(solution)/shard_map/ppermute | solution.py:170
  44.8 4.2 %collective-permute-done.11 = bf16[256,128]{1,0:T(8,128)(2,1)S(1)} collective-permute-done((bf16[256,128]{1,0:T(8,128)(2,1)S(1)}, bf16[256,128]{1,0:T(8,128)(2,1)S(1)}, u32[]{:S(2)}, u32[]{:S(2)}) %collective-permute-start.11) | collective-permute-done | bytes 65568 | tf_op jit(solution)/shard_map/ppermute | solution.py:170
  49.2 0.0 collective-permute-done.12
  49.3 0.0 collective-permute-done.13
  49.5 0.7 %convert_element_type.16 = bf16[2,256,128]{2,1,0:T(8,128)(2,1)} convert(f32[2,256,128]{2,1,0:T(8,128)S(1)} %fusion.45) | non-fusion elementwise | flops 65536 | bytes 393216 | tf_op jit(solution)/shard_map/convert_element_type | solution.py:177
  (23 shorter events, 0.6 us)
Async XLA Ops:
  0.0 1.8 %copy-start.9 = (bf16[4,2,128]{2,1,0:T(2,128)(2,1)S(1)}, bf16[4,2,128]{2,1,0:T(2,128)(2,1)}, u32[]{:S(2)}) copy-start(bf16[4,2,128]{2,1,0:T(2,128)(2,1)} %param.39) | copy-start | bytes 6148
  1.8 1.0 %copy-start.8 = (bf16[4,256,128]{2,1,0:T(8,128)(2,1)S(1)}, bf16[4,256,128]{2,1,0:T(8,128)(2,1)}, u32[]{:S(2)}) copy-start(bf16[4,256,128]{2,1,0:T(8,128)(2,1)} %param.37) | copy-start | bytes 786436
  1.8 11.4 %copy-start = (bf16[4,256,256]{2,1,0:T(8,128)(2,1)S(1)}, bf16[4,256,256]{2,1,0:T(8,128)(2,1)}, u32[]{:S(2)}) copy-start(bf16[4,256,256]{2,1,0:T(8,128)(2,1)} %refs_2_.3) | copy-start | bytes 1572868
  1.8 11.4 %copy-start.1 = (bf16[4,256,128]{2,1,0:T(8,128)(2,1)S(1)}, bf16[4,256,128]{2,1,0:T(8,128)(2,1)}, u32[]{:S(2)}) copy-start(bf16[4,256,128]{2,1,0:T(8,128)(2,1)} %refs_3_.3) | copy-start | bytes 786436
  1.9 11.3 %collective-permute-start = (bf16[4,528,256]{2,1,0:T(8,128)(2,1)S(1)}, bf16[4,528,256]{2,1,0:T(8,128)(2,1)S(1)}, u32[]{:S(2)}, u32[]{:S(2)}) collective-permute-start(bf16[4,528,256]{2,1,0:T(8,128)(2,1)S(1)} %fusion.1.refs_0_), channel_id=1, source_target_pairs={{0,1},{1,0},{2,3},{3,2},{4,5},{5,4},{6,7},{7,6},{8,9},{9,8},{10,11... | collective-permute-start | bytes 3244040 | tf_op jit(solution)/shard_map/ppermute | solution.py:16
  2.8 6.5 %collective-permute-start.1 = (bf16[256,128]{1,0:T(8,128)(2,1)S(1)}, bf16[256,128]{1,0:T(8,128)(2,1)S(1)}, u32[]{:S(2)}, u32[]{:S(2)}) collective-permute-start(bf16[256,128]{1,0:T(8,128)(2,1)S(1)} %get-tuple-element.216), channel_id=1, source_target_pairs={{0,4},{4,8},{8,12},{12,0},{1,5},{5,9},{9,13},{13,1},{2,6},{6,10},{... | collective-permute-start | bytes 196616 | tf_op jit(solution)/shard_map/ppermute | solution.py:140
  4.4 7.3 %collective-permute-start.2 = (bf16[256,128]{1,0:T(8,128)(2,1)S(1)}, bf16[256,128]{1,0:T(8,128)(2,1)S(1)}, u32[]{:S(2)}, u32[]{:S(2)}) collective-permute-start(bf16[256,128]{1,0:T(8,128)(2,1)S(1)} %get-tuple-element.218), channel_id=1, source_target_pairs={{0,8},{4,12},{8,0},{12,4},{1,9},{5,13},{9,1},{13,5},{2,10},{6,14},... | collective-permute-start | bytes 196616 | tf_op jit(solution)/shard_map/ppermute | solution.py:140
  7.0 4.8 %collective-permute-start.3 = (bf16[256,128]{1,0:T(8,128)(2,1)S(1)}, bf16[256,128]{1,0:T(8,128)(2,1)S(1)}, u32[]{:S(2)}, u32[]{:S(2)}) collective-permute-start(bf16[256,128]{1,0:T(8,128)(2,1)S(1)} %get-tuple-element.215), channel_id=1, source_target_pairs={{0,12},{4,0},{8,4},{12,8},{1,13},{5,1},{9,5},{13,9},{2,14},{6,2},{... | collective-permute-start | bytes 196616 | tf_op jit(solution)/shard_map/ppermute | solution.py:140
  8.3 3.9 %collective-permute-start.4 = (bf16[256,128]{1,0:T(8,128)(2,1)S(1)}, bf16[256,128]{1,0:T(8,128)(2,1)S(1)}, u32[]{:S(2)}, u32[]{:S(2)}) collective-permute-start(bf16[256,128]{1,0:T(8,128)(2,1)S(1)} %get-tuple-element.217.refs_4_), channel_id=1, source_target_pairs={{0,1},{1,0},{2,3},{3,2},{4,5},{5,4},{6,7},{7,6},{8,9},{9,8},{10,11... | collective-permute-start | bytes 196616 | tf_op jit(solution)/shard_map/ppermute | solution.py:16
  9.3 3.0 %collective-permute-start.5 = (bf16[256,128]{1,0:T(8,128)(2,1)S(1)}, bf16[256,128]{1,0:T(8,128)(2,1)S(1)}, u32[]{:S(2)}, u32[]{:S(2)}) collective-permute-start(bf16[256,128]{1,0:T(8,128)(2,1)S(1)} %collective-permute-done.1.refs_5_), channel_id=1, source_target_pairs={{0,1},{1,0},{2,3},{3,2},{4,5},{5,4},{6,7},{7,6},{8,9},{9,8},{10,11... | collective-permute-start | bytes 196616 | tf_op jit(solution)/shard_map/ppermute | solution.py:16
  11.7 1.3 %collective-permute-start.6 = (bf16[256,128]{1,0:T(8,128)(2,1)S(1)}, bf16[256,128]{1,0:T(8,128)(2,1)S(1)}, u32[]{:S(2)}, u32[]{:S(2)}) collective-permute-start(bf16[256,128]{1,0:T(8,128)(2,1)S(1)} %collective-permute-done.2.refs_6_), channel_id=1, source_target_pairs={{0,1},{1,0},{2,3},{3,2},{4,5},{5,4},{6,7},{7,6},{8,9},{9,8},{10,11... | collective-permute-start | bytes 196616 | tf_op jit(solution)/shard_map/ppermute | solution.py:16
  11.7 1.4 %collective-permute-start.7 = (bf16[256,128]{1,0:T(8,128)(2,1)S(1)}, bf16[256,128]{1,0:T(8,128)(2,1)S(1)}, u32[]{:S(2)}, u32[]{:S(2)}) collective-permute-start(bf16[256,128]{1,0:T(8,128)(2,1)S(1)} %collective-permute-done.3.refs_7_), channel_id=1, source_target_pairs={{0,1},{1,0},{2,3},{3,2},{4,5},{5,4},{6,7},{7,6},{8,9},{9,8},{10,11... | collective-permute-start | bytes 196616 | tf_op jit(solution)/shard_map/ppermute | solution.py:16
  13.2 0.6 %copy-start.2 = (bf16[256,128]{1,0:T(8,128)(2,1)}, bf16[256,128]{1,0:T(8,128)(2,1)S(1)}, u32[]{:S(2)}) copy-start(bf16[256,128]{1,0:T(8,128)(2,1)S(1)} %get-tuple-element.208) | copy-start | bytes 196612
  13.8 0.6 %copy-start.4 = (bf16[256,128]{1,0:T(8,128)(2,1)}, bf16[256,128]{1,0:T(8,128)(2,1)S(1)}, u32[]{:S(2)}) copy-start(bf16[256,128]{1,0:T(8,128)(2,1)S(1)} %get-tuple-element.212) | copy-start | bytes 196612
  14.4 0.6 %copy-start.6 = (bf16[256,128]{1,0:T(8,128)(2,1)}, bf16[256,128]{1,0:T(8,128)(2,1)S(1)}, u32[]{:S(2)}) copy-start(bf16[256,128]{1,0:T(8,128)(2,1)S(1)} %get-tuple-element.214) | copy-start | bytes 196612
  15.1 12.6 %collective-permute-start.8 = (bf16[512,256]{1,0:T(8,128)(2,1)S(1)}, bf16[512,256]{1,0:T(8,128)(2,1)S(1)}, u32[]{:S(2)}, u32[]{:S(2)}) collective-permute-start(bf16[512,256]{1,0:T(8,128)(2,1)S(1)} %get-tuple-element.206), channel_id=1, source_target_pairs={{0,2},{2,0},{1,3},{3,1},{4,6},{6,4},{5,7},{7,5},{8,10},{10,8},{9,1... | collective-permute-start | bytes 786440 | tf_op jit(solution)/shard_map/ppermute | solution.py:159
  27.6 1.5 %collective-permute-start.9 = (bf16[512,256]{1,0:T(8,128)(2,1)S(1)}, bf16[512,256]{1,0:T(8,128)(2,1)S(1)}, u32[]{:S(2)}, u32[]{:S(2)}) collective-permute-start(bf16[512,256]{1,0:T(8,128)(2,1)S(1)} %collective-permute-done.8.refs_4_), channel_id=1, source_target_pairs={{0,1},{1,0},{2,3},{3,2},{4,5},{5,4},{6,7},{7,6},{8,9},{9,8},{10,11... | collective-permute-start | bytes 786440 | tf_op jit(solution)/shard_map/ppermute | solution.py:16
  27.6 6.6 %copy-start.7 = (bf16[256,128]{1,0:T(8,128)(2,1)S(1)}, bf16[256,128]{1,0:T(8,128)(2,1)}, u32[]{:S(2)}) copy-start(bf16[256,128]{1,0:T(8,128)(2,1)} %copy-done.6) | copy-start | bytes 196612
  27.6 6.7 %copy-start.5 = (bf16[256,128]{1,0:T(8,128)(2,1)S(1)}, bf16[256,128]{1,0:T(8,128)(2,1)}, u32[]{:S(2)}) copy-start(bf16[256,128]{1,0:T(8,128)(2,1)} %copy-done.4) | copy-start | bytes 196612
  27.6 8.6 %copy-start.3 = (bf16[256,128]{1,0:T(8,128)(2,1)S(1)}, bf16[256,128]{1,0:T(8,128)(2,1)}, u32[]{:S(2)}) copy-start(bf16[256,128]{1,0:T(8,128)(2,1)} %copy-done.2) | copy-start | bytes 196612
  34.2 15.1 %collective-permute-start.13 = (bf16[256,128]{1,0:T(8,128)(2,1)S(1)}, bf16[256,128]{1,0:T(8,128)(2,1)S(1)}, u32[]{:S(2)}, u32[]{:S(2)}) collective-permute-start(bf16[256,128]{1,0:T(8,128)(2,1)S(1)} %broadcast_select_fusion), channel_id=1, source_target_pairs={{0,12},{2,4},{4,0},{6,8},{8,6},{10,14},{12,10},{14,2},{1,13},{3,5}... | collective-permute-start | bytes 196616 | tf_op jit(solution)/shard_map/ppermute | solution.py:170
  34.3 14.9 %collective-permute-start.12 = (bf16[256,128]{1,0:T(8,128)(2,1)S(1)}, bf16[256,128]{1,0:T(8,128)(2,1)S(1)}, u32[]{:S(2)}, u32[]{:S(2)}) collective-permute-start(bf16[256,128]{1,0:T(8,128)(2,1)S(1)} %broadcast_select_fusion.1), channel_id=1, source_target_pairs={{0,8},{2,0},{4,12},{6,4},{8,2},{10,10},{12,6},{14,14},{1,9},{3,1},... | collective-permute-start | bytes 196616 | tf_op jit(solution)/shard_map/ppermute | solution.py:170
  36.3 8.4 %collective-permute-start.10 = (bf16[256,128]{1,0:T(8,128)(2,1)S(1)}, bf16[256,128]{1,0:T(8,128)(2,1)S(1)}, u32[]{:S(2)}, u32[]{:S(2)}) collective-permute-start(bf16[256,128]{1,0:T(8,128)(2,1)S(1)} %broadcast_select_fusion.3), channel_id=1, source_target_pairs={{0,0},{2,8},{4,4},{6,12},{8,10},{10,2},{12,14},{14,6},{1,1},{3,9},... | collective-permute-start | bytes 196616 | tf_op jit(solution)/shard_map/ppermute | solution.py:170
  42.0 7.0 %collective-permute-start.11 = (bf16[256,128]{1,0:T(8,128)(2,1)S(1)}, bf16[256,128]{1,0:T(8,128)(2,1)S(1)}, u32[]{:S(2)}, u32[]{:S(2)}) collective-permute-start(bf16[256,128]{1,0:T(8,128)(2,1)S(1)} %broadcast_select_fusion.2), channel_id=1, source_target_pairs={{0,4},{2,12},{4,8},{6,0},{8,14},{10,6},{12,2},{14,10},{1,5},{3,13}... | collective-permute-start | bytes 196616 | tf_op jit(solution)/shard_map/ppermute | solution.py:170

commit v2 on v0

v2 whole, which is shorter than its diff:
```python
import functools

import jax
import jax.numpy as jnp
from jax import lax
from jax.experimental import pallas as pl
from jax.experimental.pallas import tpu as pltpu
from jax.sharding import PartitionSpec as P

VMEM = pl.BlockSpec(memory_space=pltpu.VMEM)
ROW_TILE = 256


class Plan:
    def __init__(self, count, sections, records):
        self.count, self.sections, self.records = count, sections, records
        self.share = records // sections
        self.whole_group = records <= count // 2
        self.blocks = records // 2 if self.whole_group else max(1, records // 4)

    def owner(self, z):
        return z % self.records % self.sections

    def slot(self, z):
        return z % self.records // self.sections

    def record_at(self, z):
        return self.owner(z) * self.share + self.slot(z)

    def time_block(self, z, core, half, index):
        if self.whole_group:
            return z // self.records * self.records + 2 * index + core
        return half * (self.count // 2) + 2 * index + core

    def landing_core(self, segment, half, slot):
        return (slot + half + segment + 1) % 2

    def transfers(self, stage, half, index):
        sends = {}
        for z in range(self.count):
            for core in range(2):
                t = self.time_block(z, core, half, index)
                if t // (self.count // 2) == half:
                    to = self.owner(z)
                    sends[z, stage, core] = (t, to, self.landing_core(to, half, self.slot(z)))
        return sends


def complete(sends, shape):
    devices = [(z, s, c) for z in range(shape[0]) for s in range(shape[1]) for c in range(shape[2])]
    taken = set(sends.values())
    sources = [d for d in devices if d not in sends]
    targets = [d for d in devices if d not in taken]
    pairs = dict(sends)

    def near(pair):
        a, b = pair
        return (a == b, abs(a[0] - b[0]), a[1] != b[1])

    for source in sources:
        target = min(targets, key=lambda b: near((source, b)))
        targets.remove(target)
        pairs[source] = target
    for a in [d for d in sources if pairs[d] == d]:
        b = next((d for d in sources if d != a and pairs[d] != a), None)
        if b is not None:
            pairs[a], pairs[b] = pairs[b], pairs[a]
    return pairs


def swap_cores(block):
    return lax.ppermute(block, "chan", [(0, 1), (1, 0)])


def section_kernel(stage, half, plan, lags, n_in, last, *refs):
    own_pack, other_pack, res_ref, own_skip, other_skip = refs[:5]
    inputs, refs = refs[5 : 5 + n_in], refs[5 + n_in :]
    layers, depth = res_ref.shape[:2]
    width = depth // 2
    heads = ()
    if half:
        heads, refs = refs[:layers], refs[layers:]
    skip_outs, refs = refs[: plan.blocks], refs[plan.blocks :]
    if not last:
        stream_out, refs = refs[0], refs[1:]
    if not half:
        tails, refs = refs[:layers], refs[layers:]
    streams, units, out_buf = refs[:layers], refs[layers], refs[layers + 1]
    core, place = lax.axis_index("chan"), lax.axis_index("tm")
    total = units.shape[1]
    own_rows = pl.ds(pl.multiple_of(core * width, width), width)
    other_rows = pl.ds(pl.multiple_of((1 - core) * width, width), width)

    @pl.when(lax.axis_index("segment") == stage)
    def _():
        for layer in range(layers):
            lag = lags[layer % 4]
            streams[layer][:lag, :] = heads[layer][...] if half else jnp.zeros((lag, depth), jnp.bfloat16)
        if stage == 0:
            rows = inputs[0].shape[0]
            per_half = plan.count // 2
            for side, blocks in ((own_rows, inputs[: n_in // 2]), (other_rows, inputs[n_in // 2 :])):
                for turn, block in enumerate(blocks):
                    t = lax.rem(place - turn + plan.count, plan.count)

                    @pl.when(t // per_half == half)
                    def _(t=t, block=block, side=side):
                        at = pl.multiple_of(lags[0] + (t - half * per_half) * rows, 16)
                        streams[0][pl.ds(at, rows), side] = block[...]
        else:
            part = inputs[0].shape[0]
            for side, block in ((core, inputs[0]), (1 - core, inputs[1])):
                streams[0][pl.ds(pl.multiple_of(lags[0] + side * part, 16), part), :] = block[...]

        for layer in range(layers):
            lag = lags[layer % 4]
            now_buf = streams[layer]
            next_buf, next_lag = (streams[layer + 1], lags[(layer + 1) % 4]) if layer + 1 < layers else (out_buf, 0)
            res = None
            if not (last and layer + 1 == layers):
                res = jnp.concatenate([res_ref[layer, own_rows, :], res_ref[layer, other_rows, :]], 0)

            def tile(row, layer=layer, lag=lag, now_buf=now_buf, next_buf=next_buf, next_lag=next_lag, res=res):
                past = now_buf[pl.ds(row, ROW_TILE), :]
                now = now_buf[pl.ds(lag + row, ROW_TILE), :]
                parts = []
                for pack in (own_pack, other_pack):
                    pre = jnp.dot(past, pack[layer, :depth], preferred_element_type=jnp.float32)
                    pre += jnp.dot(now, pack[layer, depth : 2 * depth], preferred_element_type=jnp.float32)
                    pre += pack[layer, 2 * depth : 2 * depth + 1].astype(jnp.float32)
                    gate = 0.5 * jnp.tanh(0.5 * pre[:, width:]) + 0.5
                    parts.append((jnp.tanh(pre[:, :width]) * gate).astype(jnp.bfloat16))
                unit = jnp.concatenate(parts, 1)
                units[layer, pl.ds(row, ROW_TILE), :] = unit
                if res is not None:
                    update = jnp.dot(unit, res, preferred_element_type=jnp.float32)
                    next_buf[pl.ds(next_lag + row, ROW_TILE), :] = (now.astype(jnp.float32) + update).astype(jnp.bfloat16)

            steps = total // ROW_TILE
            if steps <= 4:
                for step in range(steps):
                    tile(step * ROW_TILE)
            else:
                pl.loop(0, steps)(lambda step: tile(pl.multiple_of(step * ROW_TILE, ROW_TILE)))

        if not last:
            part = total // 2
            stream_out[...] = out_buf[pl.ds(pl.multiple_of(core * part, 16), part), :]
        if not half:
            for layer in range(layers):
                tails[layer][...] = streams[layer][pl.ds(total, lags[layer % 4]), :]
        for index, out in enumerate(skip_outs):
            rows = out.shape[0]
            t = plan.time_block(place, core, half, index) - half * (plan.count // 2)
            at = pl.multiple_of(jnp.clip(t, 0, total // rows - 1) * rows, rows)
            acc = jnp.zeros((rows, depth), jnp.float32)
            for layer in range(layers):
                unit = units[layer, pl.ds(at, rows), :]
                skip = jnp.concatenate(
                    [
                        jnp.concatenate([part[layer, own_rows, :], part[layer, other_rows, :]], 0)
                        for part in (own_skip, other_skip)
                    ],
                    1,
                )
                acc += jnp.dot(unit, skip, preferred_element_type=jnp.float32)
            out[:, own_rows] = acc[:, :width].astype(out.dtype)
            out[:, other_rows] = acc[:, width:].astype(out.dtype)


def run_section(stage, half, plan, lags, weights, inputs, heads, rows):
    res_weight = weights[2]
    layers, depth = res_weight.shape[:2]
    total = rows * plan.count // 2
    last = stage == plan.sections - 1
    outs = [jax.ShapeDtypeStruct((rows, depth), jnp.bfloat16)] * plan.blocks
    if not last:
        outs.append(jax.ShapeDtypeStruct((total // 2, depth), jnp.bfloat16))
    if not half:
        outs += [jax.ShapeDtypeStruct((lags[layer % 4], depth), jnp.bfloat16) for layer in range(layers)]
    scratch = [pltpu.VMEM((lags[layer % 4] + total, depth), jnp.bfloat16) for layer in range(layers)]
    scratch += [pltpu.VMEM((layers, total, depth), jnp.bfloat16), pltpu.VMEM((total, depth), jnp.bfloat16)]
    held = 2 * depth * (sum(lags) * 3 + 13 * total)
    got = pl.pallas_call(
        functools.partial(section_kernel, stage, half, plan, lags, len(inputs), last),
        out_shape=outs,
        in_specs=[VMEM] * (len(weights) + len(inputs) + len(heads)),
        out_specs=[VMEM] * len(outs),
        scratch_shapes=scratch,
        compiler_params=pltpu.CompilerParams(vmem_limit_bytes=held + (12 << 20)),
    )(*weights, *inputs, *heads)
    blocks, got = got[: plan.blocks], got[plan.blocks :]
    stream = None
    if not last:
        stream, got = got[0], got[1:]
    return blocks, stream, got


def shards(records, conv_weight, conv_bias, res_weight, skip_weight):
    record_count, rows, width = records.shape
    layers, taps = conv_weight.shape[:2]
    count, sections = lax.axis_size("tm"), lax.axis_size("segment")
    place, segment, core = lax.axis_index("tm"), lax.axis_index("segment"), lax.axis_index("chan")
    lags = [rows // 8, rows, rows * max(1, count // 8), rows * max(1, count // 2)]
    plan = Plan(count, sections, record_count)

    own_blocks = []
    for turn in range(count):
        block = lax.dynamic_index_in_dim(records, plan.record_at(lax.rem(place + turn, count)), 0, keepdims=False)
        if turn:
            block = lax.ppermute(block, "tm", [(i, (i + turn) % count) for i in range(count)])
        own_blocks.append(block)
    inputs = own_blocks + [swap_cores(block) for block in own_blocks]

    bias_rows = jnp.pad(conv_bias.reshape(layers, 1, 2 * width), ((0, 0), (0, 15), (0, 0)))
    own_pack = jnp.concatenate([conv_weight.reshape(layers, taps, 2 * width), bias_rows], 1)
    weights = (own_pack, swap_cores(own_pack), res_weight, skip_weight, swap_cores(skip_weight))

    skips = {}
    fed = [inputs, inputs]
    for stage in range(sections):
        heads, crossed = (), []
        for half in range(2):
            skips[stage, half], stream, carried = run_section(
                stage, half, plan, lags, weights, fed[half], heads, rows
            )
            heads = carried
            if stage < sections - 1:
                moved = lax.ppermute(stream, "segment", [(i, (i + 1) % sections) for i in range(sections)])
                crossed.append([moved, swap_cores(moved)])
        fed = crossed

    total = jnp.zeros((rows, 2 * width), jnp.float32)
    spot = (place * sections + segment) * 2 + core
    for early in (True, False):
        for index in range(plan.blocks):
            groups = []
            for stage in reversed(range(sections)):
                half = int((stage == sections - 1) != early)
                sends = plan.transfers(stage, half, index)
                for group in groups:
                    if not set(group[0].values()) & set(sends.values()):
                        group[0].update(sends)
                        group[1].append((stage, half))
                        break
                else:
                    groups.append((sends, [(stage, half)]))
            for sends, members in groups:
                payload = None
                for stage, half in members:
                    block = skips[stage, half][index]
                    payload = block if payload is None else jnp.where(segment == stage, block, payload)
                pairs = complete(sends, (count, sections, 2))
                number = lambda d: (d[0] * sections + d[1]) * 2 + d[2]
                got = lax.ppermute(
                    payload, ("tm", "segment", "chan"), sorted((number(a), number(b)) for a, b in pairs.items())
                )
                valid = functools.reduce(jnp.logical_or, [spot == number(d) for d in sends.values()])
                if len(sends) == 2 * count * sections:
                    total = total + got.astype(jnp.float32)
                else:
                    total = total + jnp.where(valid, got.astype(jnp.float32), 0.0)
    block = total.astype(jnp.bfloat16)
    low, high = block[:, :width], block[:, width:]
    kept = jnp.where(core == 0, low, high)
    given = swap_cores(jnp.where(core == 0, high, low))
    mine = lax.rem(core + place // (count // 2) + segment + 1, 2)
    return jnp.stack([jnp.where(mine == slot, kept, given) for slot in range(plan.share)])


def solution(mesh):
    return jax.shard_map(
        shards,
        mesh=mesh,
        in_specs=(
            P("groups", "tm", "chan"),
            P("segment", None, None, "chan"),
            P("segment", None, "chan"),
            P("segment", None, None),
            P("segment", None, "chan"),
        ),
        out_specs=P(("groups", "segment"), "tm", "chan"),
        check_vma=False,
    )
```

time: 274 us -> 45.8 us (0.17)
  starting transfers between devices: 121 us -> 9.59 us
  waiting for transfers between devices: 78.2 us -> 22.7 us
  blocking collectives: 40.5 us -> 0 us
  matrix products: 14.6 us -> 0 us
  between operations: 13.4 us -> 0.14 us
  Pallas kernels: 0 us -> 7.15 us
    ppermute x25 -> x16, starting transfers between devices: 121 us -> 9.59 us  [the longest x3 5.74 us: shards(): lax.ppermute(block, 'tm', [(i, (i + turn) % count) for i in range(count)])]
    all_gather x21 -> x0, blocking collectives: 40.5 us -> none  [the longest x20 38 us: layer_stack(): full_units = lax.all_gather(gate_out, 'chan', axis=2, tiled=True)]
    ppermute x25 -> x16, waiting for transfers between devices: 60.7 us -> 22.7 us  [the longest x2 7.67 us: shards(): lax.ppermute(payload, ('tm', 'segment', 'chan'), sorted(((number(a), numb...]
    reduce_scatter x1 -> x0, waiting for transfers between devices: 17.5 us -> none  [shards(): lax.psum_scatter(skip_acc.astype(jnp.bfloat16), 'segment', scatter_dimens...]
    dot_general x80 -> x0, matrix products: 14.6 us -> none  [the longest x20 3.77 us: layer_stack(): jnp.einsum('bsk,kc->bsc', full_units, res_columns, preferred_element_type...]
    pallas_call x0 -> x4, Pallas kernels: none -> 7.15 us  [run_section(): pl.pallas_call(functools.partial(section_kernel, stage, half, plan, lags,...]
  transfers between devices with their start and end apart: 26 -> 16, of which waited for: 26 -> 9; matrix products, arithmetic and copies ran while one was open for 3% -> 2% of each run, Pallas kernels for 0% -> 10%
where the time goes in v2:
time: 45.8 us; the launch traced here: 45.4 us
  waiting for transfers between devices  22.7 us (50%)
  starting transfers between devices  9.59 us (21%)
  Pallas kernels  7.15 us (16%)
  local copies, waits for them, and re-layouts  3.42 us (7%)
  other arithmetic  2.39 us (5%)
    ppermute x2, waiting for transfers between devices, shards(): lax.ppermute(payload, ('tm', 'segment', 'chan'), sorted(((number(a), numb...  7.67 us
    pallas_call x4, Pallas kernels, run_section(): pl.pallas_call(functools.partial(section_kernel, stage, half, plan, lags,...  7.15 us
    ppermute x3, waiting for transfers between devices, shards(): lax.ppermute(block, 'tm', [(i, (i + turn) % count) for i in range(count)])  6.96 us
    ppermute x2, waiting for transfers between devices, shards(): lax.ppermute(stream, 'segment', [(i, (i + 1) % sections) for i in range(s...  5.97 us
    ppermute x3, starting transfers between devices, shards(): lax.ppermute(block, 'tm', [(i, (i + turn) % count) for i in range(count)])  5.74 us
    ppermute x2, starting transfers between devices, shards(): lax.ppermute(payload, ('tm', 'segment', 'chan'), sorted(((number(a), numb...  2.21 us
    ppermute x9, waiting for transfers between devices, swap_cores(): return lax.ppermute(block, 'chan', [(0, 1), (1, 0)])  2.12 us
    reshape x1, local copies, waits for them, and re-layouts, shards(): conv_weight.reshape(layers, taps, 2 * width)  1.73 us
  transfers between devices with their start and end apart: 16, of which 9 were waited for; matrix products, arithmetic and copies ran while one was open for 2% of the time, Pallas kernels for 10%

profile of v2, /device:TPU:0, one launch (start us, length us, event | category | flops | bytes accessed | tf_op | source)
XLA Modules:
  0.0 45.4 jit_solution(16226017466772850338)
XLA Ops:
  0.0 0.7 %reshape.8 = bf16[4,1,256]{2,1,0:T(2,128)(2,1)S(1)} reshape(bf16[4,2,128]{2,1,0:T(2,128)(2,1)} %param.7) | data formatting | bytes 4096 | tf_op jit(solution)/shard_map/reshape | solution.py:215
  0.7 1.7 %reshape.6 = bf16[4,512,256]{2,1,0:T(8,128)(2,1)S(1)} reshape(bf16[4,512,2,128]{3,2,1,0:T(2,128)(2,1)} %param.6) | data formatting | bytes 2097152 | tf_op jit(solution)/shard_map/reshape | solution.py:216
  2.4 0.0 copy-start.1
  2.4 0.0 copy-start.4
  2.5 0.0 copy-start
  2.5 0.1 fusion.1.refs_0_
  2.6 0.5 %collective-permute-start = (bf16[4,528,256]{2,1,0:T(8,128)(2,1)S(1)}, bf16[4,528,256]{2,1,0:T(8,128)(2,1)S(1)}, u32[]{:S(2)}, u32[]{:S(2)}) collective-permute-start(bf16[4,528,256]{2,1,0:T(8,128)(2,1)S(1)} %fusion.1.refs_0_), channel_id=1, source_target_pairs={{0,1},{1,0},{2,3},{3,2},{4,5},{5,4},{6,7},{7,6},{8,9},{9,8},{10,11... | collective-permute-start | bytes 3244040 | tf_op jit(solution)/shard_map/ppermute | solution.py:72
  3.1 0.3 copy-done.1
  3.4 0.5 collective-permute-start.1
  3.8 0.0 copy-done.4
  3.9 4.7 %collective-permute-start.4 = (bf16[256,128]{1,0:T(8,128)(2,1)S(1)}, bf16[256,128]{1,0:T(8,128)(2,1)S(1)}, u32[]{:S(2)}, u32[]{:S(2)}) collective-permute-start(bf16[256,128]{1,0:T(8,128)(2,1)S(1)} %get-tuple-element.31), channel_id=1, source_target_pairs={{0,12},{4,0},{8,4},{12,8},{1,13},{5,1},{9,5},{13,9},{2,14},{6,2},{... | collective-permute-start | bytes 196616 | tf_op jit(solution)/shard_map/ppermute | solution.py:211
  8.6 0.0 collective-permute-start.2
  8.6 1.0 %collective-permute-start.3 = (bf16[256,128]{1,0:T(8,128)(2,1)S(1)}, bf16[256,128]{1,0:T(8,128)(2,1)S(1)}, u32[]{:S(2)}, u32[]{:S(2)}) collective-permute-start(bf16[256,128]{1,0:T(8,128)(2,1)S(1)} %get-tuple-element.34), channel_id=1, source_target_pairs={{0,8},{4,12},{8,0},{12,4},{1,9},{5,13},{9,1},{13,5},{2,10},{6,14},... | collective-permute-start | bytes 196616 | tf_op jit(solution)/shard_map/ppermute | solution.py:211
  9.6 1.4 %collective-permute-done.4.refs_8_ = bf16[256,128]{1,0:T(8,128)(2,1)S(1)} collective-permute-done((bf16[256,128]{1,0:T(8,128)(2,1)S(1)}, bf16[256,128]{1,0:T(8,128)(2,1)S(1)}, u32[]{:S(2)}, u32[]{:S(2)}) %collective-permute-start.4) | collective-permute-done | bytes 65568 | tf_op jit(solution)/shard_map/ppermute | solution.py:211
  11.0 0.0 collective-permute-start.5
  11.0 4.3 %collective-permute-done.2.refs_6_ = bf16[256,128]{1,0:T(8,128)(2,1)S(1)} collective-permute-done((bf16[256,128]{1,0:T(8,128)(2,1)S(1)}, bf16[256,128]{1,0:T(8,128)(2,1)S(1)}, u32[]{:S(2)}, u32[]{:S(2)}) %collective-permute-start.2) | collective-permute-done | bytes 65568 | tf_op jit(solution)/shard_map/ppermute | solution.py:211
  15.4 0.0 collective-permute-start.8
  15.4 1.2 %collective-permute-done.3.refs_7_ = bf16[256,128]{1,0:T(8,128)(2,1)S(1)} collective-permute-done((bf16[256,128]{1,0:T(8,128)(2,1)S(1)}, bf16[256,128]{1,0:T(8,128)(2,1)S(1)}, u32[]{:S(2)}, u32[]{:S(2)}) %collective-permute-start.3) | collective-permute-done | bytes 65568 | tf_op jit(solution)/shard_map/ppermute | solution.py:211
  16.6 0.0 collective-permute-start.6
  16.6 0.0 collective-permute-done.5.refs_9_
  16.6 0.5 %collective-permute-start.7 = (bf16[256,128]{1,0:T(8,128)(2,1)S(1)}, bf16[256,128]{1,0:T(8,128)(2,1)S(1)}, u32[]{:S(2)}, u32[]{:S(2)}) collective-permute-start(bf16[256,128]{1,0:T(8,128)(2,1)S(1)} %collective-permute-done.3.refs_7_), channel_id=1, source_target_pairs={{0,1},{1,0},{2,3},{3,2},{4,5},{5,4},{6,7},{7,6},{8,9},{9,8},{10,11... | collective-permute-start | bytes 196616 | tf_op jit(solution)/shard_map/ppermute | solution.py:72
  17.1 0.0 collective-permute-done.8.refs_12_
  17.1 0.7 %collective-permute-done.6.refs_10_ = bf16[256,128]{1,0:T(8,128)(2,1)S(1)} collective-permute-done((bf16[256,128]{1,0:T(8,128)(2,1)S(1)}, bf16[256,128]{1,0:T(8,128)(2,1)S(1)}, u32[]{:S(2)}, u32[]{:S(2)}) %collective-permute-start.6) | collective-permute-done | bytes 65568 | tf_op jit(solution)/shard_map/ppermute | solution.py:72
  17.8 0.2 collective-permute-done.7.refs_11_
  18.0 0.0 collective-permute-done.1.refs_4_
  18.0 0.0 collective-permute-done.refs_1_
  18.0 0.0 copy-done
  18.0 2.8 %shard_map.55 = (bf16[256,256]{1,0:T(8,128)(2,1)S(1)}, bf16[256,256]{1,0:T(8,128)(2,1)S(1)}, bf16[32,256]{1,0:T(8,128)(2,1)S(1)}, bf16[256,256]{1,0:T(8,128)(2,1...) custom-call(bf16[4,528,256]{2,1,0:T(8,128)(2,1)S(1)} %fusion.1.refs_0_, ...), custom_call_target="tpu_custom_call" | custom-call | tf_op jit(solution)/shard_map/pallas_call | solution.py:184
  20.8 0.1 collective-permute-start.9
  20.8 3.4 %shard_map.56 = (bf16[256,256]{1,0:T(8,128)(2,1)S(1)}, bf16[256,256]{1,0:T(8,128)(2,1)}) custom-call(bf16[4,528,256]{2,1,0:T(8,128)(2,1)S(1)} %fusion.1.refs_0_, bf16[4,528,256]{2,1,0:T(8,128)(2,1)S(1)} %collective-permute-done.refs_1_, bf16[4,256,256]{2,1,0:T(8,128)(2,1)S(1)} %copy-done, bf16[4,256,128]{2,1,0:T(8,128)(2,1)S(1)} %copy-done.1, ...), custom_call_target="tpu_custom_call" | custom-call | tf_op jit(solution)/shard_map/pallas_call | solution.py:184
  24.3 0.0 copy-start.2
  24.3 0.6 %copy-done.2 = bf16[256,256]{1,0:T(8,128)(2,1)} copy-done((bf16[256,256]{1,0:T(8,128)(2,1)}, bf16[256,256]{1,0:T(8,128)(2,1)S(1)}, u32[]{:S(2)}) %copy-start.2) | copy-done | bytes 131096
  24.9 0.0 collective-permute-start.12
  24.9 1.8 %collective-permute-done.9.refs_5_ = bf16[256,256]{1,0:T(8,128)(2,1)} collective-permute-done((bf16[256,256]{1,0:T(8,128)(2,1)S(1)}, bf16[256,256]{1,0:T(8,128)(2,1)}, u32[]{:S(2)}, u32[]{:S(2)}) %collective-permute-start.9) | collective-permute-done | bytes 131104 | tf_op jit(solution)/shard_map/ppermute | solution.py:229
  26.7 0.0 collective-permute-start.10
  26.7 0.0 copy-start.3
  26.7 4.2 %collective-permute-done.12.refs_5_ = bf16[256,256]{1,0:T(8,128)(2,1)S(1)} collective-permute-done((bf16[256,256]{1,0:T(8,128)(2,1)}, bf16[256,256]{1,0:T(8,128)(2,1)S(1)}, u32[]{:S(2)}, u32[]{:S(2)}) %collective-permute-start.12) | collective-permute-done | bytes 131104 | tf_op jit(solution)/shard_map/ppermute | solution.py:229
  30.9 0.0 collective-permute-start.13
  30.9 0.0 collective-permute-done.10.refs_6_
  30.9 1.0 %shard_map.57 = (bf16[256,256]{1,0:T(8,128)(2,1)S(1)}, bf16[32,256]{1,0:T(8,128)(2,1)S(1)}, bf16[256,256]{1,0:T(8,128)(2,1)S(1)}, bf16[256,256]{1,0:T(8,128)(2,1)S(1)}, bf16[512,256]{1,0:T(8,128)(2,1)S(1)}) custom-call(bf16[4,528,256]{2,1,0:T(8,128)(2,1)S(1)} %fusion.1.refs_0_, bf16[4,528,256]{2,1,0:T(8,128)(2,1)S(1)} %collective-permute-done.refs_1_, ...), custom_call_target="tpu_custom_call" | custom-call | tf_op jit(solution)/shard_map/pallas_call | solution.py:184
  31.9 0.0 copy-done.3
  31.9 0.7 %broadcast_select_fusion.1 = bf16[256,256]{1,0:T(8,128)(2,1)} fusion(bf16[256,256]{1,0:T(8,128)(2,1)S(1)} %copy-done.3, bf16[256,256]{1,0:T(8,128)(2,1)S(1)} %get-tuple-element.24, pred[]{:T(512)S(6)} %eq.29), kind=kLoop, calls=%fused_computation.6 | loop fusion | flops 65536 | bytes 393217 | tf_op jit(solution)/shard_map/jit(_where)/select_n | solution.py:252
  32.5 0.3 collective-permute-start.11
  32.8 0.0 collective-permute-done.13.refs_6_
  32.8 1.9 %collective-permute-start.14 = (bf16[256,256]{1,0:T(8,128)(2,1)S(1)}, bf16[256,256]{1,0:T(8,128)(2,1)S(1)}, u32[]{:S(2)}, u32[]{:S(2)}) collective-permute-start(bf16[256,256]{1,0:T(8,128)(2,1)S(1)} %broadcast_select_fusion), channel_id=1, source_target_pairs={{0,1},{1,5},{2,8},{3,12},{4,2},{5,6},{6,11},{7,15},{8,0},{9,4},{10... | collective-permute-start | bytes 393224 | tf_op jit(solution)/shard_map/ppermute | solution.py:255
  34.8 7.7 %collective-permute-done.11 = bf16[256,256]{1,0:T(8,128)(2,1)} collective-permute-done((bf16[256,256]{1,0:T(8,128)(2,1)}, bf16[256,256]{1,0:T(8,128)(2,1)}, u32[]{:S(2)}, u32[]{:S(2)}) %collective-permute-start.11) | collective-permute-done | bytes 131104 | tf_op jit(solution)/shard_map/ppermute | solution.py:255
  42.4 0.0 collective-permute-done.14
  42.4 0.9 %add_convert_fusion = bf16[256,256]{1,0:T(8,128)(2,1)S(1)} fusion(bf16[256,256]{1,0:T(8,128)(2,1)S(1)} %collective-permute-done.14, bf16[256,256]{1,0:T(8,128)(2,1)} %collective-permute-done.11), kind=kLoop, calls=%fused_computation.3 | loop fusion | flops 262144 | bytes 393216 | tf_op jit(solution)/shard_map/convert_element_type | solution.py:263
  43.4 0.1 collective-permute-start.15
  43.5 1.2 %collective-permute-done.15 = bf16[256,128]{1,0:T(8,128)(2,1)S(1)} collective-permute-done((bf16[256,128]{1,0:T(8,128)(2,1)S(1)}, bf16[256,128]{1,0:T(8,128)(2,1)S(1)}, u32[]{:S(2)}, u32[]{:S(2)}) %collective-permute-start.15) | collective-permute-done | bytes 65568 | tf_op jit(solution)/shard_map/ppermute | solution.py:72
  44.7 0.7 %pad_maximum_fusion = bf16[2,256,128]{2,1,0:T(8,128)(2,1)} fusion(bf16[1,256,128]{2,1,0:T(8,128)(2,1)S(1)} %get-tuple-element.36, bf16[1,256,128]{2,1,0:T(8,128)(2,1)S(1)} %get-tuple-element.35), kind=kLoop, calls=%fused_computation.4 | loop fusion | flops 65536 | bytes 262144 | tf_op jit(solution)/shard_map/stack | solution.py:268
  (5 shorter events, 0.1 us)
Async XLA Ops:
  2.4 1.0 %copy-start.1 = (bf16[4,256,128]{2,1,0:T(8,128)(2,1)S(1)}, bf16[4,256,128]{2,1,0:T(8,128)(2,1)}, u32[]{:S(2)}) copy-start(bf16[4,256,128]{2,1,0:T(8,128)(2,1)} %refs_3_.7) | copy-start | bytes 786436
  2.4 1.4 %copy-start.4 = (bf16[4,256,128]{2,1,0:T(8,128)(2,1)S(1)}, bf16[4,256,128]{2,1,0:T(8,128)(2,1)}, u32[]{:S(2)}) copy-start(bf16[4,256,128]{2,1,0:T(8,128)(2,1)} %param.5) | copy-start | bytes 786436
  2.5 15.5 %copy-start = (bf16[4,256,256]{2,1,0:T(8,128)(2,1)S(1)}, bf16[4,256,256]{2,1,0:T(8,128)(2,1)}, u32[]{:S(2)}) copy-start(bf16[4,256,256]{2,1,0:T(8,128)(2,1)} %refs_2_.7) | copy-start | bytes 1572868
  2.6 15.4 %collective-permute-start = (bf16[4,528,256]{2,1,0:T(8,128)(2,1)S(1)}, bf16[4,528,256]{2,1,0:T(8,128)(2,1)S(1)}, u32[]{:S(2)}, u32[]{:S(2)}) collective-permute-start(bf16[4,528,256]{2,1,0:T(8,128)(2,1)S(1)} %fusion.1.refs_0_), channel_id=1, source_target_pairs={{0,1},{1,0},{2,3},{3,2},{4,5},{5,4},{6,7},{7,6},{8,9},{9,8},{10,11... | collective-permute-start | bytes 3244040 | tf_op jit(solution)/shard_map/ppermute | solution.py:72
  3.4 14.6 %collective-permute-start.1 = (bf16[4,256,128]{2,1,0:T(8,128)(2,1)S(1)}, bf16[4,256,128]{2,1,0:T(8,128)(2,1)S(1)}, u32[]{:S(2)}, u32[]{:S(2)}) collective-permute-start(bf16[4,256,128]{2,1,0:T(8,128)(2,1)S(1)} %copy-done.1), channel_id=1, source_target_pairs={{0,1},{1,0},{2,3},{3,2},{4,5},{5,4},{6,7},{7,6},{8,9},{9,8},{10,11... | collective-permute-start | bytes 786440 | tf_op jit(solution)/shard_map/ppermute | solution.py:72
  3.9 7.1 %collective-permute-start.4 = (bf16[256,128]{1,0:T(8,128)(2,1)S(1)}, bf16[256,128]{1,0:T(8,128)(2,1)S(1)}, u32[]{:S(2)}, u32[]{:S(2)}) collective-permute-start(bf16[256,128]{1,0:T(8,128)(2,1)S(1)} %get-tuple-element.31), channel_id=1, source_target_pairs={{0,12},{4,0},{8,4},{12,8},{1,13},{5,1},{9,5},{13,9},{2,14},{6,2},{... | collective-permute-start | bytes 196616 | tf_op jit(solution)/shard_map/ppermute | solution.py:211
  8.6 6.8 %collective-permute-start.2 = (bf16[256,128]{1,0:T(8,128)(2,1)S(1)}, bf16[256,128]{1,0:T(8,128)(2,1)S(1)}, u32[]{:S(2)}, u32[]{:S(2)}) collective-permute-start(bf16[256,128]{1,0:T(8,128)(2,1)S(1)} %get-tuple-element.32), channel_id=1, source_target_pairs={{0,4},{4,8},{8,12},{12,0},{1,5},{5,9},{9,13},{13,1},{2,6},{6,10},{... | collective-permute-start | bytes 196616 | tf_op jit(solution)/shard_map/ppermute | solution.py:211
  8.6 8.0 %collective-permute-start.3 = (bf16[256,128]{1,0:T(8,128)(2,1)S(1)}, bf16[256,128]{1,0:T(8,128)(2,1)S(1)}, u32[]{:S(2)}, u32[]{:S(2)}) collective-permute-start(bf16[256,128]{1,0:T(8,128)(2,1)S(1)} %get-tuple-element.34), channel_id=1, source_target_pairs={{0,8},{4,12},{8,0},{12,4},{1,9},{5,13},{9,1},{13,5},{2,10},{6,14},... | collective-permute-start | bytes 196616 | tf_op jit(solution)/shard_map/ppermute | solution.py:211
  11.0 5.6 %collective-permute-start.5 = (bf16[256,128]{1,0:T(8,128)(2,1)S(1)}, bf16[256,128]{1,0:T(8,128)(2,1)S(1)}, u32[]{:S(2)}, u32[]{:S(2)}) collective-permute-start(bf16[256,128]{1,0:T(8,128)(2,1)S(1)} %get-tuple-element.33.refs_5_), channel_id=1, source_target_pairs={{0,1},{1,0},{2,3},{3,2},{4,5},{5,4},{6,7},{7,6},{8,9},{9,8},{10,11... | collective-permute-start | bytes 196616 | tf_op jit(solution)/shard_map/ppermute | solution.py:72
  15.4 1.7 %collective-permute-start.8 = (bf16[256,128]{1,0:T(8,128)(2,1)S(1)}, bf16[256,128]{1,0:T(8,128)(2,1)S(1)}, u32[]{:S(2)}, u32[]{:S(2)}) collective-permute-start(bf16[256,128]{1,0:T(8,128)(2,1)S(1)} %collective-permute-done.4.refs_8_), channel_id=1, source_target_pairs={{0,1},{1,0},{2,3},{3,2},{4,5},{5,4},{6,7},{7,6},{8,9},{9,8},{10,11... | collective-permute-start | bytes 196616 | tf_op jit(solution)/shard_map/ppermute | solution.py:72
  16.6 1.3 %collective-permute-start.6 = (bf16[256,128]{1,0:T(8,128)(2,1)S(1)}, bf16[256,128]{1,0:T(8,128)(2,1)S(1)}, u32[]{:S(2)}, u32[]{:S(2)}) collective-permute-start(bf16[256,128]{1,0:T(8,128)(2,1)S(1)} %collective-permute-done.2.refs_6_), channel_id=1, source_target_pairs={{0,1},{1,0},{2,3},{3,2},{4,5},{5,4},{6,7},{7,6},{8,9},{9,8},{10,11... | collective-permute-start | bytes 196616 | tf_op jit(solution)/shard_map/ppermute | solution.py:72
  16.6 1.4 %collective-permute-start.7 = (bf16[256,128]{1,0:T(8,128)(2,1)S(1)}, bf16[256,128]{1,0:T(8,128)(2,1)S(1)}, u32[]{:S(2)}, u32[]{:S(2)}) collective-permute-start(bf16[256,128]{1,0:T(8,128)(2,1)S(1)} %collective-permute-done.3.refs_7_), channel_id=1, source_target_pairs={{0,1},{1,0},{2,3},{3,2},{4,5},{5,4},{6,7},{7,6},{8,9},{9,8},{10,11... | collective-permute-start | bytes 196616 | tf_op jit(solution)/shard_map/ppermute | solution.py:72
  20.8 5.9 %collective-permute-start.9 = (bf16[256,256]{1,0:T(8,128)(2,1)S(1)}, bf16[256,256]{1,0:T(8,128)(2,1)}, u32[]{:S(2)}, u32[]{:S(2)}) collective-permute-start(bf16[256,256]{1,0:T(8,128)(2,1)S(1)} %get-tuple-element.23), channel_id=1, source_target_pairs={{0,2},{2,0},{1,3},{3,1},{4,6},{6,4},{5,7},{7,5},{8,10},{10,8},{9,1... | collective-permute-start | bytes 393224 | tf_op jit(solution)/shard_map/ppermute | solution.py:229
  24.3 0.6 %copy-start.2 = (bf16[256,256]{1,0:T(8,128)(2,1)}, bf16[256,256]{1,0:T(8,128)(2,1)S(1)}, u32[]{:S(2)}) copy-start(bf16[256,256]{1,0:T(8,128)(2,1)S(1)} %get-tuple-element.22) | copy-start | bytes 393220
  24.9 6.0 %collective-permute-start.12 = (bf16[256,256]{1,0:T(8,128)(2,1)}, bf16[256,256]{1,0:T(8,128)(2,1)S(1)}, u32[]{:S(2)}, u32[]{:S(2)}) collective-permute-start(bf16[256,256]{1,0:T(8,128)(2,1)} %get-tuple-element.26), channel_id=1, source_target_pairs={{0,2},{2,0},{1,3},{3,1},{4,6},{6,4},{5,7},{7,5},{8,10},{10,8},{9,1... | collective-permute-start | bytes 393224 | tf_op jit(solution)/shard_map/ppermute | solution.py:229
  26.7 4.2 %collective-permute-start.10 = (bf16[256,256]{1,0:T(8,128)(2,1)}, bf16[256,256]{1,0:T(8,128)(2,1)}, u32[]{:S(2)}, u32[]{:S(2)}) collective-permute-start(bf16[256,256]{1,0:T(8,128)(2,1)} %collective-permute-done.9.refs_5_), channel_id=1, source_target_pairs={{0,1},{1,0},{2,3},{3,2},{4,5},{5,4},{6,7},{7,6},{8,9},{9,8},{10,11... | collective-permute-start | bytes 393224 | tf_op jit(solution)/shard_map/ppermute | solution.py:72
  26.7 5.2 %copy-start.3 = (bf16[256,256]{1,0:T(8,128)(2,1)S(1)}, bf16[256,256]{1,0:T(8,128)(2,1)}, u32[]{:S(2)}) copy-start(bf16[256,256]{1,0:T(8,128)(2,1)} %copy-done.2) | copy-start | bytes 393220
  30.9 1.9 %collective-permute-start.13 = (bf16[256,256]{1,0:T(8,128)(2,1)S(1)}, bf16[256,256]{1,0:T(8,128)(2,1)S(1)}, u32[]{:S(2)}, u32[]{:S(2)}) collective-permute-start(bf16[256,256]{1,0:T(8,128)(2,1)S(1)} %collective-permute-done.12.refs_5_), channel_id=1, source_target_pairs={{0,1},{1,0},{2,3},{3,2},{4,5},{5,4},{6,7},{7,6},{8,9},{9,8},{10,11... | collective-permute-start | bytes 393224 | tf_op jit(solution)/shard_map/ppermute | solution.py:72
  32.5 9.9 %collective-permute-start.11 = (bf16[256,256]{1,0:T(8,128)(2,1)}, bf16[256,256]{1,0:T(8,128)(2,1)}, u32[]{:S(2)}, u32[]{:S(2)}) collective-permute-start(bf16[256,256]{1,0:T(8,128)(2,1)} %broadcast_select_fusion.1), channel_id=1, source_target_pairs={{0,8},{1,12},{2,1},{3,5},{4,11},{5,15},{6,2},{7,6},{8,9},{9,13},{1... | collective-permute-start | bytes 393224 | tf_op jit(solution)/shard_map/ppermute | solution.py:255
  32.8 9.6 %collective-permute-start.14 = (bf16[256,256]{1,0:T(8,128)(2,1)S(1)}, bf16[256,256]{1,0:T(8,128)(2,1)S(1)}, u32[]{:S(2)}, u32[]{:S(2)}) collective-permute-start(bf16[256,256]{1,0:T(8,128)(2,1)S(1)} %broadcast_select_fusion), channel_id=1, source_target_pairs={{0,1},{1,5},{2,8},{3,12},{4,2},{5,6},{6,11},{7,15},{8,0},{9,4},{10... | collective-permute-start | bytes 393224 | tf_op jit(solution)/shard_map/ppermute | solution.py:255
  43.4 1.3 %collective-permute-start.15 = (bf16[256,128]{1,0:T(8,128)(2,1)S(1)}, bf16[256,128]{1,0:T(8,128)(2,1)S(1)}, u32[]{:S(2)}, u32[]{:S(2)}) collective-permute-start(bf16[256,128]{1,0:T(8,128)(2,1)S(1)} %broadcast_select_fusion.2), channel_id=1, source_target_pairs={{0,1},{1,0},{2,3},{3,2},{4,5},{5,4},{6,7},{7,6},{8,9},{9,8},{10,11... | collective-permute-start | bytes 196616 | tf_op jit(solution)/shard_map/ppermute | solution.py:72

commit v3 on v2

--- a/solution.py
+++ b/solution.py
@@ -34,6 +34,33 @@
 
     def landing_core(self, segment, half, slot):
         return (slot + half + segment + 1) % 2
+
+    def turned(self, z, turn):
+        return lax.bitwise_xor(z, turn)
+
+    def trade_pairs(self, turn):
+        pairs = []
+        for z in range(self.count):
+            for s in range(self.sections):
+                to = (z ^ turn, s)
+                if turn == self.count - 1 and s < 2 <= self.sections:
+                    to = (z, 1) if s == 0 else (z ^ turn, 0)
+                pairs.append((z * self.sections + s, to[0] * self.sections + to[1]))
+        return pairs
+
+    def leave_groups(self, early, index):
+        groups = []
+        for stage in reversed(range(self.sections)):
+            half = int((stage == self.sections - 1) != early)
+            sends = self.transfers(stage, half, index)
+            for known, members in groups:
+                if not set(known.values()) & set(sends.values()):
+                    known.update(sends)
+                    members.append((stage, half))
+                    break
+            else:
+                groups.append((sends, [(stage, half)]))
+        return groups
 
     def transfers(self, stage, half, index):
         sends = {}
@@ -72,14 +99,15 @@
     return lax.ppermute(block, "chan", [(0, 1), (1, 0)])
 
 
-def section_kernel(stage, half, plan, lags, n_in, last, *refs):
-    own_pack, other_pack, res_ref, own_skip, other_skip = refs[:5]
-    inputs, refs = refs[5 : 5 + n_in], refs[5 + n_in :]
+def section_kernel(stage, half, plan, lags, n_in, n_earlier, last, *refs):
+    own_conv, other_conv, own_bias, other_bias, res_ref, own_skip, other_skip = refs[:7]
+    inputs, refs = refs[7 : 7 + n_in], refs[7 + n_in :]
     layers, depth = res_ref.shape[:2]
     width = depth // 2
     heads = ()
     if half:
         heads, refs = refs[:layers], refs[layers:]
+    earlier, refs = refs[:n_earlier], refs[n_earlier:]
     skip_outs, refs = refs[: plan.blocks], refs[plan.blocks :]
     if not last:
         stream_out, refs = refs[0], refs[1:]
@@ -91,6 +119,13 @@
     own_rows = pl.ds(pl.multiple_of(core * width, width), width)
     other_rows = pl.ds(pl.multiple_of((1 - core) * width, width), width)
 
+    if earlier:
+
+        @pl.when(lax.axis_index("segment") != stage)
+        def _():
+            for block, out in zip(earlier, skip_outs):
+                out[...] = block[...]
+
     @pl.when(lax.axis_index("segment") == stage)
     def _():
         for layer in range(layers):
@@ -101,7 +136,7 @@
             per_half = plan.count // 2
             for side, blocks in ((own_rows, inputs[: n_in // 2]), (other_rows, inputs[n_in // 2 :])):
                 for turn, block in enumerate(blocks):
-                    t = lax.rem(place - turn + plan.count, plan.count)
+                    t = plan.turned(place, turn)
 
                     @pl.when(t // per_half == half)
                     def _(t=t, block=block, side=side):
@@ -124,10 +159,11 @@
                 past = now_buf[pl.ds(row, ROW_TILE), :]
                 now = now_buf[pl.ds(lag + row, ROW_TILE), :]
                 parts = []
-                for pack in (own_pack, other_pack):
-                    pre = jnp.dot(past, pack[layer, :depth], preferred_element_type=jnp.float32)
-                    pre += jnp.dot(now, pack[layer, depth : 2 * depth], preferred_element_type=jnp.float32)
-                    pre += pack[layer, 2 * depth : 2 * depth + 1].astype(jnp.float32)
+                for conv, bias in ((own_conv, own_bias), (other_conv, other_bias)):
+                    shift = jnp.concatenate([bias[layer, 0:1, :], bias[layer, 1:2, :]], 1).astype(jnp.float32)
+                    pre = jnp.dot(past, conv[layer, :depth], preferred_element_type=jnp.float32)
+                    pre += jnp.dot(now, conv[layer, depth:], preferred_element_type=jnp.float32)
+                    pre += shift
                     gate = 0.5 * jnp.tanh(0.5 * pre[:, width:]) + 0.5
                     parts.append((jnp.tanh(pre[:, :width]) * gate).astype(jnp.bfloat16))
                 unit = jnp.concatenate(parts, 1)
@@ -168,8 +204,8 @@
             out[:, other_rows] = acc[:, width:].astype(out.dtype)
 
 
-def run_section(stage, half, plan, lags, weights, inputs, heads, rows):
-    res_weight = weights[2]
+def run_section(stage, half, plan, lags, weights, inputs, heads, earlier, rows):
+    res_weight = weights[4]
     layers, depth = res_weight.shape[:2]
     total = rows * plan.count // 2
     last = stage == plan.sections - 1
@@ -182,13 +218,14 @@
     scratch += [pltpu.VMEM((layers, total, depth), jnp.bfloat16), pltpu.VMEM((total, depth), jnp.bfloat16)]
     held = 2 * depth * (sum(lags) * 3 + 13 * total)
     got = pl.pallas_call(
-        functools.partial(section_kernel, stage, half, plan, lags, len(inputs), last),
+        functools.partial(section_kernel, stage, half, plan, lags, len(inputs), len(earlier), last),
         out_shape=outs,
-        in_specs=[VMEM] * (len(weights) + len(inputs) + len(heads)),
+        in_specs=[VMEM] * (len(weights) + len(inputs) + len(heads) + len(earlier)),
         out_specs=[VMEM] * len(outs),
         scratch_shapes=scratch,
         compiler_params=pltpu.CompilerParams(vmem_limit_bytes=held + (12 << 20)),
-    )(*weights, *inputs, *heads)
+        cost_estimate=pl.CostEstimate(flops=16 * total * depth * depth * layers, bytes_accessed=1 << 20, transcendentals=0),
+    )(*weights, *inputs, *heads, *earlier)
     blocks, got = got[: plan.blocks], got[plan.blocks :]
     stream = None
     if not last:
@@ -204,68 +241,103 @@
     lags = [rows // 8, rows, rows * max(1, count // 8), rows * max(1, count // 2)]
     plan = Plan(count, sections, record_count)
 
-    own_blocks = []
-    for turn in range(count):
-        block = lax.dynamic_index_in_dim(records, plan.record_at(lax.rem(place + turn, count)), 0, keepdims=False)
-        if turn:
-            block = lax.ppermute(block, "tm", [(i, (i + turn) % count) for i in range(count)])
-        own_blocks.append(block)
-    inputs = own_blocks + [swap_cores(block) for block in own_blocks]
-
-    bias_rows = jnp.pad(conv_bias.reshape(layers, 1, 2 * width), ((0, 0), (0, 15), (0, 0)))
-    own_pack = jnp.concatenate([conv_weight.reshape(layers, taps, 2 * width), bias_rows], 1)
-    weights = (own_pack, swap_cores(own_pack), res_weight, skip_weight, swap_cores(skip_weight))
+    blocks = [
+        lax.dynamic_index_in_dim(records, plan.record_at(plan.turned(place, turn)), 0, keepdims=False)
+        for turn in range(count)
+    ]
+    for turn in range(1, count):
+        blocks[turn] = lax.ppermute(blocks[turn], ("tm", "segment"), plan.trade_pairs(turn))
+    conv = conv_weight.reshape(layers, taps, 2 * width)
+    weights = (conv, swap_cores(conv), conv_bias, swap_cores(conv_bias), res_weight, skip_weight, swap_cores(skip_weight))
+    inputs = blocks + [swap_cores(block) for block in blocks]
 
     skips = {}
     fed = [inputs, inputs]
     for stage in range(sections):
         heads, crossed = (), []
         for half in range(2):
+            earlier = []
+            if stage == sections - 1:
+                for index in range(plan.blocks):
+                    members = plan.leave_groups(half == 0, index)[0][1][1:]
+                    if members:
+                        block = skips[members[0]][index]
+                        for member in members[1:]:
+                            block = jnp.where(segment == member[0], skips[member][index], block)
+                        earlier.append(block)
+                earlier = earlier if len(earlier) == plan.blocks else []
+            came = fed[half]
+            if stage:
+                if half:
+                    came, heads = lax.optimization_barrier((came, heads))
+                else:
+                    came, stream = lax.optimization_barrier((came, stream))
+                came = [came, swap_cores(came)]
             skips[stage, half], stream, carried = run_section(
-                stage, half, plan, lags, weights, fed[half], heads, rows
+                stage, half, plan, lags, weights, came, heads, earlier, rows
             )
             heads = carried
             if stage < sections - 1:
                 moved = lax.ppermute(stream, "segment", [(i, (i + 1) % sections) for i in range(sections)])
-                crossed.append([moved, swap_cores(moved)])
+                crossed.append(moved)
         fed = crossed
 
-    total = jnp.zeros((rows, 2 * width), jnp.float32)
+    arrived, holds = [], []
     spot = (place * sections + segment) * 2 + core
+
+    def number(device):
+        return (device[0] * sections + device[1]) * 2 + device[2]
+
     for early in (True, False):
         for index in range(plan.blocks):
-            groups = []
-            for stage in reversed(range(sections)):
-                half = int((stage == sections - 1) != early)
-                sends = plan.transfers(stage, half, index)
-                for group in groups:
-                    if not set(group[0].values()) & set(sends.values()):
-                        group[0].update(sends)
-                        group[1].append((stage, half))
-                        break
-                else:
-                    groups.append((sends, [(stage, half)]))
-            for sends, members in groups:
-                payload = None
-                for stage, half in members:
-                    block = skips[stage, half][index]
-                    payload = block if payload is None else jnp.where(segment == stage, block, payload)
+            for sends, members in plan.leave_groups(early, index):
+                payload = skips[members[0]][index]
+                if members[0][0] != sections - 1:
+                    for member in members[1:]:
+                        payload = jnp.where(segment == member[0], skips[member][index], payload)
                 pairs = complete(sends, (count, sections, 2))
-                number = lambda d: (d[0] * sections + d[1]) * 2 + d[2]
-                got = lax.ppermute(
-                    payload, ("tm", "segment", "chan"), sorted((number(a), number(b)) for a, b in pairs.items())
+                arrived.append(
+                    lax.ppermute(
+                        payload, ("tm", "segment", "chan"), sorted((number(a), number(b)) for a, b in pairs.items())
+                    )
                 )
-                valid = functools.reduce(jnp.logical_or, [spot == number(d) for d in sends.values()])
-                if len(sends) == 2 * count * sections:
-                    total = total + got.astype(jnp.float32)
-                else:
-                    total = total + jnp.where(valid, got.astype(jnp.float32), 0.0)
-    block = total.astype(jnp.bfloat16)
-    low, high = block[:, :width], block[:, width:]
-    kept = jnp.where(core == 0, low, high)
-    given = swap_cores(jnp.where(core == 0, high, low))
-    mine = lax.rem(core + place // (count // 2) + segment + 1, 2)
-    return jnp.stack([jnp.where(mine == slot, kept, given) for slot in range(plan.share)])
+                valid = jnp.bool_(True)
+                if len(sends) < 2 * count * sections:
+                    valid = functools.reduce(jnp.logical_or, [spot == number(d) for d in sends.values()])
+                holds.append(valid.astype(jnp.int32))
+    kept, given = pl.pallas_call(
+        functools.partial(sum_kernel, len(arrived)),
+        out_shape=[jax.ShapeDtypeStruct((rows, width), jnp.bfloat16)] * 2,
+        in_specs=[pl.BlockSpec(memory_space=pltpu.SMEM)] + [VMEM] * len(arrived),
+        out_specs=[VMEM] * 2,
+        compiler_params=pltpu.CompilerParams(vmem_limit_bytes=4 << 20),
+    )(jnp.stack(holds), *arrived)
+    return pl.pallas_call(
+        functools.partial(place_kernel, plan),
+        out_shape=jax.ShapeDtypeStruct((plan.share, rows, width), jnp.bfloat16),
+        in_specs=[VMEM] * 2,
+        out_specs=VMEM,
+        compiler_params=pltpu.CompilerParams(vmem_limit_bytes=4 << 20),
+    )(kept, swap_cores(given))
+
+
+def sum_kernel(count, holds, *refs):
+    arrived, (kept, given) = refs[:count], refs[count:]
+    width = kept.shape[1]
+    core = lax.axis_index("chan")
+    for side, out in ((core, kept), (1 - core, given)):
+        lanes = pl.ds(pl.multiple_of(side * width, width), width)
+        total = jnp.zeros(out.shape, jnp.float32)
+        for index, block in enumerate(arrived):
+            total += jnp.where(holds[index] == 1, block[:, lanes].astype(jnp.float32), 0.0)
+        out[...] = total.astype(out.dtype)
+
+
+def place_kernel(plan, kept, given, out):
+    half = lax.axis_index("tm") // (plan.count // 2)
+    mine = lax.rem(lax.axis_index("chan") + half + lax.axis_index("segment") + 1, 2)
+    for slot in range(plan.share):
+        out[slot] = jnp.where(mine == slot, kept[...], given[...])
 
 
 def solution(mesh):

time: 45.8 us -> 44.1 us (0.963)
  other arithmetic: 2.39 us -> 0 us
  starting transfers between devices: 9.59 us -> 11.4 us
  local copies, waits for them, and re-layouts: 3.42 us -> 1.83 us
  waiting for transfers between devices: 22.7 us -> 23.8 us
    pallas_call x4, Pallas kernels: 7.15 us -> 5.51 us  [run_section(): pl.pallas_call(functools.partial(section_kernel, stage, half, plan, lags,...]
    ppermute x2, waiting for transfers between devices: 5.97 us -> 7.54 us  [shards(): lax.ppermute(stream, 'segment', [(i, (i + 1) % sections) for i in range(s...]
    ppermute x3, waiting for transfers between devices: 6.96 us -> 5.53 us  [shards(): lax.ppermute(blocks[turn], ('tm', 'segment'), plan.trade_pairs(turn))]
    ppermute x3, starting transfers between devices: 5.74 us -> 7.14 us  [shards(): lax.ppermute(blocks[turn], ('tm', 'segment'), plan.trade_pairs(turn))]
    pallas_call x0 -> x2, Pallas kernels: none -> 1.28 us  [the longest x1 0.68 us: shards(): pl.pallas_call(functools.partial(place_kernel, plan), out_shape=jax.Shape...]
    ppermute x9 -> x10, waiting for transfers between devices: 2.12 us -> 3.21 us  [swap_cores(): return lax.ppermute(block, 'chan', [(0, 1), (1, 0)])]
    unnamed x10 -> x8, local copies, waits for them, and re-layouts: 0.98 us -> 0.02 us
    convert_element_type x1 -> x0, other arithmetic: 0.94 us -> none  [shards(): block = total.astype(jnp.bfloat16)]
  transfers between devices with their start and end apart: 16 -> 17, of which waited for: 9 -> 9; matrix products, arithmetic and copies ran while one was open for 2% -> 0% of each run, Pallas kernels for 10% -> 6%
where the time goes in v3:
time: 44.1 us; the launch traced here: 43.9 us
  waiting for transfers between devices  23.8 us (54%)
  starting transfers between devices  11.4 us (26%)
  Pallas kernels  6.8 us (15%)
  local copies, waits for them, and re-layouts  1.83 us (4%)
    ppermute x2, waiting for transfers between devices, shards(): lax.ppermute(stream, 'segment', [(i, (i + 1) % sections) for i in range(s...  7.54 us
    ppermute x2, waiting for transfers between devices, shards(): lax.ppermute(payload, ('tm', 'segment', 'chan'), sorted(((number(a), numb...  7.52 us
    ppermute x3, starting transfers between devices, shards(): lax.ppermute(blocks[turn], ('tm', 'segment'), plan.trade_pairs(turn))  7.14 us
    ppermute x3, waiting for transfers between devices, shards(): lax.ppermute(blocks[turn], ('tm', 'segment'), plan.trade_pairs(turn))  5.53 us
    pallas_call x4, Pallas kernels, run_section(): pl.pallas_call(functools.partial(section_kernel, stage, half, plan, lags,...  5.51 us
    ppermute x10, waiting for transfers between devices, swap_cores(): return lax.ppermute(block, 'chan', [(0, 1), (1, 0)])  3.21 us
    ppermute x2, starting transfers between devices, shards(): lax.ppermute(payload, ('tm', 'segment', 'chan'), sorted(((number(a), numb...  2.72 us
    reshape x1, local copies, waits for them, and re-layouts, shards(): conv = conv_weight.reshape(layers, taps, 2 * width)  1.79 us
  transfers between devices with their start and end apart: 17, of which 9 were waited for; matrix products, arithmetic and copies ran while one was open for 0% of the time, Pallas kernels for 6%

profile of v3, /device:TPU:0, one launch (start us, length us, event | category | flops | bytes accessed | tf_op | source)
XLA Modules:
  0.0 43.9 jit_solution(1414519328029743539)
XLA Ops:
  0.0 0.0 copy-start.1
  0.0 0.0 copy-start.3
  0.0 1.8 %reshape.3.refs_0_ = bf16[4,512,256]{2,1,0:T(8,128)(2,1)S(1)} reshape(bf16[4,512,2,128]{3,2,1,0:T(2,128)(2,1)} %param.6) | data formatting | bytes 2097152 | tf_op jit(solution)/shard_map/reshape | solution.py:250
  1.8 0.0 copy-start
  1.8 0.5 %collective-permute-start = (bf16[4,512,256]{2,1,0:T(8,128)(2,1)S(1)}, bf16[4,512,256]{2,1,0:T(8,128)(2,1)S(1)}, u32[]{:S(2)}, u32[]{:S(2)}) collective-permute-start(bf16[4,512,256]{2,1,0:T(8,128)(2,1)S(1)} %reshape.3.refs_0_), channel_id=1, source_target_pairs={{0,1},{1,0},{2,3},{3,2},{4,5},{5,4},{6,7},{7,6},{8,9},{9,8},{10,11... | collective-permute-start | bytes 3145736 | tf_op jit(solution)/shard_map/ppermute | solution.py:99
  2.3 0.0 copy-done.1
  2.3 0.1 collective-permute-start.2
  2.4 0.0 copy-done.3
  2.4 0.0 copy-start.2
  2.5 3.1 %collective-permute-start.3 = (bf16[256,128]{1,0:T(8,128)(2,1)S(1)}, bf16[256,128]{1,0:T(8,128)(2,1)S(1)}, u32[]{:S(2)}, u32[]{:S(2)}) collective-permute-start(bf16[256,128]{1,0:T(8,128)(2,1)S(1)} %get-tuple-element.48), channel_id=1, source_target_pairs={{0,4},{2,6},{4,0},{6,2},{8,12},{10,14},{12,8},{14,10},{1,5},{3,7},... | collective-permute-start | bytes 196616 | tf_op jit(solution)/shard_map/ppermute | solution.py:249
  5.5 0.0 copy-done.2
  5.5 0.0 collective-permute-start.1
  5.5 2.6 %collective-permute-start.4 = (bf16[256,128]{1,0:T(8,128)(2,1)S(1)}, bf16[256,128]{1,0:T(8,128)(2,1)S(1)}, u32[]{:S(2)}, u32[]{:S(2)}) collective-permute-start(bf16[256,128]{1,0:T(8,128)(2,1)S(1)} %get-tuple-element.50), channel_id=1, source_target_pairs={{0,8},{2,10},{4,12},{6,14},{8,0},{10,2},{12,4},{14,6},{1,9},{3,11}... | collective-permute-start | bytes 196616 | tf_op jit(solution)/shard_map/ppermute | solution.py:249
  8.1 0.0 collective-permute-done.1.refs_3_
  8.1 1.5 %collective-permute-start.5 = (bf16[256,128]{1,0:T(8,128)(2,1)S(1)}, bf16[256,128]{1,0:T(8,128)(2,1)S(1)}, u32[]{:S(2)}, u32[]{:S(2)}) collective-permute-start(bf16[256,128]{1,0:T(8,128)(2,1)S(1)} %get-tuple-element.47), channel_id=1, source_target_pairs={{0,2},{2,12},{4,6},{6,8},{8,10},{10,4},{12,14},{14,0},{1,3},{3,13}... | collective-permute-start | bytes 196616 | tf_op jit(solution)/shard_map/ppermute | solution.py:249
  9.6 0.0 collective-permute-done.3.refs_8_
  9.6 0.0 collective-permute-start.6
  9.6 2.7 %collective-permute-done.4.refs_9_ = bf16[256,128]{1,0:T(8,128)(2,1)S(1)} collective-permute-done((bf16[256,128]{1,0:T(8,128)(2,1)S(1)}, bf16[256,128]{1,0:T(8,128)(2,1)S(1)}, u32[]{:S(2)}, u32[]{:S(2)}) %collective-permute-start.4) | collective-permute-done | bytes 65568 | tf_op jit(solution)/shard_map/ppermute | solution.py:249
  12.3 0.0 collective-permute-start.7
  12.3 2.8 %collective-permute-done.5.refs_10_ = bf16[256,128]{1,0:T(8,128)(2,1)S(1)} collective-permute-done((bf16[256,128]{1,0:T(8,128)(2,1)S(1)}, bf16[256,128]{1,0:T(8,128)(2,1)S(1)}, u32[]{:S(2)}, u32[]{:S(2)}) %collective-permute-start.5) | collective-permute-done | bytes 65568 | tf_op jit(solution)/shard_map/ppermute | solution.py:249
  15.1 0.0 collective-permute-start.8
  15.1 0.0 collective-permute-done.6.refs_11_
  15.1 0.5 %collective-permute-start.9 = (bf16[256,128]{1,0:T(8,128)(2,1)S(1)}, bf16[256,128]{1,0:T(8,128)(2,1)S(1)}, u32[]{:S(2)}, u32[]{:S(2)}) collective-permute-start(bf16[256,128]{1,0:T(8,128)(2,1)S(1)} %collective-permute-done.5.refs_10_), channel_id=1, source_target_pairs={{0,1},{1,0},{2,3},{3,2},{4,5},{5,4},{6,7},{7,6},{8,9},{9,8},{10,11... | collective-permute-start | bytes 196616 | tf_op jit(solution)/shard_map/ppermute | solution.py:99
  15.7 0.0 collective-permute-done.7.refs_12_
  15.7 0.7 %collective-permute-done.8.refs_13_ = bf16[256,128]{1,0:T(8,128)(2,1)S(1)} collective-permute-done((bf16[256,128]{1,0:T(8,128)(2,1)S(1)}, bf16[256,128]{1,0:T(8,128)(2,1)S(1)}, u32[]{:S(2)}, u32[]{:S(2)}) %collective-permute-start.8) | collective-permute-done | bytes 65568 | tf_op jit(solution)/shard_map/ppermute | solution.py:99
  16.4 0.2 collective-permute-done.9.refs_14_
  16.6 0.0 collective-permute-done.2.refs_6_
  16.6 0.0 collective-permute-done.refs_1_
  16.6 0.0 copy-done
  16.6 2.7 %shard_map.55 = (bf16[256,256]{1,0:T(8,128)(2,1)S(1)}, bf16[256,256]{1,0:T(8,128)(2,1)S(1)}, bf16[32,256]{1,0:T(8,128)(2,1)S(1)}, bf16[256,256]{1,0:T(8,128)(2,1...) custom-call(bf16[4,512,256]{2,1,0:T(8,128)(2,1)S(1)} %reshape.3.refs_0_, ...), custom_call_target="tpu_custom_call" | custom-call | flops 2147483648 | bytes 1048576 | tf_op jit(solution)/shard_map/pallas_call | solution.py:220
  19.3 0.1 collective-permute-start.10
  19.4 2.7 %shard_map.56 = (bf16[256,256]{1,0:T(8,128)(2,1)S(1)}, bf16[256,256]{1,0:T(8,128)(2,1)S(1)}) custom-call(bf16[4,512,256]{2,1,0:T(8,128)(2,1)S(1)} %reshape.3.refs_0_, bf16[4,512,256]{2,1,0:T(8,128)(2,1)S(1)} %collective-permute-done.refs_1_, bf16[4,2,128]{2,1,0:T(2,128)(2,1)S(1)} %copy-done.2, bf16[4,2,128]{2,1,0:T(2,128)(2,1)S(1)} %collective-permute-done.1.refs_3_, ...), custom_call_target="tpu_custom_call" | custom-call | flops 2147483648 | bytes 1048576 | tf_op jit(solution)/shard_map/pallas_call | solution.py:220
  22.1 3.0 %collective-permute-done.10.refs_7_ = bf16[256,256]{1,0:T(8,128)(2,1)S(1)} collective-permute-done((bf16[256,256]{1,0:T(8,128)(2,1)S(1)}, bf16[256,256]{1,0:T(8,128)(2,1)S(1)}, u32[]{:S(2)}, u32[]{:S(2)}) %collective-permute-start.10) | collective-permute-done | bytes 131104 | tf_op jit(solution)/shard_map/ppermute | solution.py:281
  25.1 0.0 collective-permute-start.11
  25.1 0.3 collective-permute-start.13
  25.4 1.1 %collective-permute-done.11.refs_8_ = bf16[256,256]{1,0:T(8,128)(2,1)S(1)} collective-permute-done((bf16[256,256]{1,0:T(8,128)(2,1)S(1)}, bf16[256,256]{1,0:T(8,128)(2,1)S(1)}, u32[]{:S(2)}, u32[]{:S(2)}) %collective-permute-start.11) | collective-permute-done | bytes 131104 | tf_op jit(solution)/shard_map/ppermute | solution.py:99
  26.5 4.5 %collective-permute-done.13.refs_7_ = bf16[256,256]{1,0:T(8,128)(2,1)S(1)} collective-permute-done((bf16[256,256]{1,0:T(8,128)(2,1)S(1)}, bf16[256,256]{1,0:T(8,128)(2,1)S(1)}, u32[]{:S(2)}, u32[]{:S(2)}) %collective-permute-start.13) | collective-permute-done | bytes 131104 | tf_op jit(solution)/shard_map/ppermute | solution.py:281
  31.1 0.0 collective-permute-start.14
  31.1 2.7 %collective-permute-start.12 = (bf16[256,256]{1,0:T(8,128)(2,1)S(1)}, bf16[256,256]{1,0:T(8,128)(2,1)S(1)}, u32[]{:S(2)}, u32[]{:S(2)}) collective-permute-start(bf16[256,256]{1,0:T(8,128)(2,1)S(1)} %get-tuple-element.34), channel_id=1, source_target_pairs={{0,8},{1,12},{2,1},{3,5},{4,11},{5,15},{6,2},{7,6},{8,9},{9,13},{1... | collective-permute-start | bytes 393224 | tf_op jit(solution)/shard_map/ppermute | solution.py:300
  33.7 0.0 collective-permute-done.14.refs_8_
  33.7 0.1 collective-permute-start.15
  33.8 7.5 %collective-permute-done.12.refs_0_ = bf16[256,256]{1,0:T(8,128)(2,1)S(1)} collective-permute-done((bf16[256,256]{1,0:T(8,128)(2,1)S(1)}, bf16[256,256]{1,0:T(8,128)(2,1)S(1)}, u32[]{:S(2)}, u32[]{:S(2)}) %collective-permute-start.12) | collective-permute-done | bytes 131104 | tf_op jit(solution)/shard_map/ppermute | solution.py:300
  41.3 0.0 collective-permute-done.15.refs_1_
  41.3 0.6 %shard_map.59 = (bf16[256,128]{1,0:T(8,128)(2,1)S(1)}, bf16[256,128]{1,0:T(8,128)(2,1)S(1)}) custom-call(s32[2]{0:T(128)S(1)} %broadcast_1_holds.2.holds, bf16[256,256]{1,0:T(8,128)(2,1)S(1)} %collective-permute-done.12.refs_0_, bf16[256,256]{1,0:T(8,128)(2,1)S(1)} %collective-permute-done.15.refs_1_), custom_call_target="tpu_custom_call" | custom-call | tf_op jit(solution)/shard_map/pallas_call | solution.py:308
  41.9 0.1 collective-permute-start.16
  42.0 1.2 %collective-permute-done.16.given = bf16[256,128]{1,0:T(8,128)(2,1)S(1)} collective-permute-done((bf16[256,128]{1,0:T(8,128)(2,1)S(1)}, bf16[256,128]{1,0:T(8,128)(2,1)S(1)}, u32[]{:S(2)}, u32[]{:S(2)}) %collective-permute-start.16) | collective-permute-done | bytes 65568 | tf_op jit(solution)/shard_map/ppermute | solution.py:99
  43.3 0.7 %shard_map.60 = bf16[2,256,128]{2,1,0:T(8,128)(2,1)} custom-call(bf16[256,128]{1,0:T(8,128)(2,1)S(1)} %get-tuple-element.45.kept, bf16[256,128]{1,0:T(8,128)(2,1)S(1)} %collective-permute-done.16.given), custom_call_target="tpu_custom_call" | custom-call | tf_op jit(solution)/shard_map/pallas_call | solution.py:315
  (4 shorter events, 0.0 us)
Async XLA Ops:
  0.0 2.3 %copy-start.1 = (bf16[4,256,128]{2,1,0:T(8,128)(2,1)S(1)}, bf16[4,256,128]{2,1,0:T(8,128)(2,1)}, u32[]{:S(2)}) copy-start(bf16[4,256,128]{2,1,0:T(8,128)(2,1)} %refs_5_.7) | copy-start | bytes 786436
  0.0 2.4 %copy-start.3 = (bf16[4,256,128]{2,1,0:T(8,128)(2,1)S(1)}, bf16[4,256,128]{2,1,0:T(8,128)(2,1)}, u32[]{:S(2)}) copy-start(bf16[4,256,128]{2,1,0:T(8,128)(2,1)} %param.5) | copy-start | bytes 786436
  1.8 14.8 %copy-start = (bf16[4,256,256]{2,1,0:T(8,128)(2,1)S(1)}, bf16[4,256,256]{2,1,0:T(8,128)(2,1)}, u32[]{:S(2)}) copy-start(bf16[4,256,256]{2,1,0:T(8,128)(2,1)} %refs_4_.7) | copy-start | bytes 1572868
  1.8 14.7 %collective-permute-start = (bf16[4,512,256]{2,1,0:T(8,128)(2,1)S(1)}, bf16[4,512,256]{2,1,0:T(8,128)(2,1)S(1)}, u32[]{:S(2)}, u32[]{:S(2)}) collective-permute-start(bf16[4,512,256]{2,1,0:T(8,128)(2,1)S(1)} %reshape.3.refs_0_), channel_id=1, source_target_pairs={{0,1},{1,0},{2,3},{3,2},{4,5},{5,4},{6,7},{7,6},{8,9},{9,8},{10,11... | collective-permute-start | bytes 3145736 | tf_op jit(solution)/shard_map/ppermute | solution.py:99
  2.3 14.2 %collective-permute-start.2 = (bf16[4,256,128]{2,1,0:T(8,128)(2,1)S(1)}, bf16[4,256,128]{2,1,0:T(8,128)(2,1)S(1)}, u32[]{:S(2)}, u32[]{:S(2)}) collective-permute-start(bf16[4,256,128]{2,1,0:T(8,128)(2,1)S(1)} %copy-done.1), channel_id=1, source_target_pairs={{0,1},{1,0},{2,3},{3,2},{4,5},{5,4},{6,7},{7,6},{8,9},{9,8},{10,11... | collective-permute-start | bytes 786440 | tf_op jit(solution)/shard_map/ppermute | solution.py:99
  2.4 3.1 %copy-start.2 = (bf16[4,2,128]{2,1,0:T(2,128)(2,1)S(1)}, bf16[4,2,128]{2,1,0:T(2,128)(2,1)}, u32[]{:S(2)}) copy-start(bf16[4,2,128]{2,1,0:T(2,128)(2,1)} %refs_2_.7) | copy-start | bytes 6148
  2.5 7.2 %collective-permute-start.3 = (bf16[256,128]{1,0:T(8,128)(2,1)S(1)}, bf16[256,128]{1,0:T(8,128)(2,1)S(1)}, u32[]{:S(2)}, u32[]{:S(2)}) collective-permute-start(bf16[256,128]{1,0:T(8,128)(2,1)S(1)} %get-tuple-element.48), channel_id=1, source_target_pairs={{0,4},{2,6},{4,0},{6,2},{8,12},{10,14},{12,8},{14,10},{1,5},{3,7},... | collective-permute-start | bytes 196616 | tf_op jit(solution)/shard_map/ppermute | solution.py:249
  5.5 2.6 %collective-permute-start.1 = (bf16[4,2,128]{2,1,0:T(2,128)(2,1)S(1)}, bf16[4,2,128]{2,1,0:T(2,128)(2,1)S(1)}, u32[]{:S(2)}, u32[]{:S(2)}) collective-permute-start(bf16[4,2,128]{2,1,0:T(2,128)(2,1)S(1)} %copy-done.2), channel_id=1, source_target_pairs={{0,1},{1,0},{2,3},{3,2},{4,5},{5,4},{6,7},{7,6},{8,9},{9,8},{10,11... | collective-permute-start | bytes 6152 | tf_op jit(solution)/shard_map/ppermute | solution.py:99
  5.5 6.8 %collective-permute-start.4 = (bf16[256,128]{1,0:T(8,128)(2,1)S(1)}, bf16[256,128]{1,0:T(8,128)(2,1)S(1)}, u32[]{:S(2)}, u32[]{:S(2)}) collective-permute-start(bf16[256,128]{1,0:T(8,128)(2,1)S(1)} %get-tuple-element.50), channel_id=1, source_target_pairs={{0,8},{2,10},{4,12},{6,14},{8,0},{10,2},{12,4},{14,6},{1,9},{3,11}... | collective-permute-start | bytes 196616 | tf_op jit(solution)/shard_map/ppermute | solution.py:249
  8.1 7.0 %collective-permute-start.5 = (bf16[256,128]{1,0:T(8,128)(2,1)S(1)}, bf16[256,128]{1,0:T(8,128)(2,1)S(1)}, u32[]{:S(2)}, u32[]{:S(2)}) collective-permute-start(bf16[256,128]{1,0:T(8,128)(2,1)S(1)} %get-tuple-element.47), channel_id=1, source_target_pairs={{0,2},{2,12},{4,6},{6,8},{8,10},{10,4},{12,14},{14,0},{1,3},{3,13}... | collective-permute-start | bytes 196616 | tf_op jit(solution)/shard_map/ppermute | solution.py:249
  9.6 5.5 %collective-permute-start.6 = (bf16[256,128]{1,0:T(8,128)(2,1)S(1)}, bf16[256,128]{1,0:T(8,128)(2,1)S(1)}, u32[]{:S(2)}, u32[]{:S(2)}) collective-permute-start(bf16[256,128]{1,0:T(8,128)(2,1)S(1)} %get-tuple-element.49.refs_7_), channel_id=1, source_target_pairs={{0,1},{1,0},{2,3},{3,2},{4,5},{5,4},{6,7},{7,6},{8,9},{9,8},{10,11... | collective-permute-start | bytes 196616 | tf_op jit(solution)/shard_map/ppermute | solution.py:99
  12.3 3.3 %collective-permute-start.7 = (bf16[256,128]{1,0:T(8,128)(2,1)S(1)}, bf16[256,128]{1,0:T(8,128)(2,1)S(1)}, u32[]{:S(2)}, u32[]{:S(2)}) collective-permute-start(bf16[256,128]{1,0:T(8,128)(2,1)S(1)} %collective-permute-done.3.refs_8_), channel_id=1, source_target_pairs={{0,1},{1,0},{2,3},{3,2},{4,5},{5,4},{6,7},{7,6},{8,9},{9,8},{10,11... | collective-permute-start | bytes 196616 | tf_op jit(solution)/shard_map/ppermute | solution.py:99
  15.1 1.3 %collective-permute-start.8 = (bf16[256,128]{1,0:T(8,128)(2,1)S(1)}, bf16[256,128]{1,0:T(8,128)(2,1)S(1)}, u32[]{:S(2)}, u32[]{:S(2)}) collective-permute-start(bf16[256,128]{1,0:T(8,128)(2,1)S(1)} %collective-permute-done.4.refs_9_), channel_id=1, source_target_pairs={{0,1},{1,0},{2,3},{3,2},{4,5},{5,4},{6,7},{7,6},{8,9},{9,8},{10,11... | collective-permute-start | bytes 196616 | tf_op jit(solution)/shard_map/ppermute | solution.py:99
  15.1 1.4 %collective-permute-start.9 = (bf16[256,128]{1,0:T(8,128)(2,1)S(1)}, bf16[256,128]{1,0:T(8,128)(2,1)S(1)}, u32[]{:S(2)}, u32[]{:S(2)}) collective-permute-start(bf16[256,128]{1,0:T(8,128)(2,1)S(1)} %collective-permute-done.5.refs_10_), channel_id=1, source_target_pairs={{0,1},{1,0},{2,3},{3,2},{4,5},{5,4},{6,7},{7,6},{8,9},{9,8},{10,11... | collective-permute-start | bytes 196616 | tf_op jit(solution)/shard_map/ppermute | solution.py:99
  19.3 5.8 %collective-permute-start.10 = (bf16[256,256]{1,0:T(8,128)(2,1)S(1)}, bf16[256,256]{1,0:T(8,128)(2,1)S(1)}, u32[]{:S(2)}, u32[]{:S(2)}) collective-permute-start(bf16[256,256]{1,0:T(8,128)(2,1)S(1)} %get-tuple-element.26), channel_id=1, source_target_pairs={{0,2},{2,0},{1,3},{3,1},{4,6},{6,4},{5,7},{7,5},{8,10},{10,8},{9,1... | collective-permute-start | bytes 393224 | tf_op jit(solution)/shard_map/ppermute | solution.py:281
  25.1 1.3 %collective-permute-start.11 = (bf16[256,256]{1,0:T(8,128)(2,1)S(1)}, bf16[256,256]{1,0:T(8,128)(2,1)S(1)}, u32[]{:S(2)}, u32[]{:S(2)}) collective-permute-start(bf16[256,256]{1,0:T(8,128)(2,1)S(1)} %collective-permute-done.10.refs_7_), channel_id=1, source_target_pairs={{0,1},{1,0},{2,3},{3,2},{4,5},{5,4},{6,7},{7,6},{8,9},{9,8},{10,11... | collective-permute-start | bytes 393224 | tf_op jit(solution)/shard_map/ppermute | solution.py:99
  25.1 5.9 %collective-permute-start.13 = (bf16[256,256]{1,0:T(8,128)(2,1)S(1)}, bf16[256,256]{1,0:T(8,128)(2,1)S(1)}, u32[]{:S(2)}, u32[]{:S(2)}) collective-permute-start(bf16[256,256]{1,0:T(8,128)(2,1)S(1)} %get-tuple-element.31), channel_id=1, source_target_pairs={{0,2},{2,0},{1,3},{3,1},{4,6},{6,4},{5,7},{7,5},{8,10},{10,8},{9,1... | collective-permute-start | bytes 393224 | tf_op jit(solution)/shard_map/ppermute | solution.py:281
  31.1 2.7 %collective-permute-start.14 = (bf16[256,256]{1,0:T(8,128)(2,1)S(1)}, bf16[256,256]{1,0:T(8,128)(2,1)S(1)}, u32[]{:S(2)}, u32[]{:S(2)}) collective-permute-start(bf16[256,256]{1,0:T(8,128)(2,1)S(1)} %collective-permute-done.13.refs_7_), channel_id=1, source_target_pairs={{0,1},{1,0},{2,3},{3,2},{4,5},{5,4},{6,7},{7,6},{8,9},{9,8},{10,11... | collective-permute-start | bytes 393224 | tf_op jit(solution)/shard_map/ppermute | solution.py:99
  31.1 10.3 %collective-permute-start.12 = (bf16[256,256]{1,0:T(8,128)(2,1)S(1)}, bf16[256,256]{1,0:T(8,128)(2,1)S(1)}, u32[]{:S(2)}, u32[]{:S(2)}) collective-permute-start(bf16[256,256]{1,0:T(8,128)(2,1)S(1)} %get-tuple-element.34), channel_id=1, source_target_pairs={{0,8},{1,12},{2,1},{3,5},{4,11},{5,15},{6,2},{7,6},{8,9},{9,13},{1... | collective-permute-start | bytes 393224 | tf_op jit(solution)/shard_map/ppermute | solution.py:300
  33.7 7.6 %collective-permute-start.15 = (bf16[256,256]{1,0:T(8,128)(2,1)S(1)}, bf16[256,256]{1,0:T(8,128)(2,1)S(1)}, u32[]{:S(2)}, u32[]{:S(2)}) collective-permute-start(bf16[256,256]{1,0:T(8,128)(2,1)S(1)} %shard_map.58), channel_id=1, source_target_pairs={{0,1},{1,5},{2,8},{3,12},{4,2},{5,6},{6,11},{7,15},{8,0},{9,4},{10... | collective-permute-start | bytes 393224 | tf_op jit(solution)/shard_map/ppermute | solution.py:300
  41.9 1.3 %collective-permute-start.16 = (bf16[256,128]{1,0:T(8,128)(2,1)S(1)}, bf16[256,128]{1,0:T(8,128)(2,1)S(1)}, u32[]{:S(2)}, u32[]{:S(2)}) collective-permute-start(bf16[256,128]{1,0:T(8,128)(2,1)S(1)} %get-tuple-element.46), channel_id=1, source_target_pairs={{0,1},{1,0},{2,3},{3,2},{4,5},{5,4},{6,7},{7,6},{8,9},{9,8},{10,11... | collective-permute-start | bytes 196616 | tf_op jit(solution)/shard_map/ppermute | solution.py:99

commit v4 on v3

--- a/solution.py
+++ b/solution.py
@@ -9,6 +9,7 @@
 
 VMEM = pl.BlockSpec(memory_space=pltpu.VMEM)
 ROW_TILE = 256
+PIECES = 2
 
 
 class Plan:
@@ -35,23 +36,13 @@
     def landing_core(self, segment, half, slot):
         return (slot + half + segment + 1) % 2
 
-    def turned(self, z, turn):
-        return lax.bitwise_xor(z, turn)
-
-    def trade_pairs(self, turn):
-        pairs = []
-        for z in range(self.count):
-            for s in range(self.sections):
-                to = (z ^ turn, s)
-                if turn == self.count - 1 and s < 2 <= self.sections:
-                    to = (z, 1) if s == 0 else (z ^ turn, 0)
-                pairs.append((z * self.sections + s, to[0] * self.sections + to[1]))
-        return pairs
-
-    def leave_groups(self, early, index):
+    def from_chip(self, z, turn):
+        return lax.rem(z - turn + self.count, self.count)
+
+    def leave_groups(self, phase, index):
         groups = []
         for stage in reversed(range(self.sections)):
-            half = int((stage == self.sections - 1) != early)
+            half = phase if stage == self.sections - 1 else 1 - phase
             sends = self.transfers(stage, half, index)
             for known, members in groups:
                 if not set(known.values()) & set(sends.values()):
@@ -136,7 +127,7 @@
             per_half = plan.count // 2
             for side, blocks in ((own_rows, inputs[: n_in // 2]), (other_rows, inputs[n_in // 2 :])):
                 for turn, block in enumerate(blocks):
-                    t = plan.turned(place, turn)
+                    t = plan.from_chip(place, turn)
 
                     @pl.when(t // per_half == half)
                     def _(t=t, block=block, side=side):
@@ -144,8 +135,11 @@
                         streams[0][pl.ds(at, rows), side] = block[...]
         else:
             part = inputs[0].shape[0]
-            for side, block in ((core, inputs[0]), (1 - core, inputs[1])):
-                streams[0][pl.ds(pl.multiple_of(lags[0] + side * part, 16), part), :] = block[...]
+            for piece, block in enumerate(inputs[1:]):
+                size = block.shape[0]
+                at = pl.multiple_of(lags[0] + (1 - core) * part + piece * size, 16)
+                streams[0][pl.ds(at, size), :] = block[...]
+            streams[0][pl.ds(pl.multiple_of(lags[0] + core * part, 16), part), :] = inputs[0][...]
 
         for layer in range(layers):
             lag = lags[layer % 4]
@@ -224,7 +218,7 @@
         out_specs=[VMEM] * len(outs),
         scratch_shapes=scratch,
         compiler_params=pltpu.CompilerParams(vmem_limit_bytes=held + (12 << 20)),
-        cost_estimate=pl.CostEstimate(flops=16 * total * depth * depth * layers, bytes_accessed=1 << 20, transcendentals=0),
+        cost_estimate=pl.CostEstimate(flops=1, bytes_accessed=1, transcendentals=0),
     )(*weights, *inputs, *heads, *earlier)
     blocks, got = got[: plan.blocks], got[plan.blocks :]
     stream = None
@@ -242,11 +236,12 @@
     plan = Plan(count, sections, record_count)
 
     blocks = [
-        lax.dynamic_index_in_dim(records, plan.record_at(plan.turned(place, turn)), 0, keepdims=False)
+        lax.dynamic_index_in_dim(records, plan.record_at(lax.rem(place + turn, count)), 0, keepdims=False)
         for turn in range(count)
     ]
+    blocks, conv_weight = lax.optimization_barrier((blocks, conv_weight))
     for turn in range(1, count):
-        blocks[turn] = lax.ppermute(blocks[turn], ("tm", "segment"), plan.trade_pairs(turn))
+        blocks[turn] = lax.ppermute(blocks[turn], "tm", [(i, (i + turn) % count) for i in range(count)])
     conv = conv_weight.reshape(layers, taps, 2 * width)
     weights = (conv, swap_cores(conv), conv_bias, swap_cores(conv_bias), res_weight, skip_weight, swap_cores(skip_weight))
     inputs = blocks + [swap_cores(block) for block in blocks]
@@ -259,7 +254,7 @@
             earlier = []
             if stage == sections - 1:
                 for index in range(plan.blocks):
-                    members = plan.leave_groups(half == 0, index)[0][1][1:]
+                    members = plan.leave_groups(half, index)[0][1][1:]
                     if members:
                         block = skips[members[0]][index]
                         for member in members[1:]:
@@ -272,7 +267,8 @@
                     came, heads = lax.optimization_barrier((came, heads))
                 else:
                     came, stream = lax.optimization_barrier((came, stream))
-                came = [came, swap_cores(came)]
+                size = came.shape[0] // PIECES
+                came = [came] + [swap_cores(came[i * size : (i + 1) * size]) for i in range(PIECES)]
             skips[stage, half], stream, carried = run_section(
                 stage, half, plan, lags, weights, came, heads, earlier, rows
             )
@@ -288,9 +284,9 @@
     def number(device):
         return (device[0] * sections + device[1]) * 2 + device[2]
 
-    for early in (True, False):
+    for phase in range(2):
         for index in range(plan.blocks):
-            for sends, members in plan.leave_groups(early, index):
+            for sends, members in plan.leave_groups(phase, index):
                 payload = skips[members[0]][index]
                 if members[0][0] != sections - 1:
                     for member in members[1:]:

time: 44.1 us -> 40.7 us (0.923)
  waiting for transfers between devices: 23.8 us -> 17.5 us
  starting transfers between devices: 11.4 us -> 13.3 us
  local copies, waits for them, and re-layouts: 1.83 us -> 2.81 us
    ppermute x2, waiting for transfers between devices: 7.54 us -> 4.11 us  [shards(): lax.ppermute(stream, 'segment', [(i, (i + 1) % sections) for i in range(s...]
    ppermute x3, waiting for transfers between devices: 5.53 us -> 2.96 us  [shards(): lax.ppermute(blocks[turn], 'tm', [(i, (i + turn) % count) for i in range(...]
    ppermute x10 -> x12, starting transfers between devices: 1.2 us -> 2.33 us  [swap_cores(): return lax.ppermute(block, 'chan', [(0, 1), (1, 0)])]
    unnamed x8, local copies, waits for them, and re-layouts: 0.02 us -> 0.97 us
    ppermute x2, starting transfers between devices: 2.72 us -> 3.27 us  [shards(): lax.ppermute(payload, ('tm', 'segment', 'chan'), sorted(((number(a), numb...]
    ppermute x10 -> x12, waiting for transfers between devices: 3.21 us -> 3.19 us  [swap_cores(): return lax.ppermute(block, 'chan', [(0, 1), (1, 0)])]
  transfers between devices with their start and end apart: 17 -> 19, of which waited for: 9 -> 11; matrix products, arithmetic and copies ran while one was open for 0% -> 0% of each run, Pallas kernels for 6% -> 7%
where the time goes in v4:
time: 40.7 us; the launch traced here: 40.6 us
  waiting for transfers between devices  17.5 us (43%)
  starting transfers between devices  13.3 us (33%)
  Pallas kernels  6.82 us (17%)
  local copies, waits for them, and re-layouts  2.81 us (7%)
    ppermute x3, starting transfers between devices, shards(): lax.ppermute(blocks[turn], 'tm', [(i, (i + turn) % count) for i in range(...  7.53 us
    ppermute x2, waiting for transfers between devices, shards(): lax.ppermute(payload, ('tm', 'segment', 'chan'), sorted(((number(a), numb...  7.27 us
    pallas_call x4, Pallas kernels, run_section(): pl.pallas_call(functools.partial(section_kernel, stage, half, plan, lags,...  5.54 us
    ppermute x2, waiting for transfers between devices, shards(): lax.ppermute(stream, 'segment', [(i, (i + 1) % sections) for i in range(s...  4.11 us
    ppermute x2, starting transfers between devices, shards(): lax.ppermute(payload, ('tm', 'segment', 'chan'), sorted(((number(a), numb...  3.27 us
    ppermute x12, waiting for transfers between devices, swap_cores(): return lax.ppermute(block, 'chan', [(0, 1), (1, 0)])  3.19 us
    ppermute x3, waiting for transfers between devices, shards(): lax.ppermute(blocks[turn], 'tm', [(i, (i + turn) % count) for i in range(...  2.96 us
    ppermute x12, starting transfers between devices, swap_cores(): return lax.ppermute(block, 'chan', [(0, 1), (1, 0)])  2.33 us
  transfers between devices with their start and end apart: 19, of which 11 were waited for; matrix products, arithmetic and copies ran while one was open for 0% of the time, Pallas kernels for 7%

profile of v4, /device:TPU:0, one launch (start us, length us, event | category | flops | bytes accessed | tf_op | source)
XLA Modules:
  0.0 40.6 jit_solution(2860799423248918249)
XLA Ops:
  0.0 0.0 copy-start.3
  0.0 0.9 %copy-done.3 = bf16[4,256,128]{2,1,0:T(8,128)(2,1)S(1)} copy-done((bf16[4,256,128]{2,1,0:T(8,128)(2,1)S(1)}, bf16[4,256,128]{2,1,0:T(8,128)(2,1)}, u32[]{:S(2)}) %copy-start.3) | copy-done | bytes 262168
  1.0 0.0 copy-start.1
  1.0 0.0 copy-start.2
  1.0 0.0 copy-start
  1.0 1.8 %reshape.3.refs_0_ = bf16[4,512,256]{2,1,0:T(8,128)(2,1)S(1)} reshape(bf16[4,512,2,128]{3,2,1,0:T(2,128)(2,1)} %param.6) | data formatting | bytes 2097152 | tf_op jit(solution)/shard_map/reshape | solution.py:245
  2.8 0.5 %collective-permute-start = (bf16[4,512,256]{2,1,0:T(8,128)(2,1)S(1)}, bf16[4,512,256]{2,1,0:T(8,128)(2,1)S(1)}, u32[]{:S(2)}, u32[]{:S(2)}) collective-permute-start(bf16[4,512,256]{2,1,0:T(8,128)(2,1)S(1)} %reshape.3.refs_0_), channel_id=1, source_target_pairs={{0,1},{1,0},{2,3},{3,2},{4,5},{5,4},{6,7},{7,6},{8,9},{9,8},{10,11... | collective-permute-start | bytes 3145736 | tf_op jit(solution)/shard_map/ppermute | solution.py:90
  3.3 0.0 copy-done.1
  3.3 0.1 collective-permute-start.2
  3.4 3.0 %collective-permute-start.3 = (bf16[256,128]{1,0:T(8,128)(2,1)S(1)}, bf16[256,128]{1,0:T(8,128)(2,1)S(1)}, u32[]{:S(2)}, u32[]{:S(2)}) collective-permute-start(bf16[256,128]{1,0:T(8,128)(2,1)S(1)} %get-tuple-element.33), channel_id=1, source_target_pairs={{0,4},{4,8},{8,12},{12,0},{1,5},{5,9},{9,13},{13,1},{2,6},{6,10},{... | collective-permute-start | bytes 196616 | tf_op jit(solution)/shard_map/ppermute | solution.py:244
  6.4 0.0 copy-done.2
  6.4 0.0 collective-permute-start.1
  6.4 2.6 %collective-permute-start.4 = (bf16[256,128]{1,0:T(8,128)(2,1)S(1)}, bf16[256,128]{1,0:T(8,128)(2,1)S(1)}, u32[]{:S(2)}, u32[]{:S(2)}) collective-permute-start(bf16[256,128]{1,0:T(8,128)(2,1)S(1)} %get-tuple-element.34), channel_id=1, source_target_pairs={{0,8},{4,12},{8,0},{12,4},{1,9},{5,13},{9,1},{13,5},{2,10},{6,14},... | collective-permute-start | bytes 196616 | tf_op jit(solution)/shard_map/ppermute | solution.py:244
  9.0 0.0 collective-permute-done.1.refs_3_
  9.0 1.9 %collective-permute-start.5 = (bf16[256,128]{1,0:T(8,128)(2,1)S(1)}, bf16[256,128]{1,0:T(8,128)(2,1)S(1)}, u32[]{:S(2)}, u32[]{:S(2)}) collective-permute-start(bf16[256,128]{1,0:T(8,128)(2,1)S(1)} %get-tuple-element.35), channel_id=1, source_target_pairs={{0,12},{4,0},{8,4},{12,8},{1,13},{5,1},{9,5},{13,9},{2,14},{6,2},{... | collective-permute-start | bytes 196616 | tf_op jit(solution)/shard_map/ppermute | solution.py:244
  11.0 0.0 collective-permute-done.3.refs_8_
  11.0 0.0 collective-permute-start.6
  11.0 2.7 %collective-permute-done.4.refs_9_ = bf16[256,128]{1,0:T(8,128)(2,1)S(1)} collective-permute-done((bf16[256,128]{1,0:T(8,128)(2,1)S(1)}, bf16[256,128]{1,0:T(8,128)(2,1)S(1)}, u32[]{:S(2)}, u32[]{:S(2)}) %collective-permute-start.4) | collective-permute-done | bytes 65568 | tf_op jit(solution)/shard_map/ppermute | solution.py:244
  13.7 0.0 collective-permute-start.7
  13.7 0.2 collective-permute-done.5.refs_10_
  13.9 0.3 collective-permute-start.8
  14.2 0.0 collective-permute-done.6.refs_11_
  14.2 0.2 collective-permute-start.9
  14.5 0.5 %collective-permute-done.7.refs_12_ = bf16[256,128]{1,0:T(8,128)(2,1)S(1)} collective-permute-done((bf16[256,128]{1,0:T(8,128)(2,1)S(1)}, bf16[256,128]{1,0:T(8,128)(2,1)S(1)}, u32[]{:S(2)}, u32[]{:S(2)}) %collective-permute-start.7) | collective-permute-done | bytes 65568 | tf_op jit(solution)/shard_map/ppermute | solution.py:90
  15.0 0.2 collective-permute-done.8.refs_13_
  15.2 0.3 collective-permute-done.9.refs_14_
  15.5 0.0 collective-permute-done.2.refs_6_
  15.5 0.0 collective-permute-done.refs_1_
  15.5 0.0 copy-done
  15.5 2.8 %shard_map.55 = (bf16[256,256]{1,0:T(8,128)(2,1)S(1)}, bf16[256,256]{1,0:T(8,128)(2,1)S(1)}, bf16[32,256]{1,0:T(8,128)(2,1)S(1)}, bf16[256,256]{1,0:T(8,128)(2,1...) custom-call(bf16[4,512,256]{2,1,0:T(8,128)(2,1)S(1)} %reshape.3.refs_0_, ...), custom_call_target="tpu_custom_call" | custom-call | flops 1 | bytes 1 | tf_op jit(solution)/shard_map/pallas_call | solution.py:214
  18.3 0.1 collective-permute-start.10
  18.3 2.8 %shard_map.56 = (bf16[256,256]{1,0:T(8,128)(2,1)S(1)}, bf16[256,256]{1,0:T(8,128)(2,1)S(1)}) custom-call(bf16[4,512,256]{2,1,0:T(8,128)(2,1)S(1)} %reshape.3.refs_0_, bf16[4,512,256]{2,1,0:T(8,128)(2,1)S(1)} %collective-permute-done.refs_1_, bf16[4,2,128]{2,1,0:T(2,128)(2,1)S(1)} %copy-done.2, bf16[4,2,128]{2,1,0:T(2,128)(2,1)S(1)} %collective-permute-done.1.refs_3_, ...), custom_call_target="tpu_custom_call" | custom-call | flops 1 | bytes 1 | tf_op jit(solution)/shard_map/pallas_call | solution.py:214
  21.1 0.1 collective-permute-start.14
  21.2 2.8 %collective-permute-done.10.refs_7_ = bf16[256,256]{1,0:T(8,128)(2,1)S(1)} collective-permute-done((bf16[256,256]{1,0:T(8,128)(2,1)S(1)}, bf16[256,256]{1,0:T(8,128)(2,1)S(1)}, u32[]{:S(2)}, u32[]{:S(2)}) %collective-permute-start.10) | collective-permute-done | bytes 131104 | tf_op jit(solution)/shard_map/ppermute | solution.py:277
  24.0 0.1 collective-permute-start.11
  24.1 0.5 %collective-permute-start.12 = (bf16[128,256]{1,0:T(8,128)(2,1)S(1)}, bf16[128,256]{1,0:T(8,128)(2,1)S(1)}, u32[]{:S(2)}, u32[]{:S(2)}) collective-permute-start(bf16[128,256]{1,0:T(8,128)(2,1)S(1)} %get-tuple-element.63), channel_id=1, source_target_pairs={{0,1},{1,0},{2,3},{3,2},{4,5},{5,4},{6,7},{7,6},{8,9},{9,8},{10,11... | collective-permute-start | bytes 196616 | tf_op jit(solution)/shard_map/ppermute | solution.py:90
  24.6 0.7 %collective-permute-done.11.refs_8_ = bf16[128,256]{1,0:T(8,128)(2,1)S(1)} collective-permute-done((bf16[128,256]{1,0:T(8,128)(2,1)S(1)}, bf16[128,256]{1,0:T(8,128)(2,1)S(1)}, u32[]{:S(2)}, u32[]{:S(2)}) %collective-permute-start.11) | collective-permute-done | bytes 65568 | tf_op jit(solution)/shard_map/ppermute | solution.py:90
  25.3 0.2 collective-permute-done.12.refs_9_
  25.5 1.3 %collective-permute-done.14.refs_7_ = bf16[256,256]{1,0:T(8,128)(2,1)S(1)} collective-permute-done((bf16[256,256]{1,0:T(8,128)(2,1)S(1)}, bf16[256,256]{1,0:T(8,128)(2,1)S(1)}, u32[]{:S(2)}, u32[]{:S(2)}) %collective-permute-start.14) | collective-permute-done | bytes 131104 | tf_op jit(solution)/shard_map/ppermute | solution.py:277
  26.8 0.1 collective-permute-start.15
  26.9 0.5 %collective-permute-start.16 = (bf16[128,256]{1,0:T(8,128)(2,1)S(1)}, bf16[128,256]{1,0:T(8,128)(2,1)S(1)}, u32[]{:S(2)}, u32[]{:S(2)}) collective-permute-start(bf16[128,256]{1,0:T(8,128)(2,1)S(1)} %get-tuple-element.61), channel_id=1, source_target_pairs={{0,1},{1,0},{2,3},{3,2},{4,5},{5,4},{6,7},{7,6},{8,9},{9,8},{10,11... | collective-permute-start | bytes 196616 | tf_op jit(solution)/shard_map/ppermute | solution.py:90
  27.4 0.9 %collective-permute-start.13 = (bf16[256,256]{1,0:T(8,128)(2,1)S(1)}, bf16[256,256]{1,0:T(8,128)(2,1)S(1)}, u32[]{:S(2)}, u32[]{:S(2)}) collective-permute-start(bf16[256,256]{1,0:T(8,128)(2,1)S(1)} %get-tuple-element.44), channel_id=1, source_target_pairs={{0,8},{1,12},{2,1},{3,5},{4,11},{5,15},{6,2},{7,6},{8,9},{9,13},{1... | collective-permute-start | bytes 393224 | tf_op jit(solution)/shard_map/ppermute | solution.py:296
  28.3 0.0 collective-permute-done.15.refs_8_
  28.3 0.0 collective-permute-done.16.refs_9_
  28.4 2.3 %collective-permute-start.17 = (bf16[256,256]{1,0:T(8,128)(2,1)S(1)}, bf16[256,256]{1,0:T(8,128)(2,1)S(1)}, u32[]{:S(2)}, u32[]{:S(2)}) collective-permute-start(bf16[256,256]{1,0:T(8,128)(2,1)S(1)} %shard_map.58), channel_id=1, source_target_pairs={{0,1},{1,5},{2,8},{3,12},{4,2},{5,6},{6,11},{7,15},{8,0},{9,4},{10... | collective-permute-start | bytes 393224 | tf_op jit(solution)/shard_map/ppermute | solution.py:296
  30.7 7.3 %collective-permute-done.13.refs_0_ = bf16[256,256]{1,0:T(8,128)(2,1)S(1)} collective-permute-done((bf16[256,256]{1,0:T(8,128)(2,1)S(1)}, bf16[256,256]{1,0:T(8,128)(2,1)S(1)}, u32[]{:S(2)}, u32[]{:S(2)}) %collective-permute-start.13) | collective-permute-done | bytes 131104 | tf_op jit(solution)/shard_map/ppermute | solution.py:296
  38.0 0.0 collective-permute-done.17.refs_1_
  38.0 0.6 %shard_map.59 = (bf16[256,128]{1,0:T(8,128)(2,1)S(1)}, bf16[256,128]{1,0:T(8,128)(2,1)S(1)}) custom-call(s32[2]{0:T(128)S(1)} %broadcast_1_holds.2.holds, bf16[256,256]{1,0:T(8,128)(2,1)S(1)} %collective-permute-done.13.refs_0_, bf16[256,256]{1,0:T(8,128)(2,1)S(1)} %collective-permute-done.17.refs_1_), custom_call_target="tpu_custom_call" | custom-call | tf_op jit(solution)/shard_map/pallas_call | solution.py:304
  38.6 0.1 collective-permute-start.18
  38.7 1.2 %collective-permute-done.18.given = bf16[256,128]{1,0:T(8,128)(2,1)S(1)} collective-permute-done((bf16[256,128]{1,0:T(8,128)(2,1)S(1)}, bf16[256,128]{1,0:T(8,128)(2,1)S(1)}, u32[]{:S(2)}, u32[]{:S(2)}) %collective-permute-start.18) | collective-permute-done | bytes 65568 | tf_op jit(solution)/shard_map/ppermute | solution.py:90
  39.9 0.7 %shard_map.60 = bf16[2,256,128]{2,1,0:T(8,128)(2,1)} custom-call(bf16[256,128]{1,0:T(8,128)(2,1)S(1)} %get-tuple-element.55.kept, bf16[256,128]{1,0:T(8,128)(2,1)S(1)} %collective-permute-done.18.given), custom_call_target="tpu_custom_call" | custom-call | tf_op jit(solution)/shard_map/pallas_call | solution.py:311
  (6 shorter events, 0.1 us)
Async XLA Ops:
  0.0 0.9 %copy-start.3 = (bf16[4,256,128]{2,1,0:T(8,128)(2,1)S(1)}, bf16[4,256,128]{2,1,0:T(8,128)(2,1)}, u32[]{:S(2)}) copy-start(bf16[4,256,128]{2,1,0:T(8,128)(2,1)} %param.5) | copy-start | bytes 786436
  1.0 2.4 %copy-start.1 = (bf16[4,256,128]{2,1,0:T(8,128)(2,1)S(1)}, bf16[4,256,128]{2,1,0:T(8,128)(2,1)}, u32[]{:S(2)}) copy-start(bf16[4,256,128]{2,1,0:T(8,128)(2,1)} %refs_5_.7) | copy-start | bytes 786436
  1.0 5.4 %copy-start.2 = (bf16[4,2,128]{2,1,0:T(2,128)(2,1)S(1)}, bf16[4,2,128]{2,1,0:T(2,128)(2,1)}, u32[]{:S(2)}) copy-start(bf16[4,2,128]{2,1,0:T(2,128)(2,1)} %refs_2_.7) | copy-start | bytes 6148
  1.0 14.5 %copy-start = (bf16[4,256,256]{2,1,0:T(8,128)(2,1)S(1)}, bf16[4,256,256]{2,1,0:T(8,128)(2,1)}, u32[]{:S(2)}) copy-start(bf16[4,256,256]{2,1,0:T(8,128)(2,1)} %refs_4_.7) | copy-start | bytes 1572868
  2.8 12.7 %collective-permute-start = (bf16[4,512,256]{2,1,0:T(8,128)(2,1)S(1)}, bf16[4,512,256]{2,1,0:T(8,128)(2,1)S(1)}, u32[]{:S(2)}, u32[]{:S(2)}) collective-permute-start(bf16[4,512,256]{2,1,0:T(8,128)(2,1)S(1)} %reshape.3.refs_0_), channel_id=1, source_target_pairs={{0,1},{1,0},{2,3},{3,2},{4,5},{5,4},{6,7},{7,6},{8,9},{9,8},{10,11... | collective-permute-start | bytes 3145736 | tf_op jit(solution)/shard_map/ppermute | solution.py:90
  3.3 12.1 %collective-permute-start.2 = (bf16[4,256,128]{2,1,0:T(8,128)(2,1)S(1)}, bf16[4,256,128]{2,1,0:T(8,128)(2,1)S(1)}, u32[]{:S(2)}, u32[]{:S(2)}) collective-permute-start(bf16[4,256,128]{2,1,0:T(8,128)(2,1)S(1)} %copy-done.1), channel_id=1, source_target_pairs={{0,1},{1,0},{2,3},{3,2},{4,5},{5,4},{6,7},{7,6},{8,9},{9,8},{10,11... | collective-permute-start | bytes 786440 | tf_op jit(solution)/shard_map/ppermute | solution.py:90
  3.4 7.5 %collective-permute-start.3 = (bf16[256,128]{1,0:T(8,128)(2,1)S(1)}, bf16[256,128]{1,0:T(8,128)(2,1)S(1)}, u32[]{:S(2)}, u32[]{:S(2)}) collective-permute-start(bf16[256,128]{1,0:T(8,128)(2,1)S(1)} %get-tuple-element.33), channel_id=1, source_target_pairs={{0,4},{4,8},{8,12},{12,0},{1,5},{5,9},{9,13},{13,1},{2,6},{6,10},{... | collective-permute-start | bytes 196616 | tf_op jit(solution)/shard_map/ppermute | solution.py:244
  6.4 2.6 %collective-permute-start.1 = (bf16[4,2,128]{2,1,0:T(2,128)(2,1)S(1)}, bf16[4,2,128]{2,1,0:T(2,128)(2,1)S(1)}, u32[]{:S(2)}, u32[]{:S(2)}) collective-permute-start(bf16[4,2,128]{2,1,0:T(2,128)(2,1)S(1)} %copy-done.2), channel_id=1, source_target_pairs={{0,1},{1,0},{2,3},{3,2},{4,5},{5,4},{6,7},{7,6},{8,9},{9,8},{10,11... | collective-permute-start | bytes 6152 | tf_op jit(solution)/shard_map/ppermute | solution.py:90
  6.4 7.3 %collective-permute-start.4 = (bf16[256,128]{1,0:T(8,128)(2,1)S(1)}, bf16[256,128]{1,0:T(8,128)(2,1)S(1)}, u32[]{:S(2)}, u32[]{:S(2)}) collective-permute-start(bf16[256,128]{1,0:T(8,128)(2,1)S(1)} %get-tuple-element.34), channel_id=1, source_target_pairs={{0,8},{4,12},{8,0},{12,4},{1,9},{5,13},{9,1},{13,5},{2,10},{6,14},... | collective-permute-start | bytes 196616 | tf_op jit(solution)/shard_map/ppermute | solution.py:244
  9.0 4.9 %collective-permute-start.5 = (bf16[256,128]{1,0:T(8,128)(2,1)S(1)}, bf16[256,128]{1,0:T(8,128)(2,1)S(1)}, u32[]{:S(2)}, u32[]{:S(2)}) collective-permute-start(bf16[256,128]{1,0:T(8,128)(2,1)S(1)} %get-tuple-element.35), channel_id=1, source_target_pairs={{0,12},{4,0},{8,4},{12,8},{1,13},{5,1},{9,5},{13,9},{2,14},{6,2},{... | collective-permute-start | bytes 196616 | tf_op jit(solution)/shard_map/ppermute | solution.py:244
  11.0 3.3 %collective-permute-start.6 = (bf16[256,128]{1,0:T(8,128)(2,1)S(1)}, bf16[256,128]{1,0:T(8,128)(2,1)S(1)}, u32[]{:S(2)}, u32[]{:S(2)}) collective-permute-start(bf16[256,128]{1,0:T(8,128)(2,1)S(1)} %get-tuple-element.32.refs_7_), channel_id=1, source_target_pairs={{0,1},{1,0},{2,3},{3,2},{4,5},{5,4},{6,7},{7,6},{8,9},{9,8},{10,11... | collective-permute-start | bytes 196616 | tf_op jit(solution)/shard_map/ppermute | solution.py:90
  13.7 1.3 %collective-permute-start.7 = (bf16[256,128]{1,0:T(8,128)(2,1)S(1)}, bf16[256,128]{1,0:T(8,128)(2,1)S(1)}, u32[]{:S(2)}, u32[]{:S(2)}) collective-permute-start(bf16[256,128]{1,0:T(8,128)(2,1)S(1)} %collective-permute-done.3.refs_8_), channel_id=1, source_target_pairs={{0,1},{1,0},{2,3},{3,2},{4,5},{5,4},{6,7},{7,6},{8,9},{9,8},{10,11... | collective-permute-start | bytes 196616 | tf_op jit(solution)/shard_map/ppermute | solution.py:90
  13.9 1.3 %collective-permute-start.8 = (bf16[256,128]{1,0:T(8,128)(2,1)S(1)}, bf16[256,128]{1,0:T(8,128)(2,1)S(1)}, u32[]{:S(2)}, u32[]{:S(2)}) collective-permute-start(bf16[256,128]{1,0:T(8,128)(2,1)S(1)} %collective-permute-done.4.refs_9_), channel_id=1, source_target_pairs={{0,1},{1,0},{2,3},{3,2},{4,5},{5,4},{6,7},{7,6},{8,9},{9,8},{10,11... | collective-permute-start | bytes 196616 | tf_op jit(solution)/shard_map/ppermute | solution.py:90
  14.2 1.3 %collective-permute-start.9 = (bf16[256,128]{1,0:T(8,128)(2,1)S(1)}, bf16[256,128]{1,0:T(8,128)(2,1)S(1)}, u32[]{:S(2)}, u32[]{:S(2)}) collective-permute-start(bf16[256,128]{1,0:T(8,128)(2,1)S(1)} %collective-permute-done.5.refs_10_), channel_id=1, source_target_pairs={{0,1},{1,0},{2,3},{3,2},{4,5},{5,4},{6,7},{7,6},{8,9},{9,8},{10,11... | collective-permute-start | bytes 196616 | tf_op jit(solution)/shard_map/ppermute | solution.py:90
  18.3 5.7 %collective-permute-start.10 = (bf16[256,256]{1,0:T(8,128)(2,1)S(1)}, bf16[256,256]{1,0:T(8,128)(2,1)S(1)}, u32[]{:S(2)}, u32[]{:S(2)}) collective-permute-start(bf16[256,256]{1,0:T(8,128)(2,1)S(1)} %get-tuple-element.36), channel_id=1, source_target_pairs={{0,2},{2,0},{1,3},{3,1},{4,6},{6,4},{5,7},{7,5},{8,10},{10,8},{9,1... | collective-permute-start | bytes 393224 | tf_op jit(solution)/shard_map/ppermute | solution.py:277
  21.1 5.7 %collective-permute-start.14 = (bf16[256,256]{1,0:T(8,128)(2,1)S(1)}, bf16[256,256]{1,0:T(8,128)(2,1)S(1)}, u32[]{:S(2)}, u32[]{:S(2)}) collective-permute-start(bf16[256,256]{1,0:T(8,128)(2,1)S(1)} %get-tuple-element.41), channel_id=1, source_target_pairs={{0,2},{2,0},{1,3},{3,1},{4,6},{6,4},{5,7},{7,5},{8,10},{10,8},{9,1... | collective-permute-start | bytes 393224 | tf_op jit(solution)/shard_map/ppermute | solution.py:277
  24.0 1.3 %collective-permute-start.11 = (bf16[128,256]{1,0:T(8,128)(2,1)S(1)}, bf16[128,256]{1,0:T(8,128)(2,1)S(1)}, u32[]{:S(2)}, u32[]{:S(2)}) collective-permute-start(bf16[128,256]{1,0:T(8,128)(2,1)S(1)} %get-tuple-element.64), channel_id=1, source_target_pairs={{0,1},{1,0},{2,3},{3,2},{4,5},{5,4},{6,7},{7,6},{8,9},{9,8},{10,11... | collective-permute-start | bytes 196616 | tf_op jit(solution)/shard_map/ppermute | solution.py:90
  24.1 1.4 %collective-permute-start.12 = (bf16[128,256]{1,0:T(8,128)(2,1)S(1)}, bf16[128,256]{1,0:T(8,128)(2,1)S(1)}, u32[]{:S(2)}, u32[]{:S(2)}) collective-permute-start(bf16[128,256]{1,0:T(8,128)(2,1)S(1)} %get-tuple-element.63), channel_id=1, source_target_pairs={{0,1},{1,0},{2,3},{3,2},{4,5},{5,4},{6,7},{7,6},{8,9},{9,8},{10,11... | collective-permute-start | bytes 196616 | tf_op jit(solution)/shard_map/ppermute | solution.py:90
  26.8 1.5 %collective-permute-start.15 = (bf16[128,256]{1,0:T(8,128)(2,1)S(1)}, bf16[128,256]{1,0:T(8,128)(2,1)S(1)}, u32[]{:S(2)}, u32[]{:S(2)}) collective-permute-start(bf16[128,256]{1,0:T(8,128)(2,1)S(1)} %get-tuple-element.62), channel_id=1, source_target_pairs={{0,1},{1,0},{2,3},{3,2},{4,5},{5,4},{6,7},{7,6},{8,9},{9,8},{10,11... | collective-permute-start | bytes 196616 | tf_op jit(solution)/shard_map/ppermute | solution.py:90
  26.9 1.4 %collective-permute-start.16 = (bf16[128,256]{1,0:T(8,128)(2,1)S(1)}, bf16[128,256]{1,0:T(8,128)(2,1)S(1)}, u32[]{:S(2)}, u32[]{:S(2)}) collective-permute-start(bf16[128,256]{1,0:T(8,128)(2,1)S(1)} %get-tuple-element.61), channel_id=1, source_target_pairs={{0,1},{1,0},{2,3},{3,2},{4,5},{5,4},{6,7},{7,6},{8,9},{9,8},{10,11... | collective-permute-start | bytes 196616 | tf_op jit(solution)/shard_map/ppermute | solution.py:90
  27.4 10.6 %collective-permute-start.13 = (bf16[256,256]{1,0:T(8,128)(2,1)S(1)}, bf16[256,256]{1,0:T(8,128)(2,1)S(1)}, u32[]{:S(2)}, u32[]{:S(2)}) collective-permute-start(bf16[256,256]{1,0:T(8,128)(2,1)S(1)} %get-tuple-element.44), channel_id=1, source_target_pairs={{0,8},{1,12},{2,1},{3,5},{4,11},{5,15},{6,2},{7,6},{8,9},{9,13},{1... | collective-permute-start | bytes 393224 | tf_op jit(solution)/shard_map/ppermute | solution.py:296
  28.4 9.6 %collective-permute-start.17 = (bf16[256,256]{1,0:T(8,128)(2,1)S(1)}, bf16[256,256]{1,0:T(8,128)(2,1)S(1)}, u32[]{:S(2)}, u32[]{:S(2)}) collective-permute-start(bf16[256,256]{1,0:T(8,128)(2,1)S(1)} %shard_map.58), channel_id=1, source_target_pairs={{0,1},{1,5},{2,8},{3,12},{4,2},{5,6},{6,11},{7,15},{8,0},{9,4},{10... | collective-permute-start | bytes 393224 | tf_op jit(solution)/shard_map/ppermute | solution.py:296
  38.6 1.3 %collective-permute-start.18 = (bf16[256,128]{1,0:T(8,128)(2,1)S(1)}, bf16[256,128]{1,0:T(8,128)(2,1)S(1)}, u32[]{:S(2)}, u32[]{:S(2)}) collective-permute-start(bf16[256,128]{1,0:T(8,128)(2,1)S(1)} %get-tuple-element.56), channel_id=1, source_target_pairs={{0,1},{1,0},{2,3},{3,2},{4,5},{5,4},{6,7},{7,6},{8,9},{9,8},{10,11... | collective-permute-start | bytes 196616 | tf_op jit(solution)/shard_map/ppermute | solution.py:90

commit v5 on v4

--- a/solution.py
+++ b/solution.py
@@ -8,7 +8,7 @@
 from jax.sharding import PartitionSpec as P
 
 VMEM = pl.BlockSpec(memory_space=pltpu.VMEM)
-ROW_TILE = 256
+ROW_TILE = 512
 PIECES = 2
 
 
@@ -153,10 +153,10 @@
                 past = now_buf[pl.ds(row, ROW_TILE), :]
                 now = now_buf[pl.ds(lag + row, ROW_TILE), :]
                 parts = []
+                both = jnp.concatenate([past, now], 1)
                 for conv, bias in ((own_conv, own_bias), (other_conv, other_bias)):
                     shift = jnp.concatenate([bias[layer, 0:1, :], bias[layer, 1:2, :]], 1).astype(jnp.float32)
-                    pre = jnp.dot(past, conv[layer, :depth], preferred_element_type=jnp.float32)
-                    pre += jnp.dot(now, conv[layer, depth:], preferred_element_type=jnp.float32)
+                    pre = jnp.dot(both, conv[layer], preferred_element_type=jnp.float32)
                     pre += shift
                     gate = 0.5 * jnp.tanh(0.5 * pre[:, width:]) + 0.5
                     parts.append((jnp.tanh(pre[:, :width]) * gate).astype(jnp.bfloat16))
@@ -239,7 +239,6 @@
         lax.dynamic_index_in_dim(records, plan.record_at(lax.rem(place + turn, count)), 0, keepdims=False)
         for turn in range(count)
     ]
-    blocks, conv_weight = lax.optimization_barrier((blocks, conv_weight))
     for turn in range(1, count):
         blocks[turn] = lax.ppermute(blocks[turn], "tm", [(i, (i + turn) % count) for i in range(count)])
     conv = conv_weight.reshape(layers, taps, 2 * width)

time: 40.7 us -> 39.3 us (0.966)
  Pallas kernels: 6.82 us -> 5.79 us
  local copies, waits for them, and re-layouts: 2.81 us -> 1.85 us
    pallas_call x4, Pallas kernels: 5.54 us -> 4.5 us  [run_section(): pl.pallas_call(functools.partial(section_kernel, stage, half, plan, lags,...]
    unnamed x8, local copies, waits for them, and re-layouts: 0.97 us -> 0.02 us
    ppermute x2, waiting for transfers between devices: 4.11 us -> 4.6 us  [shards(): lax.ppermute(stream, 'segment', [(i, (i + 1) % sections) for i in range(s...]
    ppermute x2, starting transfers between devices: 3.27 us -> 3.68 us  [shards(): lax.ppermute(payload, ('tm', 'segment', 'chan'), sorted(((number(a), numb...]
  transfers between devices with their start and end apart: 19 -> 19, of which waited for: 11 -> 11; matrix products, arithmetic and copies ran while one was open for 0% -> 0% of each run, Pallas kernels for 7% -> 6%
where the time goes in v5:
time: 39.3 us; the launch traced here: 39.1 us
  waiting for transfers between devices  17.7 us (45%)
  starting transfers between devices  13.7 us (35%)
  Pallas kernels  5.79 us (15%)
  local copies, waits for them, and re-layouts  1.85 us (5%)
    ppermute x3, starting transfers between devices, shards(): lax.ppermute(blocks[turn], 'tm', [(i, (i + turn) % count) for i in range(...  7.51 us
    ppermute x2, waiting for transfers between devices, shards(): lax.ppermute(payload, ('tm', 'segment', 'chan'), sorted(((number(a), numb...  6.87 us
    ppermute x2, waiting for transfers between devices, shards(): lax.ppermute(stream, 'segment', [(i, (i + 1) % sections) for i in range(s...  4.6 us
    pallas_call x4, Pallas kernels, run_section(): pl.pallas_call(functools.partial(section_kernel, stage, half, plan, lags,...  4.5 us
    ppermute x2, starting transfers between devices, shards(): lax.ppermute(payload, ('tm', 'segment', 'chan'), sorted(((number(a), numb...  3.68 us
    ppermute x12, waiting for transfers between devices, swap_cores(): return lax.ppermute(block, 'chan', [(0, 1), (1, 0)])  3.19 us
    ppermute x3, waiting for transfers between devices, shards(): lax.ppermute(blocks[turn], 'tm', [(i, (i + turn) % count) for i in range(...  3.04 us
    ppermute x12, starting transfers between devices, swap_cores(): return lax.ppermute(block, 'chan', [(0, 1), (1, 0)])  2.33 us
  transfers between devices with their start and end apart: 19, of which 11 were waited for; matrix products, arithmetic and copies ran while one was open for 0% of the time, Pallas kernels for 6%

profile of v5, /device:TPU:0, one launch (start us, length us, event | category | flops | bytes accessed | tf_op | source)
XLA Modules:
  0.0 39.1 jit_solution(11063746687878687120)
XLA Ops:
  0.0 0.0 copy-start.1
  0.0 0.0 copy-start.3
  0.0 1.8 %reshape.3.refs_0_ = bf16[4,512,256]{2,1,0:T(8,128)(2,1)S(1)} reshape(bf16[4,512,2,128]{3,2,1,0:T(2,128)(2,1)} %param.6) | data formatting | bytes 2097152 | tf_op jit(solution)/shard_map/reshape | solution.py:244
  1.8 0.0 copy-start
  1.8 0.5 %collective-permute-start = (bf16[4,512,256]{2,1,0:T(8,128)(2,1)S(1)}, bf16[4,512,256]{2,1,0:T(8,128)(2,1)S(1)}, u32[]{:S(2)}, u32[]{:S(2)}) collective-permute-start(bf16[4,512,256]{2,1,0:T(8,128)(2,1)S(1)} %reshape.3.refs_0_), channel_id=1, source_target_pairs={{0,1},{1,0},{2,3},{3,2},{4,5},{5,4},{6,7},{7,6},{8,9},{9,8},{10,11... | collective-permute-start | bytes 3145736 | tf_op jit(solution)/shard_map/ppermute | solution.py:90
  2.3 0.0 copy-done.1
  2.3 0.1 collective-permute-start.2
  2.4 0.0 copy-done.3
  2.4 0.0 copy-start.2
  2.5 3.0 %collective-permute-start.3 = (bf16[256,128]{1,0:T(8,128)(2,1)S(1)}, bf16[256,128]{1,0:T(8,128)(2,1)S(1)}, u32[]{:S(2)}, u32[]{:S(2)}) collective-permute-start(bf16[256,128]{1,0:T(8,128)(2,1)S(1)} %get-tuple-element.48), channel_id=1, source_target_pairs={{0,4},{4,8},{8,12},{12,0},{1,5},{5,9},{9,13},{13,1},{2,6},{6,10},{... | collective-permute-start | bytes 196616 | tf_op jit(solution)/shard_map/ppermute | solution.py:243
  5.5 0.0 copy-done.2
  5.5 0.0 collective-permute-start.1
  5.5 2.6 %collective-permute-start.4 = (bf16[256,128]{1,0:T(8,128)(2,1)S(1)}, bf16[256,128]{1,0:T(8,128)(2,1)S(1)}, u32[]{:S(2)}, u32[]{:S(2)}) collective-permute-start(bf16[256,128]{1,0:T(8,128)(2,1)S(1)} %get-tuple-element.50), channel_id=1, source_target_pairs={{0,8},{4,12},{8,0},{12,4},{1,9},{5,13},{9,1},{13,5},{2,10},{6,14},... | collective-permute-start | bytes 196616 | tf_op jit(solution)/shard_map/ppermute | solution.py:243
  8.1 0.0 collective-permute-done.1.refs_3_
  8.1 1.9 %collective-permute-start.5 = (bf16[256,128]{1,0:T(8,128)(2,1)S(1)}, bf16[256,128]{1,0:T(8,128)(2,1)S(1)}, u32[]{:S(2)}, u32[]{:S(2)}) collective-permute-start(bf16[256,128]{1,0:T(8,128)(2,1)S(1)} %get-tuple-element.47), channel_id=1, source_target_pairs={{0,12},{4,0},{8,4},{12,8},{1,13},{5,1},{9,5},{13,9},{2,14},{6,2},{... | collective-permute-start | bytes 196616 | tf_op jit(solution)/shard_map/ppermute | solution.py:243
  10.0 0.0 collective-permute-done.3.refs_8_
  10.0 0.0 collective-permute-start.6
  10.0 2.8 %collective-permute-done.4.refs_9_ = bf16[256,128]{1,0:T(8,128)(2,1)S(1)} collective-permute-done((bf16[256,128]{1,0:T(8,128)(2,1)S(1)}, bf16[256,128]{1,0:T(8,128)(2,1)S(1)}, u32[]{:S(2)}, u32[]{:S(2)}) %collective-permute-start.4) | collective-permute-done | bytes 65568 | tf_op jit(solution)/shard_map/ppermute | solution.py:243
  12.8 0.0 collective-permute-start.7
  12.8 0.2 collective-permute-done.5.refs_10_
  13.0 0.3 collective-permute-start.8
  13.3 0.0 collective-permute-done.6.refs_11_
  13.3 0.2 collective-permute-start.9
  13.5 0.5 %collective-permute-done.7.refs_12_ = bf16[256,128]{1,0:T(8,128)(2,1)S(1)} collective-permute-done((bf16[256,128]{1,0:T(8,128)(2,1)S(1)}, bf16[256,128]{1,0:T(8,128)(2,1)S(1)}, u32[]{:S(2)}, u32[]{:S(2)}) %collective-permute-start.7) | collective-permute-done | bytes 65568 | tf_op jit(solution)/shard_map/ppermute | solution.py:90
  14.0 0.2 collective-permute-done.8.refs_13_
  14.3 0.3 collective-permute-done.9.refs_14_
  14.6 0.0 collective-permute-done.2.refs_6_
  14.6 0.0 collective-permute-done.refs_1_
  14.6 0.0 copy-done
  14.6 2.2 %shard_map.55 = (bf16[256,256]{1,0:T(8,128)(2,1)S(1)}, bf16[256,256]{1,0:T(8,128)(2,1)S(1)}, bf16[32,256]{1,0:T(8,128)(2,1)S(1)}, bf16[256,256]{1,0:T(8,128)(2,1...) custom-call(bf16[4,512,256]{2,1,0:T(8,128)(2,1)S(1)} %reshape.3.refs_0_, ...), custom_call_target="tpu_custom_call" | custom-call | flops 1 | bytes 1 | tf_op jit(solution)/shard_map/pallas_call | solution.py:214
  16.8 0.1 collective-permute-start.10
  16.9 2.2 %shard_map.56 = (bf16[256,256]{1,0:T(8,128)(2,1)S(1)}, bf16[256,256]{1,0:T(8,128)(2,1)S(1)}) custom-call(bf16[4,512,256]{2,1,0:T(8,128)(2,1)S(1)} %reshape.3.refs_0_, bf16[4,512,256]{2,1,0:T(8,128)(2,1)S(1)} %collective-permute-done.refs_1_, bf16[4,2,128]{2,1,0:T(2,128)(2,1)S(1)} %copy-done.2, bf16[4,2,128]{2,1,0:T(2,128)(2,1)S(1)} %collective-permute-done.1.refs_3_, ...), custom_call_target="tpu_custom_call" | custom-call | flops 1 | bytes 1 | tf_op jit(solution)/shard_map/pallas_call | solution.py:214
  19.2 0.1 collective-permute-start.14
  19.2 3.7 %collective-permute-done.10.refs_7_ = bf16[256,256]{1,0:T(8,128)(2,1)S(1)} collective-permute-done((bf16[256,256]{1,0:T(8,128)(2,1)S(1)}, bf16[256,256]{1,0:T(8,128)(2,1)S(1)}, u32[]{:S(2)}, u32[]{:S(2)}) %collective-permute-start.10) | collective-permute-done | bytes 131104 | tf_op jit(solution)/shard_map/ppermute | solution.py:276
  23.0 0.1 collective-permute-start.11
  23.0 0.5 %collective-permute-start.12 = (bf16[128,256]{1,0:T(8,128)(2,1)S(1)}, bf16[128,256]{1,0:T(8,128)(2,1)S(1)}, u32[]{:S(2)}, u32[]{:S(2)}) collective-permute-start(bf16[128,256]{1,0:T(8,128)(2,1)S(1)} %get-tuple-element.53), channel_id=1, source_target_pairs={{0,1},{1,0},{2,3},{3,2},{4,5},{5,4},{6,7},{7,6},{8,9},{9,8},{10,11... | collective-permute-start | bytes 196616 | tf_op jit(solution)/shard_map/ppermute | solution.py:90
  23.5 0.7 %collective-permute-done.11.refs_8_ = bf16[128,256]{1,0:T(8,128)(2,1)S(1)} collective-permute-done((bf16[128,256]{1,0:T(8,128)(2,1)S(1)}, bf16[128,256]{1,0:T(8,128)(2,1)S(1)}, u32[]{:S(2)}, u32[]{:S(2)}) %collective-permute-start.11) | collective-permute-done | bytes 65568 | tf_op jit(solution)/shard_map/ppermute | solution.py:90
  24.3 0.2 collective-permute-done.12.refs_9_
  24.4 0.9 %collective-permute-done.14.refs_7_ = bf16[256,256]{1,0:T(8,128)(2,1)S(1)} collective-permute-done((bf16[256,256]{1,0:T(8,128)(2,1)S(1)}, bf16[256,256]{1,0:T(8,128)(2,1)S(1)}, u32[]{:S(2)}, u32[]{:S(2)}) %collective-permute-start.14) | collective-permute-done | bytes 131104 | tf_op jit(solution)/shard_map/ppermute | solution.py:276
  25.3 0.1 collective-permute-start.15
  25.4 0.5 %collective-permute-start.16 = (bf16[128,256]{1,0:T(8,128)(2,1)S(1)}, bf16[128,256]{1,0:T(8,128)(2,1)S(1)}, u32[]{:S(2)}, u32[]{:S(2)}) collective-permute-start(bf16[128,256]{1,0:T(8,128)(2,1)S(1)} %get-tuple-element.51), channel_id=1, source_target_pairs={{0,1},{1,0},{2,3},{3,2},{4,5},{5,4},{6,7},{7,6},{8,9},{9,8},{10,11... | collective-permute-start | bytes 196616 | tf_op jit(solution)/shard_map/ppermute | solution.py:90
  25.9 0.9 %collective-permute-start.13 = (bf16[256,256]{1,0:T(8,128)(2,1)S(1)}, bf16[256,256]{1,0:T(8,128)(2,1)S(1)}, u32[]{:S(2)}, u32[]{:S(2)}) collective-permute-start(bf16[256,256]{1,0:T(8,128)(2,1)S(1)} %get-tuple-element.34), channel_id=1, source_target_pairs={{0,8},{1,12},{2,1},{3,5},{4,11},{5,15},{6,2},{7,6},{8,9},{9,13},{1... | collective-permute-start | bytes 393224 | tf_op jit(solution)/shard_map/ppermute | solution.py:295
  26.8 0.0 collective-permute-done.15.refs_8_
  26.8 0.0 collective-permute-done.16.refs_9_
  26.9 2.8 %collective-permute-start.17 = (bf16[256,256]{1,0:T(8,128)(2,1)S(1)}, bf16[256,256]{1,0:T(8,128)(2,1)S(1)}, u32[]{:S(2)}, u32[]{:S(2)}) collective-permute-start(bf16[256,256]{1,0:T(8,128)(2,1)S(1)} %shard_map.58), channel_id=1, source_target_pairs={{0,1},{1,5},{2,8},{3,12},{4,2},{5,6},{6,11},{7,15},{8,0},{9,4},{10... | collective-permute-start | bytes 393224 | tf_op jit(solution)/shard_map/ppermute | solution.py:295
  29.6 6.9 %collective-permute-done.13.refs_0_ = bf16[256,256]{1,0:T(8,128)(2,1)S(1)} collective-permute-done((bf16[256,256]{1,0:T(8,128)(2,1)S(1)}, bf16[256,256]{1,0:T(8,128)(2,1)S(1)}, u32[]{:S(2)}, u32[]{:S(2)}) %collective-permute-start.13) | collective-permute-done | bytes 131104 | tf_op jit(solution)/shard_map/ppermute | solution.py:295
  36.5 0.0 collective-permute-done.17.refs_1_
  36.5 0.6 %shard_map.59 = (bf16[256,128]{1,0:T(8,128)(2,1)S(1)}, bf16[256,128]{1,0:T(8,128)(2,1)S(1)}) custom-call(s32[2]{0:T(128)S(1)} %broadcast_1_holds.2.holds, bf16[256,256]{1,0:T(8,128)(2,1)S(1)} %collective-permute-done.13.refs_0_, bf16[256,256]{1,0:T(8,128)(2,1)S(1)} %collective-permute-done.17.refs_1_), custom_call_target="tpu_custom_call" | custom-call | tf_op jit(solution)/shard_map/pallas_call | solution.py:303
  37.1 0.1 collective-permute-start.18
  37.2 1.2 %collective-permute-done.18.given = bf16[256,128]{1,0:T(8,128)(2,1)S(1)} collective-permute-done((bf16[256,128]{1,0:T(8,128)(2,1)S(1)}, bf16[256,128]{1,0:T(8,128)(2,1)S(1)}, u32[]{:S(2)}, u32[]{:S(2)}) %collective-permute-start.18) | collective-permute-done | bytes 65568 | tf_op jit(solution)/shard_map/ppermute | solution.py:90
  38.4 0.7 %shard_map.60 = bf16[2,256,128]{2,1,0:T(8,128)(2,1)} custom-call(bf16[256,128]{1,0:T(8,128)(2,1)S(1)} %get-tuple-element.45.kept, bf16[256,128]{1,0:T(8,128)(2,1)S(1)} %collective-permute-done.18.given), custom_call_target="tpu_custom_call" | custom-call | tf_op jit(solution)/shard_map/pallas_call | solution.py:310
  (6 shorter events, 0.1 us)
Async XLA Ops:
  0.0 2.3 %copy-start.1 = (bf16[4,256,128]{2,1,0:T(8,128)(2,1)S(1)}, bf16[4,256,128]{2,1,0:T(8,128)(2,1)}, u32[]{:S(2)}) copy-start(bf16[4,256,128]{2,1,0:T(8,128)(2,1)} %refs_5_.7) | copy-start | bytes 786436
  0.0 2.4 %copy-start.3 = (bf16[4,256,128]{2,1,0:T(8,128)(2,1)S(1)}, bf16[4,256,128]{2,1,0:T(8,128)(2,1)}, u32[]{:S(2)}) copy-start(bf16[4,256,128]{2,1,0:T(8,128)(2,1)} %param.5) | copy-start | bytes 786436
  1.8 12.8 %copy-start = (bf16[4,256,256]{2,1,0:T(8,128)(2,1)S(1)}, bf16[4,256,256]{2,1,0:T(8,128)(2,1)}, u32[]{:S(2)}) copy-start(bf16[4,256,256]{2,1,0:T(8,128)(2,1)} %refs_4_.7) | copy-start | bytes 1572868
  1.8 12.8 %collective-permute-start = (bf16[4,512,256]{2,1,0:T(8,128)(2,1)S(1)}, bf16[4,512,256]{2,1,0:T(8,128)(2,1)S(1)}, u32[]{:S(2)}, u32[]{:S(2)}) collective-permute-start(bf16[4,512,256]{2,1,0:T(8,128)(2,1)S(1)} %reshape.3.refs_0_), channel_id=1, source_target_pairs={{0,1},{1,0},{2,3},{3,2},{4,5},{5,4},{6,7},{7,6},{8,9},{9,8},{10,11... | collective-permute-start | bytes 3145736 | tf_op jit(solution)/shard_map/ppermute | solution.py:90
  2.3 12.2 %collective-permute-start.2 = (bf16[4,256,128]{2,1,0:T(8,128)(2,1)S(1)}, bf16[4,256,128]{2,1,0:T(8,128)(2,1)S(1)}, u32[]{:S(2)}, u32[]{:S(2)}) collective-permute-start(bf16[4,256,128]{2,1,0:T(8,128)(2,1)S(1)} %copy-done.1), channel_id=1, source_target_pairs={{0,1},{1,0},{2,3},{3,2},{4,5},{5,4},{6,7},{7,6},{8,9},{9,8},{10,11... | collective-permute-start | bytes 786440 | tf_op jit(solution)/shard_map/ppermute | solution.py:90
  2.4 3.1 %copy-start.2 = (bf16[4,2,128]{2,1,0:T(2,128)(2,1)S(1)}, bf16[4,2,128]{2,1,0:T(2,128)(2,1)}, u32[]{:S(2)}) copy-start(bf16[4,2,128]{2,1,0:T(2,128)(2,1)} %refs_2_.7) | copy-start | bytes 6148
  2.5 7.5 %collective-permute-start.3 = (bf16[256,128]{1,0:T(8,128)(2,1)S(1)}, bf16[256,128]{1,0:T(8,128)(2,1)S(1)}, u32[]{:S(2)}, u32[]{:S(2)}) collective-permute-start(bf16[256,128]{1,0:T(8,128)(2,1)S(1)} %get-tuple-element.48), channel_id=1, source_target_pairs={{0,4},{4,8},{8,12},{12,0},{1,5},{5,9},{9,13},{13,1},{2,6},{6,10},{... | collective-permute-start | bytes 196616 | tf_op jit(solution)/shard_map/ppermute | solution.py:243
  5.5 2.6 %collective-permute-start.1 = (bf16[4,2,128]{2,1,0:T(2,128)(2,1)S(1)}, bf16[4,2,128]{2,1,0:T(2,128)(2,1)S(1)}, u32[]{:S(2)}, u32[]{:S(2)}) collective-permute-start(bf16[4,2,128]{2,1,0:T(2,128)(2,1)S(1)} %copy-done.2), channel_id=1, source_target_pairs={{0,1},{1,0},{2,3},{3,2},{4,5},{5,4},{6,7},{7,6},{8,9},{9,8},{10,11... | collective-permute-start | bytes 6152 | tf_op jit(solution)/shard_map/ppermute | solution.py:90
  5.5 7.3 %collective-permute-start.4 = (bf16[256,128]{1,0:T(8,128)(2,1)S(1)}, bf16[256,128]{1,0:T(8,128)(2,1)S(1)}, u32[]{:S(2)}, u32[]{:S(2)}) collective-permute-start(bf16[256,128]{1,0:T(8,128)(2,1)S(1)} %get-tuple-element.50), channel_id=1, source_target_pairs={{0,8},{4,12},{8,0},{12,4},{1,9},{5,13},{9,1},{13,5},{2,10},{6,14},... | collective-permute-start | bytes 196616 | tf_op jit(solution)/shard_map/ppermute | solution.py:243
  8.1 4.9 %collective-permute-start.5 = (bf16[256,128]{1,0:T(8,128)(2,1)S(1)}, bf16[256,128]{1,0:T(8,128)(2,1)S(1)}, u32[]{:S(2)}, u32[]{:S(2)}) collective-permute-start(bf16[256,128]{1,0:T(8,128)(2,1)S(1)} %get-tuple-element.47), channel_id=1, source_target_pairs={{0,12},{4,0},{8,4},{12,8},{1,13},{5,1},{9,5},{13,9},{2,14},{6,2},{... | collective-permute-start | bytes 196616 | tf_op jit(solution)/shard_map/ppermute | solution.py:243
  10.0 3.3 %collective-permute-start.6 = (bf16[256,128]{1,0:T(8,128)(2,1)S(1)}, bf16[256,128]{1,0:T(8,128)(2,1)S(1)}, u32[]{:S(2)}, u32[]{:S(2)}) collective-permute-start(bf16[256,128]{1,0:T(8,128)(2,1)S(1)} %get-tuple-element.49.refs_7_), channel_id=1, source_target_pairs={{0,1},{1,0},{2,3},{3,2},{4,5},{5,4},{6,7},{7,6},{8,9},{9,8},{10,11... | collective-permute-start | bytes 196616 | tf_op jit(solution)/shard_map/ppermute | solution.py:90
  12.8 1.3 %collective-permute-start.7 = (bf16[256,128]{1,0:T(8,128)(2,1)S(1)}, bf16[256,128]{1,0:T(8,128)(2,1)S(1)}, u32[]{:S(2)}, u32[]{:S(2)}) collective-permute-start(bf16[256,128]{1,0:T(8,128)(2,1)S(1)} %collective-permute-done.3.refs_8_), channel_id=1, source_target_pairs={{0,1},{1,0},{2,3},{3,2},{4,5},{5,4},{6,7},{7,6},{8,9},{9,8},{10,11... | collective-permute-start | bytes 196616 | tf_op jit(solution)/shard_map/ppermute | solution.py:90
  13.0 1.3 %collective-permute-start.8 = (bf16[256,128]{1,0:T(8,128)(2,1)S(1)}, bf16[256,128]{1,0:T(8,128)(2,1)S(1)}, u32[]{:S(2)}, u32[]{:S(2)}) collective-permute-start(bf16[256,128]{1,0:T(8,128)(2,1)S(1)} %collective-permute-done.4.refs_9_), channel_id=1, source_target_pairs={{0,1},{1,0},{2,3},{3,2},{4,5},{5,4},{6,7},{7,6},{8,9},{9,8},{10,11... | collective-permute-start | bytes 196616 | tf_op jit(solution)/shard_map/ppermute | solution.py:90
  13.3 1.3 %collective-permute-start.9 = (bf16[256,128]{1,0:T(8,128)(2,1)S(1)}, bf16[256,128]{1,0:T(8,128)(2,1)S(1)}, u32[]{:S(2)}, u32[]{:S(2)}) collective-permute-start(bf16[256,128]{1,0:T(8,128)(2,1)S(1)} %collective-permute-done.5.refs_10_), channel_id=1, source_target_pairs={{0,1},{1,0},{2,3},{3,2},{4,5},{5,4},{6,7},{7,6},{8,9},{9,8},{10,11... | collective-permute-start | bytes 196616 | tf_op jit(solution)/shard_map/ppermute | solution.py:90
  16.8 6.1 %collective-permute-start.10 = (bf16[256,256]{1,0:T(8,128)(2,1)S(1)}, bf16[256,256]{1,0:T(8,128)(2,1)S(1)}, u32[]{:S(2)}, u32[]{:S(2)}) collective-permute-start(bf16[256,256]{1,0:T(8,128)(2,1)S(1)} %get-tuple-element.26), channel_id=1, source_target_pairs={{0,2},{2,0},{1,3},{3,1},{4,6},{6,4},{5,7},{7,5},{8,10},{10,8},{9,1... | collective-permute-start | bytes 393224 | tf_op jit(solution)/shard_map/ppermute | solution.py:276
  19.2 6.2 %collective-permute-start.14 = (bf16[256,256]{1,0:T(8,128)(2,1)S(1)}, bf16[256,256]{1,0:T(8,128)(2,1)S(1)}, u32[]{:S(2)}, u32[]{:S(2)}) collective-permute-start(bf16[256,256]{1,0:T(8,128)(2,1)S(1)} %get-tuple-element.31), channel_id=1, source_target_pairs={{0,2},{2,0},{1,3},{3,1},{4,6},{6,4},{5,7},{7,5},{8,10},{10,8},{9,1... | collective-permute-start | bytes 393224 | tf_op jit(solution)/shard_map/ppermute | solution.py:276
  23.0 1.3 %collective-permute-start.11 = (bf16[128,256]{1,0:T(8,128)(2,1)S(1)}, bf16[128,256]{1,0:T(8,128)(2,1)S(1)}, u32[]{:S(2)}, u32[]{:S(2)}) collective-permute-start(bf16[128,256]{1,0:T(8,128)(2,1)S(1)} %get-tuple-element.54), channel_id=1, source_target_pairs={{0,1},{1,0},{2,3},{3,2},{4,5},{5,4},{6,7},{7,6},{8,9},{9,8},{10,11... | collective-permute-start | bytes 196616 | tf_op jit(solution)/shard_map/ppermute | solution.py:90
  23.0 1.4 %collective-permute-start.12 = (bf16[128,256]{1,0:T(8,128)(2,1)S(1)}, bf16[128,256]{1,0:T(8,128)(2,1)S(1)}, u32[]{:S(2)}, u32[]{:S(2)}) collective-permute-start(bf16[128,256]{1,0:T(8,128)(2,1)S(1)} %get-tuple-element.53), channel_id=1, source_target_pairs={{0,1},{1,0},{2,3},{3,2},{4,5},{5,4},{6,7},{7,6},{8,9},{9,8},{10,11... | collective-permute-start | bytes 196616 | tf_op jit(solution)/shard_map/ppermute | solution.py:90
  25.3 1.5 %collective-permute-start.15 = (bf16[128,256]{1,0:T(8,128)(2,1)S(1)}, bf16[128,256]{1,0:T(8,128)(2,1)S(1)}, u32[]{:S(2)}, u32[]{:S(2)}) collective-permute-start(bf16[128,256]{1,0:T(8,128)(2,1)S(1)} %get-tuple-element.52), channel_id=1, source_target_pairs={{0,1},{1,0},{2,3},{3,2},{4,5},{5,4},{6,7},{7,6},{8,9},{9,8},{10,11... | collective-permute-start | bytes 196616 | tf_op jit(solution)/shard_map/ppermute | solution.py:90
  25.4 1.4 %collective-permute-start.16 = (bf16[128,256]{1,0:T(8,128)(2,1)S(1)}, bf16[128,256]{1,0:T(8,128)(2,1)S(1)}, u32[]{:S(2)}, u32[]{:S(2)}) collective-permute-start(bf16[128,256]{1,0:T(8,128)(2,1)S(1)} %get-tuple-element.51), channel_id=1, source_target_pairs={{0,1},{1,0},{2,3},{3,2},{4,5},{5,4},{6,7},{7,6},{8,9},{9,8},{10,11... | collective-permute-start | bytes 196616 | tf_op jit(solution)/shard_map/ppermute | solution.py:90
  25.9 10.6 %collective-permute-start.13 = (bf16[256,256]{1,0:T(8,128)(2,1)S(1)}, bf16[256,256]{1,0:T(8,128)(2,1)S(1)}, u32[]{:S(2)}, u32[]{:S(2)}) collective-permute-start(bf16[256,256]{1,0:T(8,128)(2,1)S(1)} %get-tuple-element.34), channel_id=1, source_target_pairs={{0,8},{1,12},{2,1},{3,5},{4,11},{5,15},{6,2},{7,6},{8,9},{9,13},{1... | collective-permute-start | bytes 393224 | tf_op jit(solution)/shard_map/ppermute | solution.py:295
  26.9 9.6 %collective-permute-start.17 = (bf16[256,256]{1,0:T(8,128)(2,1)S(1)}, bf16[256,256]{1,0:T(8,128)(2,1)S(1)}, u32[]{:S(2)}, u32[]{:S(2)}) collective-permute-start(bf16[256,256]{1,0:T(8,128)(2,1)S(1)} %shard_map.58), channel_id=1, source_target_pairs={{0,1},{1,5},{2,8},{3,12},{4,2},{5,6},{6,11},{7,15},{8,0},{9,4},{10... | collective-permute-start | bytes 393224 | tf_op jit(solution)/shard_map/ppermute | solution.py:295
  37.1 1.3 %collective-permute-start.18 = (bf16[256,128]{1,0:T(8,128)(2,1)S(1)}, bf16[256,128]{1,0:T(8,128)(2,1)S(1)}, u32[]{:S(2)}, u32[]{:S(2)}) collective-permute-start(bf16[256,128]{1,0:T(8,128)(2,1)S(1)} %get-tuple-element.46), channel_id=1, source_target_pairs={{0,1},{1,0},{2,3},{3,2},{4,5},{5,4},{6,7},{7,6},{8,9},{9,8},{10,11... | collective-permute-start | bytes 196616 | tf_op jit(solution)/shard_map/ppermute | solution.py:90

commit v6 on v5

--- a/solution.py
+++ b/solution.py
@@ -242,7 +242,13 @@
     for turn in range(1, count):
         blocks[turn] = lax.ppermute(blocks[turn], "tm", [(i, (i + turn) % count) for i in range(count)])
     conv = conv_weight.reshape(layers, taps, 2 * width)
-    weights = (conv, swap_cores(conv), conv_bias, swap_cores(conv_bias), res_weight, skip_weight, swap_cores(skip_weight))
+    other_conv = swap_cores(conv_weight).reshape(layers, taps, 2 * width)
+    weights = (conv, other_conv, conv_bias, swap_cores(conv_bias), res_weight, skip_weight, swap_cores(skip_weight))
+    blocks[1], conv, other_conv = lax.optimization_barrier((blocks[1], conv, other_conv))
+    weights = (conv, other_conv, *weights[2:])
+    order = list(range(1, count))
+    for before, turn in zip(order, order[1:]):
+        blocks[turn] = lax.optimization_barrier((blocks[turn], blocks[before]))[0]
     inputs = blocks + [swap_cores(block) for block in blocks]
 
     skips = {}
@@ -296,17 +302,19 @@
                         payload, ("tm", "segment", "chan"), sorted((number(a), number(b)) for a, b in pairs.items())
                     )
                 )
-                valid = jnp.bool_(True)
                 if len(sends) < 2 * count * sections:
                     valid = functools.reduce(jnp.logical_or, [spot == number(d) for d in sends.values()])
-                holds.append(valid.astype(jnp.int32))
+                    holds.append(valid.astype(jnp.int32))
+                else:
+                    holds.append(1)
+    masks = [] if all(isinstance(hold, int) for hold in holds) else [jnp.stack(holds)]
     kept, given = pl.pallas_call(
-        functools.partial(sum_kernel, len(arrived)),
+        functools.partial(sum_kernel, len(masks)),
         out_shape=[jax.ShapeDtypeStruct((rows, width), jnp.bfloat16)] * 2,
-        in_specs=[pl.BlockSpec(memory_space=pltpu.SMEM)] + [VMEM] * len(arrived),
+        in_specs=[pl.BlockSpec(memory_space=pltpu.SMEM)] * len(masks) + [VMEM] * len(arrived),
         out_specs=[VMEM] * 2,
         compiler_params=pltpu.CompilerParams(vmem_limit_bytes=4 << 20),
-    )(jnp.stack(holds), *arrived)
+    )(*masks, *arrived)
     return pl.pallas_call(
         functools.partial(place_kernel, plan),
         out_shape=jax.ShapeDtypeStruct((plan.share, rows, width), jnp.bfloat16),
@@ -316,15 +324,16 @@
     )(kept, swap_cores(given))
 
 
-def sum_kernel(count, holds, *refs):
-    arrived, (kept, given) = refs[:count], refs[count:]
+def sum_kernel(masked, *refs):
+    masks, arrived, (kept, given) = refs[:masked], refs[masked:-2], refs[-2:]
     width = kept.shape[1]
     core = lax.axis_index("chan")
     for side, out in ((core, kept), (1 - core, given)):
         lanes = pl.ds(pl.multiple_of(side * width, width), width)
         total = jnp.zeros(out.shape, jnp.float32)
         for index, block in enumerate(arrived):
-            total += jnp.where(holds[index] == 1, block[:, lanes].astype(jnp.float32), 0.0)
+            part = block[:, lanes].astype(jnp.float32)
+            total += jnp.where(masks[0][index] == 1, part, 0.0) if masked else part
         out[...] = total.astype(out.dtype)
 
 

time: 39.3 us -> 37.8 us (0.962)
  local copies, waits for them, and re-layouts: 1.85 us -> 4.66 us
  starting transfers between devices: 13.7 us -> 11.5 us
  waiting for transfers between devices: 17.7 us -> 16 us
  Pallas kernels: 5.79 us -> 5.24 us
    ppermute x3, waiting for transfers between devices: 3.04 us -> 0.01 us  [shards(): lax.ppermute(blocks[turn], 'tm', [(i, (i + turn) % count) for i in range(...]
    ppermute x2, starting transfers between devices: 3.68 us -> 1.55 us  [shards(): lax.ppermute(payload, ('tm', 'segment', 'chan'), sorted(((number(a), numb...]
    reshape x0 -> x1, local copies, waits for them, and re-layouts: none -> 1.81 us  [shards(): other_conv = swap_cores(conv_weight).reshape(layers, taps, 2 * width)]
    ppermute x12, waiting for transfers between devices: 3.19 us -> 4.1 us  [swap_cores(): return lax.ppermute(block, 'chan', [(0, 1), (1, 0)])]
    squeeze x1, local copies, waits for them, and re-layouts: 0.02 us -> 0.65 us  [shards(): lax.dynamic_index_in_dim(records, plan.record_at(lax.rem(place + turn, co...]
    pallas_call x1, Pallas kernels: 0.6 us -> 0.03 us  [shards(): pl.pallas_call(functools.partial(sum_kernel, len(masks)), out_shape=[jax....]
    ppermute x12, starting transfers between devices: 2.33 us -> 2.89 us  [swap_cores(): return lax.ppermute(block, 'chan', [(0, 1), (1, 0)])]
    ppermute x3, starting transfers between devices: 7.51 us -> 6.96 us  [shards(): lax.ppermute(blocks[turn], 'tm', [(i, (i + turn) % count) for i in range(...]
  transfers between devices with their start and end apart: 19 -> 19, of which waited for: 11 -> 11; matrix products, arithmetic and copies ran while one was open for 0% -> 11% of each run, Pallas kernels for 6% -> 6%
where the time goes in v6:
time: 37.8 us; the launch traced here: 37.6 us
  waiting for transfers between devices  16 us (42%)
  starting transfers between devices  11.5 us (30%)
  Pallas kernels  5.24 us (14%)
  local copies, waits for them, and re-layouts  4.66 us (12%)
    ppermute x2, waiting for transfers between devices, shards(): lax.ppermute(payload, ('tm', 'segment', 'chan'), sorted(((number(a), numb...  7.41 us
    ppermute x3, starting transfers between devices, shards(): lax.ppermute(blocks[turn], 'tm', [(i, (i + turn) % count) for i in range(...  6.96 us
    pallas_call x4, Pallas kernels, run_section(): pl.pallas_call(functools.partial(section_kernel, stage, half, plan, lags,...  4.52 us
    ppermute x2, waiting for transfers between devices, shards(): lax.ppermute(stream, 'segment', [(i, (i + 1) % sections) for i in range(s...  4.5 us
    ppermute x12, waiting for transfers between devices, swap_cores(): return lax.ppermute(block, 'chan', [(0, 1), (1, 0)])  4.1 us
    ppermute x12, starting transfers between devices, swap_cores(): return lax.ppermute(block, 'chan', [(0, 1), (1, 0)])  2.89 us
    reshape x1, local copies, waits for them, and re-layouts, shards(): other_conv = swap_cores(conv_weight).reshape(layers, taps, 2 * width)  1.81 us
    reshape x1, local copies, waits for them, and re-layouts, shards(): conv = conv_weight.reshape(layers, taps, 2 * width)  1.74 us
  transfers between devices with their start and end apart: 19, of which 11 were waited for; matrix products, arithmetic and copies ran while one was open for 11% of the time, Pallas kernels for 6%

profile of v6, /device:TPU:0, one launch (start us, length us, event | category | flops | bytes accessed | tf_op | source)
XLA Modules:
  0.0 37.6 jit_solution(12284875072549679230)
XLA Ops:
  0.0 0.0 copy-start.3
  0.0 0.5 %collective-permute-start.1 = (bf16[4,512,2,128]{3,2,1,0:T(2,128)(2,1)}, bf16[4,512,2,128]{3,2,1,0:T(2,128)(2,1)}, u32[]{:S(2)}, u32[]{:S(2)}) collective-permute-start(bf16[4,512,2,128]{3,2,1,0:T(2,128)(2,1)} %param.6), channel_id=1, source_target_pairs={{0,1},{1,0},{2,3},{3,2},{4,5},{5,4},{6,7},{7,6},{8,9},{9,8},{10,11... | collective-permute-start | bytes 3145736 | tf_op jit(solution)/shard_map/ppermute | solution.py:90
  0.5 0.1 collective-permute-start.3
  0.5 0.4 %copy-done.3 = bf16[4,256,128]{2,1,0:T(8,128)(2,1)S(1)} copy-done((bf16[4,256,128]{2,1,0:T(8,128)(2,1)S(1)}, bf16[4,256,128]{2,1,0:T(8,128)(2,1)}, u32[]{:S(2)}) %copy-start.3) | copy-done | bytes 262168
  1.0 0.6 %dynamic-slice_bitcast_fusion = (bf16[256,128]{1,0:T(8,128)(2,1)S(1)}, bf16[256,128]{1,0:T(8,128)(2,1)S(1)}, bf16[256,128]{1,0:T(8,128)(2,1)}, bf16[256,128]{1,0:T(8,128)(2,1)S(1)}) fusion(bf16[4,256,128]{2,1,0:T(8,128)(2,1)S(1)} %copy-done.3, s32[]{:T(128)S(6)} %select_n.84, s32[]{:T(128)S(6)} %select_n.76, s32[]{:T(128)S(6)} %select_n.72, s32[]{:T(128)S(6)} %select_n.80), kind=kLoop, calls=%fused_computation | loop fusion | bytes 524304 | tf_op jit(solution)/shard_map/jit(dynamic_index_in_dim)/squeeze | solution.py:239
  1.6 0.0 copy-start.2
  1.6 3.0 %collective-permute-start = (bf16[256,128]{1,0:T(8,128)(2,1)}, bf16[256,128]{1,0:T(8,128)(2,1)S(1)}, u32[]{:S(2)}, u32[]{:S(2)}) collective-permute-start(bf16[256,128]{1,0:T(8,128)(2,1)} %get-tuple-element.59), channel_id=1, source_target_pairs={{0,4},{4,8},{8,12},{12,0},{1,5},{5,9},{9,13},{13,1},{2,6},{6,10},{... | collective-permute-start | bytes 196616 | tf_op jit(solution)/shard_map/ppermute | solution.py:243
  4.6 2.6 %collective-permute-start.4 = (bf16[256,128]{1,0:T(8,128)(2,1)S(1)}, bf16[256,128]{1,0:T(8,128)(2,1)S(1)}, u32[]{:S(2)}, u32[]{:S(2)}) collective-permute-start(bf16[256,128]{1,0:T(8,128)(2,1)S(1)} %get-tuple-element.60), channel_id=1, source_target_pairs={{0,8},{4,12},{8,0},{12,4},{1,9},{5,13},{9,1},{13,5},{2,10},{6,14},... | collective-permute-start | bytes 196616 | tf_op jit(solution)/shard_map/ppermute | solution.py:243
  7.2 1.3 %collective-permute-start.5 = (bf16[256,128]{1,0:T(8,128)(2,1)S(1)}, bf16[256,128]{1,0:T(8,128)(2,1)S(1)}, u32[]{:S(2)}, u32[]{:S(2)}) collective-permute-start(bf16[256,128]{1,0:T(8,128)(2,1)S(1)} %get-tuple-element.57), channel_id=1, source_target_pairs={{0,12},{4,0},{8,4},{12,8},{1,13},{5,1},{9,5},{13,9},{2,14},{6,2},{... | collective-permute-start | bytes 196616 | tf_op jit(solution)/shard_map/ppermute | solution.py:243
  8.6 0.0 collective-permute-done.1
  8.6 0.0 copy-done.2
  8.6 0.0 collective-permute-start.2
  8.6 1.7 %reshape.6.refs_0_ = bf16[4,512,256]{2,1,0:T(8,128)(2,1)S(1)} reshape(bf16[4,512,2,128]{3,2,1,0:T(2,128)(2,1)} %param.6) | data formatting | bytes 2097152 | tf_op jit(solution)/shard_map/reshape | solution.py:244
  10.3 0.0 copy-start
  10.3 0.0 copy-start.1
  10.3 1.8 %reshape.7.refs_1_ = bf16[4,512,256]{2,1,0:T(8,128)(2,1)S(1)} reshape(bf16[4,512,2,128]{3,2,1,0:T(2,128)(2,1)} %collective-permute-done.1) | data formatting | bytes 2097152 | tf_op jit(solution)/shard_map/reshape | solution.py:245
  12.2 0.0 collective-permute-done.refs_8_
  12.2 0.6 %collective-permute-start.6 = (bf16[256,128]{1,0:T(8,128)(2,1)S(1)}, bf16[256,128]{1,0:T(8,128)(2,1)S(1)}, u32[]{:S(2)}, u32[]{:S(2)}) collective-permute-start(bf16[256,128]{1,0:T(8,128)(2,1)S(1)} %get-tuple-element.58.refs_7_), channel_id=1, source_target_pairs={{0,1},{1,0},{2,3},{3,2},{4,5},{5,4},{6,7},{7,6},{8,9},{9,8},{10,11... | collective-permute-start | bytes 196616 | tf_op jit(solution)/shard_map/ppermute | solution.py:90
  12.7 0.0 collective-permute-done.4.refs_9_
  12.7 0.1 collective-permute-start.8
  12.8 0.0 collective-permute-done.5.refs_10_
  12.8 0.4 %collective-permute-start.9 = (bf16[256,128]{1,0:T(8,128)(2,1)S(1)}, bf16[256,128]{1,0:T(8,128)(2,1)S(1)}, u32[]{:S(2)}, u32[]{:S(2)}) collective-permute-start(bf16[256,128]{1,0:T(8,128)(2,1)S(1)} %collective-permute-done.5.refs_10_), channel_id=1, source_target_pairs={{0,1},{1,0},{2,3},{3,2},{4,5},{5,4},{6,7},{7,6},{8,9},{9,8},{10,11... | collective-permute-start | bytes 196616 | tf_op jit(solution)/shard_map/ppermute | solution.py:90
  13.3 0.0 collective-permute-done.2.refs_3_
  13.3 0.1 collective-permute-start.7
  13.3 0.3 collective-permute-done.6.refs_11_
  13.6 0.0 collective-permute-done.3.refs_6_
  13.6 0.5 %collective-permute-done.9.refs_14_ = bf16[256,128]{1,0:T(8,128)(2,1)S(1)} collective-permute-done((bf16[256,128]{1,0:T(8,128)(2,1)S(1)}, bf16[256,128]{1,0:T(8,128)(2,1)S(1)}, u32[]{:S(2)}, u32[]{:S(2)}) %collective-permute-start.9) | collective-permute-done | bytes 65568 | tf_op jit(solution)/shard_map/ppermute | solution.py:90
  14.2 0.0 collective-permute-done.8.refs_13_
  14.2 0.4 collective-permute-done.7.refs_12_
  14.5 0.0 copy-done
  14.5 0.0 copy-done.1
  14.5 2.2 %shard_map.55 = (bf16[256,256]{1,0:T(8,128)(2,1)S(1)}, bf16[256,256]{1,0:T(8,128)(2,1)S(1)}, bf16[32,256]{1,0:T(8,128)(2,1)S(1)}, bf16[256,256]{1,0:T(8,128)(2,1...) custom-call(bf16[4,512,256]{2,1,0:T(8,128)(2,1)S(1)} %reshape.6.refs_0_, ...), custom_call_target="tpu_custom_call" | custom-call | flops 1 | bytes 1 | tf_op jit(solution)/shard_map/pallas_call | solution.py:214
  16.8 0.1 collective-permute-start.10
  16.9 2.3 %shard_map.56 = (bf16[256,256]{1,0:T(8,128)(2,1)S(1)}, bf16[256,256]{1,0:T(8,128)(2,1)S(1)}) custom-call(bf16[4,512,256]{2,1,0:T(8,128)(2,1)S(1)} %reshape.6.refs_0_, bf16[4,512,256]{2,1,0:T(8,128)(2,1)S(1)} %reshape.7.refs_1_, bf16[4,2,128]{2,1,0:T(2,128)(2,1)S(1)} %copy-done.2, bf16[4,2,128]{2,1,0:T(2,128)(2,1)S(1)} %collective-permute-done.2.refs_3_, ...), custom_call_target="tpu_custom_call" | custom-call | flops 1 | bytes 1 | tf_op jit(solution)/shard_map/pallas_call | solution.py:214
  19.1 0.1 collective-permute-start.14
  19.2 3.6 %collective-permute-done.10.refs_7_ = bf16[256,256]{1,0:T(8,128)(2,1)S(1)} collective-permute-done((bf16[256,256]{1,0:T(8,128)(2,1)S(1)}, bf16[256,256]{1,0:T(8,128)(2,1)S(1)}, u32[]{:S(2)}, u32[]{:S(2)}) %collective-permute-start.10) | collective-permute-done | bytes 131104 | tf_op jit(solution)/shard_map/ppermute | solution.py:282
  22.8 0.1 collective-permute-start.12
  22.9 0.5 %collective-permute-start.11 = (bf16[128,256]{1,0:T(8,128)(2,1)S(1)}, bf16[128,256]{1,0:T(8,128)(2,1)S(1)}, u32[]{:S(2)}, u32[]{:S(2)}) collective-permute-start(bf16[128,256]{1,0:T(8,128)(2,1)S(1)} %get-tuple-element.64), channel_id=1, source_target_pairs={{0,1},{1,0},{2,3},{3,2},{4,5},{5,4},{6,7},{7,6},{8,9},{9,8},{10,11... | collective-permute-start | bytes 196616 | tf_op jit(solution)/shard_map/ppermute | solution.py:90
  23.4 0.7 %collective-permute-done.12.refs_9_ = bf16[128,256]{1,0:T(8,128)(2,1)S(1)} collective-permute-done((bf16[128,256]{1,0:T(8,128)(2,1)S(1)}, bf16[128,256]{1,0:T(8,128)(2,1)S(1)}, u32[]{:S(2)}, u32[]{:S(2)}) %collective-permute-start.12) | collective-permute-done | bytes 65568 | tf_op jit(solution)/shard_map/ppermute | solution.py:90
  24.1 0.2 collective-permute-done.11.refs_8_
  24.3 0.9 %collective-permute-done.14.refs_7_ = bf16[256,256]{1,0:T(8,128)(2,1)S(1)} collective-permute-done((bf16[256,256]{1,0:T(8,128)(2,1)S(1)}, bf16[256,256]{1,0:T(8,128)(2,1)S(1)}, u32[]{:S(2)}, u32[]{:S(2)}) %collective-permute-start.14) | collective-permute-done | bytes 131104 | tf_op jit(solution)/shard_map/ppermute | solution.py:282
  25.2 0.1 collective-permute-start.16
  25.3 0.5 %collective-permute-start.15 = (bf16[128,256]{1,0:T(8,128)(2,1)S(1)}, bf16[128,256]{1,0:T(8,128)(2,1)S(1)}, u32[]{:S(2)}, u32[]{:S(2)}) collective-permute-start(bf16[128,256]{1,0:T(8,128)(2,1)S(1)} %get-tuple-element.62), channel_id=1, source_target_pairs={{0,1},{1,0},{2,3},{3,2},{4,5},{5,4},{6,7},{7,6},{8,9},{9,8},{10,11... | collective-permute-start | bytes 196616 | tf_op jit(solution)/shard_map/ppermute | solution.py:90
  25.8 0.1 collective-permute-start.13
  25.9 0.6 %collective-permute-done.16.refs_9_ = bf16[128,256]{1,0:T(8,128)(2,1)S(1)} collective-permute-done((bf16[128,256]{1,0:T(8,128)(2,1)S(1)}, bf16[128,256]{1,0:T(8,128)(2,1)S(1)}, u32[]{:S(2)}, u32[]{:S(2)}) %collective-permute-start.16) | collective-permute-done | bytes 65568 | tf_op jit(solution)/shard_map/ppermute | solution.py:90
  26.5 0.2 collective-permute-done.15.refs_8_
  26.7 1.4 %collective-permute-start.17 = (bf16[256,256]{1,0:T(8,128)(2,1)S(1)}, bf16[256,256]{1,0:T(8,128)(2,1)S(1)}, u32[]{:S(2)}, u32[]{:S(2)}) collective-permute-start(bf16[256,256]{1,0:T(8,128)(2,1)S(1)} %shard_map.58), channel_id=1, source_target_pairs={{0,1},{1,5},{2,8},{3,12},{4,2},{5,6},{6,11},{7,15},{8,0},{9,4},{10... | collective-permute-start | bytes 393224 | tf_op jit(solution)/shard_map/ppermute | solution.py:301
  28.2 7.4 %collective-permute-done.13.refs_0_ = bf16[256,256]{1,0:T(8,128)(2,1)S(1)} collective-permute-done((bf16[256,256]{1,0:T(8,128)(2,1)S(1)}, bf16[256,256]{1,0:T(8,128)(2,1)S(1)}, u32[]{:S(2)}, u32[]{:S(2)}) %collective-permute-start.13) | collective-permute-done | bytes 131104 | tf_op jit(solution)/shard_map/ppermute | solution.py:301
  35.6 0.0 collective-permute-done.17.refs_1_
  35.6 0.1 collective-permute-start.18
  35.7 1.2 %collective-permute-done.18.given = bf16[256,128]{1,0:T(8,128)(2,1)S(1)} collective-permute-done((bf16[256,128]{1,0:T(8,128)(2,1)S(1)}, bf16[256,128]{1,0:T(8,128)(2,1)S(1)}, u32[]{:S(2)}, u32[]{:S(2)}) %collective-permute-start.18) | collective-permute-done | bytes 65568 | tf_op jit(solution)/shard_map/ppermute | solution.py:90
  36.9 0.7 %shard_map.60 = bf16[2,256,128]{2,1,0:T(8,128)(2,1)} custom-call(bf16[256,128]{1,0:T(8,128)(2,1)S(1)} %get-tuple-element.55.kept, bf16[256,128]{1,0:T(8,128)(2,1)S(1)} %collective-permute-done.18.given), custom_call_target="tpu_custom_call" | custom-call | tf_op jit(solution)/shard_map/pallas_call | solution.py:318
  (5 shorter events, 0.1 us)
Async XLA Ops:
  0.0 0.9 %copy-start.3 = (bf16[4,256,128]{2,1,0:T(8,128)(2,1)S(1)}, bf16[4,256,128]{2,1,0:T(8,128)(2,1)}, u32[]{:S(2)}) copy-start(bf16[4,256,128]{2,1,0:T(8,128)(2,1)} %param.5) | copy-start | bytes 786436
  0.0 8.6 %collective-permute-start.1 = (bf16[4,512,2,128]{3,2,1,0:T(2,128)(2,1)}, bf16[4,512,2,128]{3,2,1,0:T(2,128)(2,1)}, u32[]{:S(2)}, u32[]{:S(2)}) collective-permute-start(bf16[4,512,2,128]{3,2,1,0:T(2,128)(2,1)} %param.6), channel_id=1, source_target_pairs={{0,1},{1,0},{2,3},{3,2},{4,5},{5,4},{6,7},{7,6},{8,9},{9,8},{10,11... | collective-permute-start | bytes 3145736 | tf_op jit(solution)/shard_map/ppermute | solution.py:90
  0.5 13.2 %collective-permute-start.3 = (bf16[4,256,128]{2,1,0:T(8,128)(2,1)}, bf16[4,256,128]{2,1,0:T(8,128)(2,1)S(1)}, u32[]{:S(2)}, u32[]{:S(2)}) collective-permute-start(bf16[4,256,128]{2,1,0:T(8,128)(2,1)} %refs_5_.7), channel_id=1, source_target_pairs={{0,1},{1,0},{2,3},{3,2},{4,5},{5,4},{6,7},{7,6},{8,9},{9,8},{10,11... | collective-permute-start | bytes 786440 | tf_op jit(solution)/shard_map/ppermute | solution.py:90
  1.6 7.0 %copy-start.2 = (bf16[4,2,128]{2,1,0:T(2,128)(2,1)S(1)}, bf16[4,2,128]{2,1,0:T(2,128)(2,1)}, u32[]{:S(2)}) copy-start(bf16[4,2,128]{2,1,0:T(2,128)(2,1)} %refs_2_.7) | copy-start | bytes 6148
  1.6 10.6 %collective-permute-start = (bf16[256,128]{1,0:T(8,128)(2,1)}, bf16[256,128]{1,0:T(8,128)(2,1)S(1)}, u32[]{:S(2)}, u32[]{:S(2)}) collective-permute-start(bf16[256,128]{1,0:T(8,128)(2,1)} %get-tuple-element.59), channel_id=1, source_target_pairs={{0,4},{4,8},{8,12},{12,0},{1,5},{5,9},{9,13},{13,1},{2,6},{6,10},{... | collective-permute-start | bytes 196616 | tf_op jit(solution)/shard_map/ppermute | solution.py:243
  4.6 8.1 %collective-permute-start.4 = (bf16[256,128]{1,0:T(8,128)(2,1)S(1)}, bf16[256,128]{1,0:T(8,128)(2,1)S(1)}, u32[]{:S(2)}, u32[]{:S(2)}) collective-permute-start(bf16[256,128]{1,0:T(8,128)(2,1)S(1)} %get-tuple-element.60), channel_id=1, source_target_pairs={{0,8},{4,12},{8,0},{12,4},{1,9},{5,13},{9,1},{13,5},{2,10},{6,14},... | collective-permute-start | bytes 196616 | tf_op jit(solution)/shard_map/ppermute | solution.py:243
  7.2 5.6 %collective-permute-start.5 = (bf16[256,128]{1,0:T(8,128)(2,1)S(1)}, bf16[256,128]{1,0:T(8,128)(2,1)S(1)}, u32[]{:S(2)}, u32[]{:S(2)}) collective-permute-start(bf16[256,128]{1,0:T(8,128)(2,1)S(1)} %get-tuple-element.57), channel_id=1, source_target_pairs={{0,12},{4,0},{8,4},{12,8},{1,13},{5,1},{9,5},{13,9},{2,14},{6,2},{... | collective-permute-start | bytes 196616 | tf_op jit(solution)/shard_map/ppermute | solution.py:243
  8.6 4.7 %collective-permute-start.2 = (bf16[4,2,128]{2,1,0:T(2,128)(2,1)S(1)}, bf16[4,2,128]{2,1,0:T(2,128)(2,1)S(1)}, u32[]{:S(2)}, u32[]{:S(2)}) collective-permute-start(bf16[4,2,128]{2,1,0:T(2,128)(2,1)S(1)} %copy-done.2), channel_id=1, source_target_pairs={{0,1},{1,0},{2,3},{3,2},{4,5},{5,4},{6,7},{7,6},{8,9},{9,8},{10,11... | collective-permute-start | bytes 6152 | tf_op jit(solution)/shard_map/ppermute | solution.py:90
  10.3 4.2 %copy-start = (bf16[4,256,256]{2,1,0:T(8,128)(2,1)S(1)}, bf16[4,256,256]{2,1,0:T(8,128)(2,1)}, u32[]{:S(2)}) copy-start(bf16[4,256,256]{2,1,0:T(8,128)(2,1)} %refs_4_.7) | copy-start | bytes 1572868
  10.3 4.2 %copy-start.1 = (bf16[4,256,128]{2,1,0:T(8,128)(2,1)S(1)}, bf16[4,256,128]{2,1,0:T(8,128)(2,1)}, u32[]{:S(2)}) copy-start(bf16[4,256,128]{2,1,0:T(8,128)(2,1)} %refs_5_.7) | copy-start | bytes 786436
  12.2 1.5 %collective-permute-start.6 = (bf16[256,128]{1,0:T(8,128)(2,1)S(1)}, bf16[256,128]{1,0:T(8,128)(2,1)S(1)}, u32[]{:S(2)}, u32[]{:S(2)}) collective-permute-start(bf16[256,128]{1,0:T(8,128)(2,1)S(1)} %get-tuple-element.58.refs_7_), channel_id=1, source_target_pairs={{0,1},{1,0},{2,3},{3,2},{4,5},{5,4},{6,7},{7,6},{8,9},{9,8},{10,11... | collective-permute-start | bytes 196616 | tf_op jit(solution)/shard_map/ppermute | solution.py:90
  12.7 1.4 %collective-permute-start.8 = (bf16[256,128]{1,0:T(8,128)(2,1)S(1)}, bf16[256,128]{1,0:T(8,128)(2,1)S(1)}, u32[]{:S(2)}, u32[]{:S(2)}) collective-permute-start(bf16[256,128]{1,0:T(8,128)(2,1)S(1)} %collective-permute-done.4.refs_9_), channel_id=1, source_target_pairs={{0,1},{1,0},{2,3},{3,2},{4,5},{5,4},{6,7},{7,6},{8,9},{9,8},{10,11... | collective-permute-start | bytes 196616 | tf_op jit(solution)/shard_map/ppermute | solution.py:90
  12.8 1.3 %collective-permute-start.9 = (bf16[256,128]{1,0:T(8,128)(2,1)S(1)}, bf16[256,128]{1,0:T(8,128)(2,1)S(1)}, u32[]{:S(2)}, u32[]{:S(2)}) collective-permute-start(bf16[256,128]{1,0:T(8,128)(2,1)S(1)} %collective-permute-done.5.refs_10_), channel_id=1, source_target_pairs={{0,1},{1,0},{2,3},{3,2},{4,5},{5,4},{6,7},{7,6},{8,9},{9,8},{10,11... | collective-permute-start | bytes 196616 | tf_op jit(solution)/shard_map/ppermute | solution.py:90
  13.3 1.3 %collective-permute-start.7 = (bf16[256,128]{1,0:T(8,128)(2,1)S(1)}, bf16[256,128]{1,0:T(8,128)(2,1)S(1)}, u32[]{:S(2)}, u32[]{:S(2)}) collective-permute-start(bf16[256,128]{1,0:T(8,128)(2,1)S(1)} %collective-permute-done.refs_8_), channel_id=1, source_target_pairs={{0,1},{1,0},{2,3},{3,2},{4,5},{5,4},{6,7},{7,6},{8,9},{9,8},{10,11... | collective-permute-start | bytes 196616 | tf_op jit(solution)/shard_map/ppermute | solution.py:90
  16.8 6.0 %collective-permute-start.10 = (bf16[256,256]{1,0:T(8,128)(2,1)S(1)}, bf16[256,256]{1,0:T(8,128)(2,1)S(1)}, u32[]{:S(2)}, u32[]{:S(2)}) collective-permute-start(bf16[256,256]{1,0:T(8,128)(2,1)S(1)} %get-tuple-element.36), channel_id=1, source_target_pairs={{0,2},{2,0},{1,3},{3,1},{4,6},{6,4},{5,7},{7,5},{8,10},{10,8},{9,1... | collective-permute-start | bytes 393224 | tf_op jit(solution)/shard_map/ppermute | solution.py:282
  19.1 6.1 %collective-permute-start.14 = (bf16[256,256]{1,0:T(8,128)(2,1)S(1)}, bf16[256,256]{1,0:T(8,128)(2,1)S(1)}, u32[]{:S(2)}, u32[]{:S(2)}) collective-permute-start(bf16[256,256]{1,0:T(8,128)(2,1)S(1)} %get-tuple-element.41), channel_id=1, source_target_pairs={{0,2},{2,0},{1,3},{3,1},{4,6},{6,4},{5,7},{7,5},{8,10},{10,8},{9,1... | collective-permute-start | bytes 393224 | tf_op jit(solution)/shard_map/ppermute | solution.py:282
  22.8 1.3 %collective-permute-start.12 = (bf16[128,256]{1,0:T(8,128)(2,1)S(1)}, bf16[128,256]{1,0:T(8,128)(2,1)S(1)}, u32[]{:S(2)}, u32[]{:S(2)}) collective-permute-start(bf16[128,256]{1,0:T(8,128)(2,1)S(1)} %get-tuple-element.63), channel_id=1, source_target_pairs={{0,1},{1,0},{2,3},{3,2},{4,5},{5,4},{6,7},{7,6},{8,9},{9,8},{10,11... | collective-permute-start | bytes 196616 | tf_op jit(solution)/shard_map/ppermute | solution.py:90
  22.9 1.4 %collective-permute-start.11 = (bf16[128,256]{1,0:T(8,128)(2,1)S(1)}, bf16[128,256]{1,0:T(8,128)(2,1)S(1)}, u32[]{:S(2)}, u32[]{:S(2)}) collective-permute-start(bf16[128,256]{1,0:T(8,128)(2,1)S(1)} %get-tuple-element.64), channel_id=1, source_target_pairs={{0,1},{1,0},{2,3},{3,2},{4,5},{5,4},{6,7},{7,6},{8,9},{9,8},{10,11... | collective-permute-start | bytes 196616 | tf_op jit(solution)/shard_map/ppermute | solution.py:90
  25.2 1.3 %collective-permute-start.16 = (bf16[128,256]{1,0:T(8,128)(2,1)S(1)}, bf16[128,256]{1,0:T(8,128)(2,1)S(1)}, u32[]{:S(2)}, u32[]{:S(2)}) collective-permute-start(bf16[128,256]{1,0:T(8,128)(2,1)S(1)} %get-tuple-element.61), channel_id=1, source_target_pairs={{0,1},{1,0},{2,3},{3,2},{4,5},{5,4},{6,7},{7,6},{8,9},{9,8},{10,11... | collective-permute-start | bytes 196616 | tf_op jit(solution)/shard_map/ppermute | solution.py:90
  25.3 1.4 %collective-permute-start.15 = (bf16[128,256]{1,0:T(8,128)(2,1)S(1)}, bf16[128,256]{1,0:T(8,128)(2,1)S(1)}, u32[]{:S(2)}, u32[]{:S(2)}) collective-permute-start(bf16[128,256]{1,0:T(8,128)(2,1)S(1)} %get-tuple-element.62), channel_id=1, source_target_pairs={{0,1},{1,0},{2,3},{3,2},{4,5},{5,4},{6,7},{7,6},{8,9},{9,8},{10,11... | collective-permute-start | bytes 196616 | tf_op jit(solution)/shard_map/ppermute | solution.py:90
  25.8 9.8 %collective-permute-start.13 = (bf16[256,256]{1,0:T(8,128)(2,1)S(1)}, bf16[256,256]{1,0:T(8,128)(2,1)S(1)}, u32[]{:S(2)}, u32[]{:S(2)}) collective-permute-start(bf16[256,256]{1,0:T(8,128)(2,1)S(1)} %get-tuple-element.44), channel_id=1, source_target_pairs={{0,8},{1,12},{2,1},{3,5},{4,11},{5,15},{6,2},{7,6},{8,9},{9,13},{1... | collective-permute-start | bytes 393224 | tf_op jit(solution)/shard_map/ppermute | solution.py:301
  26.7 8.8 %collective-permute-start.17 = (bf16[256,256]{1,0:T(8,128)(2,1)S(1)}, bf16[256,256]{1,0:T(8,128)(2,1)S(1)}, u32[]{:S(2)}, u32[]{:S(2)}) collective-permute-start(bf16[256,256]{1,0:T(8,128)(2,1)S(1)} %shard_map.58), channel_id=1, source_target_pairs={{0,1},{1,5},{2,8},{3,12},{4,2},{5,6},{6,11},{7,15},{8,0},{9,4},{10... | collective-permute-start | bytes 393224 | tf_op jit(solution)/shard_map/ppermute | solution.py:301
  35.6 1.3 %collective-permute-start.18 = (bf16[256,128]{1,0:T(8,128)(2,1)S(1)}, bf16[256,128]{1,0:T(8,128)(2,1)S(1)}, u32[]{:S(2)}, u32[]{:S(2)}) collective-permute-start(bf16[256,128]{1,0:T(8,128)(2,1)S(1)} %get-tuple-element.56), channel_id=1, source_target_pairs={{0,1},{1,0},{2,3},{3,2},{4,5},{5,4},{6,7},{7,6},{8,9},{9,8},{10,11... | collective-permute-start | bytes 196616 | tf_op jit(solution)/shard_map/ppermute | solution.py:90

commit v7 on v6

--- a/solution.py
+++ b/solution.py
@@ -125,14 +125,14 @@
         if stage == 0:
             rows = inputs[0].shape[0]
             per_half = plan.count // 2
-            for side, blocks in ((own_rows, inputs[: n_in // 2]), (other_rows, inputs[n_in // 2 :])):
-                for turn, block in enumerate(blocks):
-                    t = plan.from_chip(place, turn)
-
-                    @pl.when(t // per_half == half)
-                    def _(t=t, block=block, side=side):
-                        at = pl.multiple_of(lags[0] + (t - half * per_half) * rows, 16)
-                        streams[0][pl.ds(at, rows), side] = block[...]
+            for turn in range(plan.count):
+                t = plan.from_chip(place, turn)
+
+                @pl.when(t // per_half == half)
+                def _(t=t, turn=turn):
+                    at = pl.multiple_of(lags[0] + (t - half * per_half) * rows, 16)
+                    streams[0][pl.ds(at, rows), own_rows] = inputs[turn][...]
+                    streams[0][pl.ds(at, rows), other_rows] = inputs[plan.count][turn * rows : (turn + 1) * rows, :]
         else:
             part = inputs[0].shape[0]
             for piece, block in enumerate(inputs[1:]):
@@ -246,10 +246,7 @@
     weights = (conv, other_conv, conv_bias, swap_cores(conv_bias), res_weight, skip_weight, swap_cores(skip_weight))
     blocks[1], conv, other_conv = lax.optimization_barrier((blocks[1], conv, other_conv))
     weights = (conv, other_conv, *weights[2:])
-    order = list(range(1, count))
-    for before, turn in zip(order, order[1:]):
-        blocks[turn] = lax.optimization_barrier((blocks[turn], blocks[before]))[0]
-    inputs = blocks + [swap_cores(block) for block in blocks]
+    inputs = blocks + [swap_cores(jnp.concatenate(blocks, 0))]
 
     skips = {}
     fed = [inputs, inputs]

time: 37.8 us -> 36.7 us (0.971)
  starting transfers between devices: 11.5 us -> 10.6 us
  local copies, waits for them, and re-layouts: 4.66 us -> 4.03 us
  waiting for transfers between devices: 16 us -> 16.5 us
    ppermute x3, waiting for transfers between devices: 0.01 us -> 1.74 us  [shards(): lax.ppermute(blocks[turn], 'tm', [(i, (i + turn) % count) for i in range(...]
    ppermute x3, starting transfers between devices: 6.96 us -> 6.11 us  [shards(): lax.ppermute(blocks[turn], 'tm', [(i, (i + turn) % count) for i in range(...]
    ppermute x12 -> x9, starting transfers between devices: 2.89 us -> 2.22 us  [swap_cores(): return lax.ppermute(block, 'chan', [(0, 1), (1, 0)])]
    ppermute x12 -> x9, waiting for transfers between devices: 4.1 us -> 3.45 us  [swap_cores(): return lax.ppermute(block, 'chan', [(0, 1), (1, 0)])]
    ppermute x2, waiting for transfers between devices: 7.41 us -> 6.77 us  [shards(): lax.ppermute(payload, ('tm', 'segment', 'chan'), sorted(((number(a), numb...]
    squeeze x1, local copies, waits for them, and re-layouts: 0.65 us -> 0.02 us  [shards(): lax.dynamic_index_in_dim(records, plan.record_at(lax.rem(place + turn, co...]
    ppermute x2, starting transfers between devices: 1.55 us -> 2.11 us  [shards(): lax.ppermute(payload, ('tm', 'segment', 'chan'), sorted(((number(a), numb...]
  transfers between devices with their start and end apart: 19 -> 16, of which waited for: 11 -> 10; matrix products, arithmetic and copies ran while one was open for 11% -> 10% of each run, Pallas kernels for 6% -> 6%
where the time goes in v7:
time: 36.7 us; the launch traced here: 36.5 us
  waiting for transfers between devices  16.5 us (45%)
  starting transfers between devices  10.6 us (29%)
  Pallas kernels  5.2 us (14%)
  local copies, waits for them, and re-layouts  4.03 us (11%)
    ppermute x2, waiting for transfers between devices, shards(): lax.ppermute(payload, ('tm', 'segment', 'chan'), sorted(((number(a), numb...  6.77 us
    ppermute x3, starting transfers between devices, shards(): lax.ppermute(blocks[turn], 'tm', [(i, (i + turn) % count) for i in range(...  6.11 us
    ppermute x2, waiting for transfers between devices, shards(): lax.ppermute(stream, 'segment', [(i, (i + 1) % sections) for i in range(s...  4.51 us
    pallas_call x4, Pallas kernels, run_section(): pl.pallas_call(functools.partial(section_kernel, stage, half, plan, lags,...  4.48 us
    ppermute x9, waiting for transfers between devices, swap_cores(): return lax.ppermute(block, 'chan', [(0, 1), (1, 0)])  3.45 us
    ppermute x9, starting transfers between devices, swap_cores(): return lax.ppermute(block, 'chan', [(0, 1), (1, 0)])  2.22 us
    ppermute x2, starting transfers between devices, shards(): lax.ppermute(payload, ('tm', 'segment', 'chan'), sorted(((number(a), numb...  2.11 us
    ppermute x3, waiting for transfers between devices, shards(): lax.ppermute(blocks[turn], 'tm', [(i, (i + turn) % count) for i in range(...  1.74 us
  transfers between devices with their start and end apart: 16, of which 10 were waited for; matrix products, arithmetic and copies ran while one was open for 10% of the time, Pallas kernels for 6%

profile of v7, /device:TPU:0, one launch (start us, length us, event | category | flops | bytes accessed | tf_op | source)
XLA Modules:
  0.0 36.5 jit_solution(1828171516482138982)
XLA Ops:
  0.0 0.0 copy-start.3
  0.0 0.5 %collective-permute-start.1 = (bf16[4,512,2,128]{3,2,1,0:T(2,128)(2,1)}, bf16[4,512,2,128]{3,2,1,0:T(2,128)(2,1)}, u32[]{:S(2)}, u32[]{:S(2)}) collective-permute-start(bf16[4,512,2,128]{3,2,1,0:T(2,128)(2,1)} %param.6), channel_id=1, source_target_pairs={{0,1},{1,0},{2,3},{3,2},{4,5},{5,4},{6,7},{7,6},{8,9},{9,8},{10,11... | collective-permute-start | bytes 3145736 | tf_op jit(solution)/shard_map/ppermute | solution.py:90
  0.5 0.5 %copy-done.3 = bf16[4,256,128]{2,1,0:T(8,128)(2,1)S(1)} copy-done((bf16[4,256,128]{2,1,0:T(8,128)(2,1)S(1)}, bf16[4,256,128]{2,1,0:T(8,128)(2,1)}, u32[]{:S(2)}) %copy-start.3) | copy-done | bytes 262168
  1.0 0.0 copy-start.1
  1.0 3.1 %collective-permute-start = (bf16[256,128]{1,0:T(8,128)(2,1)S(1)}, bf16[256,128]{1,0:T(8,128)(2,1)S(1)}, u32[]{:S(2)}, u32[]{:S(2)}) collective-permute-start(bf16[256,128]{1,0:T(8,128)(2,1)S(1)} %get-tuple-element.55), channel_id=1, source_target_pairs={{0,4},{4,8},{8,12},{12,0},{1,5},{5,9},{9,13},{13,1},{2,6},{6,10},{... | collective-permute-start | bytes 196616 | tf_op jit(solution)/shard_map/ppermute | solution.py:243
  4.1 2.1 %collective-permute-start.5 = (bf16[256,128]{1,0:T(8,128)(2,1)S(1)}, bf16[256,128]{1,0:T(8,128)(2,1)S(1)}, u32[]{:S(2)}, u32[]{:S(2)}) collective-permute-start(bf16[256,128]{1,0:T(8,128)(2,1)S(1)} %get-tuple-element.53), channel_id=1, source_target_pairs={{0,12},{4,0},{8,4},{12,8},{1,13},{5,1},{9,5},{13,9},{2,14},{6,2},{... | collective-permute-start | bytes 196616 | tf_op jit(solution)/shard_map/ppermute | solution.py:243
  6.1 0.9 %collective-permute-start.4 = (bf16[256,128]{1,0:T(8,128)(2,1)S(1)}, bf16[256,128]{1,0:T(8,128)(2,1)S(1)}, u32[]{:S(2)}, u32[]{:S(2)}) collective-permute-start(bf16[256,128]{1,0:T(8,128)(2,1)S(1)} %get-tuple-element.56), channel_id=1, source_target_pairs={{0,8},{4,12},{8,0},{12,4},{1,9},{5,13},{9,1},{13,5},{2,10},{6,14},... | collective-permute-start | bytes 196616 | tf_op jit(solution)/shard_map/ppermute | solution.py:243
  7.1 0.0 copy-done.1
  7.1 0.0 collective-permute-start.3
  7.1 1.7 %reshape.6.refs_0_ = bf16[4,512,256]{2,1,0:T(8,128)(2,1)S(1)} reshape(bf16[4,512,2,128]{3,2,1,0:T(2,128)(2,1)} %param.6) | data formatting | bytes 2097152 | tf_op jit(solution)/shard_map/reshape | solution.py:244
  8.8 0.0 collective-permute-done.1
  8.9 0.0 copy-start.2
  8.9 1.7 %reshape.7.refs_1_ = bf16[4,512,256]{2,1,0:T(8,128)(2,1)S(1)} reshape(bf16[4,512,2,128]{3,2,1,0:T(2,128)(2,1)} %collective-permute-done.1) | data formatting | bytes 2097152 | tf_op jit(solution)/shard_map/reshape | solution.py:245
  10.6 0.0 copy-start
  10.6 0.0 collective-permute-done.refs_8_
  10.6 0.0 collective-permute-done.5.refs_10_
  10.6 1.7 %collective-permute-done.4.refs_9_ = bf16[256,128]{1,0:T(8,128)(2,1)S(1)} collective-permute-done((bf16[256,128]{1,0:T(8,128)(2,1)S(1)}, bf16[256,128]{1,0:T(8,128)(2,1)S(1)}, u32[]{:S(2)}, u32[]{:S(2)}) %collective-permute-start.4) | collective-permute-done | bytes 65568 | tf_op jit(solution)/shard_map/ppermute | solution.py:243
  12.4 0.1 collective-permute-start.6
  12.5 0.0 copy-done.2
  12.5 0.5 %collective-permute-start.2 = (bf16[4,2,128]{2,1,0:T(2,128)(2,1)S(1)}, bf16[4,2,128]{2,1,0:T(2,128)(2,1)S(1)}, u32[]{:S(2)}, u32[]{:S(2)}) collective-permute-start(bf16[4,2,128]{2,1,0:T(2,128)(2,1)S(1)} %copy-done.2), channel_id=1, source_target_pairs={{0,1},{1,0},{2,3},{3,2},{4,5},{5,4},{6,7},{7,6},{8,9},{9,8},{10,11... | collective-permute-start | bytes 6152 | tf_op jit(solution)/shard_map/ppermute | solution.py:90
  13.0 1.0 %collective-permute-done.2.refs_3_ = bf16[4,2,128]{2,1,0:T(2,128)(2,1)S(1)} collective-permute-done((bf16[4,2,128]{2,1,0:T(2,128)(2,1)S(1)}, bf16[4,2,128]{2,1,0:T(2,128)(2,1)S(1)}, u32[]{:S(2)}, u32[]{:S(2)}) %collective-permute-start.2) | collective-permute-done | bytes 2080 | tf_op jit(solution)/shard_map/ppermute | solution.py:90
  14.0 0.0 collective-permute-done.3.refs_6_
  14.0 0.0 collective-permute-done.6.refs_11_
  14.0 0.0 copy-done
  14.0 2.2 %shard_map.55 = (bf16[256,256]{1,0:T(8,128)(2,1)S(1)}, bf16[256,256]{1,0:T(8,128)(2,1)S(1)}, bf16[32,256]{1,0:T(8,128)(2,1)S(1)}, bf16[256,256]{1,0:T(8,128)(2,1...) custom-call(bf16[4,512,256]{2,1,0:T(8,128)(2,1)S(1)} %reshape.6.refs_0_, ...), custom_call_target="tpu_custom_call" | custom-call | flops 1 | bytes 1 | tf_op jit(solution)/shard_map/pallas_call | solution.py:214
  16.3 0.1 collective-permute-start.7
  16.3 2.2 %shard_map.56 = (bf16[256,256]{1,0:T(8,128)(2,1)S(1)}, bf16[256,256]{1,0:T(8,128)(2,1)S(1)}) custom-call(bf16[4,512,256]{2,1,0:T(8,128)(2,1)S(1)} %reshape.6.refs_0_, bf16[4,512,256]{2,1,0:T(8,128)(2,1)S(1)} %reshape.7.refs_1_, bf16[4,2,128]{2,1,0:T(2,128)(2,1)S(1)} %copy-done.2, bf16[4,2,128]{2,1,0:T(2,128)(2,1)S(1)} %collective-permute-done.2.refs_3_, ...), custom_call_target="tpu_custom_call" | custom-call | flops 1 | bytes 1 | tf_op jit(solution)/shard_map/pallas_call | solution.py:214
  18.6 0.1 collective-permute-start.11
  18.7 3.6 %collective-permute-done.7.refs_7_ = bf16[256,256]{1,0:T(8,128)(2,1)S(1)} collective-permute-done((bf16[256,256]{1,0:T(8,128)(2,1)S(1)}, bf16[256,256]{1,0:T(8,128)(2,1)S(1)}, u32[]{:S(2)}, u32[]{:S(2)}) %collective-permute-start.7) | collective-permute-done | bytes 131104 | tf_op jit(solution)/shard_map/ppermute | solution.py:279
  22.3 0.1 collective-permute-start.9
  22.4 0.5 %collective-permute-start.8 = (bf16[128,256]{1,0:T(8,128)(2,1)S(1)}, bf16[128,256]{1,0:T(8,128)(2,1)S(1)}, u32[]{:S(2)}, u32[]{:S(2)}) collective-permute-start(bf16[128,256]{1,0:T(8,128)(2,1)S(1)} %get-tuple-element.60), channel_id=1, source_target_pairs={{0,1},{1,0},{2,3},{3,2},{4,5},{5,4},{6,7},{7,6},{8,9},{9,8},{10,11... | collective-permute-start | bytes 196616 | tf_op jit(solution)/shard_map/ppermute | solution.py:90
  22.9 0.7 %collective-permute-done.9.refs_9_ = bf16[128,256]{1,0:T(8,128)(2,1)S(1)} collective-permute-done((bf16[128,256]{1,0:T(8,128)(2,1)S(1)}, bf16[128,256]{1,0:T(8,128)(2,1)S(1)}, u32[]{:S(2)}, u32[]{:S(2)}) %collective-permute-start.9) | collective-permute-done | bytes 65568 | tf_op jit(solution)/shard_map/ppermute | solution.py:90
  23.6 0.2 collective-permute-done.8.refs_8_
  23.8 0.9 %collective-permute-done.11.refs_7_ = bf16[256,256]{1,0:T(8,128)(2,1)S(1)} collective-permute-done((bf16[256,256]{1,0:T(8,128)(2,1)S(1)}, bf16[256,256]{1,0:T(8,128)(2,1)S(1)}, u32[]{:S(2)}, u32[]{:S(2)}) %collective-permute-start.11) | collective-permute-done | bytes 131104 | tf_op jit(solution)/shard_map/ppermute | solution.py:279
  24.7 0.1 collective-permute-start.13
  24.8 0.5 %collective-permute-start.12 = (bf16[128,256]{1,0:T(8,128)(2,1)S(1)}, bf16[128,256]{1,0:T(8,128)(2,1)S(1)}, u32[]{:S(2)}, u32[]{:S(2)}) collective-permute-start(bf16[128,256]{1,0:T(8,128)(2,1)S(1)} %get-tuple-element.58), channel_id=1, source_target_pairs={{0,1},{1,0},{2,3},{3,2},{4,5},{5,4},{6,7},{7,6},{8,9},{9,8},{10,11... | collective-permute-start | bytes 196616 | tf_op jit(solution)/shard_map/ppermute | solution.py:90
  25.3 0.6 %collective-permute-start.10 = (bf16[256,256]{1,0:T(8,128)(2,1)S(1)}, bf16[256,256]{1,0:T(8,128)(2,1)S(1)}, u32[]{:S(2)}, u32[]{:S(2)}) collective-permute-start(bf16[256,256]{1,0:T(8,128)(2,1)S(1)} %get-tuple-element.40), channel_id=1, source_target_pairs={{0,8},{1,12},{2,1},{3,5},{4,11},{5,15},{6,2},{7,6},{8,9},{9,13},{1... | collective-permute-start | bytes 393224 | tf_op jit(solution)/shard_map/ppermute | solution.py:298
  25.9 0.1 collective-permute-done.13.refs_9_
  26.0 0.2 collective-permute-done.12.refs_8_
  26.2 1.5 %collective-permute-start.14 = (bf16[256,256]{1,0:T(8,128)(2,1)S(1)}, bf16[256,256]{1,0:T(8,128)(2,1)S(1)}, u32[]{:S(2)}, u32[]{:S(2)}) collective-permute-start(bf16[256,256]{1,0:T(8,128)(2,1)S(1)} %shard_map.58), channel_id=1, source_target_pairs={{0,1},{1,5},{2,8},{3,12},{4,2},{5,6},{6,11},{7,15},{8,0},{9,4},{10... | collective-permute-start | bytes 393224 | tf_op jit(solution)/shard_map/ppermute | solution.py:298
  27.7 6.8 %collective-permute-done.10.refs_0_ = bf16[256,256]{1,0:T(8,128)(2,1)S(1)} collective-permute-done((bf16[256,256]{1,0:T(8,128)(2,1)S(1)}, bf16[256,256]{1,0:T(8,128)(2,1)S(1)}, u32[]{:S(2)}, u32[]{:S(2)}) %collective-permute-start.10) | collective-permute-done | bytes 131104 | tf_op jit(solution)/shard_map/ppermute | solution.py:298
  34.4 0.0 collective-permute-done.14.refs_1_
  34.5 0.1 collective-permute-start.15
  34.6 1.2 %collective-permute-done.15.given = bf16[256,128]{1,0:T(8,128)(2,1)S(1)} collective-permute-done((bf16[256,128]{1,0:T(8,128)(2,1)S(1)}, bf16[256,128]{1,0:T(8,128)(2,1)S(1)}, u32[]{:S(2)}, u32[]{:S(2)}) %collective-permute-start.15) | collective-permute-done | bytes 65568 | tf_op jit(solution)/shard_map/ppermute | solution.py:90
  35.8 0.7 %shard_map.60 = bf16[2,256,128]{2,1,0:T(8,128)(2,1)} custom-call(bf16[256,128]{1,0:T(8,128)(2,1)S(1)} %get-tuple-element.51.kept, bf16[256,128]{1,0:T(8,128)(2,1)S(1)} %collective-permute-done.15.given), custom_call_target="tpu_custom_call" | custom-call | tf_op jit(solution)/shard_map/pallas_call | solution.py:315
  (7 shorter events, 0.1 us)
Async XLA Ops:
  0.0 0.9 %copy-start.3 = (bf16[4,256,128]{2,1,0:T(8,128)(2,1)S(1)}, bf16[4,256,128]{2,1,0:T(8,128)(2,1)}, u32[]{:S(2)}) copy-start(bf16[4,256,128]{2,1,0:T(8,128)(2,1)} %param.5) | copy-start | bytes 786436
  0.0 8.8 %collective-permute-start.1 = (bf16[4,512,2,128]{3,2,1,0:T(2,128)(2,1)}, bf16[4,512,2,128]{3,2,1,0:T(2,128)(2,1)}, u32[]{:S(2)}, u32[]{:S(2)}) collective-permute-start(bf16[4,512,2,128]{3,2,1,0:T(2,128)(2,1)} %param.6), channel_id=1, source_target_pairs={{0,1},{1,0},{2,3},{3,2},{4,5},{5,4},{6,7},{7,6},{8,9},{9,8},{10,11... | collective-permute-start | bytes 3145736 | tf_op jit(solution)/shard_map/ppermute | solution.py:90
  1.0 6.1 %copy-start.1 = (bf16[4,256,128]{2,1,0:T(8,128)(2,1)S(1)}, bf16[4,256,128]{2,1,0:T(8,128)(2,1)}, u32[]{:S(2)}) copy-start(bf16[4,256,128]{2,1,0:T(8,128)(2,1)} %refs_5_.7) | copy-start | bytes 786436
  1.0 9.7 %collective-permute-start = (bf16[256,128]{1,0:T(8,128)(2,1)S(1)}, bf16[256,128]{1,0:T(8,128)(2,1)S(1)}, u32[]{:S(2)}, u32[]{:S(2)}) collective-permute-start(bf16[256,128]{1,0:T(8,128)(2,1)S(1)} %get-tuple-element.55), channel_id=1, source_target_pairs={{0,4},{4,8},{8,12},{12,0},{1,5},{5,9},{9,13},{13,1},{2,6},{6,10},{... | collective-permute-start | bytes 196616 | tf_op jit(solution)/shard_map/ppermute | solution.py:243
  4.1 6.6 %collective-permute-start.5 = (bf16[256,128]{1,0:T(8,128)(2,1)S(1)}, bf16[256,128]{1,0:T(8,128)(2,1)S(1)}, u32[]{:S(2)}, u32[]{:S(2)}) collective-permute-start(bf16[256,128]{1,0:T(8,128)(2,1)S(1)} %get-tuple-element.53), channel_id=1, source_target_pairs={{0,12},{4,0},{8,4},{12,8},{1,13},{5,1},{9,5},{13,9},{2,14},{6,2},{... | collective-permute-start | bytes 196616 | tf_op jit(solution)/shard_map/ppermute | solution.py:243
  6.1 6.2 %collective-permute-start.4 = (bf16[256,128]{1,0:T(8,128)(2,1)S(1)}, bf16[256,128]{1,0:T(8,128)(2,1)S(1)}, u32[]{:S(2)}, u32[]{:S(2)}) collective-permute-start(bf16[256,128]{1,0:T(8,128)(2,1)S(1)} %get-tuple-element.56), channel_id=1, source_target_pairs={{0,8},{4,12},{8,0},{12,4},{1,9},{5,13},{9,1},{13,5},{2,10},{6,14},... | collective-permute-start | bytes 196616 | tf_op jit(solution)/shard_map/ppermute | solution.py:243
  7.1 6.9 %collective-permute-start.3 = (bf16[4,256,128]{2,1,0:T(8,128)(2,1)S(1)}, bf16[4,256,128]{2,1,0:T(8,128)(2,1)S(1)}, u32[]{:S(2)}, u32[]{:S(2)}) collective-permute-start(bf16[4,256,128]{2,1,0:T(8,128)(2,1)S(1)} %copy-done.1), channel_id=1, source_target_pairs={{0,1},{1,0},{2,3},{3,2},{4,5},{5,4},{6,7},{7,6},{8,9},{9,8},{10,11... | collective-permute-start | bytes 786440 | tf_op jit(solution)/shard_map/ppermute | solution.py:90
  8.9 3.6 %copy-start.2 = (bf16[4,2,128]{2,1,0:T(2,128)(2,1)S(1)}, bf16[4,2,128]{2,1,0:T(2,128)(2,1)}, u32[]{:S(2)}) copy-start(bf16[4,2,128]{2,1,0:T(2,128)(2,1)} %refs_2_.7) | copy-start | bytes 6148
  10.6 3.4 %copy-start = (bf16[4,256,256]{2,1,0:T(8,128)(2,1)S(1)}, bf16[4,256,256]{2,1,0:T(8,128)(2,1)}, u32[]{:S(2)}) copy-start(bf16[4,256,256]{2,1,0:T(8,128)(2,1)} %refs_4_.7) | copy-start | bytes 1572868
  12.4 1.6 %collective-permute-start.6 = (bf16[1024,128]{1,0:T(8,128)(2,1)S(1)}, bf16[1024,128]{1,0:T(8,128)(2,1)S(1)}, u32[]{:S(2)}, u32[]{:S(2)}) collective-permute-start(bf16[1024,128]{1,0:T(8,128)(2,1)S(1)} %pad_maximum_fusion), channel_id=1, source_target_pairs={{0,1},{1,0},{2,3},{3,2},{4,5},{5,4},{6,7},{7,6},{8,9},{9,8},{10,11... | collective-permute-start | bytes 786440 | tf_op jit(solution)/shard_map/ppermute | solution.py:90
  12.5 1.5 %collective-permute-start.2 = (bf16[4,2,128]{2,1,0:T(2,128)(2,1)S(1)}, bf16[4,2,128]{2,1,0:T(2,128)(2,1)S(1)}, u32[]{:S(2)}, u32[]{:S(2)}) collective-permute-start(bf16[4,2,128]{2,1,0:T(2,128)(2,1)S(1)} %copy-done.2), channel_id=1, source_target_pairs={{0,1},{1,0},{2,3},{3,2},{4,5},{5,4},{6,7},{7,6},{8,9},{9,8},{10,11... | collective-permute-start | bytes 6152 | tf_op jit(solution)/shard_map/ppermute | solution.py:90
  16.3 6.0 %collective-permute-start.7 = (bf16[256,256]{1,0:T(8,128)(2,1)S(1)}, bf16[256,256]{1,0:T(8,128)(2,1)S(1)}, u32[]{:S(2)}, u32[]{:S(2)}) collective-permute-start(bf16[256,256]{1,0:T(8,128)(2,1)S(1)} %get-tuple-element.32), channel_id=1, source_target_pairs={{0,2},{2,0},{1,3},{3,1},{4,6},{6,4},{5,7},{7,5},{8,10},{10,8},{9,1... | collective-permute-start | bytes 393224 | tf_op jit(solution)/shard_map/ppermute | solution.py:279
  18.6 6.1 %collective-permute-start.11 = (bf16[256,256]{1,0:T(8,128)(2,1)S(1)}, bf16[256,256]{1,0:T(8,128)(2,1)S(1)}, u32[]{:S(2)}, u32[]{:S(2)}) collective-permute-start(bf16[256,256]{1,0:T(8,128)(2,1)S(1)} %get-tuple-element.37), channel_id=1, source_target_pairs={{0,2},{2,0},{1,3},{3,1},{4,6},{6,4},{5,7},{7,5},{8,10},{10,8},{9,1... | collective-permute-start | bytes 393224 | tf_op jit(solution)/shard_map/ppermute | solution.py:279
  22.3 1.3 %collective-permute-start.9 = (bf16[128,256]{1,0:T(8,128)(2,1)S(1)}, bf16[128,256]{1,0:T(8,128)(2,1)S(1)}, u32[]{:S(2)}, u32[]{:S(2)}) collective-permute-start(bf16[128,256]{1,0:T(8,128)(2,1)S(1)} %get-tuple-element.59), channel_id=1, source_target_pairs={{0,1},{1,0},{2,3},{3,2},{4,5},{5,4},{6,7},{7,6},{8,9},{9,8},{10,11... | collective-permute-start | bytes 196616 | tf_op jit(solution)/shard_map/ppermute | solution.py:90
  22.4 1.4 %collective-permute-start.8 = (bf16[128,256]{1,0:T(8,128)(2,1)S(1)}, bf16[128,256]{1,0:T(8,128)(2,1)S(1)}, u32[]{:S(2)}, u32[]{:S(2)}) collective-permute-start(bf16[128,256]{1,0:T(8,128)(2,1)S(1)} %get-tuple-element.60), channel_id=1, source_target_pairs={{0,1},{1,0},{2,3},{3,2},{4,5},{5,4},{6,7},{7,6},{8,9},{9,8},{10,11... | collective-permute-start | bytes 196616 | tf_op jit(solution)/shard_map/ppermute | solution.py:90
  24.7 1.3 %collective-permute-start.13 = (bf16[128,256]{1,0:T(8,128)(2,1)S(1)}, bf16[128,256]{1,0:T(8,128)(2,1)S(1)}, u32[]{:S(2)}, u32[]{:S(2)}) collective-permute-start(bf16[128,256]{1,0:T(8,128)(2,1)S(1)} %get-tuple-element.57), channel_id=1, source_target_pairs={{0,1},{1,0},{2,3},{3,2},{4,5},{5,4},{6,7},{7,6},{8,9},{9,8},{10,11... | collective-permute-start | bytes 196616 | tf_op jit(solution)/shard_map/ppermute | solution.py:90
  24.8 1.4 %collective-permute-start.12 = (bf16[128,256]{1,0:T(8,128)(2,1)S(1)}, bf16[128,256]{1,0:T(8,128)(2,1)S(1)}, u32[]{:S(2)}, u32[]{:S(2)}) collective-permute-start(bf16[128,256]{1,0:T(8,128)(2,1)S(1)} %get-tuple-element.58), channel_id=1, source_target_pairs={{0,1},{1,0},{2,3},{3,2},{4,5},{5,4},{6,7},{7,6},{8,9},{9,8},{10,11... | collective-permute-start | bytes 196616 | tf_op jit(solution)/shard_map/ppermute | solution.py:90
  25.3 9.2 %collective-permute-start.10 = (bf16[256,256]{1,0:T(8,128)(2,1)S(1)}, bf16[256,256]{1,0:T(8,128)(2,1)S(1)}, u32[]{:S(2)}, u32[]{:S(2)}) collective-permute-start(bf16[256,256]{1,0:T(8,128)(2,1)S(1)} %get-tuple-element.40), channel_id=1, source_target_pairs={{0,8},{1,12},{2,1},{3,5},{4,11},{5,15},{6,2},{7,6},{8,9},{9,13},{1... | collective-permute-start | bytes 393224 | tf_op jit(solution)/shard_map/ppermute | solution.py:298
  26.2 8.3 %collective-permute-start.14 = (bf16[256,256]{1,0:T(8,128)(2,1)S(1)}, bf16[256,256]{1,0:T(8,128)(2,1)S(1)}, u32[]{:S(2)}, u32[]{:S(2)}) collective-permute-start(bf16[256,256]{1,0:T(8,128)(2,1)S(1)} %shard_map.58), channel_id=1, source_target_pairs={{0,1},{1,5},{2,8},{3,12},{4,2},{5,6},{6,11},{7,15},{8,0},{9,4},{10... | collective-permute-start | bytes 393224 | tf_op jit(solution)/shard_map/ppermute | solution.py:298
  34.5 1.3 %collective-permute-start.15 = (bf16[256,128]{1,0:T(8,128)(2,1)S(1)}, bf16[256,128]{1,0:T(8,128)(2,1)S(1)}, u32[]{:S(2)}, u32[]{:S(2)}) collective-permute-start(bf16[256,128]{1,0:T(8,128)(2,1)S(1)} %get-tuple-element.52), channel_id=1, source_target_pairs={{0,1},{1,0},{2,3},{3,2},{4,5},{5,4},{6,7},{7,6},{8,9},{9,8},{10,11... | collective-permute-start | bytes 196616 | tf_op jit(solution)/shard_map/ppermute | solution.py:90

commit v8 on v7

--- a/solution.py
+++ b/solution.py
@@ -276,7 +276,8 @@
             )
             heads = carried
             if stage < sections - 1:
-                moved = lax.ppermute(stream, "segment", [(i, (i + 1) % sections) for i in range(sections)])
+                ring = [(i, (i + 1) % sections) for i in range(sections - half)]
+                moved = lax.ppermute(stream, "segment", ring)
                 crossed.append(moved)
         fed = crossed
 
@@ -316,7 +317,8 @@
         functools.partial(place_kernel, plan),
         out_shape=jax.ShapeDtypeStruct((plan.share, rows, width), jnp.bfloat16),
         in_specs=[VMEM] * 2,
-        out_specs=VMEM,
+        out_specs=pl.BlockSpec(memory_space=pl.ANY),
+        scratch_shapes=[pltpu.SemaphoreType.DMA((2,))],
         compiler_params=pltpu.CompilerParams(vmem_limit_bytes=4 << 20),
     )(kept, swap_cores(given))
 
@@ -334,11 +336,26 @@
         out[...] = total.astype(out.dtype)
 
 
-def place_kernel(plan, kept, given, out):
+def place_kernel(plan, kept, given, out, sems):
     half = lax.axis_index("tm") // (plan.count // 2)
     mine = lax.rem(lax.axis_index("chan") + half + lax.axis_index("segment") + 1, 2)
-    for slot in range(plan.share):
-        out[slot] = jnp.where(mine == slot, kept[...], given[...])
+    if plan.share == 2:
+        copies = [
+            pltpu.make_async_copy(kept, out.at[mine], sems.at[0]),
+            pltpu.make_async_copy(given, out.at[1 - mine], sems.at[1]),
+        ]
+        for copy in copies:
+            copy.start()
+        for copy in copies:
+            copy.wait()
+    else:
+        for when, part in ((mine == 0, kept), (mine != 0, given)):
+
+            @pl.when(when)
+            def _(part=part):
+                copy = pltpu.make_async_copy(part, out.at[0], sems.at[0])
+                copy.start()
+                copy.wait()
 
 
 def solution(mesh):

time: 36.7 us -> 36.2 us (0.986); the launches traced: 36.5 us -> 35.5 us
  waiting for transfers between devices: 16.5 us -> 14.1 us
  starting transfers between devices: 10.6 us -> 12 us
    ppermute x2, waiting for transfers between devices: 4.51 us -> 1.61 us  [shards(): moved = lax.ppermute(stream, 'segment', ring)]
    ppermute x2, starting transfers between devices: 0.14 us -> 1.74 us  [shards(): moved = lax.ppermute(stream, 'segment', ring)]
  transfers between devices with their start and end apart: 16 -> 16, of which waited for: 10 -> 9; matrix products, arithmetic and copies ran while one was open for 10% -> 10% of each run, Pallas kernels for 6% -> 6%
where the time goes in v8:
time: 36.2 us; the launch traced here: 35.5 us
  waiting for transfers between devices  14.1 us (39%)
  starting transfers between devices  12 us (33%)
  Pallas kernels  5.18 us (14%)
  local copies, waits for them, and re-layouts  4.03 us (11%)
    ppermute x2, waiting for transfers between devices, shards(): lax.ppermute(payload, ('tm', 'segment', 'chan'), sorted(((number(a), numb...  7.1 us
    ppermute x3, starting transfers between devices, shards(): lax.ppermute(blocks[turn], 'tm', [(i, (i + turn) % count) for i in range(...  6.11 us
    pallas_call x4, Pallas kernels, run_section(): pl.pallas_call(functools.partial(section_kernel, stage, half, plan, lags,...  4.48 us
    ppermute x9, waiting for transfers between devices, swap_cores(): return lax.ppermute(block, 'chan', [(0, 1), (1, 0)])  3.64 us
    ppermute x9, starting transfers between devices, swap_cores(): return lax.ppermute(block, 'chan', [(0, 1), (1, 0)])  2.23 us
    ppermute x2, starting transfers between devices, shards(): lax.ppermute(payload, ('tm', 'segment', 'chan'), sorted(((number(a), numb...  1.91 us
    ppermute x2, starting transfers between devices, shards(): moved = lax.ppermute(stream, 'segment', ring)  1.74 us
    ppermute x3, waiting for transfers between devices, shards(): lax.ppermute(blocks[turn], 'tm', [(i, (i + turn) % count) for i in range(...  1.74 us
  transfers between devices with their start and end apart: 16, of which 9 were waited for; matrix products, arithmetic and copies ran while one was open for 10% of the time, Pallas kernels for 6%

profile of v8, /device:TPU:0, one launch (start us, length us, event | category | flops | bytes accessed | tf_op | source)
XLA Modules:
  0.0 35.5 jit_solution(17524474176829438133)
XLA Ops:
  0.0 0.0 copy-start.3
  0.0 0.5 %collective-permute-start.1 = (bf16[4,512,2,128]{3,2,1,0:T(2,128)(2,1)}, bf16[4,512,2,128]{3,2,1,0:T(2,128)(2,1)}, u32[]{:S(2)}, u32[]{:S(2)}) collective-permute-start(bf16[4,512,2,128]{3,2,1,0:T(2,128)(2,1)} %param.6), channel_id=1, source_target_pairs={{0,1},{1,0},{2,3},{3,2},{4,5},{5,4},{6,7},{7,6},{8,9},{9,8},{10,11... | collective-permute-start | bytes 3145736 | tf_op jit(solution)/shard_map/ppermute | solution.py:90
  0.5 0.5 %copy-done.3 = bf16[4,256,128]{2,1,0:T(8,128)(2,1)S(1)} copy-done((bf16[4,256,128]{2,1,0:T(8,128)(2,1)S(1)}, bf16[4,256,128]{2,1,0:T(8,128)(2,1)}, u32[]{:S(2)}) %copy-start.3) | copy-done | bytes 262168
  1.0 0.0 copy-start.1
  1.0 3.1 %collective-permute-start = (bf16[256,128]{1,0:T(8,128)(2,1)S(1)}, bf16[256,128]{1,0:T(8,128)(2,1)S(1)}, u32[]{:S(2)}, u32[]{:S(2)}) collective-permute-start(bf16[256,128]{1,0:T(8,128)(2,1)S(1)} %get-tuple-element.55), channel_id=1, source_target_pairs={{0,4},{4,8},{8,12},{12,0},{1,5},{5,9},{9,13},{13,1},{2,6},{6,10},{... | collective-permute-start | bytes 196616 | tf_op jit(solution)/shard_map/ppermute | solution.py:243
  4.1 2.1 %collective-permute-start.5 = (bf16[256,128]{1,0:T(8,128)(2,1)S(1)}, bf16[256,128]{1,0:T(8,128)(2,1)S(1)}, u32[]{:S(2)}, u32[]{:S(2)}) collective-permute-start(bf16[256,128]{1,0:T(8,128)(2,1)S(1)} %get-tuple-element.53), channel_id=1, source_target_pairs={{0,12},{4,0},{8,4},{12,8},{1,13},{5,1},{9,5},{13,9},{2,14},{6,2},{... | collective-permute-start | bytes 196616 | tf_op jit(solution)/shard_map/ppermute | solution.py:243
  6.1 0.9 %collective-permute-start.4 = (bf16[256,128]{1,0:T(8,128)(2,1)S(1)}, bf16[256,128]{1,0:T(8,128)(2,1)S(1)}, u32[]{:S(2)}, u32[]{:S(2)}) collective-permute-start(bf16[256,128]{1,0:T(8,128)(2,1)S(1)} %get-tuple-element.56), channel_id=1, source_target_pairs={{0,8},{4,12},{8,0},{12,4},{1,9},{5,13},{9,1},{13,5},{2,10},{6,14},... | collective-permute-start | bytes 196616 | tf_op jit(solution)/shard_map/ppermute | solution.py:243
  7.1 0.0 copy-done.1
  7.1 0.0 collective-permute-start.3
  7.1 1.7 %reshape.6.refs_0_ = bf16[4,512,256]{2,1,0:T(8,128)(2,1)S(1)} reshape(bf16[4,512,2,128]{3,2,1,0:T(2,128)(2,1)} %param.6) | data formatting | bytes 2097152 | tf_op jit(solution)/shard_map/reshape | solution.py:244
  8.8 0.0 collective-permute-done.1
  8.9 0.0 copy-start.2
  8.9 1.7 %reshape.7.refs_1_ = bf16[4,512,256]{2,1,0:T(8,128)(2,1)S(1)} reshape(bf16[4,512,2,128]{3,2,1,0:T(2,128)(2,1)} %collective-permute-done.1) | data formatting | bytes 2097152 | tf_op jit(solution)/shard_map/reshape | solution.py:245
  10.6 0.0 copy-start
  10.6 0.0 collective-permute-done.refs_8_
  10.6 0.0 collective-permute-done.5.refs_10_
  10.6 1.7 %collective-permute-done.4.refs_9_ = bf16[256,128]{1,0:T(8,128)(2,1)S(1)} collective-permute-done((bf16[256,128]{1,0:T(8,128)(2,1)S(1)}, bf16[256,128]{1,0:T(8,128)(2,1)S(1)}, u32[]{:S(2)}, u32[]{:S(2)}) %collective-permute-start.4) | collective-permute-done | bytes 65568 | tf_op jit(solution)/shard_map/ppermute | solution.py:243
  12.4 0.1 collective-permute-start.6
  12.5 0.0 copy-done.2
  12.5 0.5 %collective-permute-start.2 = (bf16[4,2,128]{2,1,0:T(2,128)(2,1)S(1)}, bf16[4,2,128]{2,1,0:T(2,128)(2,1)S(1)}, u32[]{:S(2)}, u32[]{:S(2)}) collective-permute-start(bf16[4,2,128]{2,1,0:T(2,128)(2,1)S(1)} %copy-done.2), channel_id=1, source_target_pairs={{0,1},{1,0},{2,3},{3,2},{4,5},{5,4},{6,7},{7,6},{8,9},{9,8},{10,11... | collective-permute-start | bytes 6152 | tf_op jit(solution)/shard_map/ppermute | solution.py:90
  13.0 1.0 %collective-permute-done.2.refs_3_ = bf16[4,2,128]{2,1,0:T(2,128)(2,1)S(1)} collective-permute-done((bf16[4,2,128]{2,1,0:T(2,128)(2,1)S(1)}, bf16[4,2,128]{2,1,0:T(2,128)(2,1)S(1)}, u32[]{:S(2)}, u32[]{:S(2)}) %collective-permute-start.2) | collective-permute-done | bytes 2080 | tf_op jit(solution)/shard_map/ppermute | solution.py:90
  14.0 0.0 collective-permute-done.3.refs_6_
  14.0 0.0 collective-permute-done.6.refs_11_
  14.0 0.0 copy-done
  14.0 2.2 %shard_map.55 = (bf16[256,256]{1,0:T(8,128)(2,1)S(1)}, bf16[256,256]{1,0:T(8,128)(2,1)S(1)}, bf16[32,256]{1,0:T(8,128)(2,1)S(1)}, bf16[256,256]{1,0:T(8,128)(2,1...) custom-call(bf16[4,512,256]{2,1,0:T(8,128)(2,1)S(1)} %reshape.6.refs_0_, ...), custom_call_target="tpu_custom_call" | custom-call | flops 1 | bytes 1 | tf_op jit(solution)/shard_map/pallas_call | solution.py:214
  16.3 0.1 collective-permute-start.7
  16.3 2.2 %shard_map.56 = (bf16[256,256]{1,0:T(8,128)(2,1)S(1)}, bf16[256,256]{1,0:T(8,128)(2,1)S(1)}) custom-call(bf16[4,512,256]{2,1,0:T(8,128)(2,1)S(1)} %reshape.6.refs_0_, bf16[4,512,256]{2,1,0:T(8,128)(2,1)S(1)} %reshape.7.refs_1_, bf16[4,2,128]{2,1,0:T(2,128)(2,1)S(1)} %copy-done.2, bf16[4,2,128]{2,1,0:T(2,128)(2,1)S(1)} %collective-permute-done.2.refs_3_, ...), custom_call_target="tpu_custom_call" | custom-call | flops 1 | bytes 1 | tf_op jit(solution)/shard_map/pallas_call | solution.py:214
  18.6 1.7 %collective-permute-start.11 = (bf16[256,256]{1,0:T(8,128)(2,1)S(1)}, bf16[256,256]{1,0:T(8,128)(2,1)S(1)}, u32[]{:S(2)}, u32[]{:S(2)}) collective-permute-start(bf16[256,256]{1,0:T(8,128)(2,1)S(1)} %get-tuple-element.37), channel_id=1, source_target_pairs={{0,2},{1,3},{4,6},{5,7},{8,10},{9,11},{12,14},{13,15},{16,18},{17,... | collective-permute-start | bytes 393224 | tf_op jit(solution)/shard_map/ppermute | solution.py:280
  20.3 1.6 %collective-permute-done.7.refs_7_ = bf16[256,256]{1,0:T(8,128)(2,1)S(1)} collective-permute-done((bf16[256,256]{1,0:T(8,128)(2,1)S(1)}, bf16[256,256]{1,0:T(8,128)(2,1)S(1)}, u32[]{:S(2)}, u32[]{:S(2)}) %collective-permute-start.7) | collective-permute-done | bytes 131104 | tf_op jit(solution)/shard_map/ppermute | solution.py:280
  21.9 0.1 collective-permute-start.9
  22.0 0.5 %collective-permute-start.8 = (bf16[128,256]{1,0:T(8,128)(2,1)S(1)}, bf16[128,256]{1,0:T(8,128)(2,1)S(1)}, u32[]{:S(2)}, u32[]{:S(2)}) collective-permute-start(bf16[128,256]{1,0:T(8,128)(2,1)S(1)} %get-tuple-element.60), channel_id=1, source_target_pairs={{0,1},{1,0},{2,3},{3,2},{4,5},{5,4},{6,7},{7,6},{8,9},{9,8},{10,11... | collective-permute-start | bytes 196616 | tf_op jit(solution)/shard_map/ppermute | solution.py:90
  22.5 0.7 %collective-permute-done.9.refs_9_ = bf16[128,256]{1,0:T(8,128)(2,1)S(1)} collective-permute-done((bf16[128,256]{1,0:T(8,128)(2,1)S(1)}, bf16[128,256]{1,0:T(8,128)(2,1)S(1)}, u32[]{:S(2)}, u32[]{:S(2)}) %collective-permute-start.9) | collective-permute-done | bytes 65568 | tf_op jit(solution)/shard_map/ppermute | solution.py:90
  23.2 0.2 collective-permute-done.8.refs_8_
  23.4 0.0 collective-permute-done.11.refs_7_
  23.4 0.4 %collective-permute-start.13 = (bf16[128,256]{1,0:T(8,128)(2,1)S(1)}, bf16[128,256]{1,0:T(8,128)(2,1)S(1)}, u32[]{:S(2)}, u32[]{:S(2)}) collective-permute-start(bf16[128,256]{1,0:T(8,128)(2,1)S(1)} %get-tuple-element.57), channel_id=1, source_target_pairs={{0,1},{1,0},{2,3},{3,2},{4,5},{5,4},{6,7},{7,6},{8,9},{9,8},{10,11... | collective-permute-start | bytes 196616 | tf_op jit(solution)/shard_map/ppermute | solution.py:90
  23.8 0.2 collective-permute-start.12
  24.0 0.6 %collective-permute-start.10 = (bf16[256,256]{1,0:T(8,128)(2,1)S(1)}, bf16[256,256]{1,0:T(8,128)(2,1)S(1)}, u32[]{:S(2)}, u32[]{:S(2)}) collective-permute-start(bf16[256,256]{1,0:T(8,128)(2,1)S(1)} %get-tuple-element.40), channel_id=1, source_target_pairs={{0,8},{1,12},{2,1},{3,5},{4,11},{5,15},{6,2},{7,6},{8,9},{9,13},{1... | collective-permute-start | bytes 393224 | tf_op jit(solution)/shard_map/ppermute | solution.py:299
  24.6 0.1 collective-permute-done.13.refs_9_
  24.7 0.4 collective-permute-done.12.refs_8_
  25.1 1.3 %collective-permute-start.14 = (bf16[256,256]{1,0:T(8,128)(2,1)S(1)}, bf16[256,256]{1,0:T(8,128)(2,1)S(1)}, u32[]{:S(2)}, u32[]{:S(2)}) collective-permute-start(bf16[256,256]{1,0:T(8,128)(2,1)S(1)} %shard_map.58), channel_id=1, source_target_pairs={{0,1},{1,5},{2,8},{3,12},{4,2},{5,6},{6,11},{7,15},{8,0},{9,4},{10... | collective-permute-start | bytes 393224 | tf_op jit(solution)/shard_map/ppermute | solution.py:299
  26.4 7.1 %collective-permute-done.10.refs_0_ = bf16[256,256]{1,0:T(8,128)(2,1)S(1)} collective-permute-done((bf16[256,256]{1,0:T(8,128)(2,1)S(1)}, bf16[256,256]{1,0:T(8,128)(2,1)S(1)}, u32[]{:S(2)}, u32[]{:S(2)}) %collective-permute-start.10) | collective-permute-done | bytes 131104 | tf_op jit(solution)/shard_map/ppermute | solution.py:299
  33.5 0.0 collective-permute-done.14.refs_1_
  33.5 0.1 collective-permute-start.15
  33.6 1.2 %collective-permute-done.15.given = bf16[256,128]{1,0:T(8,128)(2,1)S(1)} collective-permute-done((bf16[256,128]{1,0:T(8,128)(2,1)S(1)}, bf16[256,128]{1,0:T(8,128)(2,1)S(1)}, u32[]{:S(2)}, u32[]{:S(2)}) %collective-permute-start.15) | collective-permute-done | bytes 65568 | tf_op jit(solution)/shard_map/ppermute | solution.py:90
  34.8 0.7 %shard_map.60 = bf16[2,256,128]{2,1,0:T(8,128)(2,1)} custom-call(bf16[256,128]{1,0:T(8,128)(2,1)S(1)} %get-tuple-element.51.kept, bf16[256,128]{1,0:T(8,128)(2,1)S(1)} %collective-permute-done.15.given), custom_call_target="tpu_custom_call" | custom-call | tf_op jit(solution)/shard_map/pallas_call | solution.py:316
  (7 shorter events, 0.1 us)
Async XLA Ops:
  0.0 0.9 %copy-start.3 = (bf16[4,256,128]{2,1,0:T(8,128)(2,1)S(1)}, bf16[4,256,128]{2,1,0:T(8,128)(2,1)}, u32[]{:S(2)}) copy-start(bf16[4,256,128]{2,1,0:T(8,128)(2,1)} %param.5) | copy-start | bytes 786436
  0.0 8.8 %collective-permute-start.1 = (bf16[4,512,2,128]{3,2,1,0:T(2,128)(2,1)}, bf16[4,512,2,128]{3,2,1,0:T(2,128)(2,1)}, u32[]{:S(2)}, u32[]{:S(2)}) collective-permute-start(bf16[4,512,2,128]{3,2,1,0:T(2,128)(2,1)} %param.6), channel_id=1, source_target_pairs={{0,1},{1,0},{2,3},{3,2},{4,5},{5,4},{6,7},{7,6},{8,9},{9,8},{10,11... | collective-permute-start | bytes 3145736 | tf_op jit(solution)/shard_map/ppermute | solution.py:90
  1.0 6.1 %copy-start.1 = (bf16[4,256,128]{2,1,0:T(8,128)(2,1)S(1)}, bf16[4,256,128]{2,1,0:T(8,128)(2,1)}, u32[]{:S(2)}) copy-start(bf16[4,256,128]{2,1,0:T(8,128)(2,1)} %refs_5_.7) | copy-start | bytes 786436
  1.0 9.7 %collective-permute-start = (bf16[256,128]{1,0:T(8,128)(2,1)S(1)}, bf16[256,128]{1,0:T(8,128)(2,1)S(1)}, u32[]{:S(2)}, u32[]{:S(2)}) collective-permute-start(bf16[256,128]{1,0:T(8,128)(2,1)S(1)} %get-tuple-element.55), channel_id=1, source_target_pairs={{0,4},{4,8},{8,12},{12,0},{1,5},{5,9},{9,13},{13,1},{2,6},{6,10},{... | collective-permute-start | bytes 196616 | tf_op jit(solution)/shard_map/ppermute | solution.py:243
  4.1 6.6 %collective-permute-start.5 = (bf16[256,128]{1,0:T(8,128)(2,1)S(1)}, bf16[256,128]{1,0:T(8,128)(2,1)S(1)}, u32[]{:S(2)}, u32[]{:S(2)}) collective-permute-start(bf16[256,128]{1,0:T(8,128)(2,1)S(1)} %get-tuple-element.53), channel_id=1, source_target_pairs={{0,12},{4,0},{8,4},{12,8},{1,13},{5,1},{9,5},{13,9},{2,14},{6,2},{... | collective-permute-start | bytes 196616 | tf_op jit(solution)/shard_map/ppermute | solution.py:243
  6.1 6.2 %collective-permute-start.4 = (bf16[256,128]{1,0:T(8,128)(2,1)S(1)}, bf16[256,128]{1,0:T(8,128)(2,1)S(1)}, u32[]{:S(2)}, u32[]{:S(2)}) collective-permute-start(bf16[256,128]{1,0:T(8,128)(2,1)S(1)} %get-tuple-element.56), channel_id=1, source_target_pairs={{0,8},{4,12},{8,0},{12,4},{1,9},{5,13},{9,1},{13,5},{2,10},{6,14},... | collective-permute-start | bytes 196616 | tf_op jit(solution)/shard_map/ppermute | solution.py:243
  7.1 6.9 %collective-permute-start.3 = (bf16[4,256,128]{2,1,0:T(8,128)(2,1)S(1)}, bf16[4,256,128]{2,1,0:T(8,128)(2,1)S(1)}, u32[]{:S(2)}, u32[]{:S(2)}) collective-permute-start(bf16[4,256,128]{2,1,0:T(8,128)(2,1)S(1)} %copy-done.1), channel_id=1, source_target_pairs={{0,1},{1,0},{2,3},{3,2},{4,5},{5,4},{6,7},{7,6},{8,9},{9,8},{10,11... | collective-permute-start | bytes 786440 | tf_op jit(solution)/shard_map/ppermute | solution.py:90
  8.9 3.6 %copy-start.2 = (bf16[4,2,128]{2,1,0:T(2,128)(2,1)S(1)}, bf16[4,2,128]{2,1,0:T(2,128)(2,1)}, u32[]{:S(2)}) copy-start(bf16[4,2,128]{2,1,0:T(2,128)(2,1)} %refs_2_.7) | copy-start | bytes 6148
  10.6 3.4 %copy-start = (bf16[4,256,256]{2,1,0:T(8,128)(2,1)S(1)}, bf16[4,256,256]{2,1,0:T(8,128)(2,1)}, u32[]{:S(2)}) copy-start(bf16[4,256,256]{2,1,0:T(8,128)(2,1)} %refs_4_.7) | copy-start | bytes 1572868
  12.4 1.6 %collective-permute-start.6 = (bf16[1024,128]{1,0:T(8,128)(2,1)S(1)}, bf16[1024,128]{1,0:T(8,128)(2,1)S(1)}, u32[]{:S(2)}, u32[]{:S(2)}) collective-permute-start(bf16[1024,128]{1,0:T(8,128)(2,1)S(1)} %pad_maximum_fusion), channel_id=1, source_target_pairs={{0,1},{1,0},{2,3},{3,2},{4,5},{5,4},{6,7},{7,6},{8,9},{9,8},{10,11... | collective-permute-start | bytes 786440 | tf_op jit(solution)/shard_map/ppermute | solution.py:90
  12.5 1.5 %collective-permute-start.2 = (bf16[4,2,128]{2,1,0:T(2,128)(2,1)S(1)}, bf16[4,2,128]{2,1,0:T(2,128)(2,1)S(1)}, u32[]{:S(2)}, u32[]{:S(2)}) collective-permute-start(bf16[4,2,128]{2,1,0:T(2,128)(2,1)S(1)} %copy-done.2), channel_id=1, source_target_pairs={{0,1},{1,0},{2,3},{3,2},{4,5},{5,4},{6,7},{7,6},{8,9},{9,8},{10,11... | collective-permute-start | bytes 6152 | tf_op jit(solution)/shard_map/ppermute | solution.py:90
  16.3 5.6 %collective-permute-start.7 = (bf16[256,256]{1,0:T(8,128)(2,1)S(1)}, bf16[256,256]{1,0:T(8,128)(2,1)S(1)}, u32[]{:S(2)}, u32[]{:S(2)}) collective-permute-start(bf16[256,256]{1,0:T(8,128)(2,1)S(1)} %get-tuple-element.32), channel_id=1, source_target_pairs={{0,2},{2,0},{1,3},{3,1},{4,6},{6,4},{5,7},{7,5},{8,10},{10,8},{9,1... | collective-permute-start | bytes 393224 | tf_op jit(solution)/shard_map/ppermute | solution.py:280
  18.6 4.8 %collective-permute-start.11 = (bf16[256,256]{1,0:T(8,128)(2,1)S(1)}, bf16[256,256]{1,0:T(8,128)(2,1)S(1)}, u32[]{:S(2)}, u32[]{:S(2)}) collective-permute-start(bf16[256,256]{1,0:T(8,128)(2,1)S(1)} %get-tuple-element.37), channel_id=1, source_target_pairs={{0,2},{1,3},{4,6},{5,7},{8,10},{9,11},{12,14},{13,15},{16,18},{17,... | collective-permute-start | bytes 393224 | tf_op jit(solution)/shard_map/ppermute | solution.py:280
  21.9 1.3 %collective-permute-start.9 = (bf16[128,256]{1,0:T(8,128)(2,1)S(1)}, bf16[128,256]{1,0:T(8,128)(2,1)S(1)}, u32[]{:S(2)}, u32[]{:S(2)}) collective-permute-start(bf16[128,256]{1,0:T(8,128)(2,1)S(1)} %get-tuple-element.59), channel_id=1, source_target_pairs={{0,1},{1,0},{2,3},{3,2},{4,5},{5,4},{6,7},{7,6},{8,9},{9,8},{10,11... | collective-permute-start | bytes 196616 | tf_op jit(solution)/shard_map/ppermute | solution.py:90
  22.0 1.4 %collective-permute-start.8 = (bf16[128,256]{1,0:T(8,128)(2,1)S(1)}, bf16[128,256]{1,0:T(8,128)(2,1)S(1)}, u32[]{:S(2)}, u32[]{:S(2)}) collective-permute-start(bf16[128,256]{1,0:T(8,128)(2,1)S(1)} %get-tuple-element.60), channel_id=1, source_target_pairs={{0,1},{1,0},{2,3},{3,2},{4,5},{5,4},{6,7},{7,6},{8,9},{9,8},{10,11... | collective-permute-start | bytes 196616 | tf_op jit(solution)/shard_map/ppermute | solution.py:90
  23.4 1.3 %collective-permute-start.13 = (bf16[128,256]{1,0:T(8,128)(2,1)S(1)}, bf16[128,256]{1,0:T(8,128)(2,1)S(1)}, u32[]{:S(2)}, u32[]{:S(2)}) collective-permute-start(bf16[128,256]{1,0:T(8,128)(2,1)S(1)} %get-tuple-element.57), channel_id=1, source_target_pairs={{0,1},{1,0},{2,3},{3,2},{4,5},{5,4},{6,7},{7,6},{8,9},{9,8},{10,11... | collective-permute-start | bytes 196616 | tf_op jit(solution)/shard_map/ppermute | solution.py:90
  23.8 1.3 %collective-permute-start.12 = (bf16[128,256]{1,0:T(8,128)(2,1)S(1)}, bf16[128,256]{1,0:T(8,128)(2,1)S(1)}, u32[]{:S(2)}, u32[]{:S(2)}) collective-permute-start(bf16[128,256]{1,0:T(8,128)(2,1)S(1)} %get-tuple-element.58), channel_id=1, source_target_pairs={{0,1},{1,0},{2,3},{3,2},{4,5},{5,4},{6,7},{7,6},{8,9},{9,8},{10,11... | collective-permute-start | bytes 196616 | tf_op jit(solution)/shard_map/ppermute | solution.py:90
  24.0 9.5 %collective-permute-start.10 = (bf16[256,256]{1,0:T(8,128)(2,1)S(1)}, bf16[256,256]{1,0:T(8,128)(2,1)S(1)}, u32[]{:S(2)}, u32[]{:S(2)}) collective-permute-start(bf16[256,256]{1,0:T(8,128)(2,1)S(1)} %get-tuple-element.40), channel_id=1, source_target_pairs={{0,8},{1,12},{2,1},{3,5},{4,11},{5,15},{6,2},{7,6},{8,9},{9,13},{1... | collective-permute-start | bytes 393224 | tf_op jit(solution)/shard_map/ppermute | solution.py:299
  25.1 8.4 %collective-permute-start.14 = (bf16[256,256]{1,0:T(8,128)(2,1)S(1)}, bf16[256,256]{1,0:T(8,128)(2,1)S(1)}, u32[]{:S(2)}, u32[]{:S(2)}) collective-permute-start(bf16[256,256]{1,0:T(8,128)(2,1)S(1)} %shard_map.58), channel_id=1, source_target_pairs={{0,1},{1,5},{2,8},{3,12},{4,2},{5,6},{6,11},{7,15},{8,0},{9,4},{10... | collective-permute-start | bytes 393224 | tf_op jit(solution)/shard_map/ppermute | solution.py:299
  33.5 1.3 %collective-permute-start.15 = (bf16[256,128]{1,0:T(8,128)(2,1)S(1)}, bf16[256,128]{1,0:T(8,128)(2,1)S(1)}, u32[]{:S(2)}, u32[]{:S(2)}) collective-permute-start(bf16[256,128]{1,0:T(8,128)(2,1)S(1)} %get-tuple-element.52), channel_id=1, source_target_pairs={{0,1},{1,0},{2,3},{3,2},{4,5},{5,4},{6,7},{7,6},{8,9},{9,8},{10,11... | collective-permute-start | bytes 196616 | tf_op jit(solution)/shard_map/ppermute | solution.py:90

commit v9 on v8

--- a/solution.py
+++ b/solution.py
@@ -99,12 +99,13 @@
     if half:
         heads, refs = refs[:layers], refs[layers:]
     earlier, refs = refs[:n_earlier], refs[n_earlier:]
-    skip_outs, refs = refs[: plan.blocks], refs[plan.blocks :]
+    skip_outs, refs = (refs[: plan.blocks], refs[plan.blocks :]) if last else (refs[:1], refs[1:])
     if not last:
         stream_out, refs = refs[0], refs[1:]
     if not half:
         tails, refs = refs[:layers], refs[layers:]
-    streams, units, out_buf = refs[:layers], refs[layers], refs[layers + 1]
+    streams, out_buf = refs[:layers], refs[layers]
+    units = refs[layers + 1] if last else skip_outs[0]
     core, place = lax.axis_index("chan"), lax.axis_index("tm")
     total = units.shape[1]
     own_rows = pl.ds(pl.multiple_of(core * width, width), width)
@@ -179,23 +180,39 @@
         if not half:
             for layer in range(layers):
                 tails[layer][...] = streams[layer][pl.ds(total, lags[layer % 4]), :]
-        for index, out in enumerate(skip_outs):
-            rows = out.shape[0]
-            t = plan.time_block(place, core, half, index) - half * (plan.count // 2)
-            at = pl.multiple_of(jnp.clip(t, 0, total // rows - 1) * rows, rows)
-            acc = jnp.zeros((rows, depth), jnp.float32)
-            for layer in range(layers):
-                unit = units[layer, pl.ds(at, rows), :]
-                skip = jnp.concatenate(
-                    [
-                        jnp.concatenate([part[layer, own_rows, :], part[layer, other_rows, :]], 0)
-                        for part in (own_skip, other_skip)
-                    ],
-                    1,
-                )
-                acc += jnp.dot(unit, skip, preferred_element_type=jnp.float32)
-            out[:, own_rows] = acc[:, :width].astype(out.dtype)
-            out[:, other_rows] = acc[:, width:].astype(out.dtype)
+        if last:
+            emit(half, plan, units, own_skip, other_skip, skip_outs)
+
+
+def emit(half, plan, units, own_skip, other_skip, skip_outs):
+    core, place = lax.axis_index("chan"), lax.axis_index("tm")
+    layers, total, depth = units.shape
+    width = depth // 2
+    own_rows = pl.ds(pl.multiple_of(core * width, width), width)
+    other_rows = pl.ds(pl.multiple_of((1 - core) * width, width), width)
+    for index, out in enumerate(skip_outs):
+        rows = out.shape[0]
+        t = plan.time_block(place, core, half, index) - half * (plan.count // 2)
+        at = pl.multiple_of(jnp.clip(t, 0, total // rows - 1) * rows, rows)
+        acc = jnp.zeros((rows, depth), jnp.float32)
+        for layer in range(layers):
+            unit = units[layer, pl.ds(at, rows), :]
+            skip = jnp.concatenate(
+                [
+                    jnp.concatenate([part[layer, own_rows, :], part[layer, other_rows, :]], 0)
+                    for part in (own_skip, other_skip)
+                ],
+                1,
+            )
+            acc += jnp.dot(unit, skip, preferred_element_type=jnp.float32)
+        out[:, own_rows] = acc[:, :width].astype(out.dtype)
+        out[:, other_rows] = acc[:, width:].astype(out.dtype)
+
+
+def skip_kernel(stage, half, plan, own_skip, other_skip, units, *skip_outs):
+    @pl.when(lax.axis_index("segment") == stage)
+    def _():
+        emit(half, plan, units, own_skip, other_skip, skip_outs)
 
 
 def run_section(stage, half, plan, lags, weights, inputs, heads, earlier, rows):
@@ -203,13 +220,16 @@
     layers, depth = res_weight.shape[:2]
     total = rows * plan.count // 2
     last = stage == plan.sections - 1
-    outs = [jax.ShapeDtypeStruct((rows, depth), jnp.bfloat16)] * plan.blocks
+    block_shapes = [jax.ShapeDtypeStruct((rows, depth), jnp.bfloat16)] * plan.blocks
+    outs = list(block_shapes) if last else [jax.ShapeDtypeStruct((layers, total, depth), jnp.bfloat16)]
     if not last:
         outs.append(jax.ShapeDtypeStruct((total // 2, depth), jnp.bfloat16))
     if not half:
         outs += [jax.ShapeDtypeStruct((lags[layer % 4], depth), jnp.bfloat16) for layer in range(layers)]
     scratch = [pltpu.VMEM((lags[layer % 4] + total, depth), jnp.bfloat16) for layer in range(layers)]
-    scratch += [pltpu.VMEM((layers, total, depth), jnp.bfloat16), pltpu.VMEM((total, depth), jnp.bfloat16)]
+    scratch.append(pltpu.VMEM((total, depth), jnp.bfloat16))
+    if last:
+        scratch.append(pltpu.VMEM((layers, total, depth), jnp.bfloat16))
     held = 2 * depth * (sum(lags) * 3 + 13 * total)
     got = pl.pallas_call(
         functools.partial(section_kernel, stage, half, plan, lags, len(inputs), len(earlier), last),
@@ -220,7 +240,18 @@
         compiler_params=pltpu.CompilerParams(vmem_limit_bytes=held + (12 << 20)),
         cost_estimate=pl.CostEstimate(flops=1, bytes_accessed=1, transcendentals=0),
     )(*weights, *inputs, *heads, *earlier)
-    blocks, got = got[: plan.blocks], got[plan.blocks :]
+    if last:
+        blocks, got = got[: plan.blocks], got[plan.blocks :]
+    else:
+        blocks = pl.pallas_call(
+            functools.partial(skip_kernel, stage, half, plan),
+            out_shape=block_shapes,
+            in_specs=[VMEM] * 3,
+            out_specs=[VMEM] * plan.blocks,
+            compiler_params=pltpu.CompilerParams(vmem_limit_bytes=held + (12 << 20)),
+            cost_estimate=pl.CostEstimate(flops=1, bytes_accessed=1, transcendentals=0),
+        )(*weights[5:7], got[0])
+        got = got[1:]
     stream = None
     if not last:
         stream, got = got[0], got[1:]

time: 36.2 us -> 35.9 us (level)
  waiting for transfers between devices: 14.1 us -> 13.1 us
  starting transfers between devices: 12 us -> 12.7 us
    ppermute x9, waiting for transfers between devices: 3.64 us -> 2.94 us  [swap_cores(): return lax.ppermute(block, 'chan', [(0, 1), (1, 0)])]
    pallas_call x0 -> x2, Pallas kernels: none -> 0.62 us  [run_section(): pl.pallas_call(functools.partial(skip_kernel, stage, half, plan), out_sha...]
    pallas_call x4, Pallas kernels: 4.48 us -> 3.93 us  [run_section(): pl.pallas_call(functools.partial(section_kernel, stage, half, plan, lags,...]
    ppermute x2, starting transfers between devices: 1.91 us -> 2.36 us  [shards(): lax.ppermute(payload, ('tm', 'segment', 'chan'), sorted(((number(a), numb...]
  transfers between devices with their start and end apart: 16 -> 16, of which waited for: 9 -> 8; matrix products, arithmetic and copies ran while one was open for 10% -> 10% of each run, Pallas kernels for 6% -> 7%
where the time goes in v9:
time: 35.9 us; the launch traced here: 35.3 us
  waiting for transfers between devices  13.1 us (36%)
  starting transfers between devices  12.7 us (35%)
  Pallas kernels  5.26 us (15%)
  local copies, waits for them, and re-layouts  4.03 us (11%)
    ppermute x2, waiting for transfers between devices, shards(): lax.ppermute(payload, ('tm', 'segment', 'chan'), sorted(((number(a), numb...  6.77 us
    ppermute x3, starting transfers between devices, shards(): lax.ppermute(blocks[turn], 'tm', [(i, (i + turn) % count) for i in range(...  6.11 us
    pallas_call x4, Pallas kernels, run_section(): pl.pallas_call(functools.partial(section_kernel, stage, half, plan, lags,...  3.93 us
    ppermute x9, waiting for transfers between devices, swap_cores(): return lax.ppermute(block, 'chan', [(0, 1), (1, 0)])  2.94 us
    ppermute x2, starting transfers between devices, shards(): lax.ppermute(payload, ('tm', 'segment', 'chan'), sorted(((number(a), numb...  2.36 us
    ppermute x9, starting transfers between devices, swap_cores(): return lax.ppermute(block, 'chan', [(0, 1), (1, 0)])  2.23 us
    ppermute x2, starting transfers between devices, shards(): moved = lax.ppermute(stream, 'segment', ring)  2.02 us
    ppermute x3, waiting for transfers between devices, shards(): lax.ppermute(blocks[turn], 'tm', [(i, (i + turn) % count) for i in range(...  1.74 us
  transfers between devices with their start and end apart: 16, of which 8 were waited for; matrix products, arithmetic and copies ran while one was open for 10% of the time, Pallas kernels for 7%

profile of v9, /device:TPU:0, one launch (start us, length us, event | category | flops | bytes accessed | tf_op | source)
XLA Modules:
  0.0 35.3 jit_solution(11619023511266114371)
XLA Ops:
  0.0 0.0 copy-start.3
  0.0 0.5 %collective-permute-start.1 = (bf16[4,512,2,128]{3,2,1,0:T(2,128)(2,1)}, bf16[4,512,2,128]{3,2,1,0:T(2,128)(2,1)}, u32[]{:S(2)}, u32[]{:S(2)}) collective-permute-start(bf16[4,512,2,128]{3,2,1,0:T(2,128)(2,1)} %param.6), channel_id=1, source_target_pairs={{0,1},{1,0},{2,3},{3,2},{4,5},{5,4},{6,7},{7,6},{8,9},{9,8},{10,11... | collective-permute-start | bytes 3145736 | tf_op jit(solution)/shard_map/ppermute | solution.py:90
  0.5 0.5 %copy-done.3 = bf16[4,256,128]{2,1,0:T(8,128)(2,1)S(1)} copy-done((bf16[4,256,128]{2,1,0:T(8,128)(2,1)S(1)}, bf16[4,256,128]{2,1,0:T(8,128)(2,1)}, u32[]{:S(2)}) %copy-start.3) | copy-done | bytes 262168
  1.0 0.0 copy-start
  1.0 3.1 %collective-permute-start = (bf16[256,128]{1,0:T(8,128)(2,1)S(1)}, bf16[256,128]{1,0:T(8,128)(2,1)S(1)}, u32[]{:S(2)}, u32[]{:S(2)}) collective-permute-start(bf16[256,128]{1,0:T(8,128)(2,1)S(1)} %get-tuple-element.55), channel_id=1, source_target_pairs={{0,4},{4,8},{8,12},{12,0},{1,5},{5,9},{9,13},{13,1},{2,6},{6,10},{... | collective-permute-start | bytes 196616 | tf_op jit(solution)/shard_map/ppermute | solution.py:274
  4.1 2.1 %collective-permute-start.5 = (bf16[256,128]{1,0:T(8,128)(2,1)S(1)}, bf16[256,128]{1,0:T(8,128)(2,1)S(1)}, u32[]{:S(2)}, u32[]{:S(2)}) collective-permute-start(bf16[256,128]{1,0:T(8,128)(2,1)S(1)} %get-tuple-element.53), channel_id=1, source_target_pairs={{0,12},{4,0},{8,4},{12,8},{1,13},{5,1},{9,5},{13,9},{2,14},{6,2},{... | collective-permute-start | bytes 196616 | tf_op jit(solution)/shard_map/ppermute | solution.py:274
  6.1 0.9 %collective-permute-start.4 = (bf16[256,128]{1,0:T(8,128)(2,1)S(1)}, bf16[256,128]{1,0:T(8,128)(2,1)S(1)}, u32[]{:S(2)}, u32[]{:S(2)}) collective-permute-start(bf16[256,128]{1,0:T(8,128)(2,1)S(1)} %get-tuple-element.56), channel_id=1, source_target_pairs={{0,8},{4,12},{8,0},{12,4},{1,9},{5,13},{9,1},{13,5},{2,10},{6,14},... | collective-permute-start | bytes 196616 | tf_op jit(solution)/shard_map/ppermute | solution.py:274
  7.1 0.0 copy-done
  7.1 0.0 collective-permute-start.3
  7.1 1.7 %reshape.6.refs_0_ = bf16[4,512,256]{2,1,0:T(8,128)(2,1)S(1)} reshape(bf16[4,512,2,128]{3,2,1,0:T(2,128)(2,1)} %param.6) | data formatting | bytes 2097152 | tf_op jit(solution)/shard_map/reshape | solution.py:275
  8.8 0.0 collective-permute-done.1
  8.9 0.0 copy-start.2
  8.9 1.7 %reshape.7.refs_1_ = bf16[4,512,256]{2,1,0:T(8,128)(2,1)S(1)} reshape(bf16[4,512,2,128]{3,2,1,0:T(2,128)(2,1)} %collective-permute-done.1) | data formatting | bytes 2097152 | tf_op jit(solution)/shard_map/reshape | solution.py:276
  10.6 0.0 copy-start.1
  10.6 0.0 collective-permute-done.refs_8_
  10.6 0.0 collective-permute-done.5.refs_10_
  10.6 1.7 %collective-permute-done.4.refs_9_ = bf16[256,128]{1,0:T(8,128)(2,1)S(1)} collective-permute-done((bf16[256,128]{1,0:T(8,128)(2,1)S(1)}, bf16[256,128]{1,0:T(8,128)(2,1)S(1)}, u32[]{:S(2)}, u32[]{:S(2)}) %collective-permute-start.4) | collective-permute-done | bytes 65568 | tf_op jit(solution)/shard_map/ppermute | solution.py:274
  12.4 0.1 collective-permute-start.6
  12.5 0.0 copy-done.2
  12.5 0.5 %collective-permute-start.2 = (bf16[4,2,128]{2,1,0:T(2,128)(2,1)S(1)}, bf16[4,2,128]{2,1,0:T(2,128)(2,1)S(1)}, u32[]{:S(2)}, u32[]{:S(2)}) collective-permute-start(bf16[4,2,128]{2,1,0:T(2,128)(2,1)S(1)} %copy-done.2), channel_id=1, source_target_pairs={{0,1},{1,0},{2,3},{3,2},{4,5},{5,4},{6,7},{7,6},{8,9},{9,8},{10,11... | collective-permute-start | bytes 6152 | tf_op jit(solution)/shard_map/ppermute | solution.py:90
  13.0 1.0 %collective-permute-done.2.refs_3_ = bf16[4,2,128]{2,1,0:T(2,128)(2,1)S(1)} collective-permute-done((bf16[4,2,128]{2,1,0:T(2,128)(2,1)S(1)}, bf16[4,2,128]{2,1,0:T(2,128)(2,1)S(1)}, u32[]{:S(2)}, u32[]{:S(2)}) %collective-permute-start.2) | collective-permute-done | bytes 2080 | tf_op jit(solution)/shard_map/ppermute | solution.py:90
  14.0 0.0 collective-permute-done.3.refs_6_.other_skip
  14.0 0.0 collective-permute-done.6.refs_11_
  14.0 0.0 copy-done.1
  14.0 2.0 %shard_map.55 = (bf16[4,512,256]{2,1,0:T(8,128)(2,1)S(1)}, bf16[256,256]{1,0:T(8,128)(2,1)S(1)}, bf16[32,256]{1,0:T(8,128)(2,1)S(1)}, bf16[256,256]{1,0:T(8,128)...) custom-call(bf16[4,512,256]{2,1,0:T(8,128)(2,1)S(1)} %reshape.6.refs_0_, ...), custom_call_target="tpu_custom_call" | custom-call | flops 1 | bytes 1 | tf_op jit(solution)/shard_map/pallas_call | solution.py:234
  16.0 0.1 collective-permute-start.7
  16.1 2.0 %shard_map.56 = (bf16[4,512,256]{2,1,0:T(8,128)(2,1)S(1)}, bf16[256,256]{1,0:T(8,128)(2,1)S(1)}) custom-call(bf16[4,512,256]{2,1,0:T(8,128)(2,1)S(1)} %reshape.6.refs_0_, bf16[4,512,256]{2,1,0:T(8,128)(2,1)S(1)} %reshape.7.refs_1_, bf16[4,2,128]{2,1,0:T(2,128)(2,1)S(1)} %copy-done.2, bf16[4,2,128]{2,1,0:T(2,128)(2,1)S(1)} %collective-permute-done.2.refs_3_, ...), custom_call_target="tpu_custom_call" | custom-call | flops 1 | bytes 1 | tf_op jit(solution)/shard_map/pallas_call | solution.py:234
  18.0 1.9 %collective-permute-start.11 = (bf16[256,256]{1,0:T(8,128)(2,1)S(1)}, bf16[256,256]{1,0:T(8,128)(2,1)S(1)}, u32[]{:S(2)}, u32[]{:S(2)}) collective-permute-start(bf16[256,256]{1,0:T(8,128)(2,1)S(1)} %get-tuple-element.37), channel_id=1, source_target_pairs={{0,2},{1,3},{4,6},{5,7},{8,10},{9,11},{12,14},{13,15},{16,18},{17,... | collective-permute-start | bytes 393224 | tf_op jit(solution)/shard_map/ppermute | solution.py:311
  20.0 1.6 %collective-permute-done.7.refs_7_ = bf16[256,256]{1,0:T(8,128)(2,1)S(1)} collective-permute-done((bf16[256,256]{1,0:T(8,128)(2,1)S(1)}, bf16[256,256]{1,0:T(8,128)(2,1)S(1)}, u32[]{:S(2)}, u32[]{:S(2)}) %collective-permute-start.7) | collective-permute-done | bytes 131104 | tf_op jit(solution)/shard_map/ppermute | solution.py:311
  21.6 0.1 collective-permute-start.9
  21.7 0.5 %collective-permute-start.8 = (bf16[128,256]{1,0:T(8,128)(2,1)S(1)}, bf16[128,256]{1,0:T(8,128)(2,1)S(1)}, u32[]{:S(2)}, u32[]{:S(2)}) collective-permute-start(bf16[128,256]{1,0:T(8,128)(2,1)S(1)} %get-tuple-element.60), channel_id=1, source_target_pairs={{0,1},{1,0},{2,3},{3,2},{4,5},{5,4},{6,7},{7,6},{8,9},{9,8},{10,11... | collective-permute-start | bytes 196616 | tf_op jit(solution)/shard_map/ppermute | solution.py:90
  22.2 0.3 shard_map.57.refs_10_
  22.5 0.4 %collective-permute-done.9.refs_9_ = bf16[128,256]{1,0:T(8,128)(2,1)S(1)} collective-permute-done((bf16[128,256]{1,0:T(8,128)(2,1)S(1)}, bf16[128,256]{1,0:T(8,128)(2,1)S(1)}, u32[]{:S(2)}, u32[]{:S(2)}) %collective-permute-start.9) | collective-permute-done | bytes 65568 | tf_op jit(solution)/shard_map/ppermute | solution.py:90
  22.9 0.2 collective-permute-done.8.refs_8_
  23.1 0.0 collective-permute-done.11.refs_7_
  23.1 0.4 %collective-permute-start.13 = (bf16[128,256]{1,0:T(8,128)(2,1)S(1)}, bf16[128,256]{1,0:T(8,128)(2,1)S(1)}, u32[]{:S(2)}, u32[]{:S(2)}) collective-permute-start(bf16[128,256]{1,0:T(8,128)(2,1)S(1)} %get-tuple-element.57), channel_id=1, source_target_pairs={{0,1},{1,0},{2,3},{3,2},{4,5},{5,4},{6,7},{7,6},{8,9},{9,8},{10,11... | collective-permute-start | bytes 196616 | tf_op jit(solution)/shard_map/ppermute | solution.py:90
  23.6 0.2 collective-permute-start.12
  23.7 0.3 shard_map.59.refs_14_
  24.0 0.7 %collective-permute-start.10 = (bf16[256,256]{1,0:T(8,128)(2,1)S(1)}, bf16[256,256]{1,0:T(8,128)(2,1)S(1)}, u32[]{:S(2)}, u32[]{:S(2)}) collective-permute-start(bf16[256,256]{1,0:T(8,128)(2,1)S(1)} %get-tuple-element.40), channel_id=1, source_target_pairs={{0,8},{1,12},{2,1},{3,5},{4,11},{5,15},{6,2},{7,6},{8,9},{9,13},{1... | collective-permute-start | bytes 393224 | tf_op jit(solution)/shard_map/ppermute | solution.py:330
  24.7 0.0 collective-permute-done.13.refs_9_
  24.7 0.1 collective-permute-done.12.refs_8_
  24.8 1.7 %collective-permute-start.14 = (bf16[256,256]{1,0:T(8,128)(2,1)S(1)}, bf16[256,256]{1,0:T(8,128)(2,1)S(1)}, u32[]{:S(2)}, u32[]{:S(2)}) collective-permute-start(bf16[256,256]{1,0:T(8,128)(2,1)S(1)} %shard_map.60), channel_id=1, source_target_pairs={{0,1},{1,5},{2,8},{3,12},{4,2},{5,6},{6,11},{7,15},{8,0},{9,4},{10... | collective-permute-start | bytes 393224 | tf_op jit(solution)/shard_map/ppermute | solution.py:330
  26.5 6.8 %collective-permute-done.10.refs_0_ = bf16[256,256]{1,0:T(8,128)(2,1)S(1)} collective-permute-done((bf16[256,256]{1,0:T(8,128)(2,1)S(1)}, bf16[256,256]{1,0:T(8,128)(2,1)S(1)}, u32[]{:S(2)}, u32[]{:S(2)}) %collective-permute-start.10) | collective-permute-done | bytes 131104 | tf_op jit(solution)/shard_map/ppermute | solution.py:330
  33.3 0.0 collective-permute-done.14.refs_1_
  33.3 0.1 collective-permute-start.15
  33.4 1.2 %collective-permute-done.15.given = bf16[256,128]{1,0:T(8,128)(2,1)S(1)} collective-permute-done((bf16[256,128]{1,0:T(8,128)(2,1)S(1)}, bf16[256,128]{1,0:T(8,128)(2,1)S(1)}, u32[]{:S(2)}, u32[]{:S(2)}) %collective-permute-start.15) | collective-permute-done | bytes 65568 | tf_op jit(solution)/shard_map/ppermute | solution.py:90
  34.6 0.7 %shard_map.62 = bf16[2,256,128]{2,1,0:T(8,128)(2,1)} custom-call(bf16[256,128]{1,0:T(8,128)(2,1)S(1)} %get-tuple-element.51.kept, bf16[256,128]{1,0:T(8,128)(2,1)S(1)} %collective-permute-done.15.given), custom_call_target="tpu_custom_call" | custom-call | tf_op jit(solution)/shard_map/pallas_call | solution.py:347
  (7 shorter events, 0.1 us)
Async XLA Ops:
  0.0 0.9 %copy-start.3 = (bf16[4,256,128]{2,1,0:T(8,128)(2,1)S(1)}, bf16[4,256,128]{2,1,0:T(8,128)(2,1)}, u32[]{:S(2)}) copy-start(bf16[4,256,128]{2,1,0:T(8,128)(2,1)} %param.5) | copy-start | bytes 786436
  0.0 8.8 %collective-permute-start.1 = (bf16[4,512,2,128]{3,2,1,0:T(2,128)(2,1)}, bf16[4,512,2,128]{3,2,1,0:T(2,128)(2,1)}, u32[]{:S(2)}, u32[]{:S(2)}) collective-permute-start(bf16[4,512,2,128]{3,2,1,0:T(2,128)(2,1)} %param.6), channel_id=1, source_target_pairs={{0,1},{1,0},{2,3},{3,2},{4,5},{5,4},{6,7},{7,6},{8,9},{9,8},{10,11... | collective-permute-start | bytes 3145736 | tf_op jit(solution)/shard_map/ppermute | solution.py:90
  1.0 6.1 %copy-start = (bf16[4,256,128]{2,1,0:T(8,128)(2,1)S(1)}, bf16[4,256,128]{2,1,0:T(8,128)(2,1)}, u32[]{:S(2)}) copy-start(bf16[4,256,128]{2,1,0:T(8,128)(2,1)} %refs_5_.7) | copy-start | bytes 786436
  1.0 9.7 %collective-permute-start = (bf16[256,128]{1,0:T(8,128)(2,1)S(1)}, bf16[256,128]{1,0:T(8,128)(2,1)S(1)}, u32[]{:S(2)}, u32[]{:S(2)}) collective-permute-start(bf16[256,128]{1,0:T(8,128)(2,1)S(1)} %get-tuple-element.55), channel_id=1, source_target_pairs={{0,4},{4,8},{8,12},{12,0},{1,5},{5,9},{9,13},{13,1},{2,6},{6,10},{... | collective-permute-start | bytes 196616 | tf_op jit(solution)/shard_map/ppermute | solution.py:274
  4.1 6.6 %collective-permute-start.5 = (bf16[256,128]{1,0:T(8,128)(2,1)S(1)}, bf16[256,128]{1,0:T(8,128)(2,1)S(1)}, u32[]{:S(2)}, u32[]{:S(2)}) collective-permute-start(bf16[256,128]{1,0:T(8,128)(2,1)S(1)} %get-tuple-element.53), channel_id=1, source_target_pairs={{0,12},{4,0},{8,4},{12,8},{1,13},{5,1},{9,5},{13,9},{2,14},{6,2},{... | collective-permute-start | bytes 196616 | tf_op jit(solution)/shard_map/ppermute | solution.py:274
  6.1 6.2 %collective-permute-start.4 = (bf16[256,128]{1,0:T(8,128)(2,1)S(1)}, bf16[256,128]{1,0:T(8,128)(2,1)S(1)}, u32[]{:S(2)}, u32[]{:S(2)}) collective-permute-start(bf16[256,128]{1,0:T(8,128)(2,1)S(1)} %get-tuple-element.56), channel_id=1, source_target_pairs={{0,8},{4,12},{8,0},{12,4},{1,9},{5,13},{9,1},{13,5},{2,10},{6,14},... | collective-permute-start | bytes 196616 | tf_op jit(solution)/shard_map/ppermute | solution.py:274
  7.1 6.9 %collective-permute-start.3 = (bf16[4,256,128]{2,1,0:T(8,128)(2,1)S(1)}, bf16[4,256,128]{2,1,0:T(8,128)(2,1)S(1)}, u32[]{:S(2)}, u32[]{:S(2)}) collective-permute-start(bf16[4,256,128]{2,1,0:T(8,128)(2,1)S(1)} %copy-done), channel_id=1, source_target_pairs={{0,1},{1,0},{2,3},{3,2},{4,5},{5,4},{6,7},{7,6},{8,9},{9,8},{10,11... | collective-permute-start | bytes 786440 | tf_op jit(solution)/shard_map/ppermute | solution.py:90
  8.9 3.6 %copy-start.2 = (bf16[4,2,128]{2,1,0:T(2,128)(2,1)S(1)}, bf16[4,2,128]{2,1,0:T(2,128)(2,1)}, u32[]{:S(2)}) copy-start(bf16[4,2,128]{2,1,0:T(2,128)(2,1)} %refs_2_.7) | copy-start | bytes 6148
  10.6 3.4 %copy-start.1 = (bf16[4,256,256]{2,1,0:T(8,128)(2,1)S(1)}, bf16[4,256,256]{2,1,0:T(8,128)(2,1)}, u32[]{:S(2)}) copy-start(bf16[4,256,256]{2,1,0:T(8,128)(2,1)} %refs_4_.7) | copy-start | bytes 1572868
  12.4 1.6 %collective-permute-start.6 = (bf16[1024,128]{1,0:T(8,128)(2,1)S(1)}, bf16[1024,128]{1,0:T(8,128)(2,1)S(1)}, u32[]{:S(2)}, u32[]{:S(2)}) collective-permute-start(bf16[1024,128]{1,0:T(8,128)(2,1)S(1)} %pad_maximum_fusion), channel_id=1, source_target_pairs={{0,1},{1,0},{2,3},{3,2},{4,5},{5,4},{6,7},{7,6},{8,9},{9,8},{10,11... | collective-permute-start | bytes 786440 | tf_op jit(solution)/shard_map/ppermute | solution.py:90
  12.5 1.5 %collective-permute-start.2 = (bf16[4,2,128]{2,1,0:T(2,128)(2,1)S(1)}, bf16[4,2,128]{2,1,0:T(2,128)(2,1)S(1)}, u32[]{:S(2)}, u32[]{:S(2)}) collective-permute-start(bf16[4,2,128]{2,1,0:T(2,128)(2,1)S(1)} %copy-done.2), channel_id=1, source_target_pairs={{0,1},{1,0},{2,3},{3,2},{4,5},{5,4},{6,7},{7,6},{8,9},{9,8},{10,11... | collective-permute-start | bytes 6152 | tf_op jit(solution)/shard_map/ppermute | solution.py:90
  16.0 5.6 %collective-permute-start.7 = (bf16[256,256]{1,0:T(8,128)(2,1)S(1)}, bf16[256,256]{1,0:T(8,128)(2,1)S(1)}, u32[]{:S(2)}, u32[]{:S(2)}) collective-permute-start(bf16[256,256]{1,0:T(8,128)(2,1)S(1)} %get-tuple-element.32), channel_id=1, source_target_pairs={{0,2},{2,0},{1,3},{3,1},{4,6},{6,4},{5,7},{7,5},{8,10},{10,8},{9,1... | collective-permute-start | bytes 393224 | tf_op jit(solution)/shard_map/ppermute | solution.py:311
  18.0 5.1 %collective-permute-start.11 = (bf16[256,256]{1,0:T(8,128)(2,1)S(1)}, bf16[256,256]{1,0:T(8,128)(2,1)S(1)}, u32[]{:S(2)}, u32[]{:S(2)}) collective-permute-start(bf16[256,256]{1,0:T(8,128)(2,1)S(1)} %get-tuple-element.37), channel_id=1, source_target_pairs={{0,2},{1,3},{4,6},{5,7},{8,10},{9,11},{12,14},{13,15},{16,18},{17,... | collective-permute-start | bytes 393224 | tf_op jit(solution)/shard_map/ppermute | solution.py:311
  21.6 1.3 %collective-permute-start.9 = (bf16[128,256]{1,0:T(8,128)(2,1)S(1)}, bf16[128,256]{1,0:T(8,128)(2,1)S(1)}, u32[]{:S(2)}, u32[]{:S(2)}) collective-permute-start(bf16[128,256]{1,0:T(8,128)(2,1)S(1)} %get-tuple-element.59), channel_id=1, source_target_pairs={{0,1},{1,0},{2,3},{3,2},{4,5},{5,4},{6,7},{7,6},{8,9},{9,8},{10,11... | collective-permute-start | bytes 196616 | tf_op jit(solution)/shard_map/ppermute | solution.py:90
  21.7 1.4 %collective-permute-start.8 = (bf16[128,256]{1,0:T(8,128)(2,1)S(1)}, bf16[128,256]{1,0:T(8,128)(2,1)S(1)}, u32[]{:S(2)}, u32[]{:S(2)}) collective-permute-start(bf16[128,256]{1,0:T(8,128)(2,1)S(1)} %get-tuple-element.60), channel_id=1, source_target_pairs={{0,1},{1,0},{2,3},{3,2},{4,5},{5,4},{6,7},{7,6},{8,9},{9,8},{10,11... | collective-permute-start | bytes 196616 | tf_op jit(solution)/shard_map/ppermute | solution.py:90
  23.1 1.6 %collective-permute-start.13 = (bf16[128,256]{1,0:T(8,128)(2,1)S(1)}, bf16[128,256]{1,0:T(8,128)(2,1)S(1)}, u32[]{:S(2)}, u32[]{:S(2)}) collective-permute-start(bf16[128,256]{1,0:T(8,128)(2,1)S(1)} %get-tuple-element.57), channel_id=1, source_target_pairs={{0,1},{1,0},{2,3},{3,2},{4,5},{5,4},{6,7},{7,6},{8,9},{9,8},{10,11... | collective-permute-start | bytes 196616 | tf_op jit(solution)/shard_map/ppermute | solution.py:90
  23.6 1.3 %collective-permute-start.12 = (bf16[128,256]{1,0:T(8,128)(2,1)S(1)}, bf16[128,256]{1,0:T(8,128)(2,1)S(1)}, u32[]{:S(2)}, u32[]{:S(2)}) collective-permute-start(bf16[128,256]{1,0:T(8,128)(2,1)S(1)} %get-tuple-element.58), channel_id=1, source_target_pairs={{0,1},{1,0},{2,3},{3,2},{4,5},{5,4},{6,7},{7,6},{8,9},{9,8},{10,11... | collective-permute-start | bytes 196616 | tf_op jit(solution)/shard_map/ppermute | solution.py:90
  24.0 9.2 %collective-permute-start.10 = (bf16[256,256]{1,0:T(8,128)(2,1)S(1)}, bf16[256,256]{1,0:T(8,128)(2,1)S(1)}, u32[]{:S(2)}, u32[]{:S(2)}) collective-permute-start(bf16[256,256]{1,0:T(8,128)(2,1)S(1)} %get-tuple-element.40), channel_id=1, source_target_pairs={{0,8},{1,12},{2,1},{3,5},{4,11},{5,15},{6,2},{7,6},{8,9},{9,13},{1... | collective-permute-start | bytes 393224 | tf_op jit(solution)/shard_map/ppermute | solution.py:330
  24.8 8.4 %collective-permute-start.14 = (bf16[256,256]{1,0:T(8,128)(2,1)S(1)}, bf16[256,256]{1,0:T(8,128)(2,1)S(1)}, u32[]{:S(2)}, u32[]{:S(2)}) collective-permute-start(bf16[256,256]{1,0:T(8,128)(2,1)S(1)} %shard_map.60), channel_id=1, source_target_pairs={{0,1},{1,5},{2,8},{3,12},{4,2},{5,6},{6,11},{7,15},{8,0},{9,4},{10... | collective-permute-start | bytes 393224 | tf_op jit(solution)/shard_map/ppermute | solution.py:330
  33.3 1.3 %collective-permute-start.15 = (bf16[256,128]{1,0:T(8,128)(2,1)S(1)}, bf16[256,128]{1,0:T(8,128)(2,1)S(1)}, u32[]{:S(2)}, u32[]{:S(2)}) collective-permute-start(bf16[256,128]{1,0:T(8,128)(2,1)S(1)} %get-tuple-element.52), channel_id=1, source_target_pairs={{0,1},{1,0},{2,3},{3,2},{4,5},{5,4},{6,7},{7,6},{8,9},{9,8},{10,11... | collective-permute-start | bytes 196616 | tf_op jit(solution)/shard_map/ppermute | solution.py:90

commit v10 on v9

--- a/solution.py
+++ b/solution.py
@@ -154,10 +154,11 @@
                 past = now_buf[pl.ds(row, ROW_TILE), :]
                 now = now_buf[pl.ds(lag + row, ROW_TILE), :]
                 parts = []
-                both = jnp.concatenate([past, now], 1)
+                blank = not half and lag >= total
+                both = now if blank else jnp.concatenate([past, now], 1)
                 for conv, bias in ((own_conv, own_bias), (other_conv, other_bias)):
                     shift = jnp.concatenate([bias[layer, 0:1, :], bias[layer, 1:2, :]], 1).astype(jnp.float32)
-                    pre = jnp.dot(both, conv[layer], preferred_element_type=jnp.float32)
+                    pre = jnp.dot(both, conv[layer, depth if blank else 0 :], preferred_element_type=jnp.float32)
                     pre += shift
                     gate = 0.5 * jnp.tanh(0.5 * pre[:, width:]) + 0.5
                     parts.append((jnp.tanh(pre[:, :width]) * gate).astype(jnp.bfloat16))
@@ -300,8 +301,9 @@
                     came, heads = lax.optimization_barrier((came, heads))
                 else:
                     came, stream = lax.optimization_barrier((came, stream))
-                size = came.shape[0] // PIECES
-                came = [came] + [swap_cores(came[i * size : (i + 1) * size]) for i in range(PIECES)]
+                pieces = 1 if half else PIECES
+                size = came.shape[0] // pieces
+                came = [came] + [swap_cores(came[i * size : (i + 1) * size]) for i in range(pieces)]
             skips[stage, half], stream, carried = run_section(
                 stage, half, plan, lags, weights, came, heads, earlier, rows
             )

time: 35.9 us -> 35.6 us (level)
    ppermute x9 -> x8, starting transfers between devices: 2.23 us -> 2.07 us  [swap_cores(): return lax.ppermute(block, 'chan', [(0, 1), (1, 0)])]
    ppermute x9 -> x8, waiting for transfers between devices: 2.94 us -> 2.87 us  [swap_cores(): return lax.ppermute(block, 'chan', [(0, 1), (1, 0)])]
  transfers between devices with their start and end apart: 16 -> 15, of which waited for: 8 -> 7; matrix products, arithmetic and copies ran while one was open for 10% -> 10% of each run, Pallas kernels for 7% -> 7%
where the time goes in v10:
time: 35.6 us; the launch traced here: 35 us
  waiting for transfers between devices  13 us (37%)
  starting transfers between devices  12.6 us (35%)
  Pallas kernels  5.12 us (14%)
  local copies, waits for them, and re-layouts  4.02 us (11%)
    ppermute x2, waiting for transfers between devices, shards(): lax.ppermute(payload, ('tm', 'segment', 'chan'), sorted(((number(a), numb...  6.77 us
    ppermute x3, starting transfers between devices, shards(): lax.ppermute(blocks[turn], 'tm', [(i, (i + turn) % count) for i in range(...  6.11 us
    pallas_call x4, Pallas kernels, run_section(): pl.pallas_call(functools.partial(section_kernel, stage, half, plan, lags,...  3.8 us
    ppermute x8, waiting for transfers between devices, swap_cores(): return lax.ppermute(block, 'chan', [(0, 1), (1, 0)])  2.87 us
    ppermute x2, starting transfers between devices, shards(): lax.ppermute(payload, ('tm', 'segment', 'chan'), sorted(((number(a), numb...  2.43 us
    ppermute x8, starting transfers between devices, swap_cores(): return lax.ppermute(block, 'chan', [(0, 1), (1, 0)])  2.07 us
    ppermute x2, starting transfers between devices, shards(): moved = lax.ppermute(stream, 'segment', ring)  2.02 us
    ppermute x3, waiting for transfers between devices, shards(): lax.ppermute(blocks[turn], 'tm', [(i, (i + turn) % count) for i in range(...  1.74 us
  transfers between devices with their start and end apart: 15, of which 7 were waited for; matrix products, arithmetic and copies ran while one was open for 10% of the time, Pallas kernels for 7%

profile of v10, /device:TPU:0, one launch (start us, length us, event | category | flops | bytes accessed | tf_op | source)
XLA Modules:
  0.0 35.0 jit_solution(11534550433625608517)
XLA Ops:
  0.0 0.0 copy-start.3
  0.0 0.5 %collective-permute-start.1 = (bf16[4,512,2,128]{3,2,1,0:T(2,128)(2,1)}, bf16[4,512,2,128]{3,2,1,0:T(2,128)(2,1)}, u32[]{:S(2)}, u32[]{:S(2)}) collective-permute-start(bf16[4,512,2,128]{3,2,1,0:T(2,128)(2,1)} %param.6), channel_id=1, source_target_pairs={{0,1},{1,0},{2,3},{3,2},{4,5},{5,4},{6,7},{7,6},{8,9},{9,8},{10,11... | collective-permute-start | bytes 3145736 | tf_op jit(solution)/shard_map/ppermute | solution.py:90
  0.5 0.5 %copy-done.3 = bf16[4,256,128]{2,1,0:T(8,128)(2,1)S(1)} copy-done((bf16[4,256,128]{2,1,0:T(8,128)(2,1)S(1)}, bf16[4,256,128]{2,1,0:T(8,128)(2,1)}, u32[]{:S(2)}) %copy-start.3) | copy-done | bytes 262168
  1.0 0.0 copy-start
  1.0 3.1 %collective-permute-start = (bf16[256,128]{1,0:T(8,128)(2,1)S(1)}, bf16[256,128]{1,0:T(8,128)(2,1)S(1)}, u32[]{:S(2)}, u32[]{:S(2)}) collective-permute-start(bf16[256,128]{1,0:T(8,128)(2,1)S(1)} %get-tuple-element.55), channel_id=1, source_target_pairs={{0,4},{4,8},{8,12},{12,0},{1,5},{5,9},{9,13},{13,1},{2,6},{6,10},{... | collective-permute-start | bytes 196616 | tf_op jit(solution)/shard_map/ppermute | solution.py:275
  4.1 2.1 %collective-permute-start.5 = (bf16[256,128]{1,0:T(8,128)(2,1)S(1)}, bf16[256,128]{1,0:T(8,128)(2,1)S(1)}, u32[]{:S(2)}, u32[]{:S(2)}) collective-permute-start(bf16[256,128]{1,0:T(8,128)(2,1)S(1)} %get-tuple-element.53), channel_id=1, source_target_pairs={{0,12},{4,0},{8,4},{12,8},{1,13},{5,1},{9,5},{13,9},{2,14},{6,2},{... | collective-permute-start | bytes 196616 | tf_op jit(solution)/shard_map/ppermute | solution.py:275
  6.1 0.9 %collective-permute-start.4 = (bf16[256,128]{1,0:T(8,128)(2,1)S(1)}, bf16[256,128]{1,0:T(8,128)(2,1)S(1)}, u32[]{:S(2)}, u32[]{:S(2)}) collective-permute-start(bf16[256,128]{1,0:T(8,128)(2,1)S(1)} %get-tuple-element.56), channel_id=1, source_target_pairs={{0,8},{4,12},{8,0},{12,4},{1,9},{5,13},{9,1},{13,5},{2,10},{6,14},... | collective-permute-start | bytes 196616 | tf_op jit(solution)/shard_map/ppermute | solution.py:275
  7.1 0.0 copy-done
  7.1 0.0 collective-permute-start.3
  7.1 1.7 %reshape.6.refs_0_ = bf16[4,512,256]{2,1,0:T(8,128)(2,1)S(1)} reshape(bf16[4,512,2,128]{3,2,1,0:T(2,128)(2,1)} %param.6) | data formatting | bytes 2097152 | tf_op jit(solution)/shard_map/reshape | solution.py:276
  8.8 0.0 collective-permute-done.1
  8.9 0.0 copy-start.2
  8.9 1.7 %reshape.7.refs_1_ = bf16[4,512,256]{2,1,0:T(8,128)(2,1)S(1)} reshape(bf16[4,512,2,128]{3,2,1,0:T(2,128)(2,1)} %collective-permute-done.1) | data formatting | bytes 2097152 | tf_op jit(solution)/shard_map/reshape | solution.py:277
  10.6 0.0 copy-start.1
  10.6 0.0 collective-permute-done.refs_8_
  10.6 0.0 collective-permute-done.5.refs_10_
  10.6 1.7 %collective-permute-done.4.refs_9_ = bf16[256,128]{1,0:T(8,128)(2,1)S(1)} collective-permute-done((bf16[256,128]{1,0:T(8,128)(2,1)S(1)}, bf16[256,128]{1,0:T(8,128)(2,1)S(1)}, u32[]{:S(2)}, u32[]{:S(2)}) %collective-permute-start.4) | collective-permute-done | bytes 65568 | tf_op jit(solution)/shard_map/ppermute | solution.py:275
  12.4 0.1 collective-permute-start.6
  12.5 0.0 copy-done.2
  12.5 0.5 %collective-permute-start.2 = (bf16[4,2,128]{2,1,0:T(2,128)(2,1)S(1)}, bf16[4,2,128]{2,1,0:T(2,128)(2,1)S(1)}, u32[]{:S(2)}, u32[]{:S(2)}) collective-permute-start(bf16[4,2,128]{2,1,0:T(2,128)(2,1)S(1)} %copy-done.2), channel_id=1, source_target_pairs={{0,1},{1,0},{2,3},{3,2},{4,5},{5,4},{6,7},{7,6},{8,9},{9,8},{10,11... | collective-permute-start | bytes 6152 | tf_op jit(solution)/shard_map/ppermute | solution.py:90
  13.0 1.0 %collective-permute-done.2.refs_3_ = bf16[4,2,128]{2,1,0:T(2,128)(2,1)S(1)} collective-permute-done((bf16[4,2,128]{2,1,0:T(2,128)(2,1)S(1)}, bf16[4,2,128]{2,1,0:T(2,128)(2,1)S(1)}, u32[]{:S(2)}, u32[]{:S(2)}) %collective-permute-start.2) | collective-permute-done | bytes 2080 | tf_op jit(solution)/shard_map/ppermute | solution.py:90
  14.0 0.0 collective-permute-done.3.refs_6_.other_skip
  14.0 0.0 collective-permute-done.6.refs_11_
  14.0 0.0 copy-done.1
  14.0 1.8 %shard_map.55 = (bf16[4,512,256]{2,1,0:T(8,128)(2,1)S(1)}, bf16[256,256]{1,0:T(8,128)(2,1)S(1)}, bf16[32,256]{1,0:T(8,128)(2,1)S(1)}, bf16[256,256]{1,0:T(8,128)...) custom-call(bf16[4,512,256]{2,1,0:T(8,128)(2,1)S(1)} %reshape.6.refs_0_, ...), custom_call_target="tpu_custom_call" | custom-call | flops 1 | bytes 1 | tf_op jit(solution)/shard_map/pallas_call | solution.py:235
  15.8 0.1 collective-permute-start.7
  15.9 2.0 %shard_map.56 = (bf16[4,512,256]{2,1,0:T(8,128)(2,1)S(1)}, bf16[256,256]{1,0:T(8,128)(2,1)S(1)}) custom-call(bf16[4,512,256]{2,1,0:T(8,128)(2,1)S(1)} %reshape.6.refs_0_, bf16[4,512,256]{2,1,0:T(8,128)(2,1)S(1)} %reshape.7.refs_1_, bf16[4,2,128]{2,1,0:T(2,128)(2,1)S(1)} %copy-done.2, bf16[4,2,128]{2,1,0:T(2,128)(2,1)S(1)} %collective-permute-done.2.refs_3_, ...), custom_call_target="tpu_custom_call" | custom-call | flops 1 | bytes 1 | tf_op jit(solution)/shard_map/pallas_call | solution.py:235
  17.9 1.9 %collective-permute-start.11 = (bf16[256,256]{1,0:T(8,128)(2,1)S(1)}, bf16[256,256]{1,0:T(8,128)(2,1)S(1)}, u32[]{:S(2)}, u32[]{:S(2)}) collective-permute-start(bf16[256,256]{1,0:T(8,128)(2,1)S(1)} %get-tuple-element.37), channel_id=1, source_target_pairs={{0,2},{1,3},{4,6},{5,7},{8,10},{9,11},{12,14},{13,15},{16,18},{17,... | collective-permute-start | bytes 393224 | tf_op jit(solution)/shard_map/ppermute | solution.py:313
  19.8 1.6 %collective-permute-done.7.refs_7_ = bf16[256,256]{1,0:T(8,128)(2,1)S(1)} collective-permute-done((bf16[256,256]{1,0:T(8,128)(2,1)S(1)}, bf16[256,256]{1,0:T(8,128)(2,1)S(1)}, u32[]{:S(2)}, u32[]{:S(2)}) %collective-permute-start.7) | collective-permute-done | bytes 131104 | tf_op jit(solution)/shard_map/ppermute | solution.py:313
  21.5 0.1 collective-permute-start.9
  21.6 0.5 %collective-permute-start.8 = (bf16[128,256]{1,0:T(8,128)(2,1)S(1)}, bf16[128,256]{1,0:T(8,128)(2,1)S(1)}, u32[]{:S(2)}, u32[]{:S(2)}) collective-permute-start(bf16[128,256]{1,0:T(8,128)(2,1)S(1)} %get-tuple-element.58), channel_id=1, source_target_pairs={{0,1},{1,0},{2,3},{3,2},{4,5},{5,4},{6,7},{7,6},{8,9},{9,8},{10,11... | collective-permute-start | bytes 196616 | tf_op jit(solution)/shard_map/ppermute | solution.py:90
  22.1 0.3 shard_map.57.refs_10_
  22.4 0.4 %collective-permute-done.9.refs_9_ = bf16[128,256]{1,0:T(8,128)(2,1)S(1)} collective-permute-done((bf16[128,256]{1,0:T(8,128)(2,1)S(1)}, bf16[128,256]{1,0:T(8,128)(2,1)S(1)}, u32[]{:S(2)}, u32[]{:S(2)}) %collective-permute-start.9) | collective-permute-done | bytes 65568 | tf_op jit(solution)/shard_map/ppermute | solution.py:90
  22.8 0.2 collective-permute-done.8.refs_8_
  23.0 0.0 collective-permute-done.11.refs_7_
  23.0 0.4 %collective-permute-start.12 = (bf16[256,256]{1,0:T(8,128)(2,1)S(1)}, bf16[256,256]{1,0:T(8,128)(2,1)S(1)}, u32[]{:S(2)}, u32[]{:S(2)}) collective-permute-start(bf16[256,256]{1,0:T(8,128)(2,1)S(1)} %collective-permute-done.11.refs_7_), channel_id=1, source_target_pairs={{0,1},{1,0},{2,3},{3,2},{4,5},{5,4},{6,7},{7,6},{8,9},{9,8},{10,11... | collective-permute-start | bytes 393224 | tf_op jit(solution)/shard_map/ppermute | solution.py:90
  23.4 0.3 shard_map.59.refs_13_
  23.7 0.7 %collective-permute-start.10 = (bf16[256,256]{1,0:T(8,128)(2,1)S(1)}, bf16[256,256]{1,0:T(8,128)(2,1)S(1)}, u32[]{:S(2)}, u32[]{:S(2)}) collective-permute-start(bf16[256,256]{1,0:T(8,128)(2,1)S(1)} %get-tuple-element.40), channel_id=1, source_target_pairs={{0,8},{1,12},{2,1},{3,5},{4,11},{5,15},{6,2},{7,6},{8,9},{9,13},{1... | collective-permute-start | bytes 393224 | tf_op jit(solution)/shard_map/ppermute | solution.py:332
  24.4 0.0 collective-permute-done.12.refs_8_
  24.4 1.7 %collective-permute-start.13 = (bf16[256,256]{1,0:T(8,128)(2,1)S(1)}, bf16[256,256]{1,0:T(8,128)(2,1)S(1)}, u32[]{:S(2)}, u32[]{:S(2)}) collective-permute-start(bf16[256,256]{1,0:T(8,128)(2,1)S(1)} %shard_map.60), channel_id=1, source_target_pairs={{0,1},{1,5},{2,8},{3,12},{4,2},{5,6},{6,11},{7,15},{8,0},{9,4},{10... | collective-permute-start | bytes 393224 | tf_op jit(solution)/shard_map/ppermute | solution.py:332
  26.2 6.8 %collective-permute-done.10.refs_0_ = bf16[256,256]{1,0:T(8,128)(2,1)S(1)} collective-permute-done((bf16[256,256]{1,0:T(8,128)(2,1)S(1)}, bf16[256,256]{1,0:T(8,128)(2,1)S(1)}, u32[]{:S(2)}, u32[]{:S(2)}) %collective-permute-start.10) | collective-permute-done | bytes 131104 | tf_op jit(solution)/shard_map/ppermute | solution.py:332
  33.0 0.0 collective-permute-done.13.refs_1_
  33.0 0.1 collective-permute-start.14
  33.1 1.2 %collective-permute-done.14.given = bf16[256,128]{1,0:T(8,128)(2,1)S(1)} collective-permute-done((bf16[256,128]{1,0:T(8,128)(2,1)S(1)}, bf16[256,128]{1,0:T(8,128)(2,1)S(1)}, u32[]{:S(2)}, u32[]{:S(2)}) %collective-permute-start.14) | collective-permute-done | bytes 65568 | tf_op jit(solution)/shard_map/ppermute | solution.py:90
  34.3 0.7 %shard_map.62 = bf16[2,256,128]{2,1,0:T(8,128)(2,1)} custom-call(bf16[256,128]{1,0:T(8,128)(2,1)S(1)} %get-tuple-element.51.kept, bf16[256,128]{1,0:T(8,128)(2,1)S(1)} %collective-permute-done.14.given), custom_call_target="tpu_custom_call" | custom-call | tf_op jit(solution)/shard_map/pallas_call | solution.py:349
  (6 shorter events, 0.1 us)
Async XLA Ops:
  0.0 0.9 %copy-start.3 = (bf16[4,256,128]{2,1,0:T(8,128)(2,1)S(1)}, bf16[4,256,128]{2,1,0:T(8,128)(2,1)}, u32[]{:S(2)}) copy-start(bf16[4,256,128]{2,1,0:T(8,128)(2,1)} %param.5) | copy-start | bytes 786436
  0.0 8.8 %collective-permute-start.1 = (bf16[4,512,2,128]{3,2,1,0:T(2,128)(2,1)}, bf16[4,512,2,128]{3,2,1,0:T(2,128)(2,1)}, u32[]{:S(2)}, u32[]{:S(2)}) collective-permute-start(bf16[4,512,2,128]{3,2,1,0:T(2,128)(2,1)} %param.6), channel_id=1, source_target_pairs={{0,1},{1,0},{2,3},{3,2},{4,5},{5,4},{6,7},{7,6},{8,9},{9,8},{10,11... | collective-permute-start | bytes 3145736 | tf_op jit(solution)/shard_map/ppermute | solution.py:90
  1.0 6.1 %copy-start = (bf16[4,256,128]{2,1,0:T(8,128)(2,1)S(1)}, bf16[4,256,128]{2,1,0:T(8,128)(2,1)}, u32[]{:S(2)}) copy-start(bf16[4,256,128]{2,1,0:T(8,128)(2,1)} %refs_5_.7) | copy-start | bytes 786436
  1.0 9.7 %collective-permute-start = (bf16[256,128]{1,0:T(8,128)(2,1)S(1)}, bf16[256,128]{1,0:T(8,128)(2,1)S(1)}, u32[]{:S(2)}, u32[]{:S(2)}) collective-permute-start(bf16[256,128]{1,0:T(8,128)(2,1)S(1)} %get-tuple-element.55), channel_id=1, source_target_pairs={{0,4},{4,8},{8,12},{12,0},{1,5},{5,9},{9,13},{13,1},{2,6},{6,10},{... | collective-permute-start | bytes 196616 | tf_op jit(solution)/shard_map/ppermute | solution.py:275
  4.1 6.6 %collective-permute-start.5 = (bf16[256,128]{1,0:T(8,128)(2,1)S(1)}, bf16[256,128]{1,0:T(8,128)(2,1)S(1)}, u32[]{:S(2)}, u32[]{:S(2)}) collective-permute-start(bf16[256,128]{1,0:T(8,128)(2,1)S(1)} %get-tuple-element.53), channel_id=1, source_target_pairs={{0,12},{4,0},{8,4},{12,8},{1,13},{5,1},{9,5},{13,9},{2,14},{6,2},{... | collective-permute-start | bytes 196616 | tf_op jit(solution)/shard_map/ppermute | solution.py:275
  6.1 6.2 %collective-permute-start.4 = (bf16[256,128]{1,0:T(8,128)(2,1)S(1)}, bf16[256,128]{1,0:T(8,128)(2,1)S(1)}, u32[]{:S(2)}, u32[]{:S(2)}) collective-permute-start(bf16[256,128]{1,0:T(8,128)(2,1)S(1)} %get-tuple-element.56), channel_id=1, source_target_pairs={{0,8},{4,12},{8,0},{12,4},{1,9},{5,13},{9,1},{13,5},{2,10},{6,14},... | collective-permute-start | bytes 196616 | tf_op jit(solution)/shard_map/ppermute | solution.py:275
  7.1 6.9 %collective-permute-start.3 = (bf16[4,256,128]{2,1,0:T(8,128)(2,1)S(1)}, bf16[4,256,128]{2,1,0:T(8,128)(2,1)S(1)}, u32[]{:S(2)}, u32[]{:S(2)}) collective-permute-start(bf16[4,256,128]{2,1,0:T(8,128)(2,1)S(1)} %copy-done), channel_id=1, source_target_pairs={{0,1},{1,0},{2,3},{3,2},{4,5},{5,4},{6,7},{7,6},{8,9},{9,8},{10,11... | collective-permute-start | bytes 786440 | tf_op jit(solution)/shard_map/ppermute | solution.py:90
  8.9 3.6 %copy-start.2 = (bf16[4,2,128]{2,1,0:T(2,128)(2,1)S(1)}, bf16[4,2,128]{2,1,0:T(2,128)(2,1)}, u32[]{:S(2)}) copy-start(bf16[4,2,128]{2,1,0:T(2,128)(2,1)} %refs_2_.7) | copy-start | bytes 6148
  10.6 3.4 %copy-start.1 = (bf16[4,256,256]{2,1,0:T(8,128)(2,1)S(1)}, bf16[4,256,256]{2,1,0:T(8,128)(2,1)}, u32[]{:S(2)}) copy-start(bf16[4,256,256]{2,1,0:T(8,128)(2,1)} %refs_4_.7) | copy-start | bytes 1572868
  12.4 1.6 %collective-permute-start.6 = (bf16[1024,128]{1,0:T(8,128)(2,1)S(1)}, bf16[1024,128]{1,0:T(8,128)(2,1)S(1)}, u32[]{:S(2)}, u32[]{:S(2)}) collective-permute-start(bf16[1024,128]{1,0:T(8,128)(2,1)S(1)} %pad_maximum_fusion), channel_id=1, source_target_pairs={{0,1},{1,0},{2,3},{3,2},{4,5},{5,4},{6,7},{7,6},{8,9},{9,8},{10,11... | collective-permute-start | bytes 786440 | tf_op jit(solution)/shard_map/ppermute | solution.py:90
  12.5 1.5 %collective-permute-start.2 = (bf16[4,2,128]{2,1,0:T(2,128)(2,1)S(1)}, bf16[4,2,128]{2,1,0:T(2,128)(2,1)S(1)}, u32[]{:S(2)}, u32[]{:S(2)}) collective-permute-start(bf16[4,2,128]{2,1,0:T(2,128)(2,1)S(1)} %copy-done.2), channel_id=1, source_target_pairs={{0,1},{1,0},{2,3},{3,2},{4,5},{5,4},{6,7},{7,6},{8,9},{9,8},{10,11... | collective-permute-start | bytes 6152 | tf_op jit(solution)/shard_map/ppermute | solution.py:90
  15.8 5.6 %collective-permute-start.7 = (bf16[256,256]{1,0:T(8,128)(2,1)S(1)}, bf16[256,256]{1,0:T(8,128)(2,1)S(1)}, u32[]{:S(2)}, u32[]{:S(2)}) collective-permute-start(bf16[256,256]{1,0:T(8,128)(2,1)S(1)} %get-tuple-element.32), channel_id=1, source_target_pairs={{0,2},{2,0},{1,3},{3,1},{4,6},{6,4},{5,7},{7,5},{8,10},{10,8},{9,1... | collective-permute-start | bytes 393224 | tf_op jit(solution)/shard_map/ppermute | solution.py:313
  17.9 5.1 %collective-permute-start.11 = (bf16[256,256]{1,0:T(8,128)(2,1)S(1)}, bf16[256,256]{1,0:T(8,128)(2,1)S(1)}, u32[]{:S(2)}, u32[]{:S(2)}) collective-permute-start(bf16[256,256]{1,0:T(8,128)(2,1)S(1)} %get-tuple-element.37), channel_id=1, source_target_pairs={{0,2},{1,3},{4,6},{5,7},{8,10},{9,11},{12,14},{13,15},{16,18},{17,... | collective-permute-start | bytes 393224 | tf_op jit(solution)/shard_map/ppermute | solution.py:313
  21.5 1.3 %collective-permute-start.9 = (bf16[128,256]{1,0:T(8,128)(2,1)S(1)}, bf16[128,256]{1,0:T(8,128)(2,1)S(1)}, u32[]{:S(2)}, u32[]{:S(2)}) collective-permute-start(bf16[128,256]{1,0:T(8,128)(2,1)S(1)} %get-tuple-element.57), channel_id=1, source_target_pairs={{0,1},{1,0},{2,3},{3,2},{4,5},{5,4},{6,7},{7,6},{8,9},{9,8},{10,11... | collective-permute-start | bytes 196616 | tf_op jit(solution)/shard_map/ppermute | solution.py:90
  21.6 1.4 %collective-permute-start.8 = (bf16[128,256]{1,0:T(8,128)(2,1)S(1)}, bf16[128,256]{1,0:T(8,128)(2,1)S(1)}, u32[]{:S(2)}, u32[]{:S(2)}) collective-permute-start(bf16[128,256]{1,0:T(8,128)(2,1)S(1)} %get-tuple-element.58), channel_id=1, source_target_pairs={{0,1},{1,0},{2,3},{3,2},{4,5},{5,4},{6,7},{7,6},{8,9},{9,8},{10,11... | collective-permute-start | bytes 196616 | tf_op jit(solution)/shard_map/ppermute | solution.py:90
  23.0 1.4 %collective-permute-start.12 = (bf16[256,256]{1,0:T(8,128)(2,1)S(1)}, bf16[256,256]{1,0:T(8,128)(2,1)S(1)}, u32[]{:S(2)}, u32[]{:S(2)}) collective-permute-start(bf16[256,256]{1,0:T(8,128)(2,1)S(1)} %collective-permute-done.11.refs_7_), channel_id=1, source_target_pairs={{0,1},{1,0},{2,3},{3,2},{4,5},{5,4},{6,7},{7,6},{8,9},{9,8},{10,11... | collective-permute-start | bytes 393224 | tf_op jit(solution)/shard_map/ppermute | solution.py:90
  23.7 9.2 %collective-permute-start.10 = (bf16[256,256]{1,0:T(8,128)(2,1)S(1)}, bf16[256,256]{1,0:T(8,128)(2,1)S(1)}, u32[]{:S(2)}, u32[]{:S(2)}) collective-permute-start(bf16[256,256]{1,0:T(8,128)(2,1)S(1)} %get-tuple-element.40), channel_id=1, source_target_pairs={{0,8},{1,12},{2,1},{3,5},{4,11},{5,15},{6,2},{7,6},{8,9},{9,13},{1... | collective-permute-start | bytes 393224 | tf_op jit(solution)/shard_map/ppermute | solution.py:332
  24.4 8.5 %collective-permute-start.13 = (bf16[256,256]{1,0:T(8,128)(2,1)S(1)}, bf16[256,256]{1,0:T(8,128)(2,1)S(1)}, u32[]{:S(2)}, u32[]{:S(2)}) collective-permute-start(bf16[256,256]{1,0:T(8,128)(2,1)S(1)} %shard_map.60), channel_id=1, source_target_pairs={{0,1},{1,5},{2,8},{3,12},{4,2},{5,6},{6,11},{7,15},{8,0},{9,4},{10... | collective-permute-start | bytes 393224 | tf_op jit(solution)/shard_map/ppermute | solution.py:332
  33.0 1.3 %collective-permute-start.14 = (bf16[256,128]{1,0:T(8,128)(2,1)S(1)}, bf16[256,128]{1,0:T(8,128)(2,1)S(1)}, u32[]{:S(2)}, u32[]{:S(2)}) collective-permute-start(bf16[256,128]{1,0:T(8,128)(2,1)S(1)} %get-tuple-element.52), channel_id=1, source_target_pairs={{0,1},{1,0},{2,3},{3,2},{4,5},{5,4},{6,7},{7,6},{8,9},{9,8},{10,11... | collective-permute-start | bytes 196616 | tf_op jit(solution)/shard_map/ppermute | solution.py:90

commit v11 on v10

--- a/solution.py
+++ b/solution.py
@@ -142,6 +142,7 @@
                 streams[0][pl.ds(at, size), :] = block[...]
             streams[0][pl.ds(pl.multiple_of(lags[0] + core * part, 16), part), :] = inputs[0][...]
 
+        narrow = last and plan.count == 4 and plan.blocks == 1 and not plan.whole_group and lags[(layers - 1) % 4] == total
         for layer in range(layers):
             lag = lags[layer % 4]
             now_buf = streams[layer]
@@ -150,9 +151,9 @@
             if not (last and layer + 1 == layers):
                 res = jnp.concatenate([res_ref[layer, own_rows, :], res_ref[layer, other_rows, :]], 0)
 
-            def tile(row, layer=layer, lag=lag, now_buf=now_buf, next_buf=next_buf, next_lag=next_lag, res=res):
-                past = now_buf[pl.ds(row, ROW_TILE), :]
-                now = now_buf[pl.ds(lag + row, ROW_TILE), :]
+            def tile(row, size=ROW_TILE, layer=layer, lag=lag, now_buf=now_buf, next_buf=next_buf, next_lag=next_lag, res=res):
+                past = now_buf[pl.ds(row, size), :]
+                now = now_buf[pl.ds(lag + row, size), :]
                 parts = []
                 blank = not half and lag >= total
                 both = now if blank else jnp.concatenate([past, now], 1)
@@ -163,11 +164,14 @@
                     gate = 0.5 * jnp.tanh(0.5 * pre[:, width:]) + 0.5
                     parts.append((jnp.tanh(pre[:, :width]) * gate).astype(jnp.bfloat16))
                 unit = jnp.concatenate(parts, 1)
-                units[layer, pl.ds(row, ROW_TILE), :] = unit
+                units[layer, pl.ds(row, size), :] = unit
                 if res is not None:
                     update = jnp.dot(unit, res, preferred_element_type=jnp.float32)
-                    next_buf[pl.ds(next_lag + row, ROW_TILE), :] = (now.astype(jnp.float32) + update).astype(jnp.bfloat16)
-
+                    next_buf[pl.ds(next_lag + row, size), :] = (now.astype(jnp.float32) + update).astype(jnp.bfloat16)
+
+            if narrow and layer >= layers - 2:
+                tile(pl.multiple_of(core * (total // 2), 16), total // 2)
+                continue
             steps = total // ROW_TILE
             if steps <= 4:
                 for step in range(steps):

time: 35.6 us -> 35.4 us (level)
  no operation moved by 1% of the time
where the time goes in v11:
time: 35.4 us; the launch traced here: 35 us
  waiting for transfers between devices  13 us (37%)
  starting transfers between devices  12.6 us (36%)
  Pallas kernels  5.12 us (14%)
  local copies, waits for them, and re-layouts  4.02 us (11%)
    ppermute x2, waiting for transfers between devices, shards(): lax.ppermute(payload, ('tm', 'segment', 'chan'), sorted(((number(a), numb...  6.77 us
    ppermute x3, starting transfers between devices, shards(): lax.ppermute(blocks[turn], 'tm', [(i, (i + turn) % count) for i in range(...  6.11 us
    pallas_call x4, Pallas kernels, run_section(): pl.pallas_call(functools.partial(section_kernel, stage, half, plan, lags,...  3.8 us
    ppermute x8, waiting for transfers between devices, swap_cores(): return lax.ppermute(block, 'chan', [(0, 1), (1, 0)])  2.87 us
    ppermute x2, starting transfers between devices, shards(): lax.ppermute(payload, ('tm', 'segment', 'chan'), sorted(((number(a), numb...  2.43 us
    ppermute x8, starting transfers between devices, swap_cores(): return lax.ppermute(block, 'chan', [(0, 1), (1, 0)])  2.07 us
    ppermute x2, starting transfers between devices, shards(): moved = lax.ppermute(stream, 'segment', ring)  2.02 us
    ppermute x3, waiting for transfers between devices, shards(): lax.ppermute(blocks[turn], 'tm', [(i, (i + turn) % count) for i in range(...  1.74 us
  transfers between devices with their start and end apart: 15, of which 7 were waited for; matrix products, arithmetic and copies ran while one was open for 10% of the time, Pallas kernels for 7%

profile of v11, /device:TPU:0, one launch (start us, length us, event | category | flops | bytes accessed | tf_op | source)
XLA Modules:
  0.0 35.0 jit_solution(7135301621561629038)
XLA Ops:
  0.0 0.0 copy-start.3
  0.0 0.5 %collective-permute-start.1 = (bf16[4,512,2,128]{3,2,1,0:T(2,128)(2,1)}, bf16[4,512,2,128]{3,2,1,0:T(2,128)(2,1)}, u32[]{:S(2)}, u32[]{:S(2)}) collective-permute-start(bf16[4,512,2,128]{3,2,1,0:T(2,128)(2,1)} %param.6), channel_id=1, source_target_pairs={{0,1},{1,0},{2,3},{3,2},{4,5},{5,4},{6,7},{7,6},{8,9},{9,8},{10,11... | collective-permute-start | bytes 3145736 | tf_op jit(solution)/shard_map/ppermute | solution.py:90
  0.5 0.5 %copy-done.3 = bf16[4,256,128]{2,1,0:T(8,128)(2,1)S(1)} copy-done((bf16[4,256,128]{2,1,0:T(8,128)(2,1)S(1)}, bf16[4,256,128]{2,1,0:T(8,128)(2,1)}, u32[]{:S(2)}) %copy-start.3) | copy-done | bytes 262168
  1.0 0.0 copy-start
  1.0 3.1 %collective-permute-start = (bf16[256,128]{1,0:T(8,128)(2,1)S(1)}, bf16[256,128]{1,0:T(8,128)(2,1)S(1)}, u32[]{:S(2)}, u32[]{:S(2)}) collective-permute-start(bf16[256,128]{1,0:T(8,128)(2,1)S(1)} %get-tuple-element.55), channel_id=1, source_target_pairs={{0,4},{4,8},{8,12},{12,0},{1,5},{5,9},{9,13},{13,1},{2,6},{6,10},{... | collective-permute-start | bytes 196616 | tf_op jit(solution)/shard_map/ppermute | solution.py:279
  4.1 2.1 %collective-permute-start.5 = (bf16[256,128]{1,0:T(8,128)(2,1)S(1)}, bf16[256,128]{1,0:T(8,128)(2,1)S(1)}, u32[]{:S(2)}, u32[]{:S(2)}) collective-permute-start(bf16[256,128]{1,0:T(8,128)(2,1)S(1)} %get-tuple-element.53), channel_id=1, source_target_pairs={{0,12},{4,0},{8,4},{12,8},{1,13},{5,1},{9,5},{13,9},{2,14},{6,2},{... | collective-permute-start | bytes 196616 | tf_op jit(solution)/shard_map/ppermute | solution.py:279
  6.1 0.9 %collective-permute-start.4 = (bf16[256,128]{1,0:T(8,128)(2,1)S(1)}, bf16[256,128]{1,0:T(8,128)(2,1)S(1)}, u32[]{:S(2)}, u32[]{:S(2)}) collective-permute-start(bf16[256,128]{1,0:T(8,128)(2,1)S(1)} %get-tuple-element.56), channel_id=1, source_target_pairs={{0,8},{4,12},{8,0},{12,4},{1,9},{5,13},{9,1},{13,5},{2,10},{6,14},... | collective-permute-start | bytes 196616 | tf_op jit(solution)/shard_map/ppermute | solution.py:279
  7.1 0.0 copy-done
  7.1 0.0 collective-permute-start.3
  7.1 1.7 %reshape.6.refs_0_ = bf16[4,512,256]{2,1,0:T(8,128)(2,1)S(1)} reshape(bf16[4,512,2,128]{3,2,1,0:T(2,128)(2,1)} %param.6) | data formatting | bytes 2097152 | tf_op jit(solution)/shard_map/reshape | solution.py:280
  8.8 0.0 collective-permute-done.1
  8.9 0.0 copy-start.2
  8.9 1.7 %reshape.7.refs_1_ = bf16[4,512,256]{2,1,0:T(8,128)(2,1)S(1)} reshape(bf16[4,512,2,128]{3,2,1,0:T(2,128)(2,1)} %collective-permute-done.1) | data formatting | bytes 2097152 | tf_op jit(solution)/shard_map/reshape | solution.py:281
  10.6 0.0 copy-start.1
  10.6 0.0 collective-permute-done.refs_8_
  10.6 0.0 collective-permute-done.5.refs_10_
  10.6 1.7 %collective-permute-done.4.refs_9_ = bf16[256,128]{1,0:T(8,128)(2,1)S(1)} collective-permute-done((bf16[256,128]{1,0:T(8,128)(2,1)S(1)}, bf16[256,128]{1,0:T(8,128)(2,1)S(1)}, u32[]{:S(2)}, u32[]{:S(2)}) %collective-permute-start.4) | collective-permute-done | bytes 65568 | tf_op jit(solution)/shard_map/ppermute | solution.py:279
  12.4 0.1 collective-permute-start.6
  12.5 0.0 copy-done.2
  12.5 0.5 %collective-permute-start.2 = (bf16[4,2,128]{2,1,0:T(2,128)(2,1)S(1)}, bf16[4,2,128]{2,1,0:T(2,128)(2,1)S(1)}, u32[]{:S(2)}, u32[]{:S(2)}) collective-permute-start(bf16[4,2,128]{2,1,0:T(2,128)(2,1)S(1)} %copy-done.2), channel_id=1, source_target_pairs={{0,1},{1,0},{2,3},{3,2},{4,5},{5,4},{6,7},{7,6},{8,9},{9,8},{10,11... | collective-permute-start | bytes 6152 | tf_op jit(solution)/shard_map/ppermute | solution.py:90
  13.0 1.0 %collective-permute-done.2.refs_3_ = bf16[4,2,128]{2,1,0:T(2,128)(2,1)S(1)} collective-permute-done((bf16[4,2,128]{2,1,0:T(2,128)(2,1)S(1)}, bf16[4,2,128]{2,1,0:T(2,128)(2,1)S(1)}, u32[]{:S(2)}, u32[]{:S(2)}) %collective-permute-start.2) | collective-permute-done | bytes 2080 | tf_op jit(solution)/shard_map/ppermute | solution.py:90
  14.0 0.0 collective-permute-done.3.refs_6_.other_skip
  14.0 0.0 collective-permute-done.6.refs_11_
  14.0 0.0 copy-done.1
  14.0 1.8 %shard_map.55 = (bf16[4,512,256]{2,1,0:T(8,128)(2,1)S(1)}, bf16[256,256]{1,0:T(8,128)(2,1)S(1)}, bf16[32,256]{1,0:T(8,128)(2,1)S(1)}, bf16[256,256]{1,0:T(8,128)...) custom-call(bf16[4,512,256]{2,1,0:T(8,128)(2,1)S(1)} %reshape.6.refs_0_, ...), custom_call_target="tpu_custom_call" | custom-call | flops 1 | bytes 1 | tf_op jit(solution)/shard_map/pallas_call | solution.py:239
  15.8 0.1 collective-permute-start.7
  15.9 2.0 %shard_map.56 = (bf16[4,512,256]{2,1,0:T(8,128)(2,1)S(1)}, bf16[256,256]{1,0:T(8,128)(2,1)S(1)}) custom-call(bf16[4,512,256]{2,1,0:T(8,128)(2,1)S(1)} %reshape.6.refs_0_, bf16[4,512,256]{2,1,0:T(8,128)(2,1)S(1)} %reshape.7.refs_1_, bf16[4,2,128]{2,1,0:T(2,128)(2,1)S(1)} %copy-done.2, bf16[4,2,128]{2,1,0:T(2,128)(2,1)S(1)} %collective-permute-done.2.refs_3_, ...), custom_call_target="tpu_custom_call" | custom-call | flops 1 | bytes 1 | tf_op jit(solution)/shard_map/pallas_call | solution.py:239
  17.9 1.9 %collective-permute-start.11 = (bf16[256,256]{1,0:T(8,128)(2,1)S(1)}, bf16[256,256]{1,0:T(8,128)(2,1)S(1)}, u32[]{:S(2)}, u32[]{:S(2)}) collective-permute-start(bf16[256,256]{1,0:T(8,128)(2,1)S(1)} %get-tuple-element.37), channel_id=1, source_target_pairs={{0,2},{1,3},{4,6},{5,7},{8,10},{9,11},{12,14},{13,15},{16,18},{17,... | collective-permute-start | bytes 393224 | tf_op jit(solution)/shard_map/ppermute | solution.py:317
  19.8 1.6 %collective-permute-done.7.refs_7_ = bf16[256,256]{1,0:T(8,128)(2,1)S(1)} collective-permute-done((bf16[256,256]{1,0:T(8,128)(2,1)S(1)}, bf16[256,256]{1,0:T(8,128)(2,1)S(1)}, u32[]{:S(2)}, u32[]{:S(2)}) %collective-permute-start.7) | collective-permute-done | bytes 131104 | tf_op jit(solution)/shard_map/ppermute | solution.py:317
  21.5 0.1 collective-permute-start.9
  21.6 0.5 %collective-permute-start.8 = (bf16[128,256]{1,0:T(8,128)(2,1)S(1)}, bf16[128,256]{1,0:T(8,128)(2,1)S(1)}, u32[]{:S(2)}, u32[]{:S(2)}) collective-permute-start(bf16[128,256]{1,0:T(8,128)(2,1)S(1)} %get-tuple-element.58), channel_id=1, source_target_pairs={{0,1},{1,0},{2,3},{3,2},{4,5},{5,4},{6,7},{7,6},{8,9},{9,8},{10,11... | collective-permute-start | bytes 196616 | tf_op jit(solution)/shard_map/ppermute | solution.py:90
  22.1 0.3 shard_map.57.refs_10_
  22.4 0.4 %collective-permute-done.9.refs_9_ = bf16[128,256]{1,0:T(8,128)(2,1)S(1)} collective-permute-done((bf16[128,256]{1,0:T(8,128)(2,1)S(1)}, bf16[128,256]{1,0:T(8,128)(2,1)S(1)}, u32[]{:S(2)}, u32[]{:S(2)}) %collective-permute-start.9) | collective-permute-done | bytes 65568 | tf_op jit(solution)/shard_map/ppermute | solution.py:90
  22.8 0.2 collective-permute-done.8.refs_8_
  23.0 0.0 collective-permute-done.11.refs_7_
  23.0 0.4 %collective-permute-start.12 = (bf16[256,256]{1,0:T(8,128)(2,1)S(1)}, bf16[256,256]{1,0:T(8,128)(2,1)S(1)}, u32[]{:S(2)}, u32[]{:S(2)}) collective-permute-start(bf16[256,256]{1,0:T(8,128)(2,1)S(1)} %collective-permute-done.11.refs_7_), channel_id=1, source_target_pairs={{0,1},{1,0},{2,3},{3,2},{4,5},{5,4},{6,7},{7,6},{8,9},{9,8},{10,11... | collective-permute-start | bytes 393224 | tf_op jit(solution)/shard_map/ppermute | solution.py:90
  23.4 0.3 shard_map.59.refs_13_
  23.7 0.7 %collective-permute-start.10 = (bf16[256,256]{1,0:T(8,128)(2,1)S(1)}, bf16[256,256]{1,0:T(8,128)(2,1)S(1)}, u32[]{:S(2)}, u32[]{:S(2)}) collective-permute-start(bf16[256,256]{1,0:T(8,128)(2,1)S(1)} %get-tuple-element.40), channel_id=1, source_target_pairs={{0,8},{1,12},{2,1},{3,5},{4,11},{5,15},{6,2},{7,6},{8,9},{9,13},{1... | collective-permute-start | bytes 393224 | tf_op jit(solution)/shard_map/ppermute | solution.py:336
  24.4 0.0 collective-permute-done.12.refs_8_
  24.4 1.7 %collective-permute-start.13 = (bf16[256,256]{1,0:T(8,128)(2,1)S(1)}, bf16[256,256]{1,0:T(8,128)(2,1)S(1)}, u32[]{:S(2)}, u32[]{:S(2)}) collective-permute-start(bf16[256,256]{1,0:T(8,128)(2,1)S(1)} %shard_map.60), channel_id=1, source_target_pairs={{0,1},{1,5},{2,8},{3,12},{4,2},{5,6},{6,11},{7,15},{8,0},{9,4},{10... | collective-permute-start | bytes 393224 | tf_op jit(solution)/shard_map/ppermute | solution.py:336
  26.2 6.8 %collective-permute-done.10.refs_0_ = bf16[256,256]{1,0:T(8,128)(2,1)S(1)} collective-permute-done((bf16[256,256]{1,0:T(8,128)(2,1)S(1)}, bf16[256,256]{1,0:T(8,128)(2,1)S(1)}, u32[]{:S(2)}, u32[]{:S(2)}) %collective-permute-start.10) | collective-permute-done | bytes 131104 | tf_op jit(solution)/shard_map/ppermute | solution.py:336
  33.0 0.0 collective-permute-done.13.refs_1_
  33.0 0.1 collective-permute-start.14
  33.1 1.2 %collective-permute-done.14.given = bf16[256,128]{1,0:T(8,128)(2,1)S(1)} collective-permute-done((bf16[256,128]{1,0:T(8,128)(2,1)S(1)}, bf16[256,128]{1,0:T(8,128)(2,1)S(1)}, u32[]{:S(2)}, u32[]{:S(2)}) %collective-permute-start.14) | collective-permute-done | bytes 65568 | tf_op jit(solution)/shard_map/ppermute | solution.py:90
  34.3 0.7 %shard_map.62 = bf16[2,256,128]{2,1,0:T(8,128)(2,1)} custom-call(bf16[256,128]{1,0:T(8,128)(2,1)S(1)} %get-tuple-element.51.kept, bf16[256,128]{1,0:T(8,128)(2,1)S(1)} %collective-permute-done.14.given), custom_call_target="tpu_custom_call" | custom-call | tf_op jit(solution)/shard_map/pallas_call | solution.py:353
  (6 shorter events, 0.1 us)
Async XLA Ops:
  0.0 0.9 %copy-start.3 = (bf16[4,256,128]{2,1,0:T(8,128)(2,1)S(1)}, bf16[4,256,128]{2,1,0:T(8,128)(2,1)}, u32[]{:S(2)}) copy-start(bf16[4,256,128]{2,1,0:T(8,128)(2,1)} %param.5) | copy-start | bytes 786436
  0.0 8.8 %collective-permute-start.1 = (bf16[4,512,2,128]{3,2,1,0:T(2,128)(2,1)}, bf16[4,512,2,128]{3,2,1,0:T(2,128)(2,1)}, u32[]{:S(2)}, u32[]{:S(2)}) collective-permute-start(bf16[4,512,2,128]{3,2,1,0:T(2,128)(2,1)} %param.6), channel_id=1, source_target_pairs={{0,1},{1,0},{2,3},{3,2},{4,5},{5,4},{6,7},{7,6},{8,9},{9,8},{10,11... | collective-permute-start | bytes 3145736 | tf_op jit(solution)/shard_map/ppermute | solution.py:90
  1.0 6.1 %copy-start = (bf16[4,256,128]{2,1,0:T(8,128)(2,1)S(1)}, bf16[4,256,128]{2,1,0:T(8,128)(2,1)}, u32[]{:S(2)}) copy-start(bf16[4,256,128]{2,1,0:T(8,128)(2,1)} %refs_5_.7) | copy-start | bytes 786436
  1.0 9.7 %collective-permute-start = (bf16[256,128]{1,0:T(8,128)(2,1)S(1)}, bf16[256,128]{1,0:T(8,128)(2,1)S(1)}, u32[]{:S(2)}, u32[]{:S(2)}) collective-permute-start(bf16[256,128]{1,0:T(8,128)(2,1)S(1)} %get-tuple-element.55), channel_id=1, source_target_pairs={{0,4},{4,8},{8,12},{12,0},{1,5},{5,9},{9,13},{13,1},{2,6},{6,10},{... | collective-permute-start | bytes 196616 | tf_op jit(solution)/shard_map/ppermute | solution.py:279
  4.1 6.6 %collective-permute-start.5 = (bf16[256,128]{1,0:T(8,128)(2,1)S(1)}, bf16[256,128]{1,0:T(8,128)(2,1)S(1)}, u32[]{:S(2)}, u32[]{:S(2)}) collective-permute-start(bf16[256,128]{1,0:T(8,128)(2,1)S(1)} %get-tuple-element.53), channel_id=1, source_target_pairs={{0,12},{4,0},{8,4},{12,8},{1,13},{5,1},{9,5},{13,9},{2,14},{6,2},{... | collective-permute-start | bytes 196616 | tf_op jit(solution)/shard_map/ppermute | solution.py:279
  6.1 6.2 %collective-permute-start.4 = (bf16[256,128]{1,0:T(8,128)(2,1)S(1)}, bf16[256,128]{1,0:T(8,128)(2,1)S(1)}, u32[]{:S(2)}, u32[]{:S(2)}) collective-permute-start(bf16[256,128]{1,0:T(8,128)(2,1)S(1)} %get-tuple-element.56), channel_id=1, source_target_pairs={{0,8},{4,12},{8,0},{12,4},{1,9},{5,13},{9,1},{13,5},{2,10},{6,14},... | collective-permute-start | bytes 196616 | tf_op jit(solution)/shard_map/ppermute | solution.py:279
  7.1 6.9 %collective-permute-start.3 = (bf16[4,256,128]{2,1,0:T(8,128)(2,1)S(1)}, bf16[4,256,128]{2,1,0:T(8,128)(2,1)S(1)}, u32[]{:S(2)}, u32[]{:S(2)}) collective-permute-start(bf16[4,256,128]{2,1,0:T(8,128)(2,1)S(1)} %copy-done), channel_id=1, source_target_pairs={{0,1},{1,0},{2,3},{3,2},{4,5},{5,4},{6,7},{7,6},{8,9},{9,8},{10,11... | collective-permute-start | bytes 786440 | tf_op jit(solution)/shard_map/ppermute | solution.py:90
  8.9 3.6 %copy-start.2 = (bf16[4,2,128]{2,1,0:T(2,128)(2,1)S(1)}, bf16[4,2,128]{2,1,0:T(2,128)(2,1)}, u32[]{:S(2)}) copy-start(bf16[4,2,128]{2,1,0:T(2,128)(2,1)} %refs_2_.7) | copy-start | bytes 6148
  10.6 3.4 %copy-start.1 = (bf16[4,256,256]{2,1,0:T(8,128)(2,1)S(1)}, bf16[4,256,256]{2,1,0:T(8,128)(2,1)}, u32[]{:S(2)}) copy-start(bf16[4,256,256]{2,1,0:T(8,128)(2,1)} %refs_4_.7) | copy-start | bytes 1572868
  12.4 1.6 %collective-permute-start.6 = (bf16[1024,128]{1,0:T(8,128)(2,1)S(1)}, bf16[1024,128]{1,0:T(8,128)(2,1)S(1)}, u32[]{:S(2)}, u32[]{:S(2)}) collective-permute-start(bf16[1024,128]{1,0:T(8,128)(2,1)S(1)} %pad_maximum_fusion), channel_id=1, source_target_pairs={{0,1},{1,0},{2,3},{3,2},{4,5},{5,4},{6,7},{7,6},{8,9},{9,8},{10,11... | collective-permute-start | bytes 786440 | tf_op jit(solution)/shard_map/ppermute | solution.py:90
  12.5 1.5 %collective-permute-start.2 = (bf16[4,2,128]{2,1,0:T(2,128)(2,1)S(1)}, bf16[4,2,128]{2,1,0:T(2,128)(2,1)S(1)}, u32[]{:S(2)}, u32[]{:S(2)}) collective-permute-start(bf16[4,2,128]{2,1,0:T(2,128)(2,1)S(1)} %copy-done.2), channel_id=1, source_target_pairs={{0,1},{1,0},{2,3},{3,2},{4,5},{5,4},{6,7},{7,6},{8,9},{9,8},{10,11... | collective-permute-start | bytes 6152 | tf_op jit(solution)/shard_map/ppermute | solution.py:90
  15.8 5.6 %collective-permute-start.7 = (bf16[256,256]{1,0:T(8,128)(2,1)S(1)}, bf16[256,256]{1,0:T(8,128)(2,1)S(1)}, u32[]{:S(2)}, u32[]{:S(2)}) collective-permute-start(bf16[256,256]{1,0:T(8,128)(2,1)S(1)} %get-tuple-element.32), channel_id=1, source_target_pairs={{0,2},{2,0},{1,3},{3,1},{4,6},{6,4},{5,7},{7,5},{8,10},{10,8},{9,1... | collective-permute-start | bytes 393224 | tf_op jit(solution)/shard_map/ppermute | solution.py:317
  17.9 5.1 %collective-permute-start.11 = (bf16[256,256]{1,0:T(8,128)(2,1)S(1)}, bf16[256,256]{1,0:T(8,128)(2,1)S(1)}, u32[]{:S(2)}, u32[]{:S(2)}) collective-permute-start(bf16[256,256]{1,0:T(8,128)(2,1)S(1)} %get-tuple-element.37), channel_id=1, source_target_pairs={{0,2},{1,3},{4,6},{5,7},{8,10},{9,11},{12,14},{13,15},{16,18},{17,... | collective-permute-start | bytes 393224 | tf_op jit(solution)/shard_map/ppermute | solution.py:317
  21.5 1.3 %collective-permute-start.9 = (bf16[128,256]{1,0:T(8,128)(2,1)S(1)}, bf16[128,256]{1,0:T(8,128)(2,1)S(1)}, u32[]{:S(2)}, u32[]{:S(2)}) collective-permute-start(bf16[128,256]{1,0:T(8,128)(2,1)S(1)} %get-tuple-element.57), channel_id=1, source_target_pairs={{0,1},{1,0},{2,3},{3,2},{4,5},{5,4},{6,7},{7,6},{8,9},{9,8},{10,11... | collective-permute-start | bytes 196616 | tf_op jit(solution)/shard_map/ppermute | solution.py:90
  21.6 1.4 %collective-permute-start.8 = (bf16[128,256]{1,0:T(8,128)(2,1)S(1)}, bf16[128,256]{1,0:T(8,128)(2,1)S(1)}, u32[]{:S(2)}, u32[]{:S(2)}) collective-permute-start(bf16[128,256]{1,0:T(8,128)(2,1)S(1)} %get-tuple-element.58), channel_id=1, source_target_pairs={{0,1},{1,0},{2,3},{3,2},{4,5},{5,4},{6,7},{7,6},{8,9},{9,8},{10,11... | collective-permute-start | bytes 196616 | tf_op jit(solution)/shard_map/ppermute | solution.py:90
  23.0 1.4 %collective-permute-start.12 = (bf16[256,256]{1,0:T(8,128)(2,1)S(1)}, bf16[256,256]{1,0:T(8,128)(2,1)S(1)}, u32[]{:S(2)}, u32[]{:S(2)}) collective-permute-start(bf16[256,256]{1,0:T(8,128)(2,1)S(1)} %collective-permute-done.11.refs_7_), channel_id=1, source_target_pairs={{0,1},{1,0},{2,3},{3,2},{4,5},{5,4},{6,7},{7,6},{8,9},{9,8},{10,11... | collective-permute-start | bytes 393224 | tf_op jit(solution)/shard_map/ppermute | solution.py:90
  23.7 9.2 %collective-permute-start.10 = (bf16[256,256]{1,0:T(8,128)(2,1)S(1)}, bf16[256,256]{1,0:T(8,128)(2,1)S(1)}, u32[]{:S(2)}, u32[]{:S(2)}) collective-permute-start(bf16[256,256]{1,0:T(8,128)(2,1)S(1)} %get-tuple-element.40), channel_id=1, source_target_pairs={{0,8},{1,12},{2,1},{3,5},{4,11},{5,15},{6,2},{7,6},{8,9},{9,13},{1... | collective-permute-start | bytes 393224 | tf_op jit(solution)/shard_map/ppermute | solution.py:336
  24.4 8.5 %collective-permute-start.13 = (bf16[256,256]{1,0:T(8,128)(2,1)S(1)}, bf16[256,256]{1,0:T(8,128)(2,1)S(1)}, u32[]{:S(2)}, u32[]{:S(2)}) collective-permute-start(bf16[256,256]{1,0:T(8,128)(2,1)S(1)} %shard_map.60), channel_id=1, source_target_pairs={{0,1},{1,5},{2,8},{3,12},{4,2},{5,6},{6,11},{7,15},{8,0},{9,4},{10... | collective-permute-start | bytes 393224 | tf_op jit(solution)/shard_map/ppermute | solution.py:336
  33.0 1.3 %collective-permute-start.14 = (bf16[256,128]{1,0:T(8,128)(2,1)S(1)}, bf16[256,128]{1,0:T(8,128)(2,1)S(1)}, u32[]{:S(2)}, u32[]{:S(2)}) collective-permute-start(bf16[256,128]{1,0:T(8,128)(2,1)S(1)} %get-tuple-element.52), channel_id=1, source_target_pairs={{0,1},{1,0},{2,3},{3,2},{4,5},{5,4},{6,7},{7,6},{8,9},{9,8},{10,11... | collective-permute-start | bytes 196616 | tf_op jit(solution)/shard_map/ppermute | solution.py:90
